TPU v7x, 128 devices: a whole 4x4x4 slice. The times are simulated.
128 devices in a mesh: row: 8 (over z, y_hi), col: 16 (over x, y_lo, core).
Axes of the slice: x: 4, y: 4 (y_hi: 2, y_lo: 2; y = y_hi * 2 + y_lo), z: 4, core: 2. Of those that a mesh axis runs over, the one named last changes fastest.
Arguments:
- features: bfloat16 [64, 512, 512], P('row', 'col'), may hold values from -6 to 6
- cotangent: bfloat16 [64, 512, 512], P('row', 'col'), may hold values from -6 to 6
- dw_kernel: float32 [49, 512], replicated, may hold values from -0.875 to 0.875
- dw_bias: float32 [512], replicated, may hold values from -3 to 3
- norm_gain_vector: float32 [512], replicated, may hold values from 0.25 to 1.75
- norm_bias: float32 [512], replicated, may hold values from -3 to 3
- pw_in_weight: bfloat16 [512, 2048], replicated, may hold values from -0.25 to 0.25
- pw_in_bias: float32 [2048], replicated, may hold values from -3 to 3
- pw_out_weight: bfloat16 [2048, 512], replicated, may hold values from -0.125 to 0.125
- pw_out_bias: float32 [512], replicated, may hold values from -3 to 3
- layer_scale: float32 [512], replicated, may hold values from 0.25 to 1
Outputs:
- block_out: bfloat16 [64, 512, 512], P('row', 'col')
- grad_features: bfloat16 [64, 512, 512], P('row', 'col')
- grad_pw_in: float32 [512, 2048], P(('row', 'col'))
- grad_pw_out: float32 [2048, 512], P(('row', 'col'))
- grad_channel: float32 [54, 512], P(None, ('row', 'col'))
- grad_pw_in_bias: float32 [2048], P(('row', 'col'))
All inputs are finite; a program needn't handle non-finite values.
Results may differ from a plain program's by a relative error of at most 0.013.
Values may be sent and summed in bfloat16 or wider, within the bound.
No kernel may reach another device: no remote copies, remote signals or barrier semaphores. Data moves between devices by JAX's collectives and lax.ppermute only.
A program may use at most 64 MiB of HBM per device.

v0:
```python
import math

import jax
import jax.numpy as jnp
from jax import lax
from jax.sharding import PartitionSpec as P


def with_halo(cells, sides, width):
    for axis, dim in sides:
        count = lax.axis_size(axis)
        ends = count - 1
        head = lax.slice_in_dim(cells, 0, width, axis=dim)
        tail = lax.slice_in_dim(cells, cells.shape[dim] - width, cells.shape[dim], axis=dim)
        cells = jnp.concatenate(
            [
                lax.ppermute(tail, axis, [(i, (i + 1) % count) for i in range(ends)]),
                cells,
                lax.ppermute(head, axis, [((i + 1) % count, i) for i in range(ends)]),
            ],
            axis=dim,
        )
    return cells


def gelu_plain(value):
    return 0.5 * value * (1.0 + jax.scipy.special.erf(value * 0.7071067811865476))


def gelu_slope(value):
    cumul = 0.5 * (1.0 + jax.scipy.special.erf(value * 0.7071067811865476))
    return cumul + value * jnp.exp(-0.5 * value * value) * 0.3989422804014327


def interior_rows(left, right):
    return lax.dot_general(
        left, right, (((0,), (0,)), ((), ())), preferred_element_type=jnp.float32
    )


def inner_cols(left, right):
    return lax.dot_general(
        left, right, (((1,), (1,)), ((), ())), preferred_element_type=jnp.float32
    )


def extend(field):
    return with_halo(field, (("row", 0), ("col", 1)), 3)


def kernel_entry(dw_kernel, index):
    return lax.dynamic_index_in_dim(dw_kernel, index, 0, keepdims=False)


def depthwise(padded, dw_kernel, dw_bias, height, width):

    def depthwise_step(row_tap, total):
        band = lax.dynamic_slice_in_dim(padded, row_tap, height, 0).astype(jnp.float32)
        for col_tap in range(7):
            total = total + band[:, col_tap : col_tap + width, :] * kernel_entry(
                dw_kernel, 7 * row_tap + col_tap
            )
        return total

    total = lax.fori_loop(
        0, 7, depthwise_step, jnp.zeros((height, width, padded.shape[2]), jnp.float32)
    )
    return total + dw_bias


def transposed(d_padded, dw_kernel, height, width):

    def transposed_step(row_tap, total):
        band = lax.dynamic_slice_in_dim(d_padded, 6 - row_tap, height, 0).astype(jnp.float32)
        for col_tap in range(7):
            total = total + band[:, 6 - col_tap : 6 - col_tap + width, :] * kernel_entry(
                dw_kernel, 7 * row_tap + col_tap
            )
        return total

    return lax.fori_loop(
        0, 7, transposed_step, jnp.zeros((height, width, d_padded.shape[2]), jnp.float32)
    )


def kernel_terms(padded, convolution_gradient, height, width):
    d_float = convolution_gradient.astype(jnp.float32)

    def kernel_step(row_tap, stacked):
        band = lax.dynamic_slice_in_dim(padded, row_tap, height, 0).astype(jnp.float32)
        seven = jnp.stack(
            [
                jnp.sum(band[:, col_tap : col_tap + width, :] * d_float, axis=(0, 1))
                for col_tap in range(7)
            ],
            axis=0,
        )
        return lax.dynamic_update_slice_in_dim(stacked, seven, 7 * row_tap, 0)

    return lax.fori_loop(0, 7, kernel_step, jnp.zeros((49, padded.shape[2]), jnp.float32))


def pointwise(
    conv_rows,
    feat_rows,
    cot_rows,
    norm_gain_vector,
    norm_bias,
    pw_in_weight,
    pw_in_bias,
    pw_out_weight,
    pw_out_bias,
    layer_scale,
):
    mean_c = jnp.mean(conv_rows, axis=-1, keepdims=True)
    centred = conv_rows - mean_c
    inverse_deviation = lax.rsqrt(jnp.mean(centred * centred, axis=-1, keepdims=True) + 1e-06)
    centered_input = centred * inverse_deviation
    normed = (centered_input * norm_gain_vector + norm_bias).astype(jnp.bfloat16)
    pre_act = jnp.dot(normed, pw_in_weight, preferred_element_type=jnp.float32) + pw_in_bias
    act = gelu_plain(pre_act).astype(jnp.bfloat16)
    branch = jnp.dot(act, pw_out_weight, preferred_element_type=jnp.float32) + pw_out_bias
    block_rows = (feat_rows.astype(jnp.float32) + layer_scale * branch).astype(jnp.bfloat16)
    cot_float = cot_rows.astype(jnp.float32)
    g_scale = jnp.sum(cot_float * branch, axis=0)
    d_branch = (cot_float * layer_scale).astype(jnp.bfloat16)
    g_out_bias = jnp.sum(d_branch.astype(jnp.float32), axis=0)
    d_act = inner_cols(d_branch, pw_out_weight)
    d_pre = (d_act * gelu_slope(pre_act)).astype(jnp.bfloat16)
    g_in_bias = jnp.sum(d_pre.astype(jnp.float32), axis=0)
    normalized_gradient = inner_cols(d_pre, pw_in_weight)
    g_gain = jnp.sum(normalized_gradient * centered_input, axis=0)
    g_nbias = jnp.sum(normalized_gradient, axis=0)
    centered_input_gradient = normalized_gradient * norm_gain_vector
    convolution_gradient = inverse_deviation * (
        centered_input_gradient
        - jnp.mean(centered_input_gradient, axis=-1, keepdims=True)
        - centered_input
        * jnp.mean(centered_input_gradient * centered_input, axis=-1, keepdims=True)
    )
    convolution_gradient = convolution_gradient.astype(jnp.bfloat16)
    return (
        block_rows,
        convolution_gradient,
        normed,
        act,
        d_branch,
        d_pre,
        (g_in_bias, g_out_bias, g_scale, g_gain, g_nbias),
    )


def shards(
    features,
    cotangent,
    dw_kernel,
    dw_bias,
    norm_gain_vector,
    norm_bias,
    pw_in_weight,
    pw_in_bias,
    pw_out_weight,
    pw_out_bias,
    layer_scale,
):
    tile_rows, tile_cols, channels = features.shape
    hidden = pw_in_weight.shape[1]
    count = tile_rows * tile_cols
    devices_all = lax.axis_size("row") * lax.axis_size("col")
    tokens = count * devices_all
    factor = 1.0 / math.sqrt(tokens)
    padded = extend(features)
    conv_out = depthwise(padded, dw_kernel, dw_bias, tile_rows, tile_cols)
    block_rows, convolution_gradient, normed, act, d_branch, d_pre, smalls = pointwise(
        conv_out.reshape(count, channels),
        features.reshape(count, channels),
        cotangent.reshape(count, channels),
        norm_gain_vector,
        norm_bias,
        pw_in_weight,
        pw_in_bias,
        pw_out_weight,
        pw_out_bias,
        layer_scale,
    )
    piece = act
    grad_out = lax.psum_scatter(
        interior_rows(piece, d_branch) * factor, ("row", "col"), scatter_dimension=0, tiled=True
    )
    piece = normed
    grad_in = lax.psum_scatter(
        interior_rows(piece, d_pre) * factor, ("row", "col"), scatter_dimension=0, tiled=True
    )
    d_tile = convolution_gradient.reshape(tile_rows, tile_cols, channels)
    d_padded = extend(d_tile)
    grad_features = (
        cotangent.astype(jnp.float32) + transposed(d_padded, dw_kernel, tile_rows, tile_cols)
    ).astype(jnp.bfloat16)
    g_in_bias, g_out_bias, g_scale, g_gain, g_nbias = smalls
    kernel_rows = kernel_terms(padded, d_tile, tile_rows, tile_cols)
    bias_gradient = jnp.sum(d_tile.astype(jnp.float32), axis=(0, 1))
    channel_rows = (
        jnp.concatenate(
            [kernel_rows, jnp.stack([bias_gradient, g_gain, g_nbias, g_out_bias, g_scale], axis=0)],
            axis=0,
        )
        * factor
    )
    channel_part, bias_part = (
        lax.psum_scatter(channel_rows, ("row", "col"), scatter_dimension=1, tiled=True),
        lax.psum_scatter(
            (g_in_bias * factor).reshape(1, hidden), ("row", "col"), scatter_dimension=1, tiled=True
        ),
    )
    return (
        block_rows.reshape(tile_rows, tile_cols, channels),
        grad_features,
        grad_in,
        grad_out,
        channel_part,
        bias_part.reshape(-1),
    )


def solution(mesh):
    return jax.shard_map(
        shards,
        mesh=mesh,
        in_specs=(
            P("row", "col", None),
            P("row", "col", None),
            P(),
            P(),
            P(),
            P(),
            P(),
            P(),
            P(),
            P(),
            P(),
        ),
        out_specs=(
            P("row", "col", None),
            P("row", "col", None),
            P(("row", "col"), None),
            P(("row", "col"), None),
            P(None, ("row", "col")),
            P(("row", "col")),
        ),
        check_vma=False,
    )
```

profile of v0, /device:TPU:0, one launch (start us, length us, event | category | flops | bytes accessed | tf_op | source)
XLA Modules:
  0.0 1535.1 jit_solution(15457423238635716409)
XLA Ops:
  8.3 5.2 collective-permute-start
  13.5 1.3 collective-permute-start.1
  16.7 4.8 collective-permute-done.1
  22.4 1.3 collective-permute-start.2
  23.7 1.3 collective-permute-start.3
  25.0 2.7 collective-permute-done.3
  29.0 11.4 while.46
  45.9 1.5 fusion.30
  47.4 1.4 convert_reduce_fusion
  50.7 1.3 collective-permute-start.5
  52.0 7.3 collective-permute-start.4
  60.0 13.8 while.45
  60.6 1.4 dynamic_update_slice.8
  62.5 1.4 dynamic_update_slice.8
  64.5 1.4 dynamic_update_slice.8
  66.5 1.4 dynamic_update_slice.8
  68.4 1.4 dynamic_update_slice.8
  70.4 1.4 dynamic_update_slice.8
  72.4 1.4 dynamic_update_slice.8
  73.7 4.0 convolution_multiply_fusion.1
  78.6 4.5 collective-permute-start.6
  83.1 1.3 collective-permute-start.7
  84.4 1.4 copy.26
  87.6 11.5 while.47
  99.1 1.7 convert_reduce_fusion.1
  103.0 2.7 convolution_multiply_fusion
  105.7 624.2 %reduce-scatter.7.cloned.1.call-done = f32[16,1]{1,0:T(8,128)} async-done(((f32[2048,1]{1,0:T(8,128)}), f32[16,1]{1,0:T(8,128)}) %reduce-scatter.7.cloned.1.call-update) | async-done | bytes 80
  729.9 1.3 copy.27
  731.2 153.4 %all-reduce.5.cloned.1.call-done = (f32[512,2048]{1,0:T(8,128)}, f32[54,512]{0,1:T(8,128)}) async-done(((f32[512,2048]{1,0:T(8,128)}, f32[54,512]{0,1:T(8,128)}), (f32[512,2048]{1,0:T(8,128)}, f32[54,512]{0,1:T(8,128)})) %all-reduce.5.cloned.1.call-update) | async-done | bytes 4304912
  884.5 1.3 constant_dynamic-slice_fusion.14
  885.8 1.5 constant_dynamic-slice_fusion.15
  887.3 641.3 %reduce-scatter.5.cloned.1.call-done = f32[16,512]{1,0:T(8,128)} async-done(((f32[2048,512]{1,0:T(8,128)}), f32[16,512]{1,0:T(8,128)}) %reduce-scatter.5.cloned.1.call-update) | async-done | bytes 32784 | tf_op jit(solution)/shard_map/reduce_scatter | solution.py:187
  (143 shorter events, 43.8 us)
Async XLA Ops:
  7.2 36.8 %copy-start = (bf16[512,2048]{1,0:T(8,128)(2,1)S(1)}, bf16[512,2048]{1,0:T(8,128)(2,1)}, u32[]{:S(2)}) copy-start(bf16[512,2048]{1,0:T(8,128)(2,1)} %param.23) | copy-start | bytes 6291460
  7.2 722.7 %reduce-scatter.7.cloned.1.call-start = ((), (), s32[]{:S(2)}) async-start(), calls=%async_computation.3 | async-start | bytes 1056768
  8.3 7.4 collective-permute-start
  13.5 8.0 collective-permute-start.1
  21.5 0.8 copy-start.7
  22.4 2.6 collective-permute-start.2
  23.7 4.0 collective-permute-start.3
  29.0 11.5 copy-start.15
  29.0 13.8 copy-start.14
  29.0 13.8 copy-start.16
  40.5 3.5 copy-start.13
  44.0 1.1 copy-start.5
  44.0 1.1 copy-start.8
  44.0 1.1 copy-start.12
  44.0 1.1 copy-start.17
  44.0 1.8 copy-start.18
  44.0 1.8 copy-start.19
  45.1 2.3 copy-start.3
  47.3 1.4 copy-start.10
  47.4 1.4 copy-start.2
  48.7 1.0 copy-start.6
  50.7 27.0 %collective-permute-start.5 = (bf16[3,32,512]{2,1,0:T(8,128)(2,1)}, bf16[3,32,512]{2,1,0:T(8,128)(2,1)}, u32[]{:S(2)}, u32[]{:S(2)}) collective-permute-start(bf16[3,32,512]{2,1,0:T(8,128)(2,1)} %bitcast.13), channel_id=1, source_target_pairs={{16,0},{32,16},{48,32},{64,48},{80,64},{96,80},{112,96},{17,1},{33... | collective-permute-start | bytes 294920 | tf_op jit(solution)/shard_map/ppermute | solution.py:19
  52.0 25.8 %collective-permute-start.4 = (bf16[3,32,512]{2,1,0:T(8,128)(2,1)}, bf16[3,32,512]{2,1,0:T(8,128)(2,1)}, u32[]{:S(2)}, u32[]{:S(2)}) collective-permute-start(bf16[3,32,512]{2,1,0:T(8,128)(2,1)} %bitcast.11), channel_id=1, source_target_pairs={{0,16},{16,32},{32,48},{48,64},{64,80},{80,96},{96,112},{1,17},{17... | collective-permute-start | bytes 294920 | tf_op jit(solution)/shard_map/ppermute | solution.py:17
  77.7 9.9 copy-start.1
  78.6 7.3 collective-permute-start.6
  83.1 3.3 collective-permute-start.7
  85.9 798.7 %all-reduce.5.cloned.1.call-start = ((), (), s32[]{:S(2)}) async-start(), calls=%async_computation.4 | async-start | bytes 8912896
  87.6 13.2 copy-start.9
  101.7 1.2 copy-start.4
  101.7 1.3 copy-start.11
  101.7 1426.9 %reduce-scatter.5.cloned.1.call-start = ((), (), s32[]{:S(2)}) async-start(), calls=%async_computation.2 | async-start | bytes 4227072 | tf_op jit(solution)/shard_map/reduce_scatter | solution.py:187
Sparse Core Ops, SparseCore 0:
  86.0 643.8 reduce-scatter.6
  735.8 148.7 all-reduce.4
  887.6 640.9 reduce-scatter.4
where the time goes:
time: 1540 us
  waiting for transfers between devices  1430 us (93%)
  local copies, waits for them, and re-layouts  35.8 us (2%)
  starting transfers between devices  23.5 us (2%)
  other arithmetic  21.3 us (1%)
    unnamed x5, waiting for transfers between devices  778 us
    reduce_scatter x1, waiting for transfers between devices, shards(): lax.psum_scatter(interior_rows(piece, d_branch) * factor, ('row', 'col'),...  641 us
  transfers between devices with their start and end apart: 11, of which 7 were waited for; matrix products, arithmetic and copies ran while one was open for 3% of the time, Pallas kernels for 0%

commit v1 on v0

--- a/solution.py
+++ b/solution.py
@@ -3,7 +3,13 @@
 import jax
 import jax.numpy as jnp
 from jax import lax
+from jax.sharding import Mesh
 from jax.sharding import PartitionSpec as P
+
+CHIPS = ("z", "yh", "x", "yl")
+EVERY = CHIPS + ("c",)
+ROW = ("z", "yh")
+COL = ("x", "yl", "c")
 
 
 def with_halo(cells, sides, width):
@@ -45,7 +51,7 @@
 
 
 def extend(field):
-    return with_halo(field, (("row", 0), ("col", 1)), 3)
+    return with_halo(field, ((ROW, 0), (COL, 1)), 3)
 
 
 def kernel_entry(dw_kernel, index):
@@ -166,7 +172,7 @@
     tile_rows, tile_cols, channels = features.shape
     hidden = pw_in_weight.shape[1]
     count = tile_rows * tile_cols
-    devices_all = lax.axis_size("row") * lax.axis_size("col")
+    devices_all = lax.axis_size(EVERY)
     tokens = count * devices_all
     factor = 1.0 / math.sqrt(tokens)
     padded = extend(features)
@@ -183,14 +189,19 @@
         pw_out_bias,
         layer_scale,
     )
-    piece = act
-    grad_out = lax.psum_scatter(
-        interior_rows(piece, d_branch) * factor, ("row", "col"), scatter_dimension=0, tiled=True
-    )
-    piece = normed
-    grad_in = lax.psum_scatter(
-        interior_rows(piece, d_pre) * factor, ("row", "col"), scatter_dimension=0, tiled=True
-    )
+    core = lax.axis_index("c")
+    out_term = interior_rows(act, d_branch).reshape(64, 2, 16, channels)
+    in_term = interior_rows(normed, d_pre).reshape(64, 2, 4, 4, channels)
+    in_term = in_term.reshape(64, 2, 16, channels)
+    both = jnp.concatenate([out_term, in_term], axis=2).astype(jnp.bfloat16)
+    mine = lax.dynamic_index_in_dim(both, core, 1, keepdims=False)
+    theirs = lax.dynamic_index_in_dim(both, 1 - core, 1, keepdims=False)
+    met = lax.ppermute(theirs, "c", [(0, 1), (1, 0)])
+    chip_sum = (mine.astype(jnp.float32) + met.astype(jnp.float32)).astype(jnp.bfloat16)
+    spread = lax.all_to_all(chip_sum, CHIPS, 0, 0, tiled=True)
+    summed = jnp.sum(spread.astype(jnp.float32), axis=0) * factor
+    grad_out = summed[:16]
+    grad_in = summed[16:].reshape(4, hidden)
     d_tile = convolution_gradient.reshape(tile_rows, tile_cols, channels)
     d_padded = extend(d_tile)
     grad_features = (
@@ -206,46 +217,38 @@
         )
         * factor
     )
-    channel_part, bias_part = (
-        lax.psum_scatter(channel_rows, ("row", "col"), scatter_dimension=1, tiled=True),
-        lax.psum_scatter(
-            (g_in_bias * factor).reshape(1, hidden), ("row", "col"), scatter_dimension=1, tiled=True
-        ),
-    )
+    small = jnp.concatenate(
+        [
+            channel_rows.T.reshape(128, 4, 54),
+            (g_in_bias * factor).reshape(128, 4, 4),
+            jnp.zeros((128, 4, 70), jnp.float32),
+        ],
+        axis=2,
+    )
+    small = jnp.sum(lax.all_to_all(small, EVERY, 0, 0, tiled=True), axis=0)
     return (
         block_rows.reshape(tile_rows, tile_cols, channels),
         grad_features,
         grad_in,
         grad_out,
-        channel_part,
-        bias_part.reshape(-1),
+        small[:, :54].T,
+        small[:, 54:58].reshape(-1),
     )
 
 
 def solution(mesh):
+    fine = Mesh(mesh.devices.reshape(4, 2, 4, 2, 2), EVERY)
     return jax.shard_map(
         shards,
-        mesh=mesh,
-        in_specs=(
-            P("row", "col", None),
-            P("row", "col", None),
-            P(),
-            P(),
-            P(),
-            P(),
-            P(),
-            P(),
-            P(),
-            P(),
-            P(),
-        ),
+        mesh=fine,
+        in_specs=(P(ROW, COL, None), P(ROW, COL, None)) + (P(),) * 9,
         out_specs=(
-            P("row", "col", None),
-            P("row", "col", None),
-            P(("row", "col"), None),
-            P(("row", "col"), None),
-            P(None, ("row", "col")),
-            P(("row", "col")),
+            P(ROW, COL, None),
+            P(ROW, COL, None),
+            P(EVERY, None),
+            P(EVERY, None),
+            P(None, EVERY),
+            P(EVERY),
         ),
         check_vma=False,
     )

time: 1540 us -> 192 us (0.12)
  waiting for transfers between devices: 1430 us -> 43.5 us
  other arithmetic: 21.3 us -> 50.5 us
  starting transfers between devices: 23.5 us -> 44.2 us
    unnamed x5 -> x0, waiting for transfers between devices: 778 us -> none
    reduce_scatter x1 -> x0, waiting for transfers between devices: 641 us -> none  [shards(): lax.psum_scatter(interior_rows(piece, d_branch) * factor, ('row', 'col'),...]
    all_to_all x0 -> x2, waiting for transfers between devices: none -> 35.4 us  [the longest x1 29.1 us: shards(): spread = lax.all_to_all(chip_sum, CHIPS, 0, 0, tiled=True)]
    all_to_all x0 -> x2, starting transfers between devices: none -> 19.9 us  [the longest x1 14.3 us: shards(): small = jnp.sum(lax.all_to_all(small, EVERY, 0, 0, tiled=True), axis=0)]
  transfers between devices with their start and end apart: 11 -> 11, of which waited for: 7 -> 6; matrix products, arithmetic and copies ran while one was open for 3% -> 18% of each run, Pallas kernels for 0% -> 0%
where the time goes in v1:
time: 192 us; the launch traced here: 189 us
  other arithmetic  50.5 us (26%)
  starting transfers between devices  44.2 us (23%)
  waiting for transfers between devices  43.5 us (23%)
  local copies, waits for them, and re-layouts  39.6 us (21%)
  matrix products  9.92 us (5%)
    all_to_all x1, waiting for transfers between devices, shards(): spread = lax.all_to_all(chip_sum, CHIPS, 0, 0, tiled=True)  29.1 us
    ppermute x4, starting transfers between devices, with_halo(): lax.ppermute(tail, axis, [(i, (i + 1) % count) for i in range(ends)])  18 us
    add x7, other arithmetic, transposed_step(): total + band[:, 6 - col_tap:6 - col_tap + width, :] * kernel_entry(dw_ker...  15.2 us
    all_to_all x1, starting transfers between devices, shards(): small = jnp.sum(lax.all_to_all(small, EVERY, 0, 0, tiled=True), axis=0)  14.3 us
    dynamic_slice x14, local copies, waits for them, and re-layouts, kernel_entry(): return lax.dynamic_index_in_dim(dw_kernel, index, 0, keepdims=False)  13.2 us
    dynamic_update_slice x7, local copies, waits for them, and re-layouts, kernel_step(): return lax.dynamic_update_slice_in_dim(stacked, seven, 7 * row_tap, 0)  9.59 us
    convert_element_type x7, other arithmetic, transposed_step(): lax.dynamic_slice_in_dim(d_padded, 6 - row_tap, height, 0)  7.31 us
    ppermute x4, waiting for transfers between devices, with_halo(): lax.ppermute(head, axis, [((i + 1) % count, i) for i in range(ends)])  6.97 us
  transfers between devices with their start and end apart: 11, of which 6 were waited for; matrix products, arithmetic and copies ran while one was open for 18% of the time, Pallas kernels for 0%

profile of v1, /device:TPU:0, one launch (start us, length us, event | category | flops | bytes accessed | tf_op | source)
XLA Modules:
  0.0 189.4 jit_solution(6373315272056155197)
XLA Ops:
  1.8 5.2 %collective-permute-start = (bf16[3,32,512]{2,1,0:T(8,128)(2,1)S(1)}, bf16[3,32,512]{2,1,0:T(8,128)(2,1)S(1)}, u32[]{:S(2)}, u32[]{:S(2)}) collective-permute-start(bf16[3,32,512]{2,1,0:T(8,128)(2,1)S(1)} %get-tuple-element.415), channel_id=1, source_target_pairs={{0,16},{16,32},{32,48},{48,64},{64,80},{80,96},{96,112},{1,17},{17... | collective-permute-start | bytes 294920 | tf_op jit(solution)/shard_map/ppermute | solution.py:23
  10.1 4.8 %collective-permute-done.1 = bf16[3,32,512]{2,1,0:T(8,128)(2,1)S(1)} collective-permute-done((bf16[3,32,512]{2,1,0:T(8,128)(2,1)S(1)}, bf16[3,32,512]{2,1,0:T(8,128)(2,1)S(1)}, u32[]{:S(2)}, u32[]{:S(2)}) %collective-permute-start.1) | collective-permute-done | bytes 98336 | tf_op jit(solution)/shard_map/ppermute | solution.py:25
  18.3 2.1 %collective-permute-done.3 = bf16[14,3,512]{2,1,0:T(4,128)(2,1)S(1)} collective-permute-done((bf16[14,3,512]{2,1,0:T(4,128)(2,1)S(1)}, bf16[14,3,512]{2,1,0:T(4,128)(2,1)S(1)}, u32[]{:S(2)}, u32[]{:S(2)}) %collective-permute-start.3) | collective-permute-done | bytes 43040 | tf_op jit(solution)/shard_map/ppermute | solution.py:25
  21.7 11.5 %while.46 = (s32[]{:T(128)}, f32[8,32,512]{2,1,0:T(8,128)S(1)}, bf16[14,38,512]{2,1,0:T(8,128)(2,1)S(1)}, f32[49,512]{1,0:T(8,128)}, s32[]{:T(128)}, /*index=5*/...) while((s32[]{:T(128)}, f32[8,32,512]{2,1,0:T(8,128)S(1)}, ...), condition=%wide.region_1.2_spmd.clone, body=%wide.region_0.1_spmd.clone.sunk | while | flops 2121759 | bytes 5696033 | solution.py:71
  38.5 2.1 %fusion.35 = (f32[512]{0:T(512)}, bf16[256,512]{1,0:T(8,128)(2,1)}, bf16[256,512]{1,0:T(8,128)(2,1)S(1)}) fusion(bf16[8,32,512]{2,1,0:T(8,128)(2,1)S(1)} %copy-done.9, f32[512]{0:T(512)S(1)} %copy-done.16, bf16[8,32,512]{2,1,0:T(8,128)(2,1)S(1)} %copy-done.7, f32[512]{0:T(512)S(1)} %copy-done.23, bf16[256,2048]{1,0:T(8,128)(2,1)S(1)} %get-tuple-element.418, ...), kind=kOutput, calls=%fused_computation.95 | convolution fusion | flops 538181120 | bytes 4200448 | tf_op jit(solution)/shard_map/dot_general | solution.py:128
  40.5 1.4 convert_reduce_fusion.1
  41.9 1.5 multiply_reduce_fusion
  45.6 6.6 %collective-permute-start.4 = (bf16[3,32,512]{2,1,0:T(8,128)(2,1)S(1)}, bf16[3,32,512]{2,1,0:T(8,128)(2,1)S(1)}, u32[]{:S(2)}, u32[]{:S(2)}) collective-permute-start(bf16[3,32,512]{2,1,0:T(8,128)(2,1)S(1)} %bitcast.154), channel_id=1, source_target_pairs={{0,16},{16,32},{32,48},{48,64},{64,80},{80,96},{96,112},{1,17},{17... | collective-permute-start | bytes 294920 | tf_op jit(solution)/shard_map/ppermute | solution.py:23
  52.2 2.0 %convolution_convert_fusion = bf16[512,2048]{1,0:T(8,128)(2,1)} fusion(bf16[256,512]{1,0:T(8,128)(2,1)S(1)} %add_convert_fusion, bf16[256,2048]{1,0:T(8,128)(2,1)S(1)} %get-tuple-element.422), kind=kOutput, calls=%fused_computation.67 | convolution fusion | flops 537919488 | bytes 3407872 | tf_op jit(solution)/shard_map/dot_general | solution.py:42
  55.1 4.9 %collective-permute-start.6 = (bf16[14,3,512]{2,1,0:T(4,128)(2,1)}, bf16[14,3,512]{2,1,0:T(4,128)(2,1)}, u32[]{:S(2)}, u32[]{:S(2)}) collective-permute-start(bf16[14,3,512]{2,1,0:T(4,128)(2,1)} %get-tuple-element.406), channel_id=1, source_target_pairs={{0,1},{1,2},{2,3},{3,4},{4,5},{5,6},{6,7},{7,8},{8,9},{9,10},{10,1... | collective-permute-start | bytes 129032 | tf_op jit(solution)/shard_map/ppermute | solution.py:23
  62.0 1.8 mul.720
  63.8 4.4 %reshape_reshape.4 = bf16[64,2,16,512]{3,2,1,0:T(8,128)(2,1)} reshape(bf16[512,2048]{1,0:T(8,128)(2,1)} %convolution_convert_fusion) | data formatting | bytes 4194304 | tf_op jit(solution)/shard_map/reshape;reshape | solution.py:195
  68.1 2.3 %copy.25 = bf16[2048,256]{1,0:T(8,128)(2,1)} copy(bf16[2048,256]{0,1:T(8,128)(2,1)} %bitcast.130) | data formatting | bytes 2097152 | tf_op jit(solution)/shard_map/convert_element_type | solution.py:127
  70.4 2.0 %pad_maximum_fusion.1 = bf16[14,38,512]{2,1,0:T(8,128)(2,1)} fusion(bf16[14,3,512]{2,1,0:T(4,128)(2,1)} %collective-permute-done.7, bf16[3,32,512]{2,1,0:T(8,128)(2,1)S(1)} %collective-permute-done.5, bf16[8,32,512]{2,1,0:T(8,128)(2,1)S(1)} %bitcast.128, bf16[3,32,512]{2,1,0:T(8,128)(2,1)} %copy-done.8, bf16[14,3,512]{2,1,0:T(4,128)(2,1)} %collective-permute-done.6), kind=kLoop, calls=%fused_computation.85 | loop fusion | flops 2723840 | bytes 1089536 | tf_op jit(solution)/shard_map/concatenate | solution.py:21
  72.4 29.2 %while.47 = (s32[]{:T(128)}, f32[8,32,512]{2,1,0:T(8,128)}, bf16[14,38,512]{2,1,0:T(8,128)(2,1)}, f32[49,512]{1,0:T(8,128)}, s32[]{:T(128)}, /*index=5*/s32[]{:T...) while((s32[]{:T(128)}, f32[8,32,512]{2,1,0:T(8,128)}, ...), condition=%wide.region_7.8_spmd.clone, body=%wide.region_6.7_spmd.clone.sunk | while | flops 2121763 | bytes 5696087 | solution.py:87
  77.7 2.3 %fusion.60 = f32[8,32,512]{2,1,0:T(8,128)} fusion(f32[8,38,512]{2,1,0:T(8,128)S(1)} %dynamic-slice_convert_fusion.8, f32[8,32,512]{2,1,0:T(8,128)} %get-tuple-element.620, f32[512]{0:T(512)S(1)} %bitcast.141, f32[512]{0:T(512)S(1)} %bitcast.142, f32[512]{0:T(512)S(1)} %bitcast.143, f32[512]{0:T(512)S(1)} %bitcast.144, f32[512]{0:T(512)S(1)} %bitcast.145, ...), kind=kLoop, calls=%fused_computation.38.clone.1 | loop fusion | flops 1966080 | bytes 4732929 | tf_op jit(solution)/shard_map/while/body/eval_jaxpr/add | solution.py:82
  82.0 2.3 %fusion.60 = f32[8,32,512]{2,1,0:T(8,128)} fusion(f32[8,38,512]{2,1,0:T(8,128)S(1)} %dynamic-slice_convert_fusion.8, f32[8,32,512]{2,1,0:T(8,128)} %get-tuple-element.620, f32[512]{0:T(512)S(1)} %bitcast.141, f32[512]{0:T(512)S(1)} %bitcast.142, f32[512]{0:T(512)S(1)} %bitcast.143, f32[512]{0:T(512)S(1)} %bitcast.144, f32[512]{0:T(512)S(1)} %bitcast.145, ...), kind=kLoop, calls=%fused_computation.38.clone.1 | loop fusion | flops 1966080 | bytes 4732929 | tf_op jit(solution)/shard_map/while/body/eval_jaxpr/add | solution.py:82
  86.3 2.3 %fusion.60 = f32[8,32,512]{2,1,0:T(8,128)} fusion(f32[8,38,512]{2,1,0:T(8,128)S(1)} %dynamic-slice_convert_fusion.8, f32[8,32,512]{2,1,0:T(8,128)} %get-tuple-element.620, f32[512]{0:T(512)S(1)} %bitcast.141, f32[512]{0:T(512)S(1)} %bitcast.142, f32[512]{0:T(512)S(1)} %bitcast.143, f32[512]{0:T(512)S(1)} %bitcast.144, f32[512]{0:T(512)S(1)} %bitcast.145, ...), kind=kLoop, calls=%fused_computation.38.clone.1 | loop fusion | flops 1966080 | bytes 4732929 | tf_op jit(solution)/shard_map/while/body/eval_jaxpr/add | solution.py:82
  90.6 2.3 %fusion.60 = f32[8,32,512]{2,1,0:T(8,128)} fusion(f32[8,38,512]{2,1,0:T(8,128)S(1)} %dynamic-slice_convert_fusion.8, f32[8,32,512]{2,1,0:T(8,128)} %get-tuple-element.620, f32[512]{0:T(512)S(1)} %bitcast.141, f32[512]{0:T(512)S(1)} %bitcast.142, f32[512]{0:T(512)S(1)} %bitcast.143, f32[512]{0:T(512)S(1)} %bitcast.144, f32[512]{0:T(512)S(1)} %bitcast.145, ...), kind=kLoop, calls=%fused_computation.38.clone.1 | loop fusion | flops 1966080 | bytes 4732929 | tf_op jit(solution)/shard_map/while/body/eval_jaxpr/add | solution.py:82
  94.9 2.3 %fusion.60 = f32[8,32,512]{2,1,0:T(8,128)} fusion(f32[8,38,512]{2,1,0:T(8,128)S(1)} %dynamic-slice_convert_fusion.8, f32[8,32,512]{2,1,0:T(8,128)} %get-tuple-element.620, f32[512]{0:T(512)S(1)} %bitcast.141, f32[512]{0:T(512)S(1)} %bitcast.142, f32[512]{0:T(512)S(1)} %bitcast.143, f32[512]{0:T(512)S(1)} %bitcast.144, f32[512]{0:T(512)S(1)} %bitcast.145, ...), kind=kLoop, calls=%fused_computation.38.clone.1 | loop fusion | flops 1966080 | bytes 4732929 | tf_op jit(solution)/shard_map/while/body/eval_jaxpr/add | solution.py:82
  99.2 2.3 %fusion.60 = f32[8,32,512]{2,1,0:T(8,128)} fusion(f32[8,38,512]{2,1,0:T(8,128)S(1)} %dynamic-slice_convert_fusion.8, f32[8,32,512]{2,1,0:T(8,128)} %get-tuple-element.620, f32[512]{0:T(512)S(1)} %bitcast.141, f32[512]{0:T(512)S(1)} %bitcast.142, f32[512]{0:T(512)S(1)} %bitcast.143, f32[512]{0:T(512)S(1)} %bitcast.144, f32[512]{0:T(512)S(1)} %bitcast.145, ...), kind=kLoop, calls=%fused_computation.38.clone.1 | loop fusion | flops 1966080 | bytes 4732929 | tf_op jit(solution)/shard_map/while/body/eval_jaxpr/add | solution.py:82
  101.6 2.0 %convert_reduce_fusion.2 = (f32[512]{0:T(512)S(1)}, bf16[8,32,512]{2,1,0:T(8,128)(2,1)S(1)}, bf16[8,32,512]{2,1,0:T(8,128)(2,1)}) fusion(f32[512]{0:T(512)S(1)} %copy-done.17, bf16[8,32,512]{2,1,0:T(8,128)(2,1)S(1)} %copy-done.10, f32[8,32,512]{2,1,0:T(8,128)} %get-tuple-element.317), kind=kLoop, calls=%fused_computation.98 | loop fusion | flops 916992 | bytes 1314816 | tf_op jit(solution)/shard_map/reduce_sum | solution.py:133
  103.5 1.9 %convolution_convert_fusion.1 = bf16[64,2,16,512]{3,2,1,0:T(8,128)(2,1)S(1)} fusion(bf16[64,2,16,256]{3,2,1,0:T(8,128)(2,1)} %bitcast.129, bf16[256,512,1,1]{1,0,3,2:T(8,128)(2,1)S(1)} %bitcast.132), kind=kOutput, calls=%fused_computation.82 | convolution fusion | flops 537919488 | bytes 3407872 | tf_op jit(solution)/shard_map/dot_general | solution.py:42
  105.5 1.6 fusion.28
  109.2 13.8 %while.45 = (s32[]{:T(128)}, f32[49,512]{1,0:T(8,128)}, bf16[14,38,512]{2,1,0:T(8,128)(2,1)S(1)}, f32[8,32,512]{2,1,0:T(8,128)S(1)}, s32[]{:T(128)}, /*index=5*/s32[]{:T(128)}, s32[]{:T(128)}, s32[]{:T(128)}) while((s32[]{:T(128)}, f32[49,512]{1,0:T(8,128)}, bf16[14,38,512]{2,1,0:T(8,128)(2,1)S(1)}, f32[8,32,512]{2,1,0:T(8,128)S(1)}, ...), condition=%wide.region_17.18_spmd, body=%wide.region_9.17_spmd.sunk | while | flops 1987078 | bytes 5200019 | solution.py:106
  119.6 1.4 dynamic_update_slice.8
  125.0 14.3 %all-to-all-start.1 = ((f32[128,4,128]{2,1,0:T(4,128)}), f32[128,4,128]{2,1,0:T(4,128)S(1)}, u32[]{:S(2)}, u32[]{:S(2)}) async-start(f32[128,4,128]{2,1,0:T(4,128)} %maximum_maximum_fusion), calls=%async_computation.1 | async-start | bytes 524288 | tf_op jit(solution)/shard_map/all_to_all | solution.py:228
  139.4 4.4 %fusion.21 = bf16[64,32,512]{2,1,0:T(8,128)(2,1)} fusion(bf16[64,32,512]{2,1,0:T(8,128)(2,1)} %collective-permute-done.8, s32[]{:T(128)S(6)} %select_n.178, bf16[64,2,16,512]{3,2,1,0:T(8,128)(2,1)} %copy-done.2, bf16[64,2,16,512]{3,2,1,0:T(8,128)(2,1)} %reshape_reshape.4), kind=kLoop, calls=%fused_computation.64 | loop fusion | flops 8388608 | bytes 8388612 | tf_op jit(solution)/shard_map/convert_element_type | solution.py:200
  143.8 6.3 %all-to-all-done.1 = f32[128,4,128]{2,1,0:T(4,128)S(1)} async-done(((f32[128,4,128]{2,1,0:T(4,128)}), f32[128,4,128]{2,1,0:T(4,128)S(1)}, u32[]{:S(2)}, u32[]{:S(2)}) %all-to-all-start.1) | async-done | bytes 262176 | tf_op jit(solution)/shard_map/all_to_all | solution.py:228
  150.1 5.6 %all-to-all-start = ((bf16[64,32,512]{2,1,0:T(8,128)(2,1)}), bf16[64,32,512]{2,1,0:T(8,128)(2,1)}, u32[]{:S(2)}, u32[]{:S(2)}) async-start(bf16[64,32,512]{2,1,0:T(8,128)(2,1)} %fusion.21), calls=%async_computation | async-start | bytes 4194304 | tf_op jit(solution)/shard_map/all_to_all | solution.py:201
  157.1 29.1 %all-to-all-done = bf16[64,32,512]{2,1,0:T(8,128)(2,1)} async-done(((bf16[64,32,512]{2,1,0:T(8,128)(2,1)}), bf16[64,32,512]{2,1,0:T(8,128)(2,1)}, u32[]{:S(2)}, u32[]{:S(2)}) %all-to-all-start) | async-done | bytes 2097184 | tf_op jit(solution)/shard_map/all_to_all | solution.py:201
  186.2 1.9 %convert_reduce_fusion = f32[32,512]{1,0:T(8,128)S(1)} fusion(bf16[64,32,512]{2,1,0:T(8,128)(2,1)} %all-to-all-done), kind=kLoop, calls=%fused_computation.65 | loop fusion | flops 2080768 | bytes 2162688 | tf_op jit(solution)/shard_map/reduce_sum | solution.py:202
  (160 shorter events, 64.1 us)
Async XLA Ops:
  0.6 36.0 %copy-start = (bf16[512,2048]{1,0:T(8,128)(2,1)S(1)}, bf16[512,2048]{1,0:T(8,128)(2,1)}, u32[]{:S(2)}) copy-start(bf16[512,2048]{1,0:T(8,128)(2,1)} %param.23) | copy-start | bytes 6291460
  1.8 7.4 %collective-permute-start = (bf16[3,32,512]{2,1,0:T(8,128)(2,1)S(1)}, bf16[3,32,512]{2,1,0:T(8,128)(2,1)S(1)}, u32[]{:S(2)}, u32[]{:S(2)}) collective-permute-start(bf16[3,32,512]{2,1,0:T(8,128)(2,1)S(1)} %get-tuple-element.415), channel_id=1, source_target_pairs={{0,16},{16,32},{32,48},{48,64},{64,80},{80,96},{96,112},{1,17},{17... | collective-permute-start | bytes 294920 | tf_op jit(solution)/shard_map/ppermute | solution.py:23
  6.9 8.0 %collective-permute-start.1 = (bf16[3,32,512]{2,1,0:T(8,128)(2,1)S(1)}, bf16[3,32,512]{2,1,0:T(8,128)(2,1)S(1)}, u32[]{:S(2)}, u32[]{:S(2)}) collective-permute-start(bf16[3,32,512]{2,1,0:T(8,128)(2,1)S(1)} %get-tuple-element.414), channel_id=1, source_target_pairs={{16,0},{32,16},{48,32},{64,48},{80,64},{96,80},{112,96},{17,1},{33... | collective-permute-start | bytes 294920 | tf_op jit(solution)/shard_map/ppermute | solution.py:25
  15.0 3.3 %copy-start.6 = (bf16[14,32,512]{2,1,0:T(8,128)(2,1)}, bf16[14,32,512]{2,1,0:T(8,128)(2,1)S(1)}, u32[]{:S(2)}) copy-start(bf16[14,32,512]{2,1,0:T(8,128)(2,1)S(1)} %constant_dynamic-update-slice_fusion) | copy-start | bytes 1376260
  15.0 3.2 %collective-permute-start.2 = (bf16[14,3,512]{2,1,0:T(4,128)(2,1)S(1)}, bf16[14,3,512]{2,1,0:T(4,128)(2,1)S(1)}, u32[]{:S(2)}, u32[]{:S(2)}) collective-permute-start(bf16[14,3,512]{2,1,0:T(4,128)(2,1)S(1)} %get-tuple-element.408), channel_id=1, source_target_pairs={{0,1},{1,2},{2,3},{3,4},{4,5},{5,6},{6,7},{7,8},{8,9},{9,10},{10,1... | collective-permute-start | bytes 129032 | tf_op jit(solution)/shard_map/ppermute | solution.py:23
  16.3 4.0 %collective-permute-start.3 = (bf16[14,3,512]{2,1,0:T(4,128)(2,1)S(1)}, bf16[14,3,512]{2,1,0:T(4,128)(2,1)S(1)}, u32[]{:S(2)}, u32[]{:S(2)}) collective-permute-start(bf16[14,3,512]{2,1,0:T(4,128)(2,1)S(1)} %get-tuple-element.409), channel_id=1, source_target_pairs={{1,0},{2,1},{3,2},{4,3},{5,4},{6,5},{7,6},{8,7},{9,8},{10,9},{11,1... | collective-permute-start | bytes 129032 | tf_op jit(solution)/shard_map/ppermute | solution.py:25
  21.6 11.5 %copy-start.14 = (f32[512]{0:T(512)S(1)}, f32[512]{0:T(512)}, u32[]{:S(2)}) copy-start(f32[512]{0:T(512)} %param.20) | copy-start | bytes 6148
  21.7 13.8 %copy-start.12 = (f32[512]{0:T(512)S(1)}, f32[512]{0:T(512)}, u32[]{:S(2)}) copy-start(f32[512]{0:T(512)} %param.21) | copy-start | bytes 6148
  21.7 13.8 %copy-start.15 = (f32[512]{0:T(512)S(1)}, f32[512]{0:T(512)}, u32[]{:S(2)}) copy-start(f32[512]{0:T(512)} %param.22) | copy-start | bytes 6148
  33.2 3.5 %copy-start.11 = (f32[2048]{0:T(1024)S(1)}, f32[2048]{0:T(1024)}, u32[]{:S(2)}) copy-start(f32[2048]{0:T(1024)} %param.24) | copy-start | bytes 24580
  36.7 1.8 copy-start.22
  36.7 1.8 copy-start.23
  37.8 2.8 %copy-start.4 = (bf16[256,2048]{1,0:T(8,128)(2,1)}, bf16[256,2048]{1,0:T(8,128)(2,1)S(1)}, u32[]{:S(2)}) copy-start(bf16[256,2048]{1,0:T(8,128)(2,1)S(1)} %get-tuple-element.418) | copy-start | bytes 3145732
  40.5 1.4 copy-start.3
  44.3 10.0 %collective-permute-start.5 = (bf16[3,32,512]{2,1,0:T(8,128)(2,1)S(1)}, bf16[3,32,512]{2,1,0:T(8,128)(2,1)S(1)}, u32[]{:S(2)}, u32[]{:S(2)}) collective-permute-start(bf16[3,32,512]{2,1,0:T(8,128)(2,1)S(1)} %bitcast.155), channel_id=1, source_target_pairs={{16,0},{32,16},{48,32},{64,48},{80,64},{96,80},{112,96},{17,1},{33... | collective-permute-start | bytes 294920 | tf_op jit(solution)/shard_map/ppermute | solution.py:25
  45.6 8.8 %collective-permute-start.4 = (bf16[3,32,512]{2,1,0:T(8,128)(2,1)S(1)}, bf16[3,32,512]{2,1,0:T(8,128)(2,1)S(1)}, u32[]{:S(2)}, u32[]{:S(2)}) collective-permute-start(bf16[3,32,512]{2,1,0:T(8,128)(2,1)S(1)} %bitcast.154), channel_id=1, source_target_pairs={{0,16},{16,32},{32,48},{48,64},{64,80},{80,96},{96,112},{1,17},{17... | collective-permute-start | bytes 294920 | tf_op jit(solution)/shard_map/ppermute | solution.py:23
  54.4 6.9 %copy-start.8 = (bf16[3,32,512]{2,1,0:T(8,128)(2,1)}, bf16[3,32,512]{2,1,0:T(8,128)(2,1)S(1)}, u32[]{:S(2)}) copy-start(bf16[3,32,512]{2,1,0:T(8,128)(2,1)S(1)} %collective-permute-done.4) | copy-start | bytes 294916
  55.1 15.3 %collective-permute-start.6 = (bf16[14,3,512]{2,1,0:T(4,128)(2,1)}, bf16[14,3,512]{2,1,0:T(4,128)(2,1)}, u32[]{:S(2)}, u32[]{:S(2)}) collective-permute-start(bf16[14,3,512]{2,1,0:T(4,128)(2,1)} %get-tuple-element.406), channel_id=1, source_target_pairs={{0,1},{1,2},{2,3},{3,4},{4,5},{5,6},{6,7},{7,8},{8,9},{9,10},{10,1... | collective-permute-start | bytes 129032 | tf_op jit(solution)/shard_map/ppermute | solution.py:23
  60.0 10.4 %collective-permute-start.7 = (bf16[14,3,512]{2,1,0:T(4,128)(2,1)}, bf16[14,3,512]{2,1,0:T(4,128)(2,1)}, u32[]{:S(2)}, u32[]{:S(2)}) collective-permute-start(bf16[14,3,512]{2,1,0:T(4,128)(2,1)} %get-tuple-element.407), channel_id=1, source_target_pairs={{1,0},{2,1},{3,2},{4,3},{5,4},{6,5},{7,6},{8,7},{9,8},{10,9},{11,1... | collective-permute-start | bytes 129032 | tf_op jit(solution)/shard_map/ppermute | solution.py:25
  72.4 29.2 %copy-start.10 = (bf16[8,32,512]{2,1,0:T(8,128)(2,1)S(1)}, bf16[8,32,512]{2,1,0:T(8,128)(2,1)}, u32[]{:S(2)}) copy-start(bf16[8,32,512]{2,1,0:T(8,128)(2,1)} %param.18) | copy-start | bytes 786436
  72.4 29.2 %copy-start.17 = (f32[512]{0:T(512)S(1)}, f32[512]{0:T(512)}, u32[]{:S(2)}) copy-start(f32[512]{0:T(512)} %param.27) | copy-start | bytes 6148
  101.5 3.9 %copy-start.1 = (bf16[64,2,16,512]{3,2,1,0:T(8,128)(2,1)S(1)}, bf16[64,2,16,512]{3,2,1,0:T(8,128)(2,1)}, u32[]{:S(2)}) copy-start(bf16[64,2,16,512]{3,2,1,0:T(8,128)(2,1)} %reshape_reshape.4) | copy-start | bytes 6291460
  105.5 1.9 %copy-start.2 = (bf16[64,2,16,512]{3,2,1,0:T(8,128)(2,1)}, bf16[64,2,16,512]{3,2,1,0:T(8,128)(2,1)S(1)}, u32[]{:S(2)}) copy-start(bf16[64,2,16,512]{3,2,1,0:T(8,128)(2,1)S(1)} %convolution_convert_fusion.1) | copy-start | bytes 6291460
  107.4 31.9 %collective-permute-start.8 = (bf16[64,32,512]{2,1,0:T(8,128)(2,1)}, bf16[64,32,512]{2,1,0:T(8,128)(2,1)}, u32[]{:S(2)}, u32[]{:S(2)}) collective-permute-start(bf16[64,32,512]{2,1,0:T(8,128)(2,1)} %fusion.28), channel_id=1, source_target_pairs={{0,1},{1,0},{2,3},{3,2},{4,5},{5,4},{6,7},{7,6},{8,9},{9,8},{10,11... | collective-permute-start | bytes 6291464 | tf_op jit(solution)/shard_map/ppermute | solution.py:199
  109.2 13.8 %copy-start.13 = (f32[512]{0:T(512)S(1)}, f32[512]{0:T(512)}, u32[]{:S(2)}) copy-start(f32[512]{0:T(512)} %get-tuple-element.386) | copy-start | bytes 6148
  109.2 13.8 %copy-start.18 = (f32[512]{0:T(512)S(1)}, f32[512]{0:T(512)}, u32[]{:S(2)}) copy-start(f32[512]{0:T(512)} %get-tuple-element.404) | copy-start | bytes 6148
  109.2 13.8 %copy-start.19 = (f32[512]{0:T(512)S(1)}, f32[512]{0:T(512)}, u32[]{:S(2)}) copy-start(f32[512]{0:T(512)} %get-tuple-element.356) | copy-start | bytes 6148
  109.2 13.8 %copy-start.20 = (f32[512]{0:T(512)S(1)}, f32[512]{0:T(512)}, u32[]{:S(2)}) copy-start(f32[512]{0:T(512)} %get-tuple-element.359) | copy-start | bytes 6148
  109.2 14.9 %copy-start.5 = (f32[128,4,4]{2,1,0:T(4,128)S(1)}, f32[128,4,4]{2,1,0:T(4,128)}, u32[]{:S(2)}) copy-start(f32[128,4,4]{2,1,0:T(4,128)} %mul.720) | copy-start | bytes 24580
  109.2 14.9 %copy-start.21 = (f32[128]{0:T(128)S(1)}, f32[128]{0:T(128)}, u32[]{:S(2)}) copy-start(f32[128]{0:T(128)} %pad.2.clone) | copy-start | bytes 1540
  125.0 25.1 %all-to-all-start.1 = ((f32[128,4,128]{2,1,0:T(4,128)}), f32[128,4,128]{2,1,0:T(4,128)S(1)}, u32[]{:S(2)}, u32[]{:S(2)}) async-start(f32[128,4,128]{2,1,0:T(4,128)} %maximum_maximum_fusion), calls=%async_computation.1 | async-start | bytes 524288 | tf_op jit(solution)/shard_map/all_to_all | solution.py:228
  150.1 36.1 %all-to-all-start = ((bf16[64,32,512]{2,1,0:T(8,128)(2,1)}), bf16[64,32,512]{2,1,0:T(8,128)(2,1)}, u32[]{:S(2)}, u32[]{:S(2)}) async-start(bf16[64,32,512]{2,1,0:T(8,128)(2,1)} %fusion.21), calls=%async_computation | async-start | bytes 4194304 | tf_op jit(solution)/shard_map/all_to_all | solution.py:201
  (3 other events, 3.3 us)

commit v2 on v1

v2 whole, which is shorter than its diff:
```python
import math

import jax
import jax.numpy as jnp
from jax import lax
from jax.experimental import pallas as pl
from jax.experimental.pallas import tpu as pltpu
from jax.sharding import Mesh
from jax.sharding import PartitionSpec as P

CHIPS = ("z", "yh", "x", "yl")
EVERY = CHIPS + ("c",)
ROW = ("z", "yh")
COL = ("x", "yl", "c")
ROWS, COLS, CH, HID, CHUNK = 8, 32, 512, 2048, 512
COUNT = ROWS * COLS
STEPS = HID // CHUNK
PAD = (ROWS + 6, COLS + 8, CH)
F32, BF16 = jnp.float32, jnp.bfloat16
VMEM_BYTES = 40 * 1024 * 1024


def dot_nn(left, right):
    return lax.dot_general(left, right, (((1,), (0,)), ((), ())), preferred_element_type=F32)


def dot_nt(left, right):
    return lax.dot_general(left, right, (((1,), (1,)), ((), ())), preferred_element_type=F32)


def dot_tn(left, right):
    return lax.dot_general(left, right, (((0,), (0,)), ((), ())), preferred_element_type=F32)


def assemble(pad, tile, top, bottom, left, right):
    pad[0:3, 3 : 3 + COLS, :] = top[...].astype(F32)
    pad[3 : 3 + ROWS, 3 : 3 + COLS, :] = tile[...].astype(F32)
    pad[3 + ROWS : 6 + ROWS, 3 : 3 + COLS, :] = bottom[...].astype(F32)
    pad[:, 0:3, :] = left[...].astype(F32)
    pad[:, 3 + COLS : 6 + COLS, :] = right[...].astype(F32)


def lanes_of(block):
    return pl.ds(pl.multiple_of(block * 128, 128), 128)


def depthwise(pad, taps, finish, flip):
    def block(cb, carry):
        lanes = lanes_of(cb)
        totals = [jnp.zeros((ROWS, 8, 128), F32) for _ in range(COLS // 8)]
        for s in range(7):
            weights = []
            for r in range(7):
                tap = 7 * (6 - r) + 6 - s if flip else 7 * r + s
                weights.append(taps[tap : tap + 1, lanes].reshape(1, 1, 128))
            for cg in range(COLS // 8):
                band = pad[:, 8 * cg + s : 8 * cg + s + 8, lanes]
                for r in range(7):
                    totals[cg] = totals[cg] + band[r : r + ROWS] * weights[r]
        for cg in range(COLS // 8):
            finish(cg, lanes, totals[cg])
        return carry

    lax.fori_loop(0, CH // 128, block, 0)


def grads_kernel(
    core_ref, tile, top, bottom, left, right, cot, taps, dw_bias, gain, shift, scale,
    w_in, b_in, w_out,
    pad, x_hat, rstd, act_out, d_pre_out, g_in_bias, mine, theirs,
    conv, normed, d_branch, g_in,
):
    step = pl.program_id(0)
    core = core_ref[0]

    @pl.when(step == 0)
    def _():
        assemble(pad, tile, top, bottom, left, right)

        def finish(cg, lanes, total):
            conv[:, 8 * cg : 8 * cg + 8, lanes] = total

        depthwise(pad, taps, finish, False)
        rows = conv[...].reshape(COUNT, CH) + dw_bias[...]
        centred = rows - jnp.mean(rows, axis=-1, keepdims=True)
        inverse = lax.rsqrt(jnp.mean(centred * centred, axis=-1, keepdims=True) + 1e-06)
        hat = centred * inverse
        x_hat[...] = hat
        rstd[...] = inverse
        normed[...] = (hat * gain[...] + shift[...]).astype(BF16)
        d_branch[...] = (cot[...].astype(F32) * scale[...]).astype(BF16)

    pre_act = dot_nn(normed[...], w_in[...]) + b_in[...]
    cumul = 0.5 * (1.0 + lax.erf(pre_act * 0.7071067811865476))
    act = (pre_act * cumul).astype(BF16)
    slope = cumul + pre_act * jnp.exp(-0.5 * pre_act * pre_act) * 0.3989422804014327
    d_pre = (dot_nt(d_branch[...], w_out[...]) * slope).astype(BF16)
    act_out[...] = act
    d_pre_out[...] = d_pre
    g_in_bias[...] = jnp.sum(d_pre.astype(F32), axis=0, keepdims=True)
    term = dot_tn(act, d_branch[...]).reshape(CHUNK // 32, 2, 16, CH)
    chips = pl.ds(step * (CHUNK // 32), CHUNK // 32)
    first = core == 0
    mine[chips, 0:16, :] = jnp.where(first, term[:, 0], term[:, 1]).astype(BF16)
    theirs[chips, 0:16, :] = jnp.where(first, term[:, 1], term[:, 0]).astype(BF16)
    g_in[step] = dot_tn(normed[...], d_pre)

    @pl.when(step == STEPS - 1)
    def _():
        upper = lax.broadcasted_iota(jnp.int32, (8, 8, CHUNK), 1) < 4

        def group(g, carry):
            rows = pl.ds(pl.multiple_of(g * 64, 64), 64)
            kept, given = [], []
            for u in range(2):
                low = g_in[2 * u, rows, :].reshape(8, 8, CHUNK)
                high = g_in[2 * u + 1, rows, :].reshape(8, 8, CHUNK)
                low_turned, high_turned = pltpu.roll(low, 4, 1), pltpu.roll(high, 4, 1)
                zero = jnp.where(upper, low, high_turned)
                one = jnp.where(upper, low_turned, high)
                kept.append(jnp.where(first, zero, one))
                given.append(jnp.where(first, one, zero))
            at = pl.ds(pl.multiple_of(g * 8, 8), 8)
            mine[at, 16:32, :] = jnp.concatenate(kept, axis=1).astype(BF16)
            theirs[at, 16:32, :] = jnp.concatenate(given, axis=1).astype(BF16)
            return carry

        lax.fori_loop(0, 8, group, 0)


def whole(shape):
    return pl.BlockSpec(shape, lambda *_: (0,) * len(shape))


def grads(core, tile, top, bottom, left, right, cot, taps, dw_bias, gain, shift, scale, w_in, b_in, w_out):
    message = (64, 32, CH)
    return pl.pallas_call(
        grads_kernel,
        grid=(STEPS,),
        in_specs=[
            pl.BlockSpec(memory_space=pltpu.SMEM),
            whole((ROWS, COLS, CH)),
            whole((3, COLS, CH)),
            whole((3, COLS, CH)),
            whole((ROWS + 6, 3, CH)),
            whole((ROWS + 6, 3, CH)),
            whole((COUNT, CH)),
            whole((49, CH)),
            whole((1, CH)),
            whole((1, CH)),
            whole((1, CH)),
            whole((1, CH)),
            pl.BlockSpec((CH, CHUNK), lambda t: (0, t)),
            pl.BlockSpec((1, CHUNK), lambda t: (0, t)),
            pl.BlockSpec((CHUNK, CH), lambda t: (t, 0)),
        ],
        out_specs=[
            whole(PAD),
            whole((COUNT, CH)),
            whole((COUNT, 1)),
            pl.BlockSpec((COUNT, CHUNK), lambda t: (0, t)),
            pl.BlockSpec((COUNT, CHUNK), lambda t: (0, t)),
            pl.BlockSpec((1, CHUNK), lambda t: (0, t)),
            whole(message),
            whole(message),
        ],
        out_shape=[
            jax.ShapeDtypeStruct(PAD, F32),
            jax.ShapeDtypeStruct((COUNT, CH), F32),
            jax.ShapeDtypeStruct((COUNT, 1), F32),
            jax.ShapeDtypeStruct((COUNT, HID), BF16),
            jax.ShapeDtypeStruct((COUNT, HID), BF16),
            jax.ShapeDtypeStruct((1, HID), F32),
            jax.ShapeDtypeStruct(message, BF16),
            jax.ShapeDtypeStruct(message, BF16),
        ],
        scratch_shapes=[
            pltpu.VMEM((ROWS, COLS, CH), F32),
            pltpu.VMEM((COUNT, CH), BF16),
            pltpu.VMEM((COUNT, CH), BF16),
            pltpu.VMEM((STEPS, CH, CHUNK), F32),
        ],
        compiler_params=pltpu.CompilerParams(vmem_limit_bytes=VMEM_BYTES),
        cost_estimate=pl.CostEstimate(flops=2_200_000_000, bytes_accessed=12_000_000, transcendentals=1_000_000),
        name="grads",
    )(core, tile, top, bottom, left, right, cot, taps, dw_bias, gain, shift, scale, w_in, b_in, w_out)


def norm_kernel(d_pre, w_in, x_hat, rstd, gain, pad, cot, scale, d_conv, rows_out, d_tile):
    d_normed = dot_nt(d_pre[...], w_in[...])
    hat = x_hat[...]
    rows_out[50:51, :] = jnp.sum(d_normed * hat, axis=0, keepdims=True)
    rows_out[51:52, :] = jnp.sum(d_normed, axis=0, keepdims=True)
    d_branch = (cot[...].astype(F32) * scale[...]).astype(BF16)
    rows_out[52:53, :] = jnp.sum(d_branch.astype(F32), axis=0, keepdims=True)
    d_hat = d_normed * gain[...]
    grad = rstd[...] * (
        d_hat
        - jnp.mean(d_hat, axis=-1, keepdims=True)
        - hat * jnp.mean(d_hat * hat, axis=-1, keepdims=True)
    )
    grad = grad.astype(BF16)
    d_conv[...] = grad.reshape(ROWS, COLS, CH)
    wide = grad.astype(F32)
    rows_out[49:50, :] = jnp.sum(wide, axis=0, keepdims=True)
    rows_out[53:56, :] = jnp.zeros((3, CH), F32)
    d_tile[...] = wide.reshape(ROWS, COLS, CH)

    def block(cb, carry):
        lanes = lanes_of(cb)
        for s in range(7):
            totals = [jnp.zeros((8, 128), F32) for _ in range(7)]
            for cg in range(COLS // 8):
                band = pad[:, 8 * cg + s : 8 * cg + s + 8, lanes]
                own = d_tile[:, 8 * cg : 8 * cg + 8, lanes]
                for r in range(7):
                    totals[r] = totals[r] + jnp.sum(band[r : r + ROWS] * own, axis=0)
            for r in range(7):
                rows_out[7 * r + s : 7 * r + s + 1, lanes] = jnp.sum(totals[r], axis=0, keepdims=True)
        return carry

    lax.fori_loop(0, CH // 128, block, 0)


def norm_back(d_pre, w_in, x_hat, rstd, gain, pad, cot, scale):
    return pl.pallas_call(
        norm_kernel,
        out_shape=[
            jax.ShapeDtypeStruct((ROWS, COLS, CH), BF16),
            jax.ShapeDtypeStruct((56, CH), F32),
        ],
        scratch_shapes=[pltpu.VMEM((ROWS, COLS, CH), F32)],
        compiler_params=pltpu.CompilerParams(vmem_limit_bytes=VMEM_BYTES),
        cost_estimate=pl.CostEstimate(flops=600_000_000, bytes_accessed=8_000_000, transcendentals=0),
        name="norm_back",
    )(d_pre, w_in, x_hat, rstd, gain, pad, cot, scale)


def branch_kernel(act, w_out, b_out, tile, cot, scale, block_out, g_scale):
    branch = dot_nn(act[...], w_out[...]) + b_out[...]
    block_out[...] = (tile[...].astype(F32) + scale[...] * branch).astype(BF16)
    g_scale[...] = jnp.sum(cot[...].astype(F32) * branch, axis=0, keepdims=True)


def branch_part(act, w_out, b_out, tile, cot, scale):
    return pl.pallas_call(
        branch_kernel,
        out_shape=[
            jax.ShapeDtypeStruct((COUNT, CH), BF16),
            jax.ShapeDtypeStruct((1, CH), F32),
        ],
        compiler_params=pltpu.CompilerParams(vmem_limit_bytes=VMEM_BYTES),
        cost_estimate=pl.CostEstimate(flops=540_000_000, bytes_accessed=4_000_000, transcendentals=0),
        name="branch_part",
    )(act, w_out, b_out, tile, cot, scale)


def features_kernel(d_conv, top, bottom, left, right, cot, taps, out, pad):
    assemble(pad, d_conv, top, bottom, left, right)

    def finish(cg, lanes, total):
        columns = slice(8 * cg, 8 * cg + 8)
        pad[0:ROWS, columns, lanes] = total

    depthwise(pad, taps, finish, True)
    out[...] = (cot[...].astype(F32) + pad[0:ROWS, 0:COLS, :]).astype(BF16)


def features_part(d_conv, top, bottom, left, right, cot, taps):
    return pl.pallas_call(
        features_kernel,
        out_shape=jax.ShapeDtypeStruct((ROWS, COLS, CH), BF16),
        scratch_shapes=[pltpu.VMEM(PAD, F32)],
        compiler_params=pltpu.CompilerParams(vmem_limit_bytes=VMEM_BYTES),
        cost_estimate=pl.CostEstimate(flops=30_000_000, bytes_accessed=2_000_000, transcendentals=0),
        name="features_part",
    )(d_conv, top, bottom, left, right, cot, taps)


def shift_by(value, axis, way):
    count = lax.axis_size(axis)
    pairs = [(i, i + way) for i in range(count) if 0 <= i + way < count]
    return lax.ppermute(value, axis, pairs)


def halo(tile):
    top = shift_by(tile[ROWS - 3 :], ROW, 1)
    bottom = shift_by(tile[:3], ROW, -1)
    tail = [part[:, COLS - 3 :] for part in (top, tile, bottom)]
    head = [part[:, :3] for part in (top, tile, bottom)]
    left = shift_by(jnp.concatenate(tail, axis=0), COL, 1)
    right = shift_by(jnp.concatenate(head, axis=0), COL, -1)
    return top, bottom, left, right


def shards(
    features, cotangent, dw_kernel, dw_bias, norm_gain_vector, norm_bias,
    pw_in_weight, pw_in_bias, pw_out_weight, pw_out_bias, layer_scale,
):
    factor = 1.0 / math.sqrt(COUNT * lax.axis_size(EVERY))
    core = lax.axis_index("c").astype(jnp.int32).reshape(1)
    row = lambda vector: vector.reshape(1, -1)
    gain, scale = row(norm_gain_vector), row(layer_scale)
    flat_cot = cotangent.reshape(COUNT, CH)
    pad, x_hat, rstd, act, d_pre, g_in_bias, mine, theirs = grads(
        core, features, *halo(features), flat_cot, dw_kernel, row(dw_bias), gain, row(norm_bias), scale,
        pw_in_weight, row(pw_in_bias), pw_out_weight,
    )
    met = lax.ppermute(theirs, "c", [(0, 1), (1, 0)])
    d_conv, rows = norm_back(d_pre, pw_in_weight, x_hat, rstd, gain, pad, flat_cot, scale)
    chip_sum = (mine.astype(F32) + met.astype(F32)).astype(BF16)
    spread = lax.all_to_all(chip_sum, CHIPS, 0, 0, tiled=True)
    block_rows, g_scale = branch_part(
        act, pw_out_weight, row(pw_out_bias), features.reshape(COUNT, CH), flat_cot, scale
    )
    grad_features = features_part(d_conv, *halo(d_conv), cotangent, dw_kernel)
    channel_rows = jnp.concatenate([rows[:53], g_scale], axis=0) * factor
    small = jnp.concatenate(
        [
            channel_rows.T.reshape(128, 4, 54),
            (g_in_bias * factor).reshape(128, 4, 4),
            jnp.zeros((128, 4, 70), F32),
        ],
        axis=2,
    )
    small = jnp.sum(lax.all_to_all(small, EVERY, 0, 0, tiled=True), axis=0)
    summed = jnp.sum(spread.astype(F32), axis=0) * factor
    return (
        block_rows.reshape(ROWS, COLS, CH),
        grad_features,
        summed[16:].reshape(2, 2, 4, CH).transpose(2, 0, 1, 3).reshape(4, HID),
        summed[:16],
        small[:, :54].T,
        small[:, 54:58].reshape(-1),
    )


def solution(mesh):
    fine = Mesh(mesh.devices.reshape(4, 2, 4, 2, 2), EVERY)
    return jax.shard_map(
        shards,
        mesh=fine,
        in_specs=(P(ROW, COL, None), P(ROW, COL, None)) + (P(),) * 9,
        out_specs=(
            P(ROW, COL, None),
            P(ROW, COL, None),
            P(EVERY, None),
            P(EVERY, None),
            P(None, EVERY),
            P(EVERY),
        ),
        check_vma=False,
    )
```

time: 192 us -> 148 us (0.77)
  the two profiles are of different devices: /device:TPU:0 before, /device:TPU:41 now
where the time goes in v2:
time: 148 us; the launch traced here: 147 us
  starting transfers between devices  44.8 us (30%)
  waiting for transfers between devices  38.8 us (26%)
  local copies, waits for them, and re-layouts  30.5 us (21%)
  Pallas kernels  24.2 us (16%)
  other arithmetic  8.05 us (5%)
    ppermute x8, waiting for transfers between devices, shift_by(): return lax.ppermute(value, axis, pairs)  33.1 us
    ppermute x8, starting transfers between devices, shift_by(): return lax.ppermute(value, axis, pairs)  28.9 us
    unnamed x72, local copies, waits for them, and re-layouts  24.8 us
    pallas_call x1, Pallas kernels, grads(): pl.pallas_call(grads_kernel, grid=(STEPS,), in_specs=[pl.BlockSpec(memory...  11.2 us
    all_to_all x1, starting transfers between devices, shards(): small = jnp.sum(lax.all_to_all(small, EVERY, 0, 0, tiled=True), axis=0)  9.17 us
    all_to_all x1, starting transfers between devices, shards(): spread = lax.all_to_all(chip_sum, CHIPS, 0, 0, tiled=True)  6.82 us
    pallas_call x1, Pallas kernels, norm_back(): pl.pallas_call(norm_kernel, out_shape=[jax.ShapeDtypeStruct((ROWS, COLS,...  6.22 us
    all_to_all x1, waiting for transfers between devices, shards(): small = jnp.sum(lax.all_to_all(small, EVERY, 0, 0, tiled=True), axis=0)  5.65 us
  transfers between devices with their start and end apart: 11, of which 6 were waited for; matrix products, arithmetic and copies ran while one was open for 7% of the time, Pallas kernels for 9%

profile of v2, /device:TPU:41, one launch (start us, length us, event | category | flops | bytes accessed | tf_op | source)
XLA Modules:
  0.0 147.3 jit_solution(17846291383893554734)
XLA Ops:
  0.6 1.0 fusion.4
  1.6 3.9 %collective-permute-start = (bf16[3,32,512]{2,1,0:T(8,128)(2,1)S(1)}, bf16[3,32,512]{2,1,0:T(8,128)(2,1)S(1)}, u32[]{:S(2)}, u32[]{:S(2)}) collective-permute-start(bf16[3,32,512]{2,1,0:T(8,128)(2,1)S(1)} %get-tuple-element.37), channel_id=1, source_target_pairs={{0,16},{16,32},{32,48},{48,64},{64,80},{80,96},{96,112},{1,17},{17... | collective-permute-start | bytes 294920 | tf_op jit(solution)/shard_map/ppermute | solution.py:283
  5.5 3.8 %collective-permute-start.1 = (bf16[3,32,512]{2,1,0:T(8,128)(2,1)S(1)}, bf16[3,32,512]{2,1,0:T(8,128)(2,1)S(1)}, u32[]{:S(2)}, u32[]{:S(2)}) collective-permute-start(bf16[3,32,512]{2,1,0:T(8,128)(2,1)S(1)} %get-tuple-element.36), channel_id=1, source_target_pairs={{16,0},{32,16},{48,32},{64,48},{80,64},{96,80},{112,96},{17,1},{33... | collective-permute-start | bytes 294920 | tf_op jit(solution)/shard_map/ppermute | solution.py:283
  10.2 2.2 %collective-permute-done.1.bottom = bf16[3,32,512]{2,1,0:T(8,128)(2,1)S(1)} collective-permute-done((bf16[3,32,512]{2,1,0:T(8,128)(2,1)S(1)}, bf16[3,32,512]{2,1,0:T(8,128)(2,1)S(1)}, u32[]{:S(2)}, u32[]{:S(2)}) %collective-permute-start.1) | collective-permute-done | bytes 98336 | tf_op jit(solution)/shard_map/ppermute | solution.py:283
  13.8 5.9 %collective-permute-start.2 = (bf16[14,3,512]{2,1,0:T(4,128)(2,1)S(1)}, bf16[14,3,512]{2,1,0:T(4,128)(2,1)S(1)}, u32[]{:S(2)}, u32[]{:S(2)}) collective-permute-start(bf16[14,3,512]{2,1,0:T(4,128)(2,1)S(1)} %pad_maximum_fusion), channel_id=1, source_target_pairs={{0,1},{1,2},{2,3},{3,4},{4,5},{5,6},{6,7},{7,8},{8,9},{9,10},{10,1... | collective-permute-start | bytes 129032 | tf_op jit(solution)/shard_map/ppermute | solution.py:283
  19.7 1.9 %collective-permute-start.3 = (bf16[14,3,512]{2,1,0:T(4,128)(2,1)S(1)}, bf16[14,3,512]{2,1,0:T(4,128)(2,1)S(1)}, u32[]{:S(2)}, u32[]{:S(2)}) collective-permute-start(bf16[14,3,512]{2,1,0:T(4,128)(2,1)S(1)} %pad_maximum_fusion.1), channel_id=1, source_target_pairs={{1,0},{2,1},{3,2},{4,3},{5,4},{6,5},{7,6},{8,7},{9,8},{10,9},{11,1... | collective-permute-start | bytes 129032 | tf_op jit(solution)/shard_map/ppermute | solution.py:283
  22.3 3.8 %collective-permute-done.3.right = bf16[14,3,512]{2,1,0:T(4,128)(2,1)S(1)} collective-permute-done((bf16[14,3,512]{2,1,0:T(4,128)(2,1)S(1)}, bf16[14,3,512]{2,1,0:T(4,128)(2,1)S(1)}, u32[]{:S(2)}, u32[]{:S(2)}) %collective-permute-start.3) | collective-permute-done | bytes 43040 | tf_op jit(solution)/shard_map/ppermute | solution.py:283
  26.7 0.9 copy-done
  27.7 1.6 %copy-done.2 = bf16[2048,512]{1,0:T(8,128)(2,1)S(1)} copy-done((bf16[2048,512]{1,0:T(8,128)(2,1)S(1)}, bf16[2048,512]{1,0:T(8,128)(2,1)}, u32[]{:S(2)}) %copy-start.2) | copy-done | bytes 2097176
  29.3 1.6 %copy-done.4 = bf16[512,2048]{1,0:T(8,128)(2,1)S(1)} copy-done((bf16[512,2048]{1,0:T(8,128)(2,1)S(1)}, bf16[512,2048]{1,0:T(8,128)(2,1)}, u32[]{:S(2)}) %copy-start.4) | copy-done | bytes 2097176
  39.6 11.2 %grads.1 = (f32[14,40,512]{2,1,0:T(8,128)S(1)}, f32[256,512]{1,0:T(8,128)S(1)}, f32[256,1]{1,0:T(8,128)S(1)}, bf16[256,2048]{1,0:T(8,128)(2,1)S(1)}, bf16[256,20...) custom-call(s32[1]{0:T(128)} %bitcast.core_ref, ...), custom_call_target="tpu_custom_call" | custom-call | flops 2200000000 | bytes 12000000 | tf_op jit(solution)/shard_map/grads/pallas_call | solution.py:137
  50.8 1.0 copy-done.10
  51.8 1.0 copy-done.12
  54.3 1.1 reshape.70
  55.4 1.6 %copy-done.3 = bf16[2048,512]{1,0:T(8,128)(2,1)S(1)} copy-done((bf16[2048,512]{1,0:T(8,128)(2,1)S(1)}, bf16[2048,512]{1,0:T(8,128)(2,1)}, u32[]{:S(2)}) %copy-start.3) | copy-done | bytes 2097176
  57.9 1.2 copy-done.13
  59.2 1.5 %branch_part.1 = (bf16[256,512]{1,0:T(8,128)(2,1)}, f32[1,512]{1,0:T(1,128)S(1)}) custom-call(bf16[256,2048]{1,0:T(8,128)(2,1)S(1)} %copy-done.13, bf16[2048,512]{1,0:T(8,128)(2,1)S(1)} %copy-done.3, f32[1,512]{1,0:T(1,128)S(1)} %bitcast.27, bf16[256,512]{1,0:T(8,128)(2,1)S(1)} %bitcast.22, bf16[256,512]{1,0:T(8,128)(2,1)S(1)} %bitcast.20, f32[1,512]{1,0:T(1,128)S(1)} %bitcast.25), custom_call_target="tpu_custom_call" | custom-call | flops 540000000 | bytes 4000000 | tf_op jit(solution)/shard_map/branch_part/pallas_call | solution.py:246
  62.2 6.2 %norm_back.1 = (bf16[8,32,512]{2,1,0:T(8,128)(2,1)S(1)}, f32[56,512]{1,0:T(8,128)S(1)}) custom-call(bf16[256,2048]{1,0:T(8,128)(2,1)S(1)} %copy-done.11, bf16[512,2048]{1,0:T(8,128)(2,1)S(1)} %copy-done.5, f32[256,512]{1,0:T(8,128)S(1)} %copy-done.15, f32[256,1]{1,0:T(8,128)S(1)} %copy-done.17, f32[1,512]{1,0:T(1,128)S(1)} %bitcast.29, ...), custom_call_target="tpu_custom_call" | custom-call | flops 600000000 | bytes 8000000 | tf_op jit(solution)/shard_map/norm_back/pallas_call | solution.py:226
  69.3 1.9 %maximum_maximum_fusion = f32[128,4,128]{2,1,0:T(4,128)} fusion(f32[128,4,4]{2,1,0:T(4,128)} %reshape.70, f32[128,4,54]{2,1,0:T(4,128)S(1)} %bitcast.33, f32[128]{0:T(128)S(1)} %pad.2.clone), kind=kLoop, calls=%fused_computation.2 | loop fusion | flops 131072 | bytes 381440 | tf_op jit(solution)/shard_map/concatenate | solution.py:318
  71.1 9.2 %all-to-all-start.1 = ((f32[128,4,128]{2,1,0:T(4,128)}), f32[128,4,128]{2,1,0:T(4,128)S(1)}, u32[]{:S(2)}, u32[]{:S(2)}) async-start(f32[128,4,128]{2,1,0:T(4,128)} %maximum_maximum_fusion), calls=%async_computation.1 | async-start | bytes 524288 | tf_op jit(solution)/shard_map/all_to_all | solution.py:326
  80.3 3.9 %add_convert_fusion = bf16[64,32,512]{2,1,0:T(8,128)(2,1)} fusion(bf16[64,32,512]{2,1,0:T(8,128)(2,1)} %collective-permute-done.8, bf16[64,32,512]{2,1,0:T(8,128)(2,1)S(1)} %get-tuple-element.25), kind=kLoop, calls=%fused_computation.1 | loop fusion | flops 4194304 | bytes 6291456 | tf_op jit(solution)/shard_map/convert_element_type | solution.py:311
  84.2 5.6 %all-to-all-done.1 = f32[128,4,128]{2,1,0:T(4,128)S(1)} async-done(((f32[128,4,128]{2,1,0:T(4,128)}), f32[128,4,128]{2,1,0:T(4,128)S(1)}, u32[]{:S(2)}, u32[]{:S(2)}) %all-to-all-start.1) | async-done | bytes 262176 | tf_op jit(solution)/shard_map/all_to_all | solution.py:326
  89.8 6.8 %all-to-all-start = ((bf16[64,32,512]{2,1,0:T(8,128)(2,1)}), bf16[64,32,512]{2,1,0:T(8,128)(2,1)}, u32[]{:S(2)}, u32[]{:S(2)}) async-start(bf16[64,32,512]{2,1,0:T(8,128)(2,1)} %add_convert_fusion), calls=%async_computation | async-start | bytes 4194304 | tf_op jit(solution)/shard_map/all_to_all | solution.py:312
  96.7 3.6 %collective-permute-start.5 = (bf16[3,32,512]{2,1,0:T(8,128)(2,1)S(1)}, bf16[3,32,512]{2,1,0:T(8,128)(2,1)S(1)}, u32[]{:S(2)}, u32[]{:S(2)}) collective-permute-start(bf16[3,32,512]{2,1,0:T(8,128)(2,1)S(1)} %get-tuple-element.32), channel_id=1, source_target_pairs={{16,0},{32,16},{48,32},{64,48},{80,64},{96,80},{112,96},{17,1},{33... | collective-permute-start | bytes 294920 | tf_op jit(solution)/shard_map/ppermute | solution.py:283
  100.4 3.1 %collective-permute-start.4 = (bf16[3,32,512]{2,1,0:T(8,128)(2,1)S(1)}, bf16[3,32,512]{2,1,0:T(8,128)(2,1)S(1)}, u32[]{:S(2)}, u32[]{:S(2)}) collective-permute-start(bf16[3,32,512]{2,1,0:T(8,128)(2,1)S(1)} %get-tuple-element.33), channel_id=1, source_target_pairs={{0,16},{16,32},{32,48},{48,64},{64,80},{80,96},{96,112},{1,17},{17... | collective-permute-start | bytes 294920 | tf_op jit(solution)/shard_map/ppermute | solution.py:283
  103.5 20.5 %collective-permute-done.5.bottom = bf16[3,32,512]{2,1,0:T(8,128)(2,1)S(1)} collective-permute-done((bf16[3,32,512]{2,1,0:T(8,128)(2,1)S(1)}, bf16[3,32,512]{2,1,0:T(8,128)(2,1)S(1)}, u32[]{:S(2)}, u32[]{:S(2)}) %collective-permute-start.5) | collective-permute-done | bytes 98336 | tf_op jit(solution)/shard_map/ppermute | solution.py:283
  124.0 2.1 %collective-permute-done.4.top = bf16[3,32,512]{2,1,0:T(8,128)(2,1)S(1)} collective-permute-done((bf16[3,32,512]{2,1,0:T(8,128)(2,1)S(1)}, bf16[3,32,512]{2,1,0:T(8,128)(2,1)S(1)}, u32[]{:S(2)}, u32[]{:S(2)}) %collective-permute-start.4) | collective-permute-done | bytes 98336 | tf_op jit(solution)/shard_map/ppermute | solution.py:283
  126.3 4.6 %collective-permute-start.6 = (bf16[14,3,512]{2,1,0:T(4,128)(2,1)S(1)}, bf16[14,3,512]{2,1,0:T(4,128)(2,1)S(1)}, u32[]{:S(2)}, u32[]{:S(2)}) collective-permute-start(bf16[14,3,512]{2,1,0:T(4,128)(2,1)S(1)} %pad_maximum_fusion.2), channel_id=1, source_target_pairs={{0,1},{1,2},{2,3},{3,4},{4,5},{5,6},{6,7},{7,8},{8,9},{9,10},{10,1... | collective-permute-start | bytes 129032 | tf_op jit(solution)/shard_map/ppermute | solution.py:283
  131.0 1.9 %collective-permute-start.7 = (bf16[14,3,512]{2,1,0:T(4,128)(2,1)S(1)}, bf16[14,3,512]{2,1,0:T(4,128)(2,1)S(1)}, u32[]{:S(2)}, u32[]{:S(2)}) collective-permute-start(bf16[14,3,512]{2,1,0:T(4,128)(2,1)S(1)} %pad_maximum_fusion.3), channel_id=1, source_target_pairs={{1,0},{2,1},{3,2},{4,3},{5,4},{6,5},{7,6},{8,7},{9,8},{10,9},{11,1... | collective-permute-start | bytes 129032 | tf_op jit(solution)/shard_map/ppermute | solution.py:283
  132.9 4.5 %collective-permute-done.7.right = bf16[14,3,512]{2,1,0:T(4,128)(2,1)S(1)} collective-permute-done((bf16[14,3,512]{2,1,0:T(4,128)(2,1)S(1)}, bf16[14,3,512]{2,1,0:T(4,128)(2,1)S(1)}, u32[]{:S(2)}, u32[]{:S(2)}) %collective-permute-start.7) | collective-permute-done | bytes 43040 | tf_op jit(solution)/shard_map/ppermute | solution.py:283
  137.4 5.4 %features_part.1 = bf16[8,32,512]{2,1,0:T(8,128)(2,1)} custom-call(bf16[8,32,512]{2,1,0:T(8,128)(2,1)S(1)} %copy-done.9, bf16[3,32,512]{2,1,0:T(8,128)(2,1)S(1)} %collective-permute-done.4.top, bf16[3,32,512]{2,1,0:T(8,128)(2,1)S(1)} %collective-permute-done.5.bottom, bf16[14,3,512]{2,1,0:T(4,128)(2,1)S(1)} %collective-permute-done.6.left, ...), custom_call_target="tpu_custom_call" | custom-call | flops 30000000 | bytes 2000000 | tf_op jit(solution)/shard_map/features_part/pallas_call | solution.py:270
  144.1 1.9 %convert_reduce_fusion = f32[32,512]{1,0:T(8,128)S(1)} fusion(bf16[64,32,512]{2,1,0:T(8,128)(2,1)} %all-to-all-done), kind=kLoop, calls=%fused_computation | loop fusion | flops 2080768 | bytes 2162688 | tf_op jit(solution)/shard_map/reduce_sum | solution.py:327
  (94 shorter events, 20.0 us)
Async XLA Ops:
  1.6 11.5 %collective-permute-start = (bf16[3,32,512]{2,1,0:T(8,128)(2,1)S(1)}, bf16[3,32,512]{2,1,0:T(8,128)(2,1)S(1)}, u32[]{:S(2)}, u32[]{:S(2)}) collective-permute-start(bf16[3,32,512]{2,1,0:T(8,128)(2,1)S(1)} %get-tuple-element.37), channel_id=1, source_target_pairs={{0,16},{16,32},{32,48},{48,64},{64,80},{80,96},{96,112},{1,17},{17... | collective-permute-start | bytes 294920 | tf_op jit(solution)/shard_map/ppermute | solution.py:283
  5.5 6.9 %collective-permute-start.1 = (bf16[3,32,512]{2,1,0:T(8,128)(2,1)S(1)}, bf16[3,32,512]{2,1,0:T(8,128)(2,1)S(1)}, u32[]{:S(2)}, u32[]{:S(2)}) collective-permute-start(bf16[3,32,512]{2,1,0:T(8,128)(2,1)S(1)} %get-tuple-element.36), channel_id=1, source_target_pairs={{16,0},{32,16},{48,32},{64,48},{80,64},{96,80},{112,96},{17,1},{33... | collective-permute-start | bytes 294920 | tf_op jit(solution)/shard_map/ppermute | solution.py:283
  13.8 7.9 %collective-permute-start.2 = (bf16[14,3,512]{2,1,0:T(4,128)(2,1)S(1)}, bf16[14,3,512]{2,1,0:T(4,128)(2,1)S(1)}, u32[]{:S(2)}, u32[]{:S(2)}) collective-permute-start(bf16[14,3,512]{2,1,0:T(4,128)(2,1)S(1)} %pad_maximum_fusion), channel_id=1, source_target_pairs={{0,1},{1,2},{2,3},{3,4},{4,5},{5,6},{6,7},{7,8},{8,9},{9,10},{10,1... | collective-permute-start | bytes 129032 | tf_op jit(solution)/shard_map/ppermute | solution.py:283
  19.7 6.4 %collective-permute-start.3 = (bf16[14,3,512]{2,1,0:T(4,128)(2,1)S(1)}, bf16[14,3,512]{2,1,0:T(4,128)(2,1)S(1)}, u32[]{:S(2)}, u32[]{:S(2)}) collective-permute-start(bf16[14,3,512]{2,1,0:T(4,128)(2,1)S(1)} %pad_maximum_fusion.1), channel_id=1, source_target_pairs={{1,0},{2,1},{3,2},{4,3},{5,4},{6,5},{7,6},{8,7},{9,8},{10,9},{11,1... | collective-permute-start | bytes 129032 | tf_op jit(solution)/shard_map/ppermute | solution.py:283
  26.7 0.9 copy-start
  27.7 1.6 %copy-start.2 = (bf16[2048,512]{1,0:T(8,128)(2,1)S(1)}, bf16[2048,512]{1,0:T(8,128)(2,1)}, u32[]{:S(2)}) copy-start(bf16[2048,512]{1,0:T(8,128)(2,1)} %w_out.3) | copy-start | bytes 6291460
  29.3 1.6 %copy-start.4 = (bf16[512,2048]{1,0:T(8,128)(2,1)S(1)}, bf16[512,2048]{1,0:T(8,128)(2,1)}, u32[]{:S(2)}) copy-start(bf16[512,2048]{1,0:T(8,128)(2,1)} %w_in.3) | copy-start | bytes 6291460
  30.9 0.9 copy-start.6
  31.8 0.9 copy-start.18
  33.4 0.9 copy-start.23
  39.6 15.8 %copy-start.1 = (bf16[8,32,512]{2,1,0:T(8,128)(2,1)S(1)}, bf16[8,32,512]{2,1,0:T(8,128)(2,1)}, u32[]{:S(2)}) copy-start(bf16[8,32,512]{2,1,0:T(8,128)(2,1)} %cot.1) | copy-start | bytes 786436
  39.6 15.8 %copy-start.21 = (f32[512]{0:T(512)S(1)}, f32[512]{0:T(512)}, u32[]{:S(2)}) copy-start(f32[512]{0:T(512)} %param.21) | copy-start | bytes 6148
  39.6 15.8 %copy-start.26 = (f32[512]{0:T(512)S(1)}, f32[512]{0:T(512)}, u32[]{:S(2)}) copy-start(f32[512]{0:T(512)} %param.20) | copy-start | bytes 6148
  50.8 1.0 copy-start.10
  51.8 1.0 copy-start.12
  54.2 6.4 %copy-start.28 = (f32[512]{0:T(512)S(1)}, f32[512]{0:T(512)}, u32[]{:S(2)}) copy-start(f32[512]{0:T(512)} %param.15) | copy-start | bytes 6148
  54.2 26.1 %collective-permute-start.8 = (bf16[64,32,512]{2,1,0:T(8,128)(2,1)}, bf16[64,32,512]{2,1,0:T(8,128)(2,1)}, u32[]{:S(2)}, u32[]{:S(2)}) collective-permute-start(bf16[64,32,512]{2,1,0:T(8,128)(2,1)} %get-tuple-element.26), channel_id=1, source_target_pairs={{0,1},{1,0},{2,3},{3,2},{4,5},{5,4},{6,7},{7,6},{8,9},{9,8},{10,11... | collective-permute-start | bytes 6291464 | tf_op jit(solution)/shard_map/ppermute | solution.py:309
  55.4 1.6 %copy-start.3 = (bf16[2048,512]{1,0:T(8,128)(2,1)S(1)}, bf16[2048,512]{1,0:T(8,128)(2,1)}, u32[]{:S(2)}) copy-start(bf16[2048,512]{1,0:T(8,128)(2,1)} %w_out.3) | copy-start | bytes 6291460
  57.0 0.9 copy-start.7
  57.9 1.2 copy-start.13
  59.2 1.6 %copy-start.5 = (bf16[512,2048]{1,0:T(8,128)(2,1)S(1)}, bf16[512,2048]{1,0:T(8,128)(2,1)}, u32[]{:S(2)}) copy-start(bf16[512,2048]{1,0:T(8,128)(2,1)} %w_in.3) | copy-start | bytes 6291460
  59.2 1.9 %copy-start.11 = (bf16[256,2048]{1,0:T(8,128)(2,1)S(1)}, bf16[256,2048]{1,0:T(8,128)(2,1)}, u32[]{:S(2)}) copy-start(bf16[256,2048]{1,0:T(8,128)(2,1)} %copy-done.10) | copy-start | bytes 3145732
  59.2 2.1 %copy-start.15 = (f32[256,512]{1,0:T(8,128)S(1)}, f32[256,512]{1,0:T(8,128)}, u32[]{:S(2)}) copy-start(f32[256,512]{1,0:T(8,128)} %copy-done.14) | copy-start | bytes 1572868
  61.3 0.9 copy-start.17
  71.1 18.7 %all-to-all-start.1 = ((f32[128,4,128]{2,1,0:T(4,128)}), f32[128,4,128]{2,1,0:T(4,128)S(1)}, u32[]{:S(2)}, u32[]{:S(2)}) async-start(f32[128,4,128]{2,1,0:T(4,128)} %maximum_maximum_fusion), calls=%async_computation.1 | async-start | bytes 524288 | tf_op jit(solution)/shard_map/all_to_all | solution.py:326
  84.2 12.5 %copy-start.9 = (bf16[8,32,512]{2,1,0:T(8,128)(2,1)S(1)}, bf16[8,32,512]{2,1,0:T(8,128)(2,1)}, u32[]{:S(2)}) copy-start(bf16[8,32,512]{2,1,0:T(8,128)(2,1)} %copy-done.8) | copy-start | bytes 786436
  84.2 53.2 %copy-start.19 = (f32[49,512]{1,0:T(8,128)S(1)}, f32[49,512]{1,0:T(8,128)}, u32[]{:S(2)}) copy-start(f32[49,512]{1,0:T(8,128)} %taps.3) | copy-start | bytes 301060
  89.8 54.3 %all-to-all-start = ((bf16[64,32,512]{2,1,0:T(8,128)(2,1)}), bf16[64,32,512]{2,1,0:T(8,128)(2,1)}, u32[]{:S(2)}, u32[]{:S(2)}) async-start(bf16[64,32,512]{2,1,0:T(8,128)(2,1)} %add_convert_fusion), calls=%async_computation | async-start | bytes 4194304 | tf_op jit(solution)/shard_map/all_to_all | solution.py:312
  96.7 27.3 %collective-permute-start.5 = (bf16[3,32,512]{2,1,0:T(8,128)(2,1)S(1)}, bf16[3,32,512]{2,1,0:T(8,128)(2,1)S(1)}, u32[]{:S(2)}, u32[]{:S(2)}) collective-permute-start(bf16[3,32,512]{2,1,0:T(8,128)(2,1)S(1)} %get-tuple-element.32), channel_id=1, source_target_pairs={{16,0},{32,16},{48,32},{64,48},{80,64},{96,80},{112,96},{17,1},{33... | collective-permute-start | bytes 294920 | tf_op jit(solution)/shard_map/ppermute | solution.py:283
  100.4 25.8 %collective-permute-start.4 = (bf16[3,32,512]{2,1,0:T(8,128)(2,1)S(1)}, bf16[3,32,512]{2,1,0:T(8,128)(2,1)S(1)}, u32[]{:S(2)}, u32[]{:S(2)}) collective-permute-start(bf16[3,32,512]{2,1,0:T(8,128)(2,1)S(1)} %get-tuple-element.33), channel_id=1, source_target_pairs={{0,16},{16,32},{32,48},{48,64},{64,80},{80,96},{96,112},{1,17},{17... | collective-permute-start | bytes 294920 | tf_op jit(solution)/shard_map/ppermute | solution.py:283
  126.3 6.6 %collective-permute-start.6 = (bf16[14,3,512]{2,1,0:T(4,128)(2,1)S(1)}, bf16[14,3,512]{2,1,0:T(4,128)(2,1)S(1)}, u32[]{:S(2)}, u32[]{:S(2)}) collective-permute-start(bf16[14,3,512]{2,1,0:T(4,128)(2,1)S(1)} %pad_maximum_fusion.2), channel_id=1, source_target_pairs={{0,1},{1,2},{2,3},{3,4},{4,5},{5,6},{6,7},{7,8},{8,9},{9,10},{10,1... | collective-permute-start | bytes 129032 | tf_op jit(solution)/shard_map/ppermute | solution.py:283
  131.0 6.4 %collective-permute-start.7 = (bf16[14,3,512]{2,1,0:T(4,128)(2,1)S(1)}, bf16[14,3,512]{2,1,0:T(4,128)(2,1)S(1)}, u32[]{:S(2)}, u32[]{:S(2)}) collective-permute-start(bf16[14,3,512]{2,1,0:T(4,128)(2,1)S(1)} %pad_maximum_fusion.3), channel_id=1, source_target_pairs={{1,0},{2,1},{3,2},{4,3},{5,4},{6,5},{7,6},{8,7},{9,8},{10,9},{11,1... | collective-permute-start | bytes 129032 | tf_op jit(solution)/shard_map/ppermute | solution.py:283
  (15 other events, 10.7 us)

commit v3 on v2

v3 whole, which is shorter than its diff:
```python
import math

import jax
import jax.numpy as jnp
from jax import lax
from jax.experimental import pallas as pl
from jax.experimental.pallas import tpu as pltpu
from jax.sharding import Mesh
from jax.sharding import PartitionSpec as P

CHIPS = ("z", "yh", "x", "yl")
EVERY = CHIPS + ("c",)
ROW = ("z", "yh")
COL = ("x", "yl", "c")
ROWS, COLS, CH, HID, CHUNK = 8, 32, 512, 2048, 512
COUNT = ROWS * COLS
STEPS = HID // CHUNK
PAD = (ROWS + 6, COLS + 8, CH)
F32, BF16 = jnp.float32, jnp.bfloat16
VMEM_BYTES = 60 * 1024 * 1024


def dot_nn(left, right):
    return lax.dot_general(left, right, (((1,), (0,)), ((), ())), preferred_element_type=F32)


def dot_nt(left, right):
    return lax.dot_general(left, right, (((1,), (1,)), ((), ())), preferred_element_type=F32)


def dot_tn(left, right):
    return lax.dot_general(left, right, (((0,), (0,)), ((), ())), preferred_element_type=F32)


def assemble(pad, tile, top, bottom, left, right):
    pad[0:3, 3 : 3 + COLS, :] = top[...].astype(F32)
    pad[3 : 3 + ROWS, 3 : 3 + COLS, :] = tile[...].astype(F32)
    pad[3 + ROWS : 6 + ROWS, 3 : 3 + COLS, :] = bottom[...].astype(F32)
    pad[:, 0:3, :] = left[...].astype(F32)
    pad[:, 3 + COLS : 6 + COLS, :] = right[...].astype(F32)


def lanes_of(block):
    return pl.ds(pl.multiple_of(block * 128, 128), 128)


def depthwise(pad, taps, finish, flip):
    def block(cb, carry):
        lanes = lanes_of(cb)
        totals = [jnp.zeros((ROWS, 8, 128), F32) for _ in range(COLS // 8)]
        for s in range(7):
            weights = []
            for r in range(7):
                tap = 7 * (6 - r) + 6 - s if flip else 7 * r + s
                weights.append(taps[tap : tap + 1, lanes].reshape(1, 1, 128))
            for cg in range(COLS // 8):
                band = pad[:, 8 * cg + s : 8 * cg + s + 8, lanes]
                for r in range(7):
                    totals[cg] = totals[cg] + band[r : r + ROWS] * weights[r]
        for cg in range(COLS // 8):
            finish(cg, lanes, totals[cg])
        return carry

    lax.fori_loop(0, CH // 128, block, 0)


def grads_kernel(
    core_ref, tile, top, bottom, left, right, cot, taps, dw_bias, gain, shift, scale, b_out,
    w_in, b_in, w_out,
    pad, block_out, d_conv, d_first, d_last, rows_out, bias_out, mine_out, theirs_out, mine_in, theirs_in,
    conv, x_hat, rstd, normed, d_branch, branch, d_normed,
):
    step = pl.program_id(0)
    first = core_ref[0] == 0

    @pl.when(step == 0)
    def _():
        assemble(pad, tile, top, bottom, left, right)

        def finish(cg, lanes, total):
            conv[:, 8 * cg : 8 * cg + 8, lanes] = total

        depthwise(pad, taps, finish, False)
        rows = conv[...].reshape(COUNT, CH) + dw_bias[...]
        centred = rows - jnp.mean(rows, axis=-1, keepdims=True)
        inverse = lax.rsqrt(jnp.mean(centred * centred, axis=-1, keepdims=True) + 1e-06)
        hat = centred * inverse
        x_hat[...] = hat
        rstd[...] = inverse
        normed[...] = (hat * gain[...] + shift[...]).astype(BF16)
        d_branch[...] = (cot[...].astype(F32) * scale[...]).astype(BF16)
        branch[...] = jnp.broadcast_to(b_out[...], (COUNT, CH))
        d_normed[...] = jnp.zeros((COUNT, CH), F32)

    pre_act = dot_nn(normed[...], w_in[...]) + b_in[...]
    cumul = 0.5 * (1.0 + lax.erf(pre_act * 0.7071067811865476))
    act = (pre_act * cumul).astype(BF16)
    slope = cumul + pre_act * jnp.exp(-0.5 * pre_act * pre_act) * 0.3989422804014327
    d_pre = (dot_nt(d_branch[...], w_out[...]) * slope).astype(BF16)
    branch[...] += dot_nn(act, w_out[...])
    d_normed[...] += dot_nt(d_pre, w_in[...])

    bias = jnp.sum(d_pre.astype(F32), axis=0, keepdims=True)
    fourth = lax.broadcasted_iota(jnp.int32, (8, CHUNK), 1) % 4
    spaced = jnp.where(fourth == lax.broadcasted_iota(jnp.int32, (8, CHUNK), 0), bias, 0.0).astype(BF16)
    source = lax.broadcasted_iota(jnp.int32, (CHUNK, 128), 0) // 4
    pick = (source == lax.broadcasted_iota(jnp.int32, (CHUNK, 128), 1)).astype(F32).astype(BF16)
    bias_out[...] = dot_nn(spaced, pick)

    term = dot_tn(act, d_branch[...]).reshape(CHUNK // 32, 2, 16, CH)

    def by_lanes(part):
        return jnp.concatenate([part[:, :, 128 * k : 128 * k + 128] for k in range(4)], axis=1)

    mine_out[...] = by_lanes(jnp.where(first, term[:, 0], term[:, 1])).astype(BF16)
    theirs_out[...] = by_lanes(jnp.where(first, term[:, 1], term[:, 0])).astype(BF16)

    term = dot_tn(normed[...], d_pre).reshape(64, 8, CHUNK)
    upper = lax.broadcasted_iota(jnp.int32, (64, 8, 128), 1) < 4
    kept, given = [], []
    for k in range(2):
        low = term[:, :, 128 * k : 128 * k + 128]
        high = term[:, :, 256 + 128 * k : 384 + 128 * k]
        zero = jnp.where(upper, low, pltpu.roll(high, 4, 1))
        one = jnp.where(upper, pltpu.roll(low, 4, 1), high)
        kept.append(jnp.where(first, zero, one))
        given.append(jnp.where(first, one, zero))
    mine_in[...] = jnp.concatenate(kept, axis=1).astype(BF16)
    theirs_in[...] = jnp.concatenate(given, axis=1).astype(BF16)

    @pl.when(step == STEPS - 1)
    def _():
        hat = x_hat[...]
        d_norm = d_normed[...]
        d_hat = d_norm * gain[...]
        grad = rstd[...] * (
            d_hat
            - jnp.mean(d_hat, axis=-1, keepdims=True)
            - hat * jnp.mean(d_hat * hat, axis=-1, keepdims=True)
        )
        grad = grad.astype(BF16)
        out = grad.reshape(ROWS, COLS, CH)
        d_conv[...] = out
        d_first[...] = out[:3]
        d_last[...] = out[ROWS - 3 :]
        whole_branch = branch[...]
        block_out[...] = (tile[...].reshape(COUNT, CH).astype(F32) + scale[...] * whole_branch).astype(BF16)
        rows_out[0:1, :] = jnp.sum(grad.astype(F32), axis=0, keepdims=True)
        rows_out[1:2, :] = jnp.sum(d_norm * hat, axis=0, keepdims=True)
        rows_out[2:3, :] = jnp.sum(d_norm, axis=0, keepdims=True)
        rows_out[3:4, :] = jnp.sum(d_branch[...].astype(F32), axis=0, keepdims=True)
        rows_out[4:5, :] = jnp.sum(cot[...].astype(F32) * whole_branch, axis=0, keepdims=True)


def whole(shape):
    return pl.BlockSpec(shape, lambda *_: (0,) * len(shape))


def grads(*operands):
    vector = whole((1, CH))
    half = (64, 64, 128)
    by_chip = pl.BlockSpec((CHUNK // 32, 64, 128), lambda t: (t, 0, 0))
    by_row = pl.BlockSpec((64, 16, 128), lambda t: (0, t, 0))
    shape = jax.ShapeDtypeStruct
    return pl.pallas_call(
        grads_kernel,
        grid=(STEPS,),
        in_specs=[
            pl.BlockSpec(memory_space=pltpu.SMEM),
            whole((ROWS, COLS, CH)),
            whole((3, COLS, CH)),
            whole((3, COLS, CH)),
            whole((ROWS + 6, 3, CH)),
            whole((ROWS + 6, 3, CH)),
            whole((COUNT, CH)),
            whole((49, CH)),
            vector,
            vector,
            vector,
            vector,
            vector,
            pl.BlockSpec((CH, CHUNK), lambda t: (0, t)),
            pl.BlockSpec((1, CHUNK), lambda t: (0, t)),
            pl.BlockSpec((CHUNK, CH), lambda t: (t, 0)),
        ],
        out_specs=[
            whole(PAD),
            whole((COUNT, CH)),
            whole((ROWS, COLS, CH)),
            whole((3, COLS, CH)),
            whole((3, COLS, CH)),
            whole((8, CH)),
            pl.BlockSpec((8, 128), lambda t: (0, t)),
            by_chip,
            by_chip,
            by_row,
            by_row,
        ],
        out_shape=[
            shape(PAD, F32),
            shape((COUNT, CH), BF16),
            shape((ROWS, COLS, CH), BF16),
            shape((3, COLS, CH), BF16),
            shape((3, COLS, CH), BF16),
            shape((8, CH), F32),
            shape((8, CH), F32),
            shape(half, BF16),
            shape(half, BF16),
            shape(half, BF16),
            shape(half, BF16),
        ],
        scratch_shapes=[
            pltpu.VMEM((ROWS, COLS, CH), F32),
            pltpu.VMEM((COUNT, CH), F32),
            pltpu.VMEM((COUNT, 1), F32),
            pltpu.VMEM((COUNT, CH), BF16),
            pltpu.VMEM((COUNT, CH), BF16),
            pltpu.VMEM((COUNT, CH), F32),
            pltpu.VMEM((COUNT, CH), F32),
        ],
        compiler_params=pltpu.CompilerParams(vmem_limit_bytes=VMEM_BYTES),
        cost_estimate=pl.CostEstimate(flops=3_200_000_000, bytes_accessed=12_000_000, transcendentals=1_000_000),
        name="grads",
    )(*operands)


def taps_kernel(pad, d_conv, rows, bias, turned, d_tile, table):
    d_tile[...] = d_conv[...].astype(F32)
    table[48:128, :] = jnp.zeros((80, CH), F32)

    def block(cb, carry):
        lanes = lanes_of(cb)
        for s in range(7):
            totals = [jnp.zeros((8, 128), F32) for _ in range(7)]
            for cg in range(COLS // 8):
                band = pad[:, 8 * cg + s : 8 * cg + s + 8, lanes]
                own = d_tile[:, 8 * cg : 8 * cg + 8, lanes]
                for r in range(7):
                    totals[r] = totals[r] + jnp.sum(band[r : r + ROWS] * own, axis=0)
            for r in range(7):
                table[7 * r + s : 7 * r + s + 1, lanes] = jnp.sum(totals[r], axis=0, keepdims=True)
        return carry

    lax.fori_loop(0, CH // 128, block, 0)
    table[49:54, :] = rows[0:5, :]
    table[54:58, :] = bias[0:4, :]
    turned[...] = table[...].T.reshape(64, 8, 128)


def tap_rows(pad, d_conv, rows, bias):
    return pl.pallas_call(
        taps_kernel,
        out_shape=jax.ShapeDtypeStruct((64, 8, 128), F32),
        scratch_shapes=[pltpu.VMEM((ROWS, COLS, CH), F32), pltpu.VMEM((128, CH), F32)],
        compiler_params=pltpu.CompilerParams(vmem_limit_bytes=VMEM_BYTES),
        cost_estimate=pl.CostEstimate(flops=30_000_000, bytes_accessed=2_000_000, transcendentals=0),
        name="tap_rows",
    )(pad, d_conv, rows, bias)


def add_kernel(out_one, out_two, in_one, in_two, small_one, small_two, total):
    add = lambda one, two: (one[...].astype(F32) + two[...].astype(F32)).astype(BF16)
    total[:, 0:64, :] = add(out_one, out_two)
    total[:, 64:128, :] = add(in_one, in_two)
    total[:, 128:136, :] = add(small_one, small_two)


def add_pair(*operands):
    half = pl.BlockSpec((16, 64, 128), lambda t: (t, 0, 0))
    small = pl.BlockSpec((16, 8, 128), lambda t: (t, 0, 0))
    return pl.pallas_call(
        add_kernel,
        grid=(4,),
        in_specs=[half, half, half, half, small, small],
        out_specs=pl.BlockSpec((16, 136, 128), lambda t: (t, 0, 0)),
        out_shape=jax.ShapeDtypeStruct((64, 136, 128), BF16),
        compiler_params=pltpu.CompilerParams(vmem_limit_bytes=VMEM_BYTES),
        cost_estimate=pl.CostEstimate(flops=1_000_000, bytes_accessed=6_000_000, transcendentals=0),
        name="add_pair",
    )(*operands)


def sum_kernel(factor, core_ref, spread, g_in, g_out, g_channel, g_bias, total):
    step = pl.program_id(0)
    part = jnp.sum(spread[...].astype(F32), axis=0)

    @pl.when(step == 0)
    def _():
        total[...] = part

    @pl.when(step > 0)
    def _():
        total[...] += part

    @pl.when(step == pl.num_programs(0) - 1)
    def _():
        for k in range(4):
            g_out[:, 128 * k : 128 * k + 128] = total[16 * k : 16 * k + 16, :] * factor
        for t in range(STEPS):
            for k in range(2):
                own = total[64 + 16 * t + 8 * k : 72 + 16 * t + 8 * k, :] * factor
                at = CHUNK * t + 128 * k
                g_in[:, at : at + 128] = own[0:4]
                g_in[:, at + 256 : at + 384] = own[4:8]
        small = total[128:136, :] * factor
        small = jnp.where(core_ref[0] == 0, small, pltpu.roll(small, 4, 0))
        g_channel[...] = small.T[:54, :4]
        g_bias[...] = small[0:4, 54:58]


def sum_chips(core, spread, factor):
    shape = jax.ShapeDtypeStruct
    return pl.pallas_call(
        lambda *refs: sum_kernel(factor, *refs),
        grid=(4,),
        in_specs=[pl.BlockSpec(memory_space=pltpu.SMEM), pl.BlockSpec((16, 136, 128), lambda t: (t, 0, 0))],
        out_specs=[whole((4, HID)), whole((16, CH)), whole((54, 4)), whole((4, 4))],
        out_shape=[shape((4, HID), F32), shape((16, CH), F32), shape((54, 4), F32), shape((4, 4), F32)],
        scratch_shapes=[pltpu.VMEM((136, 128), F32)],
        compiler_params=pltpu.CompilerParams(vmem_limit_bytes=VMEM_BYTES),
        cost_estimate=pl.CostEstimate(flops=1_000_000, bytes_accessed=2_000_000, transcendentals=0),
        name="sum_chips",
    )(core, spread)


def features_kernel(d_conv, top, bottom, left, right, cot, taps, out, pad):
    assemble(pad, d_conv, top, bottom, left, right)

    def finish(cg, lanes, total):
        columns = slice(8 * cg, 8 * cg + 8)
        pad[0:ROWS, columns, lanes] = total

    depthwise(pad, taps, finish, True)
    out[...] = (cot[...].astype(F32) + pad[0:ROWS, 0:COLS, :]).astype(BF16)


def features_part(d_conv, top, bottom, left, right, cot, taps):
    return pl.pallas_call(
        features_kernel,
        out_shape=jax.ShapeDtypeStruct((ROWS, COLS, CH), BF16),
        scratch_shapes=[pltpu.VMEM(PAD, F32)],
        compiler_params=pltpu.CompilerParams(vmem_limit_bytes=VMEM_BYTES),
        cost_estimate=pl.CostEstimate(flops=30_000_000, bytes_accessed=2_000_000, transcendentals=0),
        name="features_part",
    )(d_conv, top, bottom, left, right, cot, taps)


def shift_by(value, axis, way):
    count = lax.axis_size(axis)
    pairs = [(i, i + way) for i in range(count) if 0 <= i + way < count]
    return lax.ppermute(value, axis, pairs)


def halo_rows(first, last):
    return shift_by(last, ROW, 1), shift_by(first, ROW, -1)


def halo_sides(top, tile, bottom):
    tail = [part[:, COLS - 3 :] for part in (top, tile, bottom)]
    head = [part[:, :3] for part in (top, tile, bottom)]
    return jnp.concatenate(tail, axis=0), jnp.concatenate(head, axis=0)


def halo_cols(tail, head):
    return shift_by(tail, COL, 1), shift_by(head, COL, -1)


def swap(value):
    return lax.ppermute(value, "c", [(0, 1), (1, 0)])


def shards(
    features, cotangent, dw_kernel, dw_bias, norm_gain_vector, norm_bias,
    pw_in_weight, pw_in_bias, pw_out_weight, pw_out_bias, layer_scale,
):
    factor = 1.0 / math.sqrt(COUNT * lax.axis_size(EVERY))
    core = lax.axis_index("c").astype(jnp.int32).reshape(1)
    row = lambda vector: vector.reshape(1, -1)
    top, bottom = halo_rows(features[:3], features[ROWS - 3 :])
    left, right = halo_cols(*halo_sides(top, features, bottom))
    pad, block_rows, d_conv, d_first, d_last, rows, bias, mine_out, theirs_out, mine_in, theirs_in = grads(
        core, features, top, bottom, left, right, cotangent.reshape(COUNT, CH), dw_kernel, row(dw_bias),
        row(norm_gain_vector), row(norm_bias), row(layer_scale), row(pw_out_bias),
        pw_in_weight, row(pw_in_bias), pw_out_weight,
    )
    met_out, met_in = swap(theirs_out), swap(theirs_in)
    d_top, d_bottom = halo_rows(d_first, d_last)
    small = tap_rows(pad, d_conv, rows, bias)
    met_small = swap(small)
    tail, head = halo_sides(d_top, d_conv, d_bottom)
    message = add_pair(mine_out, met_out, mine_in, met_in, small, met_small)
    message, tail, head = lax.optimization_barrier((message, tail, head))
    spread = lax.all_to_all(message, CHIPS, 0, 0, tiled=True)
    d_left, d_right = halo_cols(tail, head)
    grad_features = features_part(d_conv, d_top, d_bottom, d_left, d_right, cotangent, dw_kernel)
    grad_in, grad_out, grad_channel, grad_bias = sum_chips(core, spread, factor)
    return (
        block_rows.reshape(ROWS, COLS, CH),
        grad_features,
        grad_in,
        grad_out,
        grad_channel,
        grad_bias.reshape(-1),
    )


def solution(mesh):
    fine = Mesh(mesh.devices.reshape(4, 2, 4, 2, 2), EVERY)
    return jax.shard_map(
        shards,
        mesh=fine,
        in_specs=(P(ROW, COL, None), P(ROW, COL, None)) + (P(),) * 9,
        out_specs=(
            P(ROW, COL, None),
            P(ROW, COL, None),
            P(EVERY, None),
            P(EVERY, None),
            P(None, EVERY),
            P(EVERY),
        ),
        check_vma=False,
    )
```

time: 148 us -> 118 us (0.80)
  the two profiles are of different devices: /device:TPU:41 before, /device:TPU:62 now
where the time goes in v3:
time: 118 us; the launch traced here: 117 us
  starting transfers between devices  37.8 us (32%)
  Pallas kernels  36.4 us (31%)
  waiting for transfers between devices  31.2 us (26%)
  local copies, waits for them, and re-layouts  10.2 us (9%)
    ppermute x8, waiting for transfers between devices, shift_by(): return lax.ppermute(value, axis, pairs)  29.6 us
    ppermute x8, starting transfers between devices, shift_by(): return lax.ppermute(value, axis, pairs)  25.8 us
    pallas_call x1, Pallas kernels, grads(): pl.pallas_call(grads_kernel, grid=(STEPS,), in_specs=[pl.BlockSpec(memory...  14.8 us
    all_to_all x1, starting transfers between devices, shards(): spread = lax.all_to_all(message, CHIPS, 0, 0, tiled=True)  11.4 us
    pallas_call x1, Pallas kernels, tap_rows(): pl.pallas_call(taps_kernel, out_shape=jax.ShapeDtypeStruct((64, 8, 128),...  7.4 us
    pallas_call x1, Pallas kernels, features_part(): pl.pallas_call(features_kernel, out_shape=jax.ShapeDtypeStruct((ROWS, COL...  6.54 us
    unnamed x25, local copies, waits for them, and re-layouts  6.14 us
    pallas_call x1, Pallas kernels, add_pair(): pl.pallas_call(add_kernel, grid=(4,), in_specs=[half, half, half, half, s...  4.35 us
  transfers between devices with their start and end apart: 12, of which 4 were waited for; matrix products, arithmetic and copies ran while one was open for 2% of the time, Pallas kernels for 12%

profile of v3, /device:TPU:62, one launch (start us, length us, event | category | flops | bytes accessed | tf_op | source)
XLA Modules:
  0.0 116.7 jit_solution(12259151952011320131)
XLA Ops:
  0.6 1.0 fusion.2
  1.6 4.5 %collective-permute-start = (bf16[3,32,512]{2,1,0:T(8,128)(2,1)S(1)}, bf16[3,32,512]{2,1,0:T(8,128)(2,1)S(1)}, u32[]{:S(2)}, u32[]{:S(2)}) collective-permute-start(bf16[3,32,512]{2,1,0:T(8,128)(2,1)S(1)} %get-tuple-element.53), channel_id=1, source_target_pairs={{0,16},{16,32},{32,48},{48,64},{64,80},{80,96},{96,112},{1,17},{17... | collective-permute-start | bytes 294920 | tf_op jit(solution)/shard_map/ppermute | solution.py:351
  6.1 2.8 %collective-permute-start.1 = (bf16[3,32,512]{2,1,0:T(8,128)(2,1)S(1)}, bf16[3,32,512]{2,1,0:T(8,128)(2,1)S(1)}, u32[]{:S(2)}, u32[]{:S(2)}) collective-permute-start(bf16[3,32,512]{2,1,0:T(8,128)(2,1)S(1)} %get-tuple-element.52), channel_id=1, source_target_pairs={{16,0},{32,16},{48,32},{64,48},{80,64},{96,80},{112,96},{17,1},{33... | collective-permute-start | bytes 294920 | tf_op jit(solution)/shard_map/ppermute | solution.py:351
  9.0 0.9 fusion.1
  9.9 5.2 %collective-permute-done.1.bottom = bf16[3,32,512]{2,1,0:T(8,128)(2,1)S(1)} collective-permute-done((bf16[3,32,512]{2,1,0:T(8,128)(2,1)S(1)}, bf16[3,32,512]{2,1,0:T(8,128)(2,1)S(1)}, u32[]{:S(2)}, u32[]{:S(2)}) %collective-permute-start.1) | collective-permute-done | bytes 98336 | tf_op jit(solution)/shard_map/ppermute | solution.py:351
  15.1 1.9 %collective-permute-start.2 = (bf16[14,3,512]{2,1,0:T(4,128)(2,1)S(1)}, bf16[14,3,512]{2,1,0:T(4,128)(2,1)S(1)}, u32[]{:S(2)}, u32[]{:S(2)}) collective-permute-start(bf16[14,3,512]{2,1,0:T(4,128)(2,1)S(1)} %pad_maximum_fusion), channel_id=1, source_target_pairs={{0,1},{1,2},{2,3},{3,4},{4,5},{5,6},{6,7},{7,8},{8,9},{9,10},{10,1... | collective-permute-start | bytes 129032 | tf_op jit(solution)/shard_map/ppermute | solution.py:351
  17.1 3.6 %collective-permute-start.3 = (bf16[14,3,512]{2,1,0:T(4,128)(2,1)S(1)}, bf16[14,3,512]{2,1,0:T(4,128)(2,1)S(1)}, u32[]{:S(2)}, u32[]{:S(2)}) collective-permute-start(bf16[14,3,512]{2,1,0:T(4,128)(2,1)S(1)} %pad_maximum_fusion.1), channel_id=1, source_target_pairs={{1,0},{2,1},{3,2},{4,3},{5,4},{6,5},{7,6},{8,7},{9,8},{10,9},{11,1... | collective-permute-start | bytes 129032 | tf_op jit(solution)/shard_map/ppermute | solution.py:351
  20.8 1.8 %collective-permute-done.3.right = bf16[14,3,512]{2,1,0:T(4,128)(2,1)S(1)} collective-permute-done((bf16[14,3,512]{2,1,0:T(4,128)(2,1)S(1)}, bf16[14,3,512]{2,1,0:T(4,128)(2,1)S(1)}, u32[]{:S(2)}, u32[]{:S(2)}) %collective-permute-start.3) | collective-permute-done | bytes 43040 | tf_op jit(solution)/shard_map/ppermute | solution.py:351
  22.6 0.6 copy-done.11
  23.2 14.8 %grads.1 = (f32[14,40,512]{2,1,0:T(8,128)}, bf16[256,512]{1,0:T(8,128)(2,1)}, bf16[8,32,512]{2,1,0:T(8,128)(2,1)}, bf16[3,32,512]{2,1,0:T(8,128)(2,1)}, bf16[3,3...) custom-call(s32[1]{0:T(128)} %bitcast.core_ref.refs_0_, ...), custom_call_target="tpu_custom_call" | custom-call | flops 3200000000 | bytes 12000000 | tf_op jit(solution)/shard_map/grads/pallas_call | solution.py:165
  38.0 0.5 collective-permute-start.7
  38.5 3.3 %collective-permute-start.4 = (bf16[3,32,512]{2,1,0:T(8,128)(2,1)}, bf16[3,32,512]{2,1,0:T(8,128)(2,1)S(1)}, u32[]{:S(2)}, u32[]{:S(2)}) collective-permute-start(bf16[3,32,512]{2,1,0:T(8,128)(2,1)} %get-tuple-element.26), channel_id=1, source_target_pairs={{0,16},{16,32},{32,48},{48,64},{64,80},{80,96},{96,112},{1,17},{17... | collective-permute-start | bytes 294920 | tf_op jit(solution)/shard_map/ppermute | solution.py:351
  41.8 4.0 %collective-permute-start.5 = (bf16[3,32,512]{2,1,0:T(8,128)(2,1)}, bf16[3,32,512]{2,1,0:T(8,128)(2,1)S(1)}, u32[]{:S(2)}, u32[]{:S(2)}) collective-permute-start(bf16[3,32,512]{2,1,0:T(8,128)(2,1)} %get-tuple-element.27), channel_id=1, source_target_pairs={{16,0},{32,16},{48,32},{64,48},{80,64},{96,80},{112,96},{17,1},{33... | collective-permute-start | bytes 294920 | tf_op jit(solution)/shard_map/ppermute | solution.py:351
  45.9 0.9 fusion
  46.8 7.4 %tap_rows.1.small_one = f32[64,8,128]{2,1,0:T(8,128)} custom-call(f32[14,40,512]{2,1,0:T(8,128)} %get-tuple-element.32.pad, bf16[8,32,512]{2,1,0:T(8,128)(2,1)} %get-tuple-element.25.d_conv, f32[8,512]{1,0:T(8,128)} %get-tuple-element.33.rows, f32[8,512]{1,0:T(8,128)} %get-tuple-element.34.bias), custom_call_target="tpu_custom_call" | custom-call | flops 30000000 | bytes 2000000 | tf_op jit(solution)/shard_map/tap_rows/pallas_call | solution.py:251
  54.3 0.1 pad_maximum_fusion.2
  54.4 1.6 %collective-permute-done.8.small_two = f32[64,8,128]{2,1,0:T(8,128)S(1)} collective-permute-done((f32[64,8,128]{2,1,0:T(8,128)}, f32[64,8,128]{2,1,0:T(8,128)S(1)}, u32[]{:S(2)}, u32[]{:S(2)}) %collective-permute-start.8) | collective-permute-done | bytes 262176 | tf_op jit(solution)/shard_map/ppermute | solution.py:369
  56.0 0.7 copy-done.3
  56.7 0.4 copy-done.1
  57.0 0.4 copy-done.2
  57.4 4.4 %add_pair.1 = bf16[64,136,128]{2,1,0:T(8,128)(2,1)} custom-call(bf16[64,64,128]{2,1,0:T(8,128)(2,1)} %get-tuple-element.28.out_one, bf16[64,64,128]{2,1,0:T(8,128)(2,1)} %copy-done.1, bf16[64,64,128]{2,1,0:T(8,128)(2,1)} %get-tuple-element.30.in_one, bf16[64,64,128]{2,1,0:T(8,128)(2,1)} %copy-done.2, f32[64,8,128]{2,1,0:T(8,128)} %tap_rows.1.small_one, ...), custom_call_target="tpu_custom_call" | custom-call | flops 1000000 | bytes 6000000 | tf_op jit(solution)/shard_map/add_pair/pallas_call | solution.py:271
  61.8 11.4 %all-to-all-start = ((bf16[64,136,128]{2,1,0:T(8,128)(2,1)}), bf16[64,136,128]{2,1,0:T(8,128)(2,1)S(1)}, u32[]{:S(2)}, u32[]{:S(2)}) async-start(bf16[64,136,128]{2,1,0:T(8,128)(2,1)} %add_pair.1), calls=%async_computation | async-start | bytes 4456448 | tf_op jit(solution)/shard_map/all_to_all | solution.py:393
  73.2 1.9 %collective-permute-start.9 = (bf16[14,3,512]{2,1,0:T(4,128)(2,1)S(1)}, bf16[14,3,512]{2,1,0:T(4,128)(2,1)S(1)}, u32[]{:S(2)}, u32[]{:S(2)}) collective-permute-start(bf16[14,3,512]{2,1,0:T(4,128)(2,1)S(1)} %get-tuple-element.35), channel_id=1, source_target_pairs={{0,1},{1,2},{2,3},{3,4},{4,5},{5,6},{6,7},{7,8},{8,9},{9,10},{10,1... | collective-permute-start | bytes 129032 | tf_op jit(solution)/shard_map/ppermute | solution.py:351
  75.1 3.6 %collective-permute-start.10 = (bf16[14,3,512]{2,1,0:T(4,128)(2,1)S(1)}, bf16[14,3,512]{2,1,0:T(4,128)(2,1)S(1)}, u32[]{:S(2)}, u32[]{:S(2)}) collective-permute-start(bf16[14,3,512]{2,1,0:T(4,128)(2,1)S(1)} %get-tuple-element.36), channel_id=1, source_target_pairs={{1,0},{2,1},{3,2},{4,3},{5,4},{6,5},{7,6},{8,7},{9,8},{10,9},{11,1... | collective-permute-start | bytes 129032 | tf_op jit(solution)/shard_map/ppermute | solution.py:351
  78.8 22.7 %collective-permute-done.9.left = bf16[14,3,512]{2,1,0:T(4,128)(2,1)S(1)} collective-permute-done((bf16[14,3,512]{2,1,0:T(4,128)(2,1)S(1)}, bf16[14,3,512]{2,1,0:T(4,128)(2,1)S(1)}, u32[]{:S(2)}, u32[]{:S(2)}) %collective-permute-start.9) | collective-permute-done | bytes 43040 | tf_op jit(solution)/shard_map/ppermute | solution.py:351
  101.5 0.6 copy-done.6
  102.1 0.6 copy-done.7
  102.8 6.5 %features_part.1 = bf16[8,32,512]{2,1,0:T(8,128)(2,1)} custom-call(bf16[8,32,512]{2,1,0:T(8,128)(2,1)} %get-tuple-element.25.d_conv, bf16[3,32,512]{2,1,0:T(8,128)(2,1)} %copy-done.4, bf16[3,32,512]{2,1,0:T(8,128)(2,1)} %copy-done.5, bf16[14,3,512]{2,1,0:T(4,128)(2,1)} %copy-done.6, bf16[14,3,512]{2,1,0:T(4,128)(2,1)} %copy-done.7, bf16[8,32,512]{2,1,0:T(8,128)(2,1)} %cot.1, ...), custom_call_target="tpu_custom_call" | custom-call | flops 30000000 | bytes 2000000 | tf_op jit(solution)/shard_map/features_part/pallas_call | solution.py:338
  109.3 1.4 %copy-done = bf16[64,136,128]{2,1,0:T(8,128)(2,1)} copy-done((bf16[64,136,128]{2,1,0:T(8,128)(2,1)}, bf16[64,136,128]{2,1,0:T(8,128)(2,1)S(1)}, u32[]{:S(2)}) %copy-start) | copy-done | bytes 2228248
  110.7 3.3 %sum_chips.1 = (f32[4,2048]{1,0:T(4,128)}, f32[16,512]{1,0:T(8,128)}, f32[54,4]{1,0:T(8,128)}, f32[4,4]{1,0:T(4,128)}) custom-call(s32[1]{0:T(128)} %bitcast.core_ref.refs_0_, bf16[64,136,128]{2,1,0:T(8,128)(2,1)} %copy-done), custom_call_target="tpu_custom_call" | custom-call | flops 1000000 | bytes 2000000 | tf_op jit(solution)/shard_map/sum_chips/pallas_call | solution.py:313
  114.0 1.4 %copy.17 = f32[54,4]{0,1:T(4,128)} copy(f32[54,4]{1,0:T(8,128)} %get-tuple-element.46) | data formatting | bytes 1728
  115.4 1.3 %reshape.51 = f32[16]{0:T(128)} reshape(f32[4,4]{1,0:T(4,128)} %get-tuple-element.41) | data formatting | bytes 128 | tf_op jit(solution)/shard_map/reshape | solution.py:403
  (33 shorter events, 0.3 us)
Async XLA Ops:
  1.6 13.4 %collective-permute-start = (bf16[3,32,512]{2,1,0:T(8,128)(2,1)S(1)}, bf16[3,32,512]{2,1,0:T(8,128)(2,1)S(1)}, u32[]{:S(2)}, u32[]{:S(2)}) collective-permute-start(bf16[3,32,512]{2,1,0:T(8,128)(2,1)S(1)} %get-tuple-element.53), channel_id=1, source_target_pairs={{0,16},{16,32},{32,48},{48,64},{64,80},{80,96},{96,112},{1,17},{17... | collective-permute-start | bytes 294920 | tf_op jit(solution)/shard_map/ppermute | solution.py:351
  6.1 8.9 %collective-permute-start.1 = (bf16[3,32,512]{2,1,0:T(8,128)(2,1)S(1)}, bf16[3,32,512]{2,1,0:T(8,128)(2,1)S(1)}, u32[]{:S(2)}, u32[]{:S(2)}) collective-permute-start(bf16[3,32,512]{2,1,0:T(8,128)(2,1)S(1)} %get-tuple-element.52), channel_id=1, source_target_pairs={{16,0},{32,16},{48,32},{64,48},{80,64},{96,80},{112,96},{17,1},{33... | collective-permute-start | bytes 294920 | tf_op jit(solution)/shard_map/ppermute | solution.py:351
  15.0 7.6 %copy-start.9 = (bf16[3,32,512]{2,1,0:T(8,128)(2,1)}, bf16[3,32,512]{2,1,0:T(8,128)(2,1)S(1)}, u32[]{:S(2)}) copy-start(bf16[3,32,512]{2,1,0:T(8,128)(2,1)S(1)} %collective-permute-done.1.bottom) | copy-start | bytes 294916
  15.0 7.5 %copy-start.8 = (bf16[3,32,512]{2,1,0:T(8,128)(2,1)}, bf16[3,32,512]{2,1,0:T(8,128)(2,1)S(1)}, u32[]{:S(2)}) copy-start(bf16[3,32,512]{2,1,0:T(8,128)(2,1)S(1)} %collective-permute-done.top) | copy-start | bytes 294916
  15.1 5.6 %collective-permute-start.2 = (bf16[14,3,512]{2,1,0:T(4,128)(2,1)S(1)}, bf16[14,3,512]{2,1,0:T(4,128)(2,1)S(1)}, u32[]{:S(2)}, u32[]{:S(2)}) collective-permute-start(bf16[14,3,512]{2,1,0:T(4,128)(2,1)S(1)} %pad_maximum_fusion), channel_id=1, source_target_pairs={{0,1},{1,2},{2,3},{3,4},{4,5},{5,6},{6,7},{7,8},{8,9},{9,10},{10,1... | collective-permute-start | bytes 129032 | tf_op jit(solution)/shard_map/ppermute | solution.py:351
  17.1 5.5 %collective-permute-start.3 = (bf16[14,3,512]{2,1,0:T(4,128)(2,1)S(1)}, bf16[14,3,512]{2,1,0:T(4,128)(2,1)S(1)}, u32[]{:S(2)}, u32[]{:S(2)}) collective-permute-start(bf16[14,3,512]{2,1,0:T(4,128)(2,1)S(1)} %pad_maximum_fusion.1), channel_id=1, source_target_pairs={{1,0},{2,1},{3,2},{4,3},{5,4},{6,5},{7,6},{8,7},{9,8},{10,9},{11,1... | collective-permute-start | bytes 129032 | tf_op jit(solution)/shard_map/ppermute | solution.py:351
  20.8 1.8 %copy-start.10 = (bf16[14,3,512]{2,1,0:T(4,128)(2,1)}, bf16[14,3,512]{2,1,0:T(4,128)(2,1)S(1)}, u32[]{:S(2)}) copy-start(bf16[14,3,512]{2,1,0:T(4,128)(2,1)S(1)} %collective-permute-done.2.left) | copy-start | bytes 129028
  22.6 0.6 copy-start.11
  38.0 18.0 %collective-permute-start.6 = (bf16[64,64,128]{2,1,0:T(8,128)(2,1)}, bf16[64,64,128]{2,1,0:T(8,128)(2,1)S(1)}, u32[]{:S(2)}, u32[]{:S(2)}) collective-permute-start(bf16[64,64,128]{2,1,0:T(8,128)(2,1)} %get-tuple-element.29), channel_id=1, source_target_pairs={{0,1},{1,0},{2,3},{3,2},{4,5},{5,4},{6,7},{7,6},{8,9},{9,8},{10,11... | collective-permute-start | bytes 3145736 | tf_op jit(solution)/shard_map/ppermute | solution.py:369
  38.0 17.9 %collective-permute-start.7 = (bf16[64,64,128]{2,1,0:T(8,128)(2,1)}, bf16[64,64,128]{2,1,0:T(8,128)(2,1)S(1)}, u32[]{:S(2)}, u32[]{:S(2)}) collective-permute-start(bf16[64,64,128]{2,1,0:T(8,128)(2,1)} %get-tuple-element.31), channel_id=1, source_target_pairs={{0,1},{1,0},{2,3},{3,2},{4,5},{5,4},{6,7},{7,6},{8,9},{9,8},{10,11... | collective-permute-start | bytes 3145736 | tf_op jit(solution)/shard_map/ppermute | solution.py:369
  38.5 15.7 %collective-permute-start.4 = (bf16[3,32,512]{2,1,0:T(8,128)(2,1)}, bf16[3,32,512]{2,1,0:T(8,128)(2,1)S(1)}, u32[]{:S(2)}, u32[]{:S(2)}) collective-permute-start(bf16[3,32,512]{2,1,0:T(8,128)(2,1)} %get-tuple-element.26), channel_id=1, source_target_pairs={{0,16},{16,32},{32,48},{48,64},{64,80},{80,96},{96,112},{1,17},{17... | collective-permute-start | bytes 294920 | tf_op jit(solution)/shard_map/ppermute | solution.py:351
  41.8 12.4 %collective-permute-start.5 = (bf16[3,32,512]{2,1,0:T(8,128)(2,1)}, bf16[3,32,512]{2,1,0:T(8,128)(2,1)S(1)}, u32[]{:S(2)}, u32[]{:S(2)}) collective-permute-start(bf16[3,32,512]{2,1,0:T(8,128)(2,1)} %get-tuple-element.27), channel_id=1, source_target_pairs={{16,0},{32,16},{48,32},{64,48},{80,64},{96,80},{112,96},{17,1},{33... | collective-permute-start | bytes 294920 | tf_op jit(solution)/shard_map/ppermute | solution.py:351
  54.2 1.7 %collective-permute-start.8 = (f32[64,8,128]{2,1,0:T(8,128)}, f32[64,8,128]{2,1,0:T(8,128)S(1)}, u32[]{:S(2)}, u32[]{:S(2)}) collective-permute-start(f32[64,8,128]{2,1,0:T(8,128)} %tap_rows.1.small_one), channel_id=1, source_target_pairs={{0,1},{1,0},{2,3},{3,2},{4,5},{5,4},{6,7},{7,6},{8,9},{9,8},{10,11... | collective-permute-start | bytes 786440 | tf_op jit(solution)/shard_map/ppermute | solution.py:369
  54.2 7.5 %copy-start.5 = (bf16[3,32,512]{2,1,0:T(8,128)(2,1)}, bf16[3,32,512]{2,1,0:T(8,128)(2,1)S(1)}, u32[]{:S(2)}) copy-start(bf16[3,32,512]{2,1,0:T(8,128)(2,1)S(1)} %collective-permute-done.5.bottom) | copy-start | bytes 294916
  54.2 7.5 %copy-start.4 = (bf16[3,32,512]{2,1,0:T(8,128)(2,1)}, bf16[3,32,512]{2,1,0:T(8,128)(2,1)S(1)}, u32[]{:S(2)}) copy-start(bf16[3,32,512]{2,1,0:T(8,128)(2,1)S(1)} %collective-permute-done.4.top) | copy-start | bytes 294916
  55.9 0.7 copy-start.3
  56.0 1.1 copy-start.1
  56.0 1.4 %copy-start.2 = (bf16[64,64,128]{2,1,0:T(8,128)(2,1)}, bf16[64,64,128]{2,1,0:T(8,128)(2,1)S(1)}, u32[]{:S(2)}) copy-start(bf16[64,64,128]{2,1,0:T(8,128)(2,1)S(1)} %collective-permute-done.7.in_two) | copy-start | bytes 3145732
  61.8 47.5 %all-to-all-start = ((bf16[64,136,128]{2,1,0:T(8,128)(2,1)}), bf16[64,136,128]{2,1,0:T(8,128)(2,1)S(1)}, u32[]{:S(2)}, u32[]{:S(2)}) async-start(bf16[64,136,128]{2,1,0:T(8,128)(2,1)} %add_pair.1), calls=%async_computation | async-start | bytes 4456448 | tf_op jit(solution)/shard_map/all_to_all | solution.py:393
  73.2 28.3 %collective-permute-start.9 = (bf16[14,3,512]{2,1,0:T(4,128)(2,1)S(1)}, bf16[14,3,512]{2,1,0:T(4,128)(2,1)S(1)}, u32[]{:S(2)}, u32[]{:S(2)}) collective-permute-start(bf16[14,3,512]{2,1,0:T(4,128)(2,1)S(1)} %get-tuple-element.35), channel_id=1, source_target_pairs={{0,1},{1,2},{2,3},{3,4},{4,5},{5,6},{6,7},{7,8},{8,9},{9,10},{10,1... | collective-permute-start | bytes 129032 | tf_op jit(solution)/shard_map/ppermute | solution.py:351
  75.1 26.4 %collective-permute-start.10 = (bf16[14,3,512]{2,1,0:T(4,128)(2,1)S(1)}, bf16[14,3,512]{2,1,0:T(4,128)(2,1)S(1)}, u32[]{:S(2)}, u32[]{:S(2)}) collective-permute-start(bf16[14,3,512]{2,1,0:T(4,128)(2,1)S(1)} %get-tuple-element.36), channel_id=1, source_target_pairs={{1,0},{2,1},{3,2},{4,3},{5,4},{6,5},{7,6},{8,7},{9,8},{10,9},{11,1... | collective-permute-start | bytes 129032 | tf_op jit(solution)/shard_map/ppermute | solution.py:351
  101.5 0.6 copy-start.6
  102.1 0.6 copy-start.7
  109.3 1.4 %copy-start = (bf16[64,136,128]{2,1,0:T(8,128)(2,1)}, bf16[64,136,128]{2,1,0:T(8,128)(2,1)S(1)}, u32[]{:S(2)}) copy-start(bf16[64,136,128]{2,1,0:T(8,128)(2,1)S(1)} %all-to-all-done.refs_1_) | copy-start | bytes 6684676

commit v4 on v3

--- a/solution.py
+++ b/solution.py
@@ -8,10 +8,10 @@
 from jax.sharding import Mesh
 from jax.sharding import PartitionSpec as P
 
-CHIPS = ("z", "yh", "x", "yl")
-EVERY = CHIPS + ("c",)
+EVERY = ("z", "yh", "xh", "xl", "yl", "c")
 ROW = ("z", "yh")
-COL = ("x", "yl", "c")
+COL = ("xh", "xl", "yl", "c")
+GROUP = ("z", "yh", "xh", "yl")
 ROWS, COLS, CH, HID, CHUNK = 8, 32, 512, 2048, 512
 COUNT = ROWS * COLS
 STEPS = HID // CHUNK
@@ -32,12 +32,14 @@
     return lax.dot_general(left, right, (((0,), (0,)), ((), ())), preferred_element_type=F32)
 
 
-def assemble(pad, tile, top, bottom, left, right):
-    pad[0:3, 3 : 3 + COLS, :] = top[...].astype(F32)
+def assemble(pad, tile, row_one, row_two, col_one, col_two, even_row, even_col):
+    rows = row_one[...].astype(F32), row_two[...].astype(F32)
+    cols = col_one[...].astype(F32), col_two[...].astype(F32)
+    pad[0:3, 3 : 3 + COLS, :] = jnp.where(even_row, rows[1], rows[0])
     pad[3 : 3 + ROWS, 3 : 3 + COLS, :] = tile[...].astype(F32)
-    pad[3 + ROWS : 6 + ROWS, 3 : 3 + COLS, :] = bottom[...].astype(F32)
-    pad[:, 0:3, :] = left[...].astype(F32)
-    pad[:, 3 + COLS : 6 + COLS, :] = right[...].astype(F32)
+    pad[3 + ROWS : 6 + ROWS, 3 : 3 + COLS, :] = jnp.where(even_row, rows[0], rows[1])
+    pad[:, 0:3, :] = jnp.where(even_col, cols[1], cols[0])
+    pad[:, 3 + COLS : 6 + COLS, :] = jnp.where(even_col, cols[0], cols[1])
 
 
 def lanes_of(block):
@@ -65,17 +67,18 @@
 
 
 def grads_kernel(
-    core_ref, tile, top, bottom, left, right, cot, taps, dw_bias, gain, shift, scale, b_out,
+    place, tile, row_one, row_two, col_one, col_two, cot, taps, dw_bias, gain, shift, scale, b_out,
     w_in, b_in, w_out,
-    pad, block_out, d_conv, d_first, d_last, rows_out, bias_out, mine_out, theirs_out, mine_in, theirs_in,
+    pad, block_out, d_conv, d_row_one, d_row_two, rows_out, bias_out, mine_out, theirs_out, mine_in, theirs_in,
     conv, x_hat, rstd, normed, d_branch, branch, d_normed,
 ):
     step = pl.program_id(0)
-    first = core_ref[0] == 0
+    first = place[0] == 0
+    even_row = place[1] == 0
 
     @pl.when(step == 0)
     def _():
-        assemble(pad, tile, top, bottom, left, right)
+        assemble(pad, tile, row_one, row_two, col_one, col_two, even_row, first)
 
         def finish(cg, lanes, total):
             conv[:, 8 * cg : 8 * cg + 8, lanes] = total
@@ -141,8 +144,8 @@
         grad = grad.astype(BF16)
         out = grad.reshape(ROWS, COLS, CH)
         d_conv[...] = out
-        d_first[...] = out[:3]
-        d_last[...] = out[ROWS - 3 :]
+        d_row_one[...] = jnp.where(even_row, out[ROWS - 3 :], out[:3])
+        d_row_two[...] = jnp.where(even_row, out[:3], out[ROWS - 3 :])
         whole_branch = branch[...]
         block_out[...] = (tile[...].reshape(COUNT, CH).astype(F32) + scale[...] * whole_branch).astype(BF16)
         rows_out[0:1, :] = jnp.sum(grad.astype(F32), axis=0, keepdims=True)
@@ -258,73 +261,97 @@
     )(pad, d_conv, rows, bias)
 
 
-def add_kernel(out_one, out_two, in_one, in_two, small_one, small_two, total):
-    add = lambda one, two: (one[...].astype(F32) + two[...].astype(F32)).astype(BF16)
-    total[:, 0:64, :] = add(out_one, out_two)
-    total[:, 64:128, :] = add(in_one, in_two)
-    total[:, 128:136, :] = add(small_one, small_two)
+def split_kernel(place, out_one, out_two, in_one, in_two, keep, give):
+    even = place[2] == 0
+    for at, one, two in ((0, out_one, out_two), (64, in_one, in_two)):
+        total = (one[...] + two[...]).reshape(4, 2, 2, 64, 128)
+        keep[:, at : at + 64, :] = jnp.where(even, total[:, 0], total[:, 1]).reshape(8, 64, 128)
+        give[:, at : at + 64, :] = jnp.where(even, total[:, 1], total[:, 0]).reshape(8, 64, 128)
+
+
+def split_pair(*operands):
+    half = pl.BlockSpec((16, 64, 128), lambda t: (t, 0, 0))
+    block = pl.BlockSpec((8, 128, 128), lambda t: (t, 0, 0))
+    return pl.pallas_call(
+        split_kernel,
+        grid=(4,),
+        in_specs=[pl.BlockSpec(memory_space=pltpu.SMEM), half, half, half, half],
+        out_specs=[block, block],
+        out_shape=[jax.ShapeDtypeStruct((32, 128, 128), BF16)] * 2,
+        compiler_params=pltpu.CompilerParams(vmem_limit_bytes=VMEM_BYTES),
+        cost_estimate=pl.CostEstimate(flops=1_000_000, bytes_accessed=6_000_000, transcendentals=0),
+        name="split_pair",
+    )(*operands)
+
+
+def split_small_kernel(place, one, two, keep, give):
+    total = (one[...] + two[...]).reshape(16, 2, 2, 8, 128)
+    even = place[2] == 0
+    keep[...] = jnp.where(even, total[:, 0], total[:, 1]).reshape(32, 8, 128)
+    give[...] = jnp.where(even, total[:, 1], total[:, 0]).reshape(32, 8, 128)
+
+
+def split_small(*operands):
+    return pl.pallas_call(
+        split_small_kernel,
+        in_specs=[pl.BlockSpec(memory_space=pltpu.SMEM)] + [pl.BlockSpec(memory_space=pltpu.VMEM)] * 2,
+        out_shape=[jax.ShapeDtypeStruct((32, 8, 128), F32)] * 2,
+        compiler_params=pltpu.CompilerParams(vmem_limit_bytes=VMEM_BYTES),
+        cost_estimate=pl.CostEstimate(flops=100_000, bytes_accessed=700_000, transcendentals=0),
+        name="split_small",
+    )(*operands)
+
+
+def add_kernel(one, two, small_one, small_two, total):
+    total[:, 0:128, :] = one[...] + two[...]
+    total[:, 128:136, :] = (small_one[...] + small_two[...]).astype(BF16)
 
 
 def add_pair(*operands):
-    half = pl.BlockSpec((16, 64, 128), lambda t: (t, 0, 0))
-    small = pl.BlockSpec((16, 8, 128), lambda t: (t, 0, 0))
+    large = pl.BlockSpec((8, 128, 128), lambda t: (t, 0, 0))
+    small = pl.BlockSpec((8, 8, 128), lambda t: (t, 0, 0))
     return pl.pallas_call(
         add_kernel,
         grid=(4,),
-        in_specs=[half, half, half, half, small, small],
-        out_specs=pl.BlockSpec((16, 136, 128), lambda t: (t, 0, 0)),
-        out_shape=jax.ShapeDtypeStruct((64, 136, 128), BF16),
-        compiler_params=pltpu.CompilerParams(vmem_limit_bytes=VMEM_BYTES),
-        cost_estimate=pl.CostEstimate(flops=1_000_000, bytes_accessed=6_000_000, transcendentals=0),
+        in_specs=[large, large, small, small],
+        out_specs=pl.BlockSpec((8, 136, 128), lambda t: (t, 0, 0)),
+        out_shape=jax.ShapeDtypeStruct((32, 136, 128), BF16),
+        compiler_params=pltpu.CompilerParams(vmem_limit_bytes=VMEM_BYTES),
+        cost_estimate=pl.CostEstimate(flops=1_000_000, bytes_accessed=3_000_000, transcendentals=0),
         name="add_pair",
     )(*operands)
 
 
-def sum_kernel(factor, core_ref, spread, g_in, g_out, g_channel, g_bias, total):
-    step = pl.program_id(0)
-    part = jnp.sum(spread[...].astype(F32), axis=0)
-
-    @pl.when(step == 0)
-    def _():
-        total[...] = part
-
-    @pl.when(step > 0)
-    def _():
-        total[...] += part
-
-    @pl.when(step == pl.num_programs(0) - 1)
-    def _():
-        for k in range(4):
-            g_out[:, 128 * k : 128 * k + 128] = total[16 * k : 16 * k + 16, :] * factor
-        for t in range(STEPS):
-            for k in range(2):
-                own = total[64 + 16 * t + 8 * k : 72 + 16 * t + 8 * k, :] * factor
-                at = CHUNK * t + 128 * k
-                g_in[:, at : at + 128] = own[0:4]
-                g_in[:, at + 256 : at + 384] = own[4:8]
-        small = total[128:136, :] * factor
-        small = jnp.where(core_ref[0] == 0, small, pltpu.roll(small, 4, 0))
-        g_channel[...] = small.T[:54, :4]
-        g_bias[...] = small[0:4, 54:58]
-
-
-def sum_chips(core, spread, factor):
+def sum_kernel(factor, place, spread, g_in, g_out, g_channel, g_bias):
+    total = jnp.sum(spread[...].astype(F32), axis=0) * factor
+    for k in range(4):
+        g_out[:, 128 * k : 128 * k + 128] = total[16 * k : 16 * k + 16, :]
+    for t in range(STEPS):
+        for k in range(2):
+            own = total[64 + 16 * t + 8 * k : 72 + 16 * t + 8 * k, :]
+            at = CHUNK * t + 128 * k
+            g_in[:, at : at + 128] = own[0:4]
+            g_in[:, at + 256 : at + 384] = own[4:8]
+    small = total[128:136, :]
+    small = jnp.where(place[0] == 0, small, pltpu.roll(small, 4, 0))
+    g_channel[...] = small[0:4, 0:54]
+    g_bias[...] = jnp.concatenate([small[k : k + 1, 54:58] for k in range(4)], axis=1)
+
+
+def sum_chips(place, spread, factor):
     shape = jax.ShapeDtypeStruct
     return pl.pallas_call(
         lambda *refs: sum_kernel(factor, *refs),
-        grid=(4,),
-        in_specs=[pl.BlockSpec(memory_space=pltpu.SMEM), pl.BlockSpec((16, 136, 128), lambda t: (t, 0, 0))],
-        out_specs=[whole((4, HID)), whole((16, CH)), whole((54, 4)), whole((4, 4))],
-        out_shape=[shape((4, HID), F32), shape((16, CH), F32), shape((54, 4), F32), shape((4, 4), F32)],
-        scratch_shapes=[pltpu.VMEM((136, 128), F32)],
-        compiler_params=pltpu.CompilerParams(vmem_limit_bytes=VMEM_BYTES),
-        cost_estimate=pl.CostEstimate(flops=1_000_000, bytes_accessed=2_000_000, transcendentals=0),
+        in_specs=[pl.BlockSpec(memory_space=pltpu.SMEM), pl.BlockSpec(memory_space=pltpu.VMEM)],
+        out_shape=[shape((4, HID), F32), shape((16, CH), F32), shape((4, 54), F32), shape((1, 16), F32)],
+        compiler_params=pltpu.CompilerParams(vmem_limit_bytes=16 * 1024 * 1024),
+        cost_estimate=pl.CostEstimate(flops=1_000_000, bytes_accessed=1_000_000, transcendentals=0),
         name="sum_chips",
-    )(core, spread)
-
-
-def features_kernel(d_conv, top, bottom, left, right, cot, taps, out, pad):
-    assemble(pad, d_conv, top, bottom, left, right)
+    )(place, spread)
+
+
+def features_kernel(place, d_conv, row_one, row_two, col_one, col_two, cot, taps, out, pad):
+    assemble(pad, d_conv, row_one, row_two, col_one, col_two, place[1] == 0, place[0] == 0)
 
     def finish(cg, lanes, total):
         columns = slice(8 * cg, 8 * cg + 8)
@@ -334,39 +361,46 @@
     out[...] = (cot[...].astype(F32) + pad[0:ROWS, 0:COLS, :]).astype(BF16)
 
 
-def features_part(d_conv, top, bottom, left, right, cot, taps):
+def features_part(*operands):
     return pl.pallas_call(
         features_kernel,
+        in_specs=[pl.BlockSpec(memory_space=pltpu.SMEM)] + [pl.BlockSpec(memory_space=pltpu.VMEM)] * 7,
         out_shape=jax.ShapeDtypeStruct((ROWS, COLS, CH), BF16),
         scratch_shapes=[pltpu.VMEM(PAD, F32)],
         compiler_params=pltpu.CompilerParams(vmem_limit_bytes=VMEM_BYTES),
         cost_estimate=pl.CostEstimate(flops=30_000_000, bytes_accessed=2_000_000, transcendentals=0),
         name="features_part",
-    )(d_conv, top, bottom, left, right, cot, taps)
-
-
-def shift_by(value, axis, way):
+    )(*operands)
+
+
+def exchange(one, two, axis):
     count = lax.axis_size(axis)
-    pairs = [(i, i + way) for i in range(count) if 0 <= i + way < count]
-    return lax.ppermute(value, axis, pairs)
-
-
-def halo_rows(first, last):
-    return shift_by(last, ROW, 1), shift_by(first, ROW, -1)
-
-
-def halo_sides(top, tile, bottom):
-    tail = [part[:, COLS - 3 :] for part in (top, tile, bottom)]
-    head = [part[:, :3] for part in (top, tile, bottom)]
-    return jnp.concatenate(tail, axis=0), jnp.concatenate(head, axis=0)
-
-
-def halo_cols(tail, head):
-    return shift_by(tail, COL, 1), shift_by(head, COL, -1)
-
-
-def swap(value):
+    met = []
+    for value, start in ((one, 0), (two, 1)):
+        pairs = []
+        for i in range(start, count - 1, 2):
+            pairs += [(i, i + 1), (i + 1, i)]
+        met.append(lax.ppermute(value, axis, pairs))
+    return met
+
+
+def halo_sides(row_one, row_two, tile, even_row, even_col):
+    top = jnp.where(even_row, row_two, row_one)
+    bottom = jnp.where(even_row, row_one, row_two)
+    tail = jnp.concatenate([part[:, COLS - 3 :] for part in (top, tile, bottom)], axis=0)
+    head = jnp.concatenate([part[:, :3] for part in (top, tile, bottom)], axis=0)
+    return jnp.where(even_col, tail, head), jnp.where(even_col, head, tail)
+
+
+def swap_cores(value):
     return lax.ppermute(value, "c", [(0, 1), (1, 0)])
+
+
+def swap_chips(value):
+    pairs = []
+    for x in range(4):
+        pairs += [(2 * x, 2 * (x ^ 1)), (2 * x + 1, 2 * (3 - x) + 1)]
+    return lax.ppermute(value, ("xh", "xl", "c"), pairs)
 
 
 def shards(
@@ -374,38 +408,47 @@
     pw_in_weight, pw_in_bias, pw_out_weight, pw_out_bias, layer_scale,
 ):
     factor = 1.0 / math.sqrt(COUNT * lax.axis_size(EVERY))
-    core = lax.axis_index("c").astype(jnp.int32).reshape(1)
+    core, y_hi, x_lo = (lax.axis_index(name).astype(jnp.int32) for name in ("c", "yh", "xl"))
+    place = jnp.stack([core, y_hi, x_lo])
+    even_row, even_col = y_hi == 0, core == 0
     row = lambda vector: vector.reshape(1, -1)
-    top, bottom = halo_rows(features[:3], features[ROWS - 3 :])
-    left, right = halo_cols(*halo_sides(top, features, bottom))
-    pad, block_rows, d_conv, d_first, d_last, rows, bias, mine_out, theirs_out, mine_in, theirs_in = grads(
-        core, features, top, bottom, left, right, cotangent.reshape(COUNT, CH), dw_kernel, row(dw_bias),
+    ends = features[:3], features[ROWS - 3 :]
+    rows_met = exchange(jnp.where(even_row, ends[1], ends[0]), jnp.where(even_row, ends[0], ends[1]), ROW)
+    cols_met = exchange(*halo_sides(*rows_met, features, even_row, even_col), COL)
+    pad, block_rows, d_conv, d_one, d_two, rows, bias, mine_out, theirs_out, mine_in, theirs_in = grads(
+        place, features, *rows_met, *cols_met, cotangent.reshape(COUNT, CH), dw_kernel, row(dw_bias),
         row(norm_gain_vector), row(norm_bias), row(layer_scale), row(pw_out_bias),
         pw_in_weight, row(pw_in_bias), pw_out_weight,
     )
-    met_out, met_in = swap(theirs_out), swap(theirs_in)
-    d_top, d_bottom = halo_rows(d_first, d_last)
+    met_out, met_in = swap_cores(theirs_out), swap_cores(theirs_in)
+    d_rows = exchange(d_one, d_two, ROW)
+    keep, give = split_pair(place, mine_out, met_out, mine_in, met_in)
+    give, d_rows = lax.optimization_barrier((give, d_rows))
+    given = swap_chips(give)
+    sides = halo_sides(*d_rows, d_conv, even_row, even_col)
+    pad, give, sides = lax.optimization_barrier((pad, give, sides))
+    d_cols = exchange(*sides, COL)
     small = tap_rows(pad, d_conv, rows, bias)
-    met_small = swap(small)
-    tail, head = halo_sides(d_top, d_conv, d_bottom)
-    message = add_pair(mine_out, met_out, mine_in, met_in, small, met_small)
-    message, tail, head = lax.optimization_barrier((message, tail, head))
-    spread = lax.all_to_all(message, CHIPS, 0, 0, tiled=True)
-    d_left, d_right = halo_cols(tail, head)
-    grad_features = features_part(d_conv, d_top, d_bottom, d_left, d_right, cotangent, dw_kernel)
-    grad_in, grad_out, grad_channel, grad_bias = sum_chips(core, spread, factor)
+    small, d_cols = lax.optimization_barrier((small, d_cols))
+    small_keep, small_give = split_small(place, small, swap_cores(small))
+    small_given = swap_chips(small_give)
+    message = add_pair(keep, given, small_keep, small_given)
+    spread = lax.all_to_all(message, GROUP, 0, 0, tiled=True)
+    d_conv, message = lax.optimization_barrier((d_conv, message))
+    grad_features = features_part(place, d_conv, *d_rows, *d_cols, cotangent, dw_kernel)
+    grad_in, grad_out, grad_channel, grad_bias = sum_chips(place, spread, factor)
     return (
         block_rows.reshape(ROWS, COLS, CH),
         grad_features,
         grad_in,
         grad_out,
-        grad_channel,
+        grad_channel.T,
         grad_bias.reshape(-1),
     )
 
 
 def solution(mesh):
-    fine = Mesh(mesh.devices.reshape(4, 2, 4, 2, 2), EVERY)
+    fine = Mesh(mesh.devices.reshape(4, 2, 2, 2, 2, 2), EVERY)
     return jax.shard_map(
         shards,
         mesh=fine,

time: 118 us -> 107 us (0.907)
  the two profiles are of different devices: /device:TPU:62 before, /device:TPU:0 now
where the time goes in v4:
time: 107 us; the launch traced here: 106 us
  starting transfers between devices  40.5 us (38%)
  Pallas kernels  39.9 us (37%)
  waiting for transfers between devices  17.6 us (16%)
  local copies, waits for them, and re-layouts  5.5 us (5%)
  other arithmetic  1.86 us (2%)
    all_to_all x1, starting transfers between devices, shards(): spread = lax.all_to_all(message, GROUP, 0, 0, tiled=True)  15.5 us
    ppermute x8, starting transfers between devices, exchange(): met.append(lax.ppermute(value, axis, pairs))  15.5 us
    pallas_call x1, Pallas kernels, grads(): pl.pallas_call(grads_kernel, grid=(STEPS,), in_specs=[pl.BlockSpec(memory...  14.8 us
    all_to_all x1, waiting for transfers between devices, shards(): spread = lax.all_to_all(message, GROUP, 0, 0, tiled=True)  11.4 us
    pallas_call x1, Pallas kernels, tap_rows(): pl.pallas_call(taps_kernel, out_shape=jax.ShapeDtypeStruct((64, 8, 128),...  7.39 us
    pallas_call x1, Pallas kernels, features_part(): pl.pallas_call(features_kernel, in_specs=[pl.BlockSpec(memory_space=pltpu...  6.59 us
    ppermute x3, starting transfers between devices, swap_cores(): return lax.ppermute(value, 'c', [(0, 1), (1, 0)])  4.88 us
    ppermute x2, starting transfers between devices, swap_chips(): return lax.ppermute(value, ('xh', 'xl', 'c'), pairs)  4.66 us
  transfers between devices with their start and end apart: 14, of which 4 were waited for; matrix products, arithmetic and copies ran while one was open for 2% of the time, Pallas kernels for 19%

profile of v4, /device:TPU:0, one launch (start us, length us, event | category | flops | bytes accessed | tf_op | source)
XLA Modules:
  0.0 106.3 jit_solution(7618587936934537950)
XLA Ops:
  0.6 1.0 broadcast_select_fusion.4
  1.6 3.4 %collective-permute-start = (bf16[3,32,512]{2,1,0:T(8,128)(2,1)S(1)}, bf16[3,32,512]{2,1,0:T(8,128)(2,1)S(1)}, u32[]{:S(2)}, u32[]{:S(2)}) collective-permute-start(bf16[3,32,512]{2,1,0:T(8,128)(2,1)S(1)} %get-tuple-element.69), channel_id=1, source_target_pairs={{0,16},{16,0},{32,48},{48,32},{64,80},{80,64},{96,112},{112,96},{1... | collective-permute-start | bytes 294920 | tf_op jit(solution)/shard_map/ppermute | solution.py:383
  5.0 0.7 collective-permute-start.1
  5.6 0.9 fusion.1
  6.5 1.3 %collective-permute-done.row_one = bf16[3,32,512]{2,1,0:T(8,128)(2,1)S(1)} collective-permute-done((bf16[3,32,512]{2,1,0:T(8,128)(2,1)S(1)}, bf16[3,32,512]{2,1,0:T(8,128)(2,1)S(1)}, u32[]{:S(2)}, u32[]{:S(2)}) %collective-permute-start) | collective-permute-done | bytes 98336 | tf_op jit(solution)/shard_map/ppermute | solution.py:383
  8.1 0.7 collective-permute-start.3
  8.7 0.7 pad_add_fusion.place.refs_0_
  9.4 0.6 copy-done.12
  10.1 14.8 %grads.1 = (f32[14,40,512]{2,1,0:T(8,128)}, bf16[256,512]{1,0:T(8,128)(2,1)}, bf16[8,32,512]{2,1,0:T(8,128)(2,1)}, bf16[3,32,512]{2,1,0:T(8,128)(2,1)}, bf16[3,3...) custom-call(s32[3]{0:T(128)} %pad_add_fusion.place.refs_0_, ...), custom_call_target="tpu_custom_call" | custom-call | flops 3200000000 | bytes 12000000 | tf_op jit(solution)/shard_map/grads/pallas_call | solution.py:168
  24.9 4.7 %collective-permute-start.4 = (bf16[64,64,128]{2,1,0:T(8,128)(2,1)}, bf16[64,64,128]{2,1,0:T(8,128)(2,1)S(1)}, u32[]{:S(2)}, u32[]{:S(2)}) collective-permute-start(bf16[64,64,128]{2,1,0:T(8,128)(2,1)} %get-tuple-element.38), channel_id=1, source_target_pairs={{0,1},{1,0},{2,3},{3,2},{4,5},{5,4},{6,7},{7,6},{8,9},{9,8},{10,11... | collective-permute-start | bytes 3145736 | tf_op jit(solution)/shard_map/ppermute | solution.py:396
  29.7 6.7 %collective-permute-start.6 = (bf16[3,32,512]{2,1,0:T(8,128)(2,1)}, bf16[3,32,512]{2,1,0:T(8,128)(2,1)S(1)}, u32[]{:S(2)}, u32[]{:S(2)}) collective-permute-start(bf16[3,32,512]{2,1,0:T(8,128)(2,1)} %get-tuple-element.43), channel_id=1, source_target_pairs={{0,16},{16,0},{32,48},{48,32},{64,80},{80,64},{96,112},{112,96},{1... | collective-permute-start | bytes 294920 | tf_op jit(solution)/shard_map/ppermute | solution.py:383
  36.4 0.7 collective-permute-start.7
  37.1 0.9 fusion
  38.0 0.9 copy-done.1
  39.0 0.3 copy-done.2
  39.3 4.3 %split_pair.1 = (bf16[32,128,128]{2,1,0:T(8,128)(2,1)}, bf16[32,128,128]{2,1,0:T(8,128)(2,1)}) custom-call(s32[3]{0:T(128)} %pad_add_fusion.place.refs_0_, bf16[64,64,128]{2,1,0:T(8,128)(2,1)} %get-tuple-element.37.out_one, bf16[64,64,128]{2,1,0:T(8,128)(2,1)} %copy-done.1, bf16[64,64,128]{2,1,0:T(8,128)(2,1)} %get-tuple-element.39.in_one, ...), custom_call_target="tpu_custom_call" | custom-call | flops 1000000 | bytes 6000000 | tf_op jit(solution)/shard_map/split_pair/pallas_call | solution.py:275
  43.7 2.5 %collective-permute-start.8 = (bf16[32,128,128]{2,1,0:T(8,128)(2,1)}, bf16[32,128,128]{2,1,0:T(8,128)(2,1)S(1)}, u32[]{:S(2)}, u32[]{:S(2)}) collective-permute-start(bf16[32,128,128]{2,1,0:T(8,128)(2,1)} %get-tuple-element.45), channel_id=1, source_target_pairs={{0,4},{1,13},{4,0},{5,9},{8,12},{9,5},{12,8},{13,1},{2,6},{3,15},{... | collective-permute-start | bytes 3145736 | tf_op jit(solution)/shard_map/ppermute | solution.py:403
  46.3 0.7 collective-permute-start.10
  47.0 2.6 %collective-permute-start.9 = (bf16[14,3,512]{2,1,0:T(4,128)(2,1)S(1)}, bf16[14,3,512]{2,1,0:T(4,128)(2,1)S(1)}, u32[]{:S(2)}, u32[]{:S(2)}) collective-permute-start(bf16[14,3,512]{2,1,0:T(4,128)(2,1)S(1)} %get-tuple-element.52), channel_id=1, source_target_pairs={{0,1},{1,0},{2,3},{3,2},{4,5},{5,4},{6,7},{7,6},{8,9},{9,8},{10,11... | collective-permute-start | bytes 129032 | tf_op jit(solution)/shard_map/ppermute | solution.py:383
  49.6 7.4 %tap_rows.1.one = f32[64,8,128]{2,1,0:T(8,128)} custom-call(f32[14,40,512]{2,1,0:T(8,128)} %get-tuple-element.49.pad, bf16[8,32,512]{2,1,0:T(8,128)(2,1)} %get-tuple-element.57.d_conv, f32[8,512]{1,0:T(8,128)} %get-tuple-element.50.rows, f32[8,512]{1,0:T(8,128)} %get-tuple-element.51.bias), custom_call_target="tpu_custom_call" | custom-call | flops 30000000 | bytes 2000000 | tf_op jit(solution)/shard_map/tap_rows/pallas_call | solution.py:254
  57.2 1.7 %collective-permute-done.11.two = f32[64,8,128]{2,1,0:T(8,128)S(1)} collective-permute-done((f32[64,8,128]{2,1,0:T(8,128)}, f32[64,8,128]{2,1,0:T(8,128)S(1)}, u32[]{:S(2)}, u32[]{:S(2)}) %collective-permute-start.11) | collective-permute-done | bytes 262176 | tf_op jit(solution)/shard_map/ppermute | solution.py:396
  58.9 0.7 copy-done.6
  59.6 1.8 %split_small.1 = (f32[32,8,128]{2,1,0:T(8,128)}, f32[32,8,128]{2,1,0:T(8,128)}) custom-call(s32[3]{0:T(128)} %pad_add_fusion.place.refs_0_, f32[64,8,128]{2,1,0:T(8,128)} %tap_rows.1.one, f32[64,8,128]{2,1,0:T(8,128)} %copy-done.6), custom_call_target="tpu_custom_call" | custom-call | flops 100000 | bytes 700000 | tf_op jit(solution)/shard_map/split_small/pallas_call | solution.py:295
  61.4 2.2 %collective-permute-start.12 = (f32[32,8,128]{2,1,0:T(8,128)}, f32[32,8,128]{2,1,0:T(8,128)S(1)}, u32[]{:S(2)}, u32[]{:S(2)}) collective-permute-start(f32[32,8,128]{2,1,0:T(8,128)} %get-tuple-element.56), channel_id=1, source_target_pairs={{0,4},{1,13},{4,0},{5,9},{8,12},{9,5},{12,8},{13,1},{2,6},{3,15},{... | collective-permute-start | bytes 393224 | tf_op jit(solution)/shard_map/ppermute | solution.py:403
  63.5 3.2 %collective-permute-done.12.small_two = f32[32,8,128]{2,1,0:T(8,128)S(1)} collective-permute-done((f32[32,8,128]{2,1,0:T(8,128)}, f32[32,8,128]{2,1,0:T(8,128)S(1)}, u32[]{:S(2)}, u32[]{:S(2)}) %collective-permute-start.12) | collective-permute-done | bytes 131104 | tf_op jit(solution)/shard_map/ppermute | solution.py:403
  66.7 0.6 copy-done.7
  67.3 0.4 copy-done.3
  67.7 3.6 %add_pair.1 = bf16[32,136,128]{2,1,0:T(8,128)(2,1)} custom-call(bf16[32,128,128]{2,1,0:T(8,128)(2,1)} %get-tuple-element.41.one, bf16[32,128,128]{2,1,0:T(8,128)(2,1)} %copy-done.3, f32[32,8,128]{2,1,0:T(8,128)} %get-tuple-element.55.small_one, f32[32,8,128]{2,1,0:T(8,128)} %copy-done.7), custom_call_target="tpu_custom_call" | custom-call | flops 1000000 | bytes 3000000 | tf_op jit(solution)/shard_map/add_pair/pallas_call | solution.py:313
  71.4 15.5 %all-to-all-start = ((bf16[32,136,128]{2,1,0:T(8,128)(2,1)}), bf16[32,136,128]{2,1,0:T(8,128)(2,1)S(1)}, u32[]{:S(2)}, u32[]{:S(2)}) async-start(bf16[32,136,128]{2,1,0:T(8,128)(2,1)} %add_pair.1), calls=%async_computation | async-start | bytes 2228224 | tf_op jit(solution)/shard_map/all_to_all | solution.py:436
  86.9 6.6 %features_part.1 = bf16[8,32,512]{2,1,0:T(8,128)(2,1)} custom-call(s32[3]{0:T(128)} %pad_add_fusion.place.refs_0_, bf16[8,32,512]{2,1,0:T(8,128)(2,1)} %get-tuple-element.57.d_conv, bf16[3,32,512]{2,1,0:T(8,128)(2,1)} %copy-done.4, bf16[3,32,512]{2,1,0:T(8,128)(2,1)} %copy-done.5, bf16[14,3,512]{2,1,0:T(4,128)(2,1)} %copy-done.11, ...), custom_call_target="tpu_custom_call" | custom-call | flops 30000000 | bytes 2000000 | tf_op jit(solution)/shard_map/features_part/pallas_call | solution.py:365
  93.5 11.4 %all-to-all-done.refs_1_ = bf16[32,136,128]{2,1,0:T(8,128)(2,1)S(1)} async-done(((bf16[32,136,128]{2,1,0:T(8,128)(2,1)}), bf16[32,136,128]{2,1,0:T(8,128)(2,1)S(1)}, u32[]{:S(2)}, u32[]{:S(2)}) %all-to-all-start) | async-done | bytes 1114144 | tf_op jit(solution)/shard_map/all_to_all | solution.py:436
  104.9 1.4 %sum_chips.1 = (f32[4,2048]{1,0:T(4,128)}, f32[16,512]{1,0:T(8,128)}, f32[4,54]{1,0:T(4,128)}, f32[1,16]{1,0:T(1,128)}) custom-call(s32[3]{0:T(128)S(1)} %copy-done, bf16[32,136,128]{2,1,0:T(8,128)(2,1)S(1)} %all-to-all-done.refs_1_), custom_call_target="tpu_custom_call" | custom-call | flops 1000000 | bytes 1000000 | tf_op jit(solution)/shard_map/sum_chips/pallas_call | solution.py:343
  (42 shorter events, 0.7 us)
Async XLA Ops:
  1.6 6.2 %collective-permute-start = (bf16[3,32,512]{2,1,0:T(8,128)(2,1)S(1)}, bf16[3,32,512]{2,1,0:T(8,128)(2,1)S(1)}, u32[]{:S(2)}, u32[]{:S(2)}) collective-permute-start(bf16[3,32,512]{2,1,0:T(8,128)(2,1)S(1)} %get-tuple-element.69), channel_id=1, source_target_pairs={{0,16},{16,0},{32,48},{48,32},{64,80},{80,64},{96,112},{112,96},{1... | collective-permute-start | bytes 294920 | tf_op jit(solution)/shard_map/ppermute | solution.py:383
  5.0 2.8 %collective-permute-start.1 = (bf16[3,32,512]{2,1,0:T(8,128)(2,1)S(1)}, bf16[3,32,512]{2,1,0:T(8,128)(2,1)S(1)}, u32[]{:S(2)}, u32[]{:S(2)}) collective-permute-start(bf16[3,32,512]{2,1,0:T(8,128)(2,1)S(1)} %get-tuple-element.68), channel_id=1, source_target_pairs={{16,32},{32,16},{48,64},{64,48},{80,96},{96,80},{17,33},{33,17},{4... | collective-permute-start | bytes 294920 | tf_op jit(solution)/shard_map/ppermute | solution.py:383
  7.8 1.6 %copy-start.8 = (bf16[3,32,512]{2,1,0:T(8,128)(2,1)}, bf16[3,32,512]{2,1,0:T(8,128)(2,1)S(1)}, u32[]{:S(2)}) copy-start(bf16[3,32,512]{2,1,0:T(8,128)(2,1)S(1)} %collective-permute-done.row_one) | copy-start | bytes 294916
  7.8 1.6 %copy-start.9 = (bf16[3,32,512]{2,1,0:T(8,128)(2,1)}, bf16[3,32,512]{2,1,0:T(8,128)(2,1)S(1)}, u32[]{:S(2)}) copy-start(bf16[3,32,512]{2,1,0:T(8,128)(2,1)S(1)} %collective-permute-done.1.row_two) | copy-start | bytes 294916
  8.0 1.4 %collective-permute-start.2 = (bf16[14,3,512]{2,1,0:T(4,128)(2,1)S(1)}, bf16[14,3,512]{2,1,0:T(4,128)(2,1)S(1)}, u32[]{:S(2)}, u32[]{:S(2)}) collective-permute-start(bf16[14,3,512]{2,1,0:T(4,128)(2,1)S(1)} %get-tuple-element.77), channel_id=1, source_target_pairs={{0,1},{1,0},{2,3},{3,2},{4,5},{5,4},{6,7},{7,6},{8,9},{9,8},{10,11... | collective-permute-start | bytes 129032 | tf_op jit(solution)/shard_map/ppermute | solution.py:383
  8.1 1.3 %collective-permute-start.3 = (bf16[14,3,512]{2,1,0:T(4,128)(2,1)S(1)}, bf16[14,3,512]{2,1,0:T(4,128)(2,1)S(1)}, u32[]{:S(2)}, u32[]{:S(2)}) collective-permute-start(bf16[14,3,512]{2,1,0:T(4,128)(2,1)S(1)} %get-tuple-element.76), channel_id=1, source_target_pairs={{1,2},{2,1},{3,4},{4,3},{5,6},{6,5},{7,8},{8,7},{9,10},{10,9},{11,... | collective-permute-start | bytes 129032 | tf_op jit(solution)/shard_map/ppermute | solution.py:383
  9.4 0.6 copy-start.12
  9.4 0.7 copy-start.13
  24.9 13.1 %collective-permute-start.4 = (bf16[64,64,128]{2,1,0:T(8,128)(2,1)}, bf16[64,64,128]{2,1,0:T(8,128)(2,1)S(1)}, u32[]{:S(2)}, u32[]{:S(2)}) collective-permute-start(bf16[64,64,128]{2,1,0:T(8,128)(2,1)} %get-tuple-element.38), channel_id=1, source_target_pairs={{0,1},{1,0},{2,3},{3,2},{4,5},{5,4},{6,7},{7,6},{8,9},{9,8},{10,11... | collective-permute-start | bytes 3145736 | tf_op jit(solution)/shard_map/ppermute | solution.py:396
  29.6 8.4 %collective-permute-start.5 = (bf16[64,64,128]{2,1,0:T(8,128)(2,1)}, bf16[64,64,128]{2,1,0:T(8,128)(2,1)S(1)}, u32[]{:S(2)}, u32[]{:S(2)}) collective-permute-start(bf16[64,64,128]{2,1,0:T(8,128)(2,1)} %get-tuple-element.40), channel_id=1, source_target_pairs={{0,1},{1,0},{2,3},{3,2},{4,5},{5,4},{6,7},{7,6},{8,9},{9,8},{10,11... | collective-permute-start | bytes 3145736 | tf_op jit(solution)/shard_map/ppermute | solution.py:396
  29.7 13.9 %collective-permute-start.6 = (bf16[3,32,512]{2,1,0:T(8,128)(2,1)}, bf16[3,32,512]{2,1,0:T(8,128)(2,1)S(1)}, u32[]{:S(2)}, u32[]{:S(2)}) collective-permute-start(bf16[3,32,512]{2,1,0:T(8,128)(2,1)} %get-tuple-element.43), channel_id=1, source_target_pairs={{0,16},{16,0},{32,48},{48,32},{64,80},{80,64},{96,112},{112,96},{1... | collective-permute-start | bytes 294920 | tf_op jit(solution)/shard_map/ppermute | solution.py:383
  36.4 7.2 %collective-permute-start.7 = (bf16[3,32,512]{2,1,0:T(8,128)(2,1)}, bf16[3,32,512]{2,1,0:T(8,128)(2,1)S(1)}, u32[]{:S(2)}, u32[]{:S(2)}) collective-permute-start(bf16[3,32,512]{2,1,0:T(8,128)(2,1)} %get-tuple-element.44), channel_id=1, source_target_pairs={{16,32},{32,16},{48,64},{64,48},{80,96},{96,80},{17,33},{33,17},{4... | collective-permute-start | bytes 294920 | tf_op jit(solution)/shard_map/ppermute | solution.py:383
  38.0 1.0 copy-start.1
  38.0 1.3 %copy-start.2 = (bf16[64,64,128]{2,1,0:T(8,128)(2,1)}, bf16[64,64,128]{2,1,0:T(8,128)(2,1)S(1)}, u32[]{:S(2)}) copy-start(bf16[64,64,128]{2,1,0:T(8,128)(2,1)S(1)} %collective-permute-done.5.in_two) | copy-start | bytes 3145732
  43.6 13.4 %copy-start.4 = (bf16[3,32,512]{2,1,0:T(8,128)(2,1)}, bf16[3,32,512]{2,1,0:T(8,128)(2,1)S(1)}, u32[]{:S(2)}) copy-start(bf16[3,32,512]{2,1,0:T(8,128)(2,1)S(1)} %collective-permute-done.6.row_one) | copy-start | bytes 294916
  43.7 13.4 %copy-start.5 = (bf16[3,32,512]{2,1,0:T(8,128)(2,1)}, bf16[3,32,512]{2,1,0:T(8,128)(2,1)S(1)}, u32[]{:S(2)}) copy-start(bf16[3,32,512]{2,1,0:T(8,128)(2,1)S(1)} %collective-permute-done.7.row_two) | copy-start | bytes 294916
  43.7 23.0 %collective-permute-start.8 = (bf16[32,128,128]{2,1,0:T(8,128)(2,1)}, bf16[32,128,128]{2,1,0:T(8,128)(2,1)S(1)}, u32[]{:S(2)}, u32[]{:S(2)}) collective-permute-start(bf16[32,128,128]{2,1,0:T(8,128)(2,1)} %get-tuple-element.45), channel_id=1, source_target_pairs={{0,4},{1,13},{4,0},{5,9},{8,12},{9,5},{12,8},{13,1},{2,6},{3,15},{... | collective-permute-start | bytes 3145736 | tf_op jit(solution)/shard_map/ppermute | solution.py:403
  46.3 10.7 %collective-permute-start.10 = (bf16[14,3,512]{2,1,0:T(4,128)(2,1)S(1)}, bf16[14,3,512]{2,1,0:T(4,128)(2,1)S(1)}, u32[]{:S(2)}, u32[]{:S(2)}) collective-permute-start(bf16[14,3,512]{2,1,0:T(4,128)(2,1)S(1)} %get-tuple-element.53), channel_id=1, source_target_pairs={{1,2},{2,1},{3,4},{4,3},{5,6},{6,5},{7,8},{8,7},{9,10},{10,9},{11,... | collective-permute-start | bytes 129032 | tf_op jit(solution)/shard_map/ppermute | solution.py:383
  47.0 10.1 %collective-permute-start.9 = (bf16[14,3,512]{2,1,0:T(4,128)(2,1)S(1)}, bf16[14,3,512]{2,1,0:T(4,128)(2,1)S(1)}, u32[]{:S(2)}, u32[]{:S(2)}) collective-permute-start(bf16[14,3,512]{2,1,0:T(4,128)(2,1)S(1)} %get-tuple-element.52), channel_id=1, source_target_pairs={{0,1},{1,0},{2,3},{3,2},{4,5},{5,4},{6,7},{7,6},{8,9},{9,8},{10,11... | collective-permute-start | bytes 129032 | tf_op jit(solution)/shard_map/ppermute | solution.py:383
  57.0 29.9 %copy-start.10 = (bf16[14,3,512]{2,1,0:T(4,128)(2,1)}, bf16[14,3,512]{2,1,0:T(4,128)(2,1)S(1)}, u32[]{:S(2)}) copy-start(bf16[14,3,512]{2,1,0:T(4,128)(2,1)S(1)} %collective-permute-done.10.col_two) | copy-start | bytes 129028
  57.1 29.8 %copy-start.11 = (bf16[14,3,512]{2,1,0:T(4,128)(2,1)}, bf16[14,3,512]{2,1,0:T(4,128)(2,1)S(1)}, u32[]{:S(2)}) copy-start(bf16[14,3,512]{2,1,0:T(4,128)(2,1)S(1)} %collective-permute-done.9.col_one) | copy-start | bytes 129028
  57.1 1.8 %collective-permute-start.11 = (f32[64,8,128]{2,1,0:T(8,128)}, f32[64,8,128]{2,1,0:T(8,128)S(1)}, u32[]{:S(2)}, u32[]{:S(2)}) collective-permute-start(f32[64,8,128]{2,1,0:T(8,128)} %tap_rows.1.one), channel_id=1, source_target_pairs={{0,1},{1,0},{2,3},{3,2},{4,5},{5,4},{6,7},{7,6},{8,9},{9,8},{10,11... | collective-permute-start | bytes 786440 | tf_op jit(solution)/shard_map/ppermute | solution.py:396
  58.9 0.7 copy-start.6
  61.4 5.3 %collective-permute-start.12 = (f32[32,8,128]{2,1,0:T(8,128)}, f32[32,8,128]{2,1,0:T(8,128)S(1)}, u32[]{:S(2)}, u32[]{:S(2)}) collective-permute-start(f32[32,8,128]{2,1,0:T(8,128)} %get-tuple-element.56), channel_id=1, source_target_pairs={{0,4},{1,13},{4,0},{5,9},{8,12},{9,5},{12,8},{13,1},{2,6},{3,15},{... | collective-permute-start | bytes 393224 | tf_op jit(solution)/shard_map/ppermute | solution.py:403
  66.7 0.7 copy-start.7
  66.7 1.0 copy-start.3
  71.4 33.6 %all-to-all-start = ((bf16[32,136,128]{2,1,0:T(8,128)(2,1)}), bf16[32,136,128]{2,1,0:T(8,128)(2,1)S(1)}, u32[]{:S(2)}, u32[]{:S(2)}) async-start(bf16[32,136,128]{2,1,0:T(8,128)(2,1)} %add_pair.1), calls=%async_computation | async-start | bytes 2228224 | tf_op jit(solution)/shard_map/all_to_all | solution.py:436
  86.9 18.0 %copy-start = (s32[3]{0:T(128)S(1)}, s32[3]{0:T(128)}, u32[]{:S(2)}) copy-start(s32[3]{0:T(128)} %pad_add_fusion.place.refs_0_) | copy-start | bytes 40

commit v5 on v4

v5 whole, which is shorter than its diff:
```python
import math

import jax
import jax.numpy as jnp
from jax import lax
from jax.experimental import pallas as pl
from jax.experimental.pallas import tpu as pltpu
from jax.sharding import Mesh
from jax.sharding import PartitionSpec as P

EVERY = ("z", "yh", "xh", "xl", "yl", "c")
ROW = ("z", "yh")
COL = ("xh", "xl", "yl", "c")
GROUP = ("z", "yh", "xh", "yl")
ROWS, COLS, CH, HID, CHUNK = 8, 32, 512, 2048, 512
COUNT = ROWS * COLS
STEPS = HID // CHUNK
BLOCKS = CH // 128
PAD = (BLOCKS, ROWS + 6, COLS + 8, 128)
TILE = (BLOCKS, ROWS, COLS, 128)
F32, BF16 = jnp.float32, jnp.bfloat16
VMEM_BYTES = 28 * 1024 * 1024


def dot_nn(left, right):
    return lax.dot_general(left, right, (((1,), (0,)), ((), ())), preferred_element_type=F32)


def dot_nt(left, right):
    return lax.dot_general(left, right, (((1,), (1,)), ((), ())), preferred_element_type=F32)


def dot_tn(left, right):
    return lax.dot_general(left, right, (((0,), (0,)), ((), ())), preferred_element_type=F32)


def params(vmem=VMEM_BYTES):
    return pltpu.CompilerParams(vmem_limit_bytes=vmem)


def cost(flops, moved):
    return pl.CostEstimate(flops=flops, bytes_accessed=moved, transcendentals=0)


def near(value):
    return pltpu.with_memory_space_constraint(value, pltpu.VMEM)


SCALARS = pl.BlockSpec(memory_space=pltpu.SMEM)
WHOLE = pl.BlockSpec(memory_space=pltpu.VMEM)


def fetch_kernel(count, *refs):
    sources, targets, sem = refs[:count], refs[count : 2 * count], refs[2 * count]
    copies = [pltpu.make_async_copy(sources[k], targets[k], sem.at[k]) for k in range(count)]
    for copy in copies:
        copy.start()
    for copy in copies:
        copy.wait()


def fetch(*arrays):
    count = len(arrays)
    return pl.pallas_call(
        lambda *refs: fetch_kernel(count, *refs),
        in_specs=[pl.BlockSpec(memory_space=pl.ANY)] * count,
        out_specs=[WHOLE] * count,
        out_shape=[pltpu.VMEM(array.shape, array.dtype) for array in arrays],
        scratch_shapes=[pltpu.SemaphoreType.DMA((count,))],
        compiler_params=params(),
        cost_estimate=cost(0, 5_000_000),
        name="fetch",
    )(*arrays)


def assemble(pad, tile, row_one, row_two, col_one, col_two, even_row, even_col):
    for k in range(BLOCKS):
        lanes = slice(128 * k, 128 * k + 128)
        rows = row_one[:, :, lanes].astype(F32), row_two[:, :, lanes].astype(F32)
        cols = col_one[:, :, lanes].astype(F32), col_two[:, :, lanes].astype(F32)
        pad[k, 0:3, 3 : 3 + COLS, :] = jnp.where(even_row, rows[1], rows[0])
        pad[k, 3 : 3 + ROWS, 3 : 3 + COLS, :] = tile[:, :, lanes].astype(F32)
        pad[k, 3 + ROWS : 6 + ROWS, 3 : 3 + COLS, :] = jnp.where(even_row, rows[0], rows[1])
        pad[k, :, 0:3, :] = jnp.where(even_col, cols[1], cols[0])
        pad[k, :, 3 + COLS : 6 + COLS, :] = jnp.where(even_col, cols[0], cols[1])


def lanes_of(block):
    return pl.ds(pl.multiple_of(block * 128, 128), 128)


def depthwise(pad, taps, out, flip):
    def block(cb, carry):
        lanes = lanes_of(cb)
        for cg in range(COLS // 8):
            total = jnp.zeros((ROWS, 8, 128), F32)
            for s in range(7):
                band = pad[cb, :, 8 * cg + s : 8 * cg + s + 8, :]
                for r in range(7):
                    tap = 7 * (6 - r) + 6 - s if flip else 7 * r + s
                    total = total + band[r : r + ROWS] * taps[tap : tap + 1, lanes].reshape(1, 1, 128)
            out[cb, :, 8 * cg : 8 * cg + 8, :] = total
        return carry

    lax.fori_loop(0, BLOCKS, block, 0)


def grads_kernel(
    place, tile, row_one, row_two, col_one, col_two, cot, taps, vectors, w_in, b_in, w_out,
    pad, block_out, d_conv, d_row_one, d_row_two, rows_out, mine_out, theirs_out, mine_in, theirs_in,
    conv,
):
    first = place[0] == 0
    even_row = place[1] == 0
    assemble(pad, tile, row_one, row_two, col_one, col_two, even_row, first)
    depthwise(pad, taps, conv, False)
    dw_bias, gain, shift, scale, b_out = (vectors[k : k + 1, :] for k in range(5))
    rows = jnp.concatenate([conv[k].reshape(COUNT, 128) for k in range(BLOCKS)], axis=1) + dw_bias
    centred = rows - jnp.mean(rows, axis=-1, keepdims=True)
    inverse = lax.rsqrt(jnp.mean(centred * centred, axis=-1, keepdims=True) + 1e-06)
    hat = centred * inverse
    normed = (hat * gain + shift).astype(BF16)
    d_branch = (cot[...].astype(F32) * scale).astype(BF16)
    branch = b_out
    d_normed = 0.0

    fourth = lax.broadcasted_iota(jnp.int32, (8, CHUNK), 1) % 4
    fourth = fourth == lax.broadcasted_iota(jnp.int32, (8, CHUNK), 0)
    pick = lax.broadcasted_iota(jnp.int32, (CHUNK, 128), 0) // 4
    pick = (pick == lax.broadcasted_iota(jnp.int32, (CHUNK, 128), 1)).astype(F32).astype(BF16)
    upper = lax.broadcasted_iota(jnp.int32, (64, 8, 128), 1) < 4

    def by_lanes(part):
        return jnp.concatenate([part[:, :, 128 * k : 128 * k + 128] for k in range(BLOCKS)], axis=1)

    for step in range(STEPS):
        hidden = slice(CHUNK * step, CHUNK * step + CHUNK)
        pre_act = dot_nn(normed, w_in[:, hidden]) + b_in[:, hidden]
        cumul = 0.5 * (1.0 + lax.erf(pre_act * 0.7071067811865476))
        act = (pre_act * cumul).astype(BF16)
        slope = cumul + pre_act * jnp.exp(-0.5 * pre_act * pre_act) * 0.3989422804014327
        d_pre = (dot_nt(d_branch, w_out[hidden, :]) * slope).astype(BF16)
        branch = branch + dot_nn(act, w_out[hidden, :])
        d_normed = d_normed + dot_nt(d_pre, w_in[:, hidden])

        bias = jnp.sum(d_pre.astype(F32), axis=0, keepdims=True)
        rows_out[8:16, 128 * step : 128 * step + 128] = dot_nn(jnp.where(fourth, bias, 0.0).astype(BF16), pick)

        term = dot_tn(act, d_branch).reshape(CHUNK // 32, 2, 16, CH)
        chips = slice(CHUNK // 32 * step, CHUNK // 32 * (step + 1))
        mine_out[chips] = by_lanes(jnp.where(first, term[:, 0], term[:, 1])).astype(BF16)
        theirs_out[chips] = by_lanes(jnp.where(first, term[:, 1], term[:, 0])).astype(BF16)

        term = dot_tn(normed, d_pre).reshape(64, 8, CHUNK)
        kept, given = [], []
        for k in range(2):
            low = term[:, :, 128 * k : 128 * k + 128]
            high = term[:, :, 256 + 128 * k : 384 + 128 * k]
            zero = jnp.where(upper, low, pltpu.roll(high, 4, 1))
            one = jnp.where(upper, pltpu.roll(low, 4, 1), high)
            kept.append(jnp.where(first, zero, one))
            given.append(jnp.where(first, one, zero))
        mine_in[:, 16 * step : 16 * step + 16, :] = jnp.concatenate(kept, axis=1).astype(BF16)
        theirs_in[:, 16 * step : 16 * step + 16, :] = jnp.concatenate(given, axis=1).astype(BF16)

    d_hat = d_normed * gain
    grad = inverse * (
        d_hat
        - jnp.mean(d_hat, axis=-1, keepdims=True)
        - hat * jnp.mean(d_hat * hat, axis=-1, keepdims=True)
    )
    grad = grad.astype(BF16)
    out = grad.reshape(ROWS, COLS, CH)
    d_conv[...] = out
    d_row_one[...] = jnp.where(even_row, out[ROWS - 3 :], out[:3])
    d_row_two[...] = jnp.where(even_row, out[:3], out[ROWS - 3 :])
    block_out[...] = (tile[...].reshape(COUNT, CH).astype(F32) + scale * branch).astype(BF16)
    rows_out[0:1, :] = jnp.sum(grad.astype(F32), axis=0, keepdims=True)
    rows_out[1:2, :] = jnp.sum(d_normed * hat, axis=0, keepdims=True)
    rows_out[2:3, :] = jnp.sum(d_normed, axis=0, keepdims=True)
    rows_out[3:4, :] = jnp.sum(d_branch.astype(F32), axis=0, keepdims=True)
    rows_out[4:5, :] = jnp.sum(cot[...].astype(F32) * branch, axis=0, keepdims=True)


def grads(place, *operands):
    half = (64, 64, 128)
    return pl.pallas_call(
        grads_kernel,
        in_specs=[SCALARS] + [WHOLE] * len(operands),
        out_shape=[
            pltpu.VMEM(PAD, F32),
            jax.ShapeDtypeStruct((COUNT, CH), BF16),
            pltpu.VMEM((ROWS, COLS, CH), BF16),
            pltpu.VMEM((3, COLS, CH), BF16),
            pltpu.VMEM((3, COLS, CH), BF16),
            pltpu.VMEM((16, CH), F32),
            pltpu.VMEM(half, BF16),
            pltpu.VMEM(half, BF16),
            pltpu.VMEM(half, BF16),
            pltpu.VMEM(half, BF16),
        ],
        scratch_shapes=[pltpu.VMEM(TILE, F32)],
        compiler_params=params(),
        cost_estimate=cost(3_200_000_000, 12_000_000),
        name="grads",
    )(place, *(near(value) for value in operands))


def taps_kernel(place, pad, d_conv, rows, keep, give, d_tile, table):
    for k in range(BLOCKS):
        d_tile[k] = d_conv[:, :, 128 * k : 128 * k + 128].astype(F32)
    table[48:128, :] = jnp.zeros((80, CH), F32)

    def block(cb, carry):
        lanes = lanes_of(cb)
        for s in range(7):
            totals = [jnp.zeros((8, 128), F32) for _ in range(7)]
            for cg in range(COLS // 8):
                band = pad[cb, :, 8 * cg + s : 8 * cg + s + 8, :]
                own = d_tile[cb, :, 8 * cg : 8 * cg + 8, :]
                for r in range(7):
                    totals[r] = totals[r] + jnp.sum(band[r : r + ROWS] * own, axis=0)
            for r in range(7):
                table[7 * r + s : 7 * r + s + 1, lanes] = jnp.sum(totals[r], axis=0, keepdims=True)
        return carry

    lax.fori_loop(0, BLOCKS, block, 0)
    table[49:54, :] = rows[0:5, :]
    table[54:58, :] = rows[8:12, :]
    turned = table[...].T.reshape(16, 2, 2, 8, 128)
    even = place[2] == 0
    keep[...] = jnp.where(even, turned[:, 0], turned[:, 1]).reshape(32, 8, 128).astype(BF16)
    give[...] = jnp.where(even, turned[:, 1], turned[:, 0]).reshape(32, 8, 128).astype(BF16)


def tap_rows(place, *operands):
    return pl.pallas_call(
        taps_kernel,
        in_specs=[SCALARS] + [WHOLE] * len(operands),
        out_shape=[pltpu.VMEM((32, 8, 128), BF16)] * 2,
        scratch_shapes=[pltpu.VMEM(TILE, F32), pltpu.VMEM((128, CH), F32)],
        compiler_params=params(),
        cost_estimate=cost(30_000_000, 2_000_000),
        name="tap_rows",
    )(place, *(near(value) for value in operands))


def split_kernel(place, out_one, out_two, in_one, in_two, keep, give):
    even = place[2] == 0
    for at, one, two in ((0, out_one, out_two), (64, in_one, in_two)):
        for k in range(16):
            total = [(one[4 * k + 2 * p : 4 * k + 2 * p + 2] + two[4 * k + 2 * p : 4 * k + 2 * p + 2]) for p in range(2)]
            keep[2 * k : 2 * k + 2, at : at + 64, :] = jnp.where(even, total[0], total[1])
            give[2 * k : 2 * k + 2, at : at + 64, :] = jnp.where(even, total[1], total[0])


def split_pair(place, *operands):
    return pl.pallas_call(
        split_kernel,
        in_specs=[SCALARS] + [WHOLE] * len(operands),
        out_shape=[pltpu.VMEM((32, 128, 128), BF16)] * 2,
        compiler_params=params(),
        cost_estimate=cost(1_000_000, 6_000_000),
        name="split_pair",
    )(place, *(near(value) for value in operands))


def add_kernel(one, two, small_one, small_two, small_three, small_four, total):
    total[:, 0:128, :] = one[...] + two[...]
    small = small_one[...].astype(F32) + small_two[...].astype(F32)
    small = small + small_three[...].astype(F32) + small_four[...].astype(F32)
    total[:, 128:136, :] = small.astype(BF16)


def add_pair(*operands):
    return pl.pallas_call(
        add_kernel,
        in_specs=[WHOLE] * len(operands),
        out_shape=jax.ShapeDtypeStruct((32, 136, 128), BF16),
        compiler_params=params(),
        cost_estimate=cost(1_000_000, 3_000_000),
        name="add_pair",
    )(*(near(value) for value in operands))


def sum_kernel(factor, place, spread, g_in, g_out, g_channel, g_bias):
    total = jnp.sum(spread[...].astype(F32), axis=0) * factor
    for k in range(4):
        g_out[:, 128 * k : 128 * k + 128] = total[16 * k : 16 * k + 16, :]
    for t in range(STEPS):
        for k in range(2):
            own = total[64 + 16 * t + 8 * k : 72 + 16 * t + 8 * k, :]
            at = CHUNK * t + 128 * k
            g_in[:, at : at + 128] = own[0:4]
            g_in[:, at + 256 : at + 384] = own[4:8]
    small = total[128:136, :]
    small = jnp.where(place[0] == 0, small, pltpu.roll(small, 4, 0))
    g_channel[...] = small[0:4, 0:54]
    g_bias[...] = jnp.concatenate([small[k : k + 1, 54:58] for k in range(4)], axis=1)


def sum_chips(place, spread, factor):
    shape = jax.ShapeDtypeStruct
    return pl.pallas_call(
        lambda *refs: sum_kernel(factor, *refs),
        in_specs=[pl.BlockSpec(memory_space=pltpu.SMEM), pl.BlockSpec(memory_space=pltpu.VMEM)],
        out_shape=[shape((4, HID), F32), shape((16, CH), F32), shape((4, 54), F32), shape((1, 16), F32)],
        compiler_params=pltpu.CompilerParams(vmem_limit_bytes=16 * 1024 * 1024),
        cost_estimate=pl.CostEstimate(flops=1_000_000, bytes_accessed=1_000_000, transcendentals=0),
        name="sum_chips",
    )(place, spread)


def features_kernel(place, d_conv, row_one, row_two, col_one, col_two, cot, taps, out, pad, total):
    assemble(pad, d_conv, row_one, row_two, col_one, col_two, place[1] == 0, place[0] == 0)
    depthwise(pad, taps, total, True)
    cot_wide = cot[...].astype(F32).reshape(ROWS, COLS, CH)
    for k in range(BLOCKS):
        lanes = slice(128 * k, 128 * k + 128)
        out[:, :, lanes] = (cot_wide[:, :, lanes] + total[k]).astype(BF16)


def features_part(place, *operands):
    return pl.pallas_call(
        features_kernel,
        in_specs=[SCALARS] + [WHOLE] * len(operands),
        out_shape=jax.ShapeDtypeStruct((ROWS, COLS, CH), BF16),
        scratch_shapes=[pltpu.VMEM(PAD, F32), pltpu.VMEM(TILE, F32)],
        compiler_params=params(),
        cost_estimate=cost(30_000_000, 2_000_000),
        name="features_part",
    )(place, *(near(value) for value in operands))


def exchange(one, two, axis):
    count = lax.axis_size(axis)
    met = []
    for value, start in ((one, 0), (two, 1)):
        pairs = []
        for i in range(start, count - 1, 2):
            pairs += [(i, i + 1), (i + 1, i)]
        met.append(lax.ppermute(value, axis, pairs))
    return met


def halo_sides(row_one, row_two, tile, even_row, even_col):
    top = jnp.where(even_row, row_two, row_one)
    bottom = jnp.where(even_row, row_one, row_two)
    tail = jnp.concatenate([part[:, COLS - 3 :] for part in (top, tile, bottom)], axis=0)
    head = jnp.concatenate([part[:, :3] for part in (top, tile, bottom)], axis=0)
    return jnp.where(even_col, tail, head), jnp.where(even_col, head, tail)


def swap_cores(value):
    return lax.ppermute(value, "c", [(0, 1), (1, 0)])


def swap_chips(value):
    pairs = []
    for x in range(4):
        pairs += [(2 * x, 2 * (x ^ 1)), (2 * x + 1, 2 * (3 - x) + 1)]
    return lax.ppermute(value, ("xh", "xl", "c"), pairs)


def swap_across(value):
    pairs = []
    for x in range(4):
        pairs += [(2 * x, 2 * (3 - x) + 1), (2 * x + 1, 2 * (x ^ 1))]
    return lax.ppermute(value, ("xh", "xl", "c"), pairs)


def shards(
    features, cotangent, dw_kernel, dw_bias, norm_gain_vector, norm_bias,
    pw_in_weight, pw_in_bias, pw_out_weight, pw_out_bias, layer_scale,
):
    factor = 1.0 / math.sqrt(COUNT * lax.axis_size(EVERY))
    core, y_hi, x_lo = (lax.axis_index(name).astype(jnp.int32) for name in ("c", "yh", "xl"))
    place = jnp.stack([core, y_hi, x_lo])
    even_row, even_col = y_hi == 0, core == 0
    vectors = jnp.stack([dw_bias, norm_gain_vector, norm_bias, layer_scale, pw_out_bias])
    ends = features[:3], features[ROWS - 3 :]
    rows_met = exchange(jnp.where(even_row, ends[1], ends[0]), jnp.where(even_row, ends[0], ends[1]), ROW)
    tile, cot, taps, vectors, w_in, b_in, w_out = fetch(
        features, cotangent.reshape(COUNT, CH), dw_kernel, vectors, pw_in_weight,
        pw_in_bias.reshape(1, HID), pw_out_weight,
    )
    sides = halo_sides(*rows_met, features, even_row, even_col)
    sides, w_in = lax.optimization_barrier((sides, w_in))
    cols_met = exchange(*sides, COL)
    pad, block_rows, d_conv, d_one, d_two, rows, mine_out, theirs_out, mine_in, theirs_in = grads(
        place, tile, *rows_met, *cols_met, cot, taps, vectors, w_in, b_in, w_out
    )
    met_out, met_in = swap_cores(theirs_out), swap_cores(theirs_in)
    d_rows = exchange(d_one, d_two, ROW)
    small_keep, small_give = tap_rows(place, pad, d_conv, rows)
    met_out, met_in, small_keep, small_give = lax.optimization_barrier((met_out, met_in, small_keep, small_give))
    keep, give = split_pair(place, mine_out, met_out, mine_in, met_in)
    give, d_rows = lax.optimization_barrier((give, d_rows))
    given = swap_chips(give)
    sides = halo_sides(*d_rows, d_conv, even_row, even_col)
    small_keep, small_give, give, sides = lax.optimization_barrier((small_keep, small_give, give, sides))
    smalls = small_keep, swap_cores(small_keep), swap_chips(small_give), swap_across(small_give)
    d_cols = exchange(*sides, COL)
    smalls, d_cols = lax.optimization_barrier((smalls, d_cols))
    message = add_pair(keep, given, *smalls)
    spread = lax.all_to_all(message, GROUP, 0, 0, tiled=True)
    d_conv, message = lax.optimization_barrier((d_conv, message))
    grad_features = features_part(place, d_conv, *d_rows, *d_cols, cot, taps)
    grad_in, grad_out, grad_channel, grad_bias = sum_chips(place, spread, factor)
    return (
        block_rows.reshape(ROWS, COLS, CH),
        grad_features,
        grad_in,
        grad_out,
        grad_channel.T,
        grad_bias.reshape(-1),
    )


def solution(mesh):
    fine = Mesh(mesh.devices.reshape(4, 2, 2, 2, 2, 2), EVERY)
    return jax.shard_map(
        shards,
        mesh=fine,
        in_specs=(P(ROW, COL, None), P(ROW, COL, None)) + (P(),) * 9,
        out_specs=(
            P(ROW, COL, None),
            P(ROW, COL, None),
            P(EVERY, None),
            P(EVERY, None),
            P(None, EVERY),
            P(EVERY),
        ),
        check_vma=False,
    )
```

time: 107 us -> 91 us (0.85)
  Pallas kernels: 39.9 us -> 18.7 us
  waiting for transfers between devices: 17.6 us -> 27.4 us
  starting transfers between devices: 40.5 us -> 33.6 us
  local copies, waits for them, and re-layouts: 5.5 us -> 8.42 us
    pallas_call x6, Pallas kernels: 38.6 us -> 17.3 us  [the longest x1 8.06 us: grads(): pl.pallas_call(grads_kernel, in_specs=[SCALARS] + [WHOLE] * len(operands)...]
    ppermute x8, starting transfers between devices: 15.5 us -> 9.47 us  [exchange(): met.append(lax.ppermute(value, axis, pairs))]
    ppermute x2, waiting for transfers between devices: 3.16 us -> 8.93 us  [swap_chips(): return lax.ppermute(value, ('xh', 'xl', 'c'), pairs)]
    all_to_all x1, waiting for transfers between devices: 11.4 us -> 14.5 us  [shards(): spread = lax.all_to_all(message, GROUP, 0, 0, tiled=True)]
    unnamed x28 -> x12, local copies, waits for them, and re-layouts: 3.64 us -> 6.67 us
    ppermute x2, starting transfers between devices: 4.66 us -> 2.71 us  [swap_chips(): return lax.ppermute(value, ('xh', 'xl', 'c'), pairs)]
    ppermute x0 -> x1, starting transfers between devices: none -> 1.79 us  [swap_across(): return lax.ppermute(value, ('xh', 'xl', 'c'), pairs)]
    ppermute x3, waiting for transfers between devices: 1.73 us -> 0.16 us  [swap_cores(): return lax.ppermute(value, 'c', [(0, 1), (1, 0)])]
  transfers between devices with their start and end apart: 14 -> 15, of which waited for: 4 -> 6; matrix products, arithmetic and copies ran while one was open for 2% -> 2% of each run, Pallas kernels for 19% -> 9%
where the time goes in v5:
time: 91 us; the launch traced here: 90.3 us
  starting transfers between devices  33.6 us (37%)
  waiting for transfers between devices  27.4 us (30%)
  Pallas kernels  18.7 us (21%)
  local copies, waits for them, and re-layouts  8.42 us (9%)
  other arithmetic  1.27 us (1%)
    all_to_all x1, starting transfers between devices, shards(): spread = lax.all_to_all(message, GROUP, 0, 0, tiled=True)  14.7 us
    all_to_all x1, waiting for transfers between devices, shards(): spread = lax.all_to_all(message, GROUP, 0, 0, tiled=True)  14.5 us
    ppermute x8, starting transfers between devices, exchange(): met.append(lax.ppermute(value, axis, pairs))  9.47 us
    ppermute x2, waiting for transfers between devices, swap_chips(): return lax.ppermute(value, ('xh', 'xl', 'c'), pairs)  8.93 us
    pallas_call x1, Pallas kernels, grads(): pl.pallas_call(grads_kernel, in_specs=[SCALARS] + [WHOLE] * len(operands)...  8.06 us
    unnamed x12, local copies, waits for them, and re-layouts  6.67 us
    ppermute x3, starting transfers between devices, swap_cores(): return lax.ppermute(value, 'c', [(0, 1), (1, 0)])  4.97 us
    pallas_call x1, Pallas kernels, features_part(): pl.pallas_call(features_kernel, in_specs=[SCALARS] + [WHOLE] * len(operan...  3.65 us
  transfers between devices with their start and end apart: 15, of which 6 were waited for; matrix products, arithmetic and copies ran while one was open for 2% of the time, Pallas kernels for 9%

profile of v5, /device:TPU:0, one launch (start us, length us, event | category | flops | bytes accessed | tf_op | source)
XLA Modules:
  0.0 90.3 jit_solution(15962018010891741259)
XLA Ops:
  0.6 1.0 %broadcast_select_fusion.4 = (bf16[3,32,512]{2,1,0:T(8,128)(2,1)S(1)}, bf16[3,32,512]{2,1,0:T(8,128)(2,1)S(1)}) fusion(pred[]{:T(512)S(6)} %eq.6, bf16[8,32,512]{2,1,0:T(8,128)(2,1)} %refs_0_.1), kind=kLoop, calls=%fused_computation.4 | loop fusion | flops 98304 | bytes 393217 | tf_op jit(solution)/shard_map/jit(_where)/select_n | solution.py:382
  1.6 0.7 collective-permute-start.1
  2.3 6.3 %collective-permute-start = (bf16[3,32,512]{2,1,0:T(8,128)(2,1)S(1)}, bf16[3,32,512]{2,1,0:T(8,128)(2,1)S(1)}, u32[]{:S(2)}, u32[]{:S(2)}) collective-permute-start(bf16[3,32,512]{2,1,0:T(8,128)(2,1)S(1)} %get-tuple-element.103), channel_id=1, source_target_pairs={{0,16},{16,0},{32,48},{48,32},{64,80},{80,64},{96,112},{112,96},{1... | collective-permute-start | bytes 294920 | tf_op jit(solution)/shard_map/ppermute | solution.py:342
  8.6 0.9 fusion.1
  9.5 0.8 stack.39.refs_3_
  10.3 1.6 %copy-done = bf16[512,2048]{1,0:T(8,128)(2,1)S(1)} copy-done((bf16[512,2048]{1,0:T(8,128)(2,1)S(1)}, bf16[512,2048]{1,0:T(8,128)(2,1)}, u32[]{:S(2)}) %copy-start) | copy-done | bytes 2097176
  11.8 1.6 %copy-done.1 = bf16[2048,512]{1,0:T(8,128)(2,1)S(1)} copy-done((bf16[2048,512]{1,0:T(8,128)(2,1)S(1)}, bf16[2048,512]{1,0:T(8,128)(2,1)}, u32[]{:S(2)}) %copy-start.1) | copy-done | bytes 2097176
  13.4 0.9 %copy-done.2 = bf16[8,32,512]{2,1,0:T(8,128)(2,1)S(1)} copy-done((bf16[8,32,512]{2,1,0:T(8,128)(2,1)S(1)}, bf16[8,32,512]{2,1,0:T(8,128)(2,1)}, u32[]{:S(2)}) %copy-start.2) | copy-done | bytes 262168
  14.4 0.9 %copy-done.3 = bf16[8,32,512]{2,1,0:T(8,128)(2,1)S(1)} copy-done((bf16[8,32,512]{2,1,0:T(8,128)(2,1)S(1)}, bf16[8,32,512]{2,1,0:T(8,128)(2,1)}, u32[]{:S(2)}) %copy-start.3) | copy-done | bytes 262168
  15.3 0.9 copy-done.4
  16.2 0.7 copy-done.5
  16.9 0.6 fetch.1
  17.8 0.7 collective-permute-start.3
  18.5 0.5 collective-permute-done.2.col_one
  19.0 8.1 %grads.1 = (f32[4,14,40,128]{3,2,1,0:T(8,128)S(1)}, bf16[256,512]{1,0:T(8,128)(2,1)}, bf16[8,32,512]{2,1,0:T(8,128)(2,1)S(1)}, bf16[3,32,512]{2,1,0:T(8,128)(2,1...) custom-call(s32[3]{0:T(128)S(1)} %pad_add_fusion.place.refs_0_, ...), custom_call_target="tpu_custom_call" | custom-call | flops 3200000000 | bytes 12000000 | tf_op jit(solution)/shard_map/grads/pallas_call | solution.py:187
  27.1 4.7 %collective-permute-start.4 = (bf16[64,64,128]{2,1,0:T(8,128)(2,1)S(1)}, bf16[64,64,128]{2,1,0:T(8,128)(2,1)S(1)}, u32[]{:S(2)}, u32[]{:S(2)}) collective-permute-start(bf16[64,64,128]{2,1,0:T(8,128)(2,1)S(1)} %get-tuple-element.65), channel_id=1, source_target_pairs={{0,1},{1,0},{2,3},{3,2},{4,5},{5,4},{6,7},{7,6},{8,9},{9,8},{10,11... | collective-permute-start | bytes 3145736 | tf_op jit(solution)/shard_map/ppermute | solution.py:355
  31.9 0.7 collective-permute-start.7
  32.6 2.8 %tap_rows.1 = (bf16[32,8,128]{2,1,0:T(8,128)(2,1)S(1)}, bf16[32,8,128]{2,1,0:T(8,128)(2,1)S(1)}) custom-call(s32[3]{0:T(128)S(1)} %pad_add_fusion.place.refs_0_, f32[4,14,40,128]{3,2,1,0:T(8,128)S(1)} %get-tuple-element.67.pad, bf16[8,32,512]{2,1,0:T(8,128)(2,1)S(1)} %get-tuple-element.91.d_conv, f32[16,512]{1,0:T(8,128)S(1)} %get-tuple-element.68.rows), custom_call_target="tpu_custom_call" | custom-call | flops 30000000 | bytes 2000000 | tf_op jit(solution)/shard_map/tap_rows/pallas_call | solution.py:237
  35.6 0.9 %split_pair.1 = (bf16[32,128,128]{2,1,0:T(8,128)(2,1)S(1)}, bf16[32,128,128]{2,1,0:T(8,128)(2,1)S(1)}) custom-call(s32[3]{0:T(128)S(1)} %pad_add_fusion.place.refs_0_, bf16[64,64,128]{2,1,0:T(8,128)(2,1)S(1)} %get-tuple-element.64.out_one, bf16[64,64,128]{2,1,0:T(8,128)(2,1)S(1)} %collective-permute-done.4.out_two, ...), custom_call_target="tpu_custom_call" | custom-call | flops 1000000 | bytes 6000000 | tf_op jit(solution)/shard_map/split_pair/pallas_call | solution.py:258
  36.6 2.0 %collective-permute-done.6.row_one = bf16[3,32,512]{2,1,0:T(8,128)(2,1)S(1)} collective-permute-done((bf16[3,32,512]{2,1,0:T(8,128)(2,1)S(1)}, bf16[3,32,512]{2,1,0:T(8,128)(2,1)S(1)}, u32[]{:S(2)}, u32[]{:S(2)}) %collective-permute-start.6) | collective-permute-done | bytes 98336 | tf_op jit(solution)/shard_map/ppermute | solution.py:342
  38.5 2.1 %collective-permute-start.8 = (bf16[32,128,128]{2,1,0:T(8,128)(2,1)S(1)}, bf16[32,128,128]{2,1,0:T(8,128)(2,1)S(1)}, u32[]{:S(2)}, u32[]{:S(2)}) collective-permute-start(bf16[32,128,128]{2,1,0:T(8,128)(2,1)S(1)} %get-tuple-element.78), channel_id=1, source_target_pairs={{0,4},{1,13},{4,0},{5,9},{8,12},{9,5},{12,8},{13,1},{2,6},{3,15},{... | collective-permute-start | bytes 3145736 | tf_op jit(solution)/shard_map/ppermute | solution.py:362
  40.8 0.4 collective-permute-start.12
  41.4 1.8 %collective-permute-start.11 = (bf16[32,8,128]{2,1,0:T(8,128)(2,1)S(1)}, bf16[32,8,128]{2,1,0:T(8,128)(2,1)S(1)}, u32[]{:S(2)}, u32[]{:S(2)}) collective-permute-start(bf16[32,8,128]{2,1,0:T(8,128)(2,1)S(1)} %get-tuple-element.84), channel_id=1, source_target_pairs={{0,13},{1,4},{4,9},{5,0},{8,5},{9,12},{12,1},{13,8},{2,15},{3,6},{... | collective-permute-start | bytes 196616 | tf_op jit(solution)/shard_map/ppermute | solution.py:369
  43.2 0.6 collective-permute-start.10
  43.8 0.7 collective-permute-start.13
  44.5 1.4 %collective-permute-done.11.small_four = bf16[32,8,128]{2,1,0:T(8,128)(2,1)S(1)} collective-permute-done((bf16[32,8,128]{2,1,0:T(8,128)(2,1)S(1)}, bf16[32,8,128]{2,1,0:T(8,128)(2,1)S(1)}, u32[]{:S(2)}, u32[]{:S(2)}) %collective-permute-start.11) | collective-permute-done | bytes 65568 | tf_op jit(solution)/shard_map/ppermute | solution.py:369
  45.9 8.9 %collective-permute-done.10.small_three = bf16[32,8,128]{2,1,0:T(8,128)(2,1)S(1)} collective-permute-done((bf16[32,8,128]{2,1,0:T(8,128)(2,1)S(1)}, bf16[32,8,128]{2,1,0:T(8,128)(2,1)S(1)}, u32[]{:S(2)}, u32[]{:S(2)}) %collective-permute-start.10) | collective-permute-done | bytes 65568 | tf_op jit(solution)/shard_map/ppermute | solution.py:362
  54.8 1.3 %add_pair.1 = bf16[32,136,128]{2,1,0:T(8,128)(2,1)} custom-call(bf16[32,128,128]{2,1,0:T(8,128)(2,1)S(1)} %get-tuple-element.74.one, bf16[32,128,128]{2,1,0:T(8,128)(2,1)S(1)} %collective-permute-done.8.two, bf16[32,8,128]{2,1,0:T(8,128)(2,1)S(1)} %get-tuple-element.87.small_one, bf16[32,8,128]{2,1,0:T(8,128)(2,1)S(1)} %collective-permute-done.9.small_two, ...), custom_call_target="tpu_custom_call" | custom-call | flops 1000000 | bytes 3000000 | tf_op jit(solution)/shard_map/add_pair/pallas_call | solution.py:276
  56.1 14.7 %all-to-all-start = ((bf16[32,136,128]{2,1,0:T(8,128)(2,1)}), bf16[32,136,128]{2,1,0:T(8,128)(2,1)S(1)}, u32[]{:S(2)}, u32[]{:S(2)}) async-start(bf16[32,136,128]{2,1,0:T(8,128)(2,1)} %add_pair.1), calls=%async_computation | async-start | bytes 2228224 | tf_op jit(solution)/shard_map/all_to_all | solution.py:406
  70.8 3.6 %features_part.1 = bf16[8,32,512]{2,1,0:T(8,128)(2,1)} custom-call(s32[3]{0:T(128)S(1)} %pad_add_fusion.place.refs_0_, bf16[8,32,512]{2,1,0:T(8,128)(2,1)S(1)} %get-tuple-element.91.d_conv, bf16[3,32,512]{2,1,0:T(8,128)(2,1)S(1)} %collective-permute-done.6.row_one, bf16[3,32,512]{2,1,0:T(8,128)(2,1)S(1)} %collective-permute-done.7.row_two, ...), custom_call_target="tpu_custom_call" | custom-call | flops 30000000 | bytes 2000000 | tf_op jit(solution)/shard_map/features_part/pallas_call | solution.py:324
  74.4 14.5 %all-to-all-done.refs_1_ = bf16[32,136,128]{2,1,0:T(8,128)(2,1)S(1)} async-done(((bf16[32,136,128]{2,1,0:T(8,128)(2,1)}), bf16[32,136,128]{2,1,0:T(8,128)(2,1)S(1)}, u32[]{:S(2)}, u32[]{:S(2)}) %all-to-all-start) | async-done | bytes 1114144 | tf_op jit(solution)/shard_map/all_to_all | solution.py:406
  88.9 1.4 %sum_chips.1 = (f32[4,2048]{1,0:T(4,128)}, f32[16,512]{1,0:T(8,128)}, f32[4,54]{1,0:T(4,128)}, f32[1,16]{1,0:T(1,128)}) custom-call(s32[3]{0:T(128)S(1)} %pad_add_fusion.place.refs_0_, bf16[32,136,128]{2,1,0:T(8,128)(2,1)S(1)} %all-to-all-done.refs_1_), custom_call_target="tpu_custom_call" | custom-call | flops 1000000 | bytes 1000000 | tf_op jit(solution)/shard_map/sum_chips/pallas_call | solution.py:304
  (29 shorter events, 1.0 us)
Async XLA Ops:
  1.6 15.9 %collective-permute-start.1 = (bf16[3,32,512]{2,1,0:T(8,128)(2,1)S(1)}, bf16[3,32,512]{2,1,0:T(8,128)(2,1)S(1)}, u32[]{:S(2)}, u32[]{:S(2)}) collective-permute-start(bf16[3,32,512]{2,1,0:T(8,128)(2,1)S(1)} %get-tuple-element.102), channel_id=1, source_target_pairs={{16,32},{32,16},{48,64},{64,48},{80,96},{96,80},{17,33},{33,17},{4... | collective-permute-start | bytes 294920 | tf_op jit(solution)/shard_map/ppermute | solution.py:342
  2.3 15.2 %collective-permute-start = (bf16[3,32,512]{2,1,0:T(8,128)(2,1)S(1)}, bf16[3,32,512]{2,1,0:T(8,128)(2,1)S(1)}, u32[]{:S(2)}, u32[]{:S(2)}) collective-permute-start(bf16[3,32,512]{2,1,0:T(8,128)(2,1)S(1)} %get-tuple-element.103), channel_id=1, source_target_pairs={{0,16},{16,0},{32,48},{48,32},{64,80},{80,64},{96,112},{112,96},{1... | collective-permute-start | bytes 294920 | tf_op jit(solution)/shard_map/ppermute | solution.py:342
  10.2 1.6 %copy-start = (bf16[512,2048]{1,0:T(8,128)(2,1)S(1)}, bf16[512,2048]{1,0:T(8,128)(2,1)}, u32[]{:S(2)}) copy-start(bf16[512,2048]{1,0:T(8,128)(2,1)} %refs_4_.1) | copy-start | bytes 6291460
  11.8 1.6 %copy-start.1 = (bf16[2048,512]{1,0:T(8,128)(2,1)S(1)}, bf16[2048,512]{1,0:T(8,128)(2,1)}, u32[]{:S(2)}) copy-start(bf16[2048,512]{1,0:T(8,128)(2,1)} %refs_6_.1) | copy-start | bytes 6291460
  13.4 0.9 %copy-start.2 = (bf16[8,32,512]{2,1,0:T(8,128)(2,1)S(1)}, bf16[8,32,512]{2,1,0:T(8,128)(2,1)}, u32[]{:S(2)}) copy-start(bf16[8,32,512]{2,1,0:T(8,128)(2,1)} %refs_0_.1) | copy-start | bytes 786436
  14.4 0.9 %copy-start.3 = (bf16[8,32,512]{2,1,0:T(8,128)(2,1)S(1)}, bf16[8,32,512]{2,1,0:T(8,128)(2,1)}, u32[]{:S(2)}) copy-start(bf16[8,32,512]{2,1,0:T(8,128)(2,1)} %param.12) | copy-start | bytes 786436
  15.3 0.9 copy-start.4
  16.2 0.7 copy-start.5
  17.7 1.3 %collective-permute-start.2 = (bf16[14,3,512]{2,1,0:T(4,128)(2,1)S(1)}, bf16[14,3,512]{2,1,0:T(4,128)(2,1)S(1)}, u32[]{:S(2)}, u32[]{:S(2)}) collective-permute-start(bf16[14,3,512]{2,1,0:T(4,128)(2,1)S(1)} %get-tuple-element.54), channel_id=1, source_target_pairs={{0,1},{1,0},{2,3},{3,2},{4,5},{5,4},{6,7},{7,6},{8,9},{9,8},{10,11... | collective-permute-start | bytes 129032 | tf_op jit(solution)/shard_map/ppermute | solution.py:342
  17.8 1.2 %collective-permute-start.3 = (bf16[14,3,512]{2,1,0:T(4,128)(2,1)S(1)}, bf16[14,3,512]{2,1,0:T(4,128)(2,1)S(1)}, u32[]{:S(2)}, u32[]{:S(2)}) collective-permute-start(bf16[14,3,512]{2,1,0:T(4,128)(2,1)S(1)} %get-tuple-element.55), channel_id=1, source_target_pairs={{1,2},{2,1},{3,4},{4,3},{5,6},{6,5},{7,8},{8,7},{9,10},{10,9},{11,... | collective-permute-start | bytes 129032 | tf_op jit(solution)/shard_map/ppermute | solution.py:342
  27.1 8.4 %collective-permute-start.4 = (bf16[64,64,128]{2,1,0:T(8,128)(2,1)S(1)}, bf16[64,64,128]{2,1,0:T(8,128)(2,1)S(1)}, u32[]{:S(2)}, u32[]{:S(2)}) collective-permute-start(bf16[64,64,128]{2,1,0:T(8,128)(2,1)S(1)} %get-tuple-element.65), channel_id=1, source_target_pairs={{0,1},{1,0},{2,3},{3,2},{4,5},{5,4},{6,7},{7,6},{8,9},{9,8},{10,11... | collective-permute-start | bytes 3145736 | tf_op jit(solution)/shard_map/ppermute | solution.py:355
  31.8 3.8 %collective-permute-start.5 = (bf16[64,64,128]{2,1,0:T(8,128)(2,1)S(1)}, bf16[64,64,128]{2,1,0:T(8,128)(2,1)S(1)}, u32[]{:S(2)}, u32[]{:S(2)}) collective-permute-start(bf16[64,64,128]{2,1,0:T(8,128)(2,1)S(1)} %get-tuple-element.66), channel_id=1, source_target_pairs={{0,1},{1,0},{2,3},{3,2},{4,5},{5,4},{6,7},{7,6},{8,9},{9,8},{10,11... | collective-permute-start | bytes 3145736 | tf_op jit(solution)/shard_map/ppermute | solution.py:355
  31.8 6.7 %collective-permute-start.6 = (bf16[3,32,512]{2,1,0:T(8,128)(2,1)S(1)}, bf16[3,32,512]{2,1,0:T(8,128)(2,1)S(1)}, u32[]{:S(2)}, u32[]{:S(2)}) collective-permute-start(bf16[3,32,512]{2,1,0:T(8,128)(2,1)S(1)} %get-tuple-element.76), channel_id=1, source_target_pairs={{0,16},{16,0},{32,48},{48,32},{64,80},{80,64},{96,112},{112,96},{1... | collective-permute-start | bytes 294920 | tf_op jit(solution)/shard_map/ppermute | solution.py:342
  31.9 6.6 %collective-permute-start.7 = (bf16[3,32,512]{2,1,0:T(8,128)(2,1)S(1)}, bf16[3,32,512]{2,1,0:T(8,128)(2,1)S(1)}, u32[]{:S(2)}, u32[]{:S(2)}) collective-permute-start(bf16[3,32,512]{2,1,0:T(8,128)(2,1)S(1)} %get-tuple-element.77), channel_id=1, source_target_pairs={{16,32},{32,16},{48,64},{64,48},{80,96},{96,80},{17,33},{33,17},{4... | collective-permute-start | bytes 294920 | tf_op jit(solution)/shard_map/ppermute | solution.py:342
  38.5 16.3 %collective-permute-start.8 = (bf16[32,128,128]{2,1,0:T(8,128)(2,1)S(1)}, bf16[32,128,128]{2,1,0:T(8,128)(2,1)S(1)}, u32[]{:S(2)}, u32[]{:S(2)}) collective-permute-start(bf16[32,128,128]{2,1,0:T(8,128)(2,1)S(1)} %get-tuple-element.78), channel_id=1, source_target_pairs={{0,4},{1,13},{4,0},{5,9},{8,12},{9,5},{12,8},{13,1},{2,6},{3,15},{... | collective-permute-start | bytes 3145736 | tf_op jit(solution)/shard_map/ppermute | solution.py:362
  40.8 3.0 %collective-permute-start.12 = (bf16[14,3,512]{2,1,0:T(4,128)(2,1)S(1)}, bf16[14,3,512]{2,1,0:T(4,128)(2,1)S(1)}, u32[]{:S(2)}, u32[]{:S(2)}) collective-permute-start(bf16[14,3,512]{2,1,0:T(4,128)(2,1)S(1)} %get-tuple-element.85), channel_id=1, source_target_pairs={{0,1},{1,0},{2,3},{3,2},{4,5},{5,4},{6,7},{7,6},{8,9},{9,8},{10,11... | collective-permute-start | bytes 129032 | tf_op jit(solution)/shard_map/ppermute | solution.py:342
  41.2 3.3 %collective-permute-start.9 = (bf16[32,8,128]{2,1,0:T(8,128)(2,1)S(1)}, bf16[32,8,128]{2,1,0:T(8,128)(2,1)S(1)}, u32[]{:S(2)}, u32[]{:S(2)}) collective-permute-start(bf16[32,8,128]{2,1,0:T(8,128)(2,1)S(1)} %get-tuple-element.87.small_one), channel_id=1, source_target_pairs={{0,1},{1,0},{2,3},{3,2},{4,5},{5,4},{6,7},{7,6},{8,9},{9,8},{10,11... | collective-permute-start | bytes 196616 | tf_op jit(solution)/shard_map/ppermute | solution.py:355
  41.4 4.5 %collective-permute-start.11 = (bf16[32,8,128]{2,1,0:T(8,128)(2,1)S(1)}, bf16[32,8,128]{2,1,0:T(8,128)(2,1)S(1)}, u32[]{:S(2)}, u32[]{:S(2)}) collective-permute-start(bf16[32,8,128]{2,1,0:T(8,128)(2,1)S(1)} %get-tuple-element.84), channel_id=1, source_target_pairs={{0,13},{1,4},{4,9},{5,0},{8,5},{9,12},{12,1},{13,8},{2,15},{3,6},{... | collective-permute-start | bytes 196616 | tf_op jit(solution)/shard_map/ppermute | solution.py:369
  43.2 11.6 %collective-permute-start.10 = (bf16[32,8,128]{2,1,0:T(8,128)(2,1)S(1)}, bf16[32,8,128]{2,1,0:T(8,128)(2,1)S(1)}, u32[]{:S(2)}, u32[]{:S(2)}) collective-permute-start(bf16[32,8,128]{2,1,0:T(8,128)(2,1)S(1)} %get-tuple-element.84), channel_id=1, source_target_pairs={{0,4},{1,13},{4,0},{5,9},{8,12},{9,5},{12,8},{13,1},{2,6},{3,15},{... | collective-permute-start | bytes 196616 | tf_op jit(solution)/shard_map/ppermute | solution.py:362
  43.8 0.7 collective-permute-start.13
  56.1 32.8 %all-to-all-start = ((bf16[32,136,128]{2,1,0:T(8,128)(2,1)}), bf16[32,136,128]{2,1,0:T(8,128)(2,1)S(1)}, u32[]{:S(2)}, u32[]{:S(2)}) async-start(bf16[32,136,128]{2,1,0:T(8,128)(2,1)} %add_pair.1), calls=%async_computation | async-start | bytes 2228224 | tf_op jit(solution)/shard_map/all_to_all | solution.py:406

commit v6 on v5

--- a/solution.py
+++ b/solution.py
@@ -63,14 +63,14 @@
     count = len(arrays)
     return pl.pallas_call(
         lambda *refs: fetch_kernel(count, *refs),
-        in_specs=[pl.BlockSpec(memory_space=pl.ANY)] * count,
+        in_specs=[pl.BlockSpec(memory_space=pltpu.HBM)] * count,
         out_specs=[WHOLE] * count,
         out_shape=[pltpu.VMEM(array.shape, array.dtype) for array in arrays],
         scratch_shapes=[pltpu.SemaphoreType.DMA((count,))],
         compiler_params=params(),
         cost_estimate=cost(0, 5_000_000),
         name="fetch",
-    )(*arrays)
+    )(*(pltpu.with_memory_space_constraint(array, pltpu.HBM) for array in arrays))
 
 
 def assemble(pad, tile, row_one, row_two, col_one, col_two, even_row, even_col):
@@ -391,16 +391,14 @@
         place, tile, *rows_met, *cols_met, cot, taps, vectors, w_in, b_in, w_out
     )
     met_out, met_in = swap_cores(theirs_out), swap_cores(theirs_in)
-    d_rows = exchange(d_one, d_two, ROW)
     small_keep, small_give = tap_rows(place, pad, d_conv, rows)
     met_out, met_in, small_keep, small_give = lax.optimization_barrier((met_out, met_in, small_keep, small_give))
     keep, give = split_pair(place, mine_out, met_out, mine_in, met_in)
-    give, d_rows = lax.optimization_barrier((give, d_rows))
     given = swap_chips(give)
-    sides = halo_sides(*d_rows, d_conv, even_row, even_col)
-    small_keep, small_give, give, sides = lax.optimization_barrier((small_keep, small_give, give, sides))
+    small_keep, small_give, give, d_one, d_two = lax.optimization_barrier((small_keep, small_give, give, d_one, d_two))
     smalls = small_keep, swap_cores(small_keep), swap_chips(small_give), swap_across(small_give)
-    d_cols = exchange(*sides, COL)
+    d_rows = exchange(d_one, d_two, ROW)
+    d_cols = exchange(*halo_sides(*d_rows, d_conv, even_row, even_col), COL)
     smalls, d_cols = lax.optimization_barrier((smalls, d_cols))
     message = add_pair(keep, given, *smalls)
     spread = lax.all_to_all(message, GROUP, 0, 0, tiled=True)

time: 91 us -> 81.3 us (0.89)
  waiting for transfers between devices: 27.4 us -> 18.5 us
  local copies, waits for them, and re-layouts: 8.42 us -> 2.35 us
  starting transfers between devices: 33.6 us -> 37.4 us
  Pallas kernels: 18.7 us -> 20.6 us
    ppermute x2, waiting for transfers between devices: 8.93 us -> 0.01 us  [swap_chips(): return lax.ppermute(value, ('xh', 'xl', 'c'), pairs)]
    ppermute x8, starting transfers between devices: 9.47 us -> 17.6 us  [exchange(): met.append(lax.ppermute(value, axis, pairs))]
    unnamed x12 -> x0, local copies, waits for them, and re-layouts: 6.67 us -> none
    all_to_all x1, starting transfers between devices: 14.7 us -> 9.4 us  [shards(): spread = lax.all_to_all(message, GROUP, 0, 0, tiled=True)]
    ppermute x3, starting transfers between devices: 4.97 us -> 6.96 us  [swap_cores(): return lax.ppermute(value, 'c', [(0, 1), (1, 0)])]
    pallas_call x1, Pallas kernels: 0.56 us -> 2.53 us  [fetch(): pl.pallas_call(lambda *refs: fetch_kernel(count, *refs), in_specs=[pl.Blo...]
    ppermute x1, waiting for transfers between devices: 1.37 us -> 0.01 us  [swap_across(): return lax.ppermute(value, ('xh', 'xl', 'c'), pairs)]
    ppermute x1, starting transfers between devices: 1.79 us -> 0.54 us  [swap_across(): return lax.ppermute(value, ('xh', 'xl', 'c'), pairs)]
  transfers between devices with their start and end apart: 15 -> 15, of which waited for: 6 -> 5; matrix products, arithmetic and copies ran while one was open for 2% -> 3% of each run, Pallas kernels for 9% -> 11%
where the time goes in v6:
time: 81.3 us; the launch traced here: 80.9 us
  starting transfers between devices  37.4 us (46%)
  Pallas kernels  20.6 us (25%)
  waiting for transfers between devices  18.5 us (23%)
  local copies, waits for them, and re-layouts  2.35 us (3%)
  other arithmetic  1.27 us (2%)
  between operations  0.82 us (1%)
    ppermute x8, starting transfers between devices, exchange(): met.append(lax.ppermute(value, axis, pairs))  17.6 us
    all_to_all x1, waiting for transfers between devices, shards(): spread = lax.all_to_all(message, GROUP, 0, 0, tiled=True)  13.9 us
    all_to_all x1, starting transfers between devices, shards(): spread = lax.all_to_all(message, GROUP, 0, 0, tiled=True)  9.4 us
    pallas_call x1, Pallas kernels, grads(): pl.pallas_call(grads_kernel, in_specs=[SCALARS] + [WHOLE] * len(operands)...  7.95 us
    ppermute x3, starting transfers between devices, swap_cores(): return lax.ppermute(value, 'c', [(0, 1), (1, 0)])  6.96 us
    pallas_call x1, Pallas kernels, features_part(): pl.pallas_call(features_kernel, in_specs=[SCALARS] + [WHOLE] * len(operan...  3.65 us
    ppermute x8, waiting for transfers between devices, exchange(): met.append(lax.ppermute(value, axis, pairs))  3.63 us
    ppermute x2, starting transfers between devices, swap_chips(): return lax.ppermute(value, ('xh', 'xl', 'c'), pairs)  2.91 us
  transfers between devices with their start and end apart: 15, of which 5 were waited for; matrix products, arithmetic and copies ran while one was open for 3% of the time, Pallas kernels for 11%

profile of v6, /device:TPU:0, one launch (start us, length us, event | category | flops | bytes accessed | tf_op | source)
XLA Modules:
  0.0 80.9 jit_solution(2340415319686648245)
XLA Ops:
  0.6 1.0 %broadcast_select_fusion.4 = (bf16[3,32,512]{2,1,0:T(8,128)(2,1)S(1)}, bf16[3,32,512]{2,1,0:T(8,128)(2,1)S(1)}) fusion(pred[]{:T(512)S(6)} %eq.6, bf16[8,32,512]{2,1,0:T(8,128)(2,1)} %refs_0_.1), kind=kLoop, calls=%fused_computation.4 | loop fusion | flops 98304 | bytes 393217 | tf_op jit(solution)/shard_map/jit(_where)/select_n | solution.py:382
  1.6 0.7 collective-permute-start.1
  2.3 6.3 %collective-permute-start = (bf16[3,32,512]{2,1,0:T(8,128)(2,1)S(1)}, bf16[3,32,512]{2,1,0:T(8,128)(2,1)S(1)}, u32[]{:S(2)}, u32[]{:S(2)}) collective-permute-start(bf16[3,32,512]{2,1,0:T(8,128)(2,1)S(1)} %get-tuple-element.97), channel_id=1, source_target_pairs={{0,16},{16,0},{32,48},{48,32},{64,80},{80,64},{96,112},{112,96},{1... | collective-permute-start | bytes 294920 | tf_op jit(solution)/shard_map/ppermute | solution.py:342
  8.6 0.9 %fusion.1 = (bf16[8,3,512]{2,1,0:T(4,128)(2,1)S(1)}, bf16[8,3,512]{2,1,0:T(4,128)(2,1)S(1)}) fusion(bf16[8,32,512]{2,1,0:T(8,128)(2,1)} %refs_0_.1), kind=kLoop, calls=%fused_computation.16 | loop fusion | bytes 98304 | tf_op jit(solution)/shard_map/slice | solution.py:349
  9.5 1.4 %stack.39.refs_3_ = f32[5,512]{1,0:T(8,128)} concatenate(f32[1,512]{1,0:T(1,128)} %bitcast.15, f32[1,512]{1,0:T(1,128)} %bitcast.16, f32[1,512]{1,0:T(1,128)} %bitcast.17, f32[1,512]{1,0:T(1,128)} %bitcast.18, f32[1,512]{1,0:T(1,128)} %bitcast.19), dimensions={0} | concatenate | bytes 20480 | tf_op jit(solution)/shard_map/stack | solution.py:380
  10.8 2.5 %fetch.1 = (bf16[8,32,512]{2,1,0:T(8,128)(2,1)S(1)}, bf16[256,512]{1,0:T(8,128)(2,1)S(1)}, f32[49,512]{1,0:T(8,128)S(1)}, f32[5,512]{1,0:T(8,128)S(1)}, bf16[512...) custom-call(bf16[8,32,512]{2,1,0:T(8,128)(2,1)} %refs_0_.1, ...), custom_call_target="tpu_custom_call" | custom-call | bytes 5000000 | tf_op jit(solution)/shard_map/fetch/pallas_call | solution.py:64
  13.5 0.1 broadcast_select_fusion.8
  13.6 0.1 collective-permute-start.2
  13.7 0.7 collective-permute-start.3
  14.3 0.1 pad_add_fusion.place.refs_0_
  14.4 0.5 collective-permute-done.2.col_one
  14.9 7.9 %grads.1 = (f32[4,14,40,128]{3,2,1,0:T(8,128)S(1)}, bf16[256,512]{1,0:T(8,128)(2,1)}, bf16[8,32,512]{2,1,0:T(8,128)(2,1)S(1)}, bf16[3,32,512]{2,1,0:T(8,128)(2,1...) custom-call(s32[3]{0:T(128)S(1)} %pad_add_fusion.place.refs_0_, ...), custom_call_target="tpu_custom_call" | custom-call | flops 3200000000 | bytes 12000000 | tf_op jit(solution)/shard_map/grads/pallas_call | solution.py:187
  22.8 4.8 %collective-permute-start.4 = (bf16[64,64,128]{2,1,0:T(8,128)(2,1)S(1)}, bf16[64,64,128]{2,1,0:T(8,128)(2,1)S(1)}, u32[]{:S(2)}, u32[]{:S(2)}) collective-permute-start(bf16[64,64,128]{2,1,0:T(8,128)(2,1)S(1)} %get-tuple-element.62), channel_id=1, source_target_pairs={{0,1},{1,0},{2,3},{3,2},{4,5},{5,4},{6,7},{7,6},{8,9},{9,8},{10,11... | collective-permute-start | bytes 3145736 | tf_op jit(solution)/shard_map/ppermute | solution.py:355
  27.6 2.8 %tap_rows.1 = (bf16[32,8,128]{2,1,0:T(8,128)(2,1)S(1)}, bf16[32,8,128]{2,1,0:T(8,128)(2,1)S(1)}) custom-call(s32[3]{0:T(128)S(1)} %pad_add_fusion.place.refs_0_, f32[4,14,40,128]{3,2,1,0:T(8,128)S(1)} %get-tuple-element.64.pad, bf16[8,32,512]{2,1,0:T(8,128)(2,1)S(1)} %get-tuple-element.85.d_conv, f32[16,512]{1,0:T(8,128)S(1)} %get-tuple-element.65.rows), custom_call_target="tpu_custom_call" | custom-call | flops 30000000 | bytes 2000000 | tf_op jit(solution)/shard_map/tap_rows/pallas_call | solution.py:237
  30.5 0.9 %collective-permute-done.5.in_two = bf16[64,64,128]{2,1,0:T(8,128)(2,1)S(1)} collective-permute-done((bf16[64,64,128]{2,1,0:T(8,128)(2,1)S(1)}, bf16[64,64,128]{2,1,0:T(8,128)(2,1)S(1)}, u32[]{:S(2)}, u32[]{:S(2)}) %collective-permute-start.5) | collective-permute-done | bytes 1048608 | tf_op jit(solution)/shard_map/ppermute | solution.py:355
  31.4 0.9 %split_pair.1 = (bf16[32,128,128]{2,1,0:T(8,128)(2,1)S(1)}, bf16[32,128,128]{2,1,0:T(8,128)(2,1)S(1)}) custom-call(s32[3]{0:T(128)S(1)} %pad_add_fusion.place.refs_0_, bf16[64,64,128]{2,1,0:T(8,128)(2,1)S(1)} %get-tuple-element.61.out_one, bf16[64,64,128]{2,1,0:T(8,128)(2,1)S(1)} %collective-permute-done.4.out_two, ...), custom_call_target="tpu_custom_call" | custom-call | flops 1000000 | bytes 6000000 | tf_op jit(solution)/shard_map/split_pair/pallas_call | solution.py:258
  32.3 2.5 %collective-permute-start.6 = (bf16[32,128,128]{2,1,0:T(8,128)(2,1)S(1)}, bf16[32,128,128]{2,1,0:T(8,128)(2,1)S(1)}, u32[]{:S(2)}, u32[]{:S(2)}) collective-permute-start(bf16[32,128,128]{2,1,0:T(8,128)(2,1)S(1)} %get-tuple-element.72), channel_id=1, source_target_pairs={{0,4},{1,13},{4,0},{5,9},{8,12},{9,5},{12,8},{13,1},{2,6},{3,15},{... | collective-permute-start | bytes 3145736 | tf_op jit(solution)/shard_map/ppermute | solution.py:362
  34.8 0.7 collective-permute-start.10
  35.5 6.2 %collective-permute-start.11 = (bf16[3,32,512]{2,1,0:T(8,128)(2,1)S(1)}, bf16[3,32,512]{2,1,0:T(8,128)(2,1)S(1)}, u32[]{:S(2)}, u32[]{:S(2)}) collective-permute-start(bf16[3,32,512]{2,1,0:T(8,128)(2,1)S(1)} %get-tuple-element.80), channel_id=1, source_target_pairs={{0,16},{16,0},{32,48},{48,32},{64,80},{80,64},{96,112},{112,96},{1... | collective-permute-start | bytes 294920 | tf_op jit(solution)/shard_map/ppermute | solution.py:342
  41.7 0.5 collective-permute-start.9
  42.2 0.5 collective-permute-start.8
  42.7 2.2 %collective-permute-start.7 = (bf16[32,8,128]{2,1,0:T(8,128)(2,1)S(1)}, bf16[32,8,128]{2,1,0:T(8,128)(2,1)S(1)}, u32[]{:S(2)}, u32[]{:S(2)}) collective-permute-start(bf16[32,8,128]{2,1,0:T(8,128)(2,1)S(1)} %get-tuple-element.81.small_one), channel_id=1, source_target_pairs={{0,1},{1,0},{2,3},{3,2},{4,5},{5,4},{6,7},{7,6},{8,9},{9,8},{10,11... | collective-permute-start | bytes 196616 | tf_op jit(solution)/shard_map/ppermute | solution.py:355
  44.9 2.3 %collective-permute-done.11.row_one = bf16[3,32,512]{2,1,0:T(8,128)(2,1)S(1)} collective-permute-done((bf16[3,32,512]{2,1,0:T(8,128)(2,1)S(1)}, bf16[3,32,512]{2,1,0:T(8,128)(2,1)S(1)}, u32[]{:S(2)}, u32[]{:S(2)}) %collective-permute-start.11) | collective-permute-done | bytes 98336 | tf_op jit(solution)/shard_map/ppermute | solution.py:342
  47.2 0.1 broadcast_select_fusion.6
  47.3 0.7 collective-permute-start.13
  48.0 2.3 %collective-permute-start.12 = (bf16[14,3,512]{2,1,0:T(4,128)(2,1)S(1)}, bf16[14,3,512]{2,1,0:T(4,128)(2,1)S(1)}, u32[]{:S(2)}, u32[]{:S(2)}) collective-permute-start(bf16[14,3,512]{2,1,0:T(4,128)(2,1)S(1)} %get-tuple-element.103), channel_id=1, source_target_pairs={{0,1},{1,0},{2,3},{3,2},{4,5},{5,4},{6,7},{7,6},{8,9},{9,8},{10,11... | collective-permute-start | bytes 129032 | tf_op jit(solution)/shard_map/ppermute | solution.py:342
  50.4 0.9 %collective-permute-done.12.col_one = bf16[14,3,512]{2,1,0:T(4,128)(2,1)S(1)} collective-permute-done((bf16[14,3,512]{2,1,0:T(4,128)(2,1)S(1)}, bf16[14,3,512]{2,1,0:T(4,128)(2,1)S(1)}, u32[]{:S(2)}, u32[]{:S(2)}) %collective-permute-start.12) | collective-permute-done | bytes 43040 | tf_op jit(solution)/shard_map/ppermute | solution.py:342
  51.2 1.3 %add_pair.1 = bf16[32,136,128]{2,1,0:T(8,128)(2,1)} custom-call(bf16[32,128,128]{2,1,0:T(8,128)(2,1)S(1)} %get-tuple-element.71.one, bf16[32,128,128]{2,1,0:T(8,128)(2,1)S(1)} %collective-permute-done.6.two, bf16[32,8,128]{2,1,0:T(8,128)(2,1)S(1)} %get-tuple-element.81.small_one, bf16[32,8,128]{2,1,0:T(8,128)(2,1)S(1)} %collective-permute-done.7.small_two, ...), custom_call_target="tpu_custom_call" | custom-call | flops 1000000 | bytes 3000000 | tf_op jit(solution)/shard_map/add_pair/pallas_call | solution.py:276
  52.5 9.4 %all-to-all-start = ((bf16[32,136,128]{2,1,0:T(8,128)(2,1)}), bf16[32,136,128]{2,1,0:T(8,128)(2,1)S(1)}, u32[]{:S(2)}, u32[]{:S(2)}) async-start(bf16[32,136,128]{2,1,0:T(8,128)(2,1)} %add_pair.1), calls=%async_computation | async-start | bytes 2228224 | tf_op jit(solution)/shard_map/all_to_all | solution.py:404
  61.9 3.6 %features_part.1 = bf16[8,32,512]{2,1,0:T(8,128)(2,1)} custom-call(s32[3]{0:T(128)S(1)} %pad_add_fusion.place.refs_0_, bf16[8,32,512]{2,1,0:T(8,128)(2,1)S(1)} %get-tuple-element.85.d_conv, bf16[3,32,512]{2,1,0:T(8,128)(2,1)S(1)} %collective-permute-done.11.row_one, bf16[3,32,512]{2,1,0:T(8,128)(2,1)S(1)} %collective-permute-done.10.row_two, ...), custom_call_target="tpu_custom_call" | custom-call | flops 30000000 | bytes 2000000 | tf_op jit(solution)/shard_map/features_part/pallas_call | solution.py:324
  65.6 13.9 %all-to-all-done.refs_1_ = bf16[32,136,128]{2,1,0:T(8,128)(2,1)S(1)} async-done(((bf16[32,136,128]{2,1,0:T(8,128)(2,1)}), bf16[32,136,128]{2,1,0:T(8,128)(2,1)S(1)}, u32[]{:S(2)}, u32[]{:S(2)}) %all-to-all-start) | async-done | bytes 1114144 | tf_op jit(solution)/shard_map/all_to_all | solution.py:404
  79.5 1.4 %sum_chips.1 = (f32[4,2048]{1,0:T(4,128)}, f32[16,512]{1,0:T(8,128)}, f32[4,54]{1,0:T(4,128)}, f32[1,16]{1,0:T(1,128)}) custom-call(s32[3]{0:T(128)S(1)} %pad_add_fusion.place.refs_0_, bf16[32,136,128]{2,1,0:T(8,128)(2,1)S(1)} %all-to-all-done.refs_1_), custom_call_target="tpu_custom_call" | custom-call | flops 1000000 | bytes 1000000 | tf_op jit(solution)/shard_map/sum_chips/pallas_call | solution.py:304
  (17 shorter events, 0.1 us)
Async XLA Ops:
  1.6 11.8 %collective-permute-start.1 = (bf16[3,32,512]{2,1,0:T(8,128)(2,1)S(1)}, bf16[3,32,512]{2,1,0:T(8,128)(2,1)S(1)}, u32[]{:S(2)}, u32[]{:S(2)}) collective-permute-start(bf16[3,32,512]{2,1,0:T(8,128)(2,1)S(1)} %get-tuple-element.96), channel_id=1, source_target_pairs={{16,32},{32,16},{48,64},{64,48},{80,96},{96,80},{17,33},{33,17},{4... | collective-permute-start | bytes 294920 | tf_op jit(solution)/shard_map/ppermute | solution.py:342
  2.3 11.1 %collective-permute-start = (bf16[3,32,512]{2,1,0:T(8,128)(2,1)S(1)}, bf16[3,32,512]{2,1,0:T(8,128)(2,1)S(1)}, u32[]{:S(2)}, u32[]{:S(2)}) collective-permute-start(bf16[3,32,512]{2,1,0:T(8,128)(2,1)S(1)} %get-tuple-element.97), channel_id=1, source_target_pairs={{0,16},{16,0},{32,48},{48,32},{64,80},{80,64},{96,112},{112,96},{1... | collective-permute-start | bytes 294920 | tf_op jit(solution)/shard_map/ppermute | solution.py:342
  13.6 1.3 %collective-permute-start.2 = (bf16[14,3,512]{2,1,0:T(4,128)(2,1)S(1)}, bf16[14,3,512]{2,1,0:T(4,128)(2,1)S(1)}, u32[]{:S(2)}, u32[]{:S(2)}) collective-permute-start(bf16[14,3,512]{2,1,0:T(4,128)(2,1)S(1)} %get-tuple-element.51), channel_id=1, source_target_pairs={{0,1},{1,0},{2,3},{3,2},{4,5},{5,4},{6,7},{7,6},{8,9},{9,8},{10,11... | collective-permute-start | bytes 129032 | tf_op jit(solution)/shard_map/ppermute | solution.py:342
  13.7 1.2 %collective-permute-start.3 = (bf16[14,3,512]{2,1,0:T(4,128)(2,1)S(1)}, bf16[14,3,512]{2,1,0:T(4,128)(2,1)S(1)}, u32[]{:S(2)}, u32[]{:S(2)}) collective-permute-start(bf16[14,3,512]{2,1,0:T(4,128)(2,1)S(1)} %get-tuple-element.52), channel_id=1, source_target_pairs={{1,2},{2,1},{3,4},{4,3},{5,6},{6,5},{7,8},{8,7},{9,10},{10,9},{11,... | collective-permute-start | bytes 129032 | tf_op jit(solution)/shard_map/ppermute | solution.py:342
  22.8 7.6 %collective-permute-start.4 = (bf16[64,64,128]{2,1,0:T(8,128)(2,1)S(1)}, bf16[64,64,128]{2,1,0:T(8,128)(2,1)S(1)}, u32[]{:S(2)}, u32[]{:S(2)}) collective-permute-start(bf16[64,64,128]{2,1,0:T(8,128)(2,1)S(1)} %get-tuple-element.62), channel_id=1, source_target_pairs={{0,1},{1,0},{2,3},{3,2},{4,5},{5,4},{6,7},{7,6},{8,9},{9,8},{10,11... | collective-permute-start | bytes 3145736 | tf_op jit(solution)/shard_map/ppermute | solution.py:355
  27.6 3.8 %collective-permute-start.5 = (bf16[64,64,128]{2,1,0:T(8,128)(2,1)S(1)}, bf16[64,64,128]{2,1,0:T(8,128)(2,1)S(1)}, u32[]{:S(2)}, u32[]{:S(2)}) collective-permute-start(bf16[64,64,128]{2,1,0:T(8,128)(2,1)S(1)} %get-tuple-element.63), channel_id=1, source_target_pairs={{0,1},{1,0},{2,3},{3,2},{4,5},{5,4},{6,7},{7,6},{8,9},{9,8},{10,11... | collective-permute-start | bytes 3145736 | tf_op jit(solution)/shard_map/ppermute | solution.py:355
  32.3 18.9 %collective-permute-start.6 = (bf16[32,128,128]{2,1,0:T(8,128)(2,1)S(1)}, bf16[32,128,128]{2,1,0:T(8,128)(2,1)S(1)}, u32[]{:S(2)}, u32[]{:S(2)}) collective-permute-start(bf16[32,128,128]{2,1,0:T(8,128)(2,1)S(1)} %get-tuple-element.72), channel_id=1, source_target_pairs={{0,4},{1,13},{4,0},{5,9},{8,12},{9,5},{12,8},{13,1},{2,6},{3,15},{... | collective-permute-start | bytes 3145736 | tf_op jit(solution)/shard_map/ppermute | solution.py:362
  34.8 7.9 %collective-permute-start.10 = (bf16[3,32,512]{2,1,0:T(8,128)(2,1)S(1)}, bf16[3,32,512]{2,1,0:T(8,128)(2,1)S(1)}, u32[]{:S(2)}, u32[]{:S(2)}) collective-permute-start(bf16[3,32,512]{2,1,0:T(8,128)(2,1)S(1)} %get-tuple-element.79), channel_id=1, source_target_pairs={{16,32},{32,16},{48,64},{64,48},{80,96},{96,80},{17,33},{33,17},{4... | collective-permute-start | bytes 294920 | tf_op jit(solution)/shard_map/ppermute | solution.py:342
  35.5 11.7 %collective-permute-start.11 = (bf16[3,32,512]{2,1,0:T(8,128)(2,1)S(1)}, bf16[3,32,512]{2,1,0:T(8,128)(2,1)S(1)}, u32[]{:S(2)}, u32[]{:S(2)}) collective-permute-start(bf16[3,32,512]{2,1,0:T(8,128)(2,1)S(1)} %get-tuple-element.80), channel_id=1, source_target_pairs={{0,16},{16,0},{32,48},{48,32},{64,80},{80,64},{96,112},{112,96},{1... | collective-permute-start | bytes 294920 | tf_op jit(solution)/shard_map/ppermute | solution.py:342
  41.7 8.6 %collective-permute-start.9 = (bf16[32,8,128]{2,1,0:T(8,128)(2,1)S(1)}, bf16[32,8,128]{2,1,0:T(8,128)(2,1)S(1)}, u32[]{:S(2)}, u32[]{:S(2)}) collective-permute-start(bf16[32,8,128]{2,1,0:T(8,128)(2,1)S(1)} %get-tuple-element.78), channel_id=1, source_target_pairs={{0,13},{1,4},{4,9},{5,0},{8,5},{9,12},{12,1},{13,8},{2,15},{3,6},{... | collective-permute-start | bytes 196616 | tf_op jit(solution)/shard_map/ppermute | solution.py:369
  42.2 8.1 %collective-permute-start.8 = (bf16[32,8,128]{2,1,0:T(8,128)(2,1)S(1)}, bf16[32,8,128]{2,1,0:T(8,128)(2,1)S(1)}, u32[]{:S(2)}, u32[]{:S(2)}) collective-permute-start(bf16[32,8,128]{2,1,0:T(8,128)(2,1)S(1)} %get-tuple-element.78), channel_id=1, source_target_pairs={{0,4},{1,13},{4,0},{5,9},{8,12},{9,5},{12,8},{13,1},{2,6},{3,15},{... | collective-permute-start | bytes 196616 | tf_op jit(solution)/shard_map/ppermute | solution.py:362
  42.7 5.3 %collective-permute-start.7 = (bf16[32,8,128]{2,1,0:T(8,128)(2,1)S(1)}, bf16[32,8,128]{2,1,0:T(8,128)(2,1)S(1)}, u32[]{:S(2)}, u32[]{:S(2)}) collective-permute-start(bf16[32,8,128]{2,1,0:T(8,128)(2,1)S(1)} %get-tuple-element.81.small_one), channel_id=1, source_target_pairs={{0,1},{1,0},{2,3},{3,2},{4,5},{5,4},{6,7},{7,6},{8,9},{9,8},{10,11... | collective-permute-start | bytes 196616 | tf_op jit(solution)/shard_map/ppermute | solution.py:355
  47.3 3.0 %collective-permute-start.13 = (bf16[14,3,512]{2,1,0:T(4,128)(2,1)S(1)}, bf16[14,3,512]{2,1,0:T(4,128)(2,1)S(1)}, u32[]{:S(2)}, u32[]{:S(2)}) collective-permute-start(bf16[14,3,512]{2,1,0:T(4,128)(2,1)S(1)} %get-tuple-element.102), channel_id=1, source_target_pairs={{1,2},{2,1},{3,4},{4,3},{5,6},{6,5},{7,8},{8,7},{9,10},{10,9},{11,... | collective-permute-start | bytes 129032 | tf_op jit(solution)/shard_map/ppermute | solution.py:342
  48.0 3.2 %collective-permute-start.12 = (bf16[14,3,512]{2,1,0:T(4,128)(2,1)S(1)}, bf16[14,3,512]{2,1,0:T(4,128)(2,1)S(1)}, u32[]{:S(2)}, u32[]{:S(2)}) collective-permute-start(bf16[14,3,512]{2,1,0:T(4,128)(2,1)S(1)} %get-tuple-element.103), channel_id=1, source_target_pairs={{0,1},{1,0},{2,3},{3,2},{4,5},{5,4},{6,7},{7,6},{8,9},{9,8},{10,11... | collective-permute-start | bytes 129032 | tf_op jit(solution)/shard_map/ppermute | solution.py:342
  52.5 27.0 %all-to-all-start = ((bf16[32,136,128]{2,1,0:T(8,128)(2,1)}), bf16[32,136,128]{2,1,0:T(8,128)(2,1)S(1)}, u32[]{:S(2)}, u32[]{:S(2)}) async-start(bf16[32,136,128]{2,1,0:T(8,128)(2,1)} %add_pair.1), calls=%async_computation | async-start | bytes 2228224 | tf_op jit(solution)/shard_map/all_to_all | solution.py:404

commit v7 on v6

--- a/solution.py
+++ b/solution.py
@@ -8,10 +8,10 @@
 from jax.sharding import Mesh
 from jax.sharding import PartitionSpec as P
 
-EVERY = ("z", "yh", "xh", "xl", "yl", "c")
-ROW = ("z", "yh")
+EVERY = ("zh", "zl", "yh", "xh", "xl", "yl", "c")
+ROW = ("zh", "zl", "yh")
 COL = ("xh", "xl", "yl", "c")
-GROUP = ("z", "yh", "xh", "yl")
+GROUP = ("zh", "yh", "xh", "yl")
 ROWS, COLS, CH, HID, CHUNK = 8, 32, 512, 2048, 512
 COUNT = ROWS * COLS
 STEPS = HID // CHUNK
@@ -265,21 +265,43 @@
     )(place, *(near(value) for value in operands))
 
 
-def add_kernel(one, two, small_one, small_two, small_three, small_four, total):
-    total[:, 0:128, :] = one[...] + two[...]
+def add_kernel(place, one, two, small_one, small_two, small_three, small_four, keep, give):
+    even = place[3] == 0
     small = small_one[...].astype(F32) + small_two[...].astype(F32)
-    small = small + small_three[...].astype(F32) + small_four[...].astype(F32)
-    total[:, 128:136, :] = small.astype(BF16)
-
-
-def add_pair(*operands):
+    small = (small + small_three[...].astype(F32) + small_four[...].astype(F32)).astype(BF16)
+    for k in range(2):
+        at = slice(8 * k, 8 * k + 8)
+        low, high = slice(16 * k, 16 * k + 8), slice(16 * k + 8, 16 * k + 16)
+        total = one[low] + two[low], one[high] + two[high]
+        keep[at, 0:128, :] = jnp.where(even, total[0], total[1])
+        give[at, 0:128, :] = jnp.where(even, total[1], total[0])
+        keep[at, 128:136, :] = jnp.where(even, small[low], small[high])
+        give[at, 128:136, :] = jnp.where(even, small[high], small[low])
+
+
+def add_pair(place, *operands):
     return pl.pallas_call(
         add_kernel,
-        in_specs=[WHOLE] * len(operands),
-        out_shape=jax.ShapeDtypeStruct((32, 136, 128), BF16),
+        in_specs=[SCALARS] + [WHOLE] * len(operands),
+        out_shape=[pltpu.VMEM((16, 136, 128), BF16)] * 2,
         compiler_params=params(),
         cost_estimate=cost(1_000_000, 3_000_000),
         name="add_pair",
+    )(place, *(near(value) for value in operands))
+
+
+def add_last_kernel(one, two, total):
+    total[...] = one[...] + two[...]
+
+
+def add_last(*operands):
+    return pl.pallas_call(
+        add_last_kernel,
+        in_specs=[WHOLE] * 2,
+        out_shape=pltpu.VMEM((16, 136, 128), BF16),
+        compiler_params=params(),
+        cost_estimate=cost(1_000_000, 1_000_000),
+        name="add_last",
     )(*(near(value) for value in operands))
 
 
@@ -355,11 +377,11 @@
     return lax.ppermute(value, "c", [(0, 1), (1, 0)])
 
 
-def swap_chips(value):
+def swap_chips(value, axes):
     pairs = []
-    for x in range(4):
-        pairs += [(2 * x, 2 * (x ^ 1)), (2 * x + 1, 2 * (3 - x) + 1)]
-    return lax.ppermute(value, ("xh", "xl", "c"), pairs)
+    for at in range(4):
+        pairs += [(2 * at, 2 * (at ^ 1)), (2 * at + 1, 2 * (3 - at) + 1)]
+    return lax.ppermute(value, axes + ("c",), pairs)
 
 
 def swap_across(value):
@@ -374,8 +396,8 @@
     pw_in_weight, pw_in_bias, pw_out_weight, pw_out_bias, layer_scale,
 ):
     factor = 1.0 / math.sqrt(COUNT * lax.axis_size(EVERY))
-    core, y_hi, x_lo = (lax.axis_index(name).astype(jnp.int32) for name in ("c", "yh", "xl"))
-    place = jnp.stack([core, y_hi, x_lo])
+    core, y_hi, x_lo, z_lo = (lax.axis_index(name).astype(jnp.int32) for name in ("c", "yh", "xl", "zl"))
+    place = jnp.stack([core, y_hi, x_lo, z_lo])
     even_row, even_col = y_hi == 0, core == 0
     vectors = jnp.stack([dw_bias, norm_gain_vector, norm_bias, layer_scale, pw_out_bias])
     ends = features[:3], features[ROWS - 3 :]
@@ -394,13 +416,18 @@
     small_keep, small_give = tap_rows(place, pad, d_conv, rows)
     met_out, met_in, small_keep, small_give = lax.optimization_barrier((met_out, met_in, small_keep, small_give))
     keep, give = split_pair(place, mine_out, met_out, mine_in, met_in)
-    given = swap_chips(give)
+    along_x, along_z = ("xh", "xl"), ("zh", "zl")
+    given = swap_chips(give, along_x)
     small_keep, small_give, give, d_one, d_two = lax.optimization_barrier((small_keep, small_give, give, d_one, d_two))
-    smalls = small_keep, swap_cores(small_keep), swap_chips(small_give), swap_across(small_give)
+    smalls = small_keep, swap_cores(small_keep), swap_chips(small_give, along_x), swap_across(small_give)
     d_rows = exchange(d_one, d_two, ROW)
+    smalls, d_rows = lax.optimization_barrier((smalls, d_rows))
+    keep, give = add_pair(place, keep, given, *smalls)
+    given = swap_chips(give, along_z)
+    give, d_rows = lax.optimization_barrier((give, d_rows))
     d_cols = exchange(*halo_sides(*d_rows, d_conv, even_row, even_col), COL)
-    smalls, d_cols = lax.optimization_barrier((smalls, d_cols))
-    message = add_pair(keep, given, *smalls)
+    given, d_cols = lax.optimization_barrier((given, d_cols))
+    message = add_last(keep, given)
     spread = lax.all_to_all(message, GROUP, 0, 0, tiled=True)
     d_conv, message = lax.optimization_barrier((d_conv, message))
     grad_features = features_part(place, d_conv, *d_rows, *d_cols, cot, taps)
@@ -416,7 +443,7 @@
 
 
 def solution(mesh):
-    fine = Mesh(mesh.devices.reshape(4, 2, 2, 2, 2, 2), EVERY)
+    fine = Mesh(mesh.devices.reshape(2, 2, 2, 2, 2, 2, 2), EVERY)
     return jax.shard_map(
         shards,
         mesh=fine,

time: 81.3 us -> 84.8 us (1.043)
  waiting for transfers between devices: 18.5 us -> 23.7 us
  starting transfers between devices: 37.4 us -> 35.3 us
    ppermute x2 -> x3, waiting for transfers between devices: 0.01 us -> 10.9 us  [swap_chips(): return lax.ppermute(value, axes + ('c',), pairs)]
    all_to_all x1, waiting for transfers between devices: 13.9 us -> 9.72 us  [shards(): spread = lax.all_to_all(message, GROUP, 0, 0, tiled=True)]
    ppermute x8, starting transfers between devices: 17.6 us -> 13.8 us  [exchange(): met.append(lax.ppermute(value, axis, pairs))]
    ppermute x8, waiting for transfers between devices: 3.63 us -> 1.38 us  [exchange(): met.append(lax.ppermute(value, axis, pairs))]
    ppermute x2 -> x3, starting transfers between devices: 2.91 us -> 5.07 us  [swap_chips(): return lax.ppermute(value, axes + ('c',), pairs)]
    ppermute x3, starting transfers between devices: 6.96 us -> 5.89 us  [swap_cores(): return lax.ppermute(value, 'c', [(0, 1), (1, 0)])]
    pallas_call x1 -> x2, Pallas kernels: 1.29 us -> 1.78 us  [the longest x1 0.93 us: add_last(): pl.pallas_call(add_last_kernel, in_specs=[WHOLE] * 2, out_shape=pltpu.VME...]
  transfers between devices with their start and end apart: 15 -> 16, of which waited for: 5 -> 7; matrix products, arithmetic and copies ran while one was open for 3% -> 3% of each run, Pallas kernels for 11% -> 11%
where the time goes in v7:
time: 84.8 us; the launch traced here: 84.4 us
  starting transfers between devices  35.3 us (42%)
  waiting for transfers between devices  23.7 us (28%)
  Pallas kernels  21 us (25%)
  local copies, waits for them, and re-layouts  2.36 us (3%)
  other arithmetic  1.27 us (1%)
    ppermute x8, starting transfers between devices, exchange(): met.append(lax.ppermute(value, axis, pairs))  13.8 us
    ppermute x3, waiting for transfers between devices, swap_chips(): return lax.ppermute(value, axes + ('c',), pairs)  10.9 us
    all_to_all x1, waiting for transfers between devices, shards(): spread = lax.all_to_all(message, GROUP, 0, 0, tiled=True)  9.72 us
    all_to_all x1, starting transfers between devices, shards(): spread = lax.all_to_all(message, GROUP, 0, 0, tiled=True)  9.39 us
    pallas_call x1, Pallas kernels, grads(): pl.pallas_call(grads_kernel, in_specs=[SCALARS] + [WHOLE] * len(operands)...  7.95 us
    ppermute x3, starting transfers between devices, swap_cores(): return lax.ppermute(value, 'c', [(0, 1), (1, 0)])  5.89 us
    ppermute x3, starting transfers between devices, swap_chips(): return lax.ppermute(value, axes + ('c',), pairs)  5.07 us
    pallas_call x1, Pallas kernels, features_part(): pl.pallas_call(features_kernel, in_specs=[SCALARS] + [WHOLE] * len(operan...  3.65 us
  transfers between devices with their start and end apart: 16, of which 7 were waited for; matrix products, arithmetic and copies ran while one was open for 3% of the time, Pallas kernels for 11%

profile of v7, /device:TPU:0, one launch (start us, length us, event | category | flops | bytes accessed | tf_op | source)
XLA Modules:
  0.0 84.4 jit_solution(5504703928289705878)
XLA Ops:
  0.6 1.0 %broadcast_select_fusion.4 = (bf16[3,32,512]{2,1,0:T(8,128)(2,1)S(1)}, bf16[3,32,512]{2,1,0:T(8,128)(2,1)S(1)}) fusion(pred[]{:T(512)S(6)} %eq.6, bf16[8,32,512]{2,1,0:T(8,128)(2,1)} %refs_0_.1), kind=kLoop, calls=%fused_computation.4 | loop fusion | flops 98304 | bytes 393217 | tf_op jit(solution)/shard_map/jit(_where)/select_n | solution.py:404
  1.6 0.7 collective-permute-start.1
  2.3 6.3 %collective-permute-start = (bf16[3,32,512]{2,1,0:T(8,128)(2,1)S(1)}, bf16[3,32,512]{2,1,0:T(8,128)(2,1)S(1)}, u32[]{:S(2)}, u32[]{:S(2)}) collective-permute-start(bf16[3,32,512]{2,1,0:T(8,128)(2,1)S(1)} %get-tuple-element.111), channel_id=1, source_target_pairs={{0,16},{16,0},{32,48},{48,32},{64,80},{80,64},{96,112},{112,96},{1... | collective-permute-start | bytes 294920 | tf_op jit(solution)/shard_map/ppermute | solution.py:364
  8.6 0.9 %fusion.1 = (bf16[8,3,512]{2,1,0:T(4,128)(2,1)S(1)}, bf16[8,3,512]{2,1,0:T(4,128)(2,1)S(1)}) fusion(bf16[8,32,512]{2,1,0:T(8,128)(2,1)} %refs_0_.1), kind=kLoop, calls=%fused_computation.16 | loop fusion | bytes 98304 | tf_op jit(solution)/shard_map/slice | solution.py:371
  9.5 1.4 %stack.43.refs_3_ = f32[5,512]{1,0:T(8,128)} concatenate(f32[1,512]{1,0:T(1,128)} %bitcast.16, f32[1,512]{1,0:T(1,128)} %bitcast.17, f32[1,512]{1,0:T(1,128)} %bitcast.18, f32[1,512]{1,0:T(1,128)} %bitcast.19, f32[1,512]{1,0:T(1,128)} %bitcast.20), dimensions={0} | concatenate | bytes 20480 | tf_op jit(solution)/shard_map/stack | solution.py:402
  10.8 2.5 %fetch.1 = (bf16[8,32,512]{2,1,0:T(8,128)(2,1)S(1)}, bf16[256,512]{1,0:T(8,128)(2,1)S(1)}, f32[49,512]{1,0:T(8,128)S(1)}, f32[5,512]{1,0:T(8,128)S(1)}, bf16[512...) custom-call(bf16[8,32,512]{2,1,0:T(8,128)(2,1)} %refs_0_.1, ...), custom_call_target="tpu_custom_call" | custom-call | bytes 5000000 | tf_op jit(solution)/shard_map/fetch/pallas_call | solution.py:64
  13.7 0.7 collective-permute-start.3
  14.4 0.5 collective-permute-done.2.col_one
  14.9 7.9 %grads.1 = (f32[4,14,40,128]{3,2,1,0:T(8,128)S(1)}, bf16[256,512]{1,0:T(8,128)(2,1)}, bf16[8,32,512]{2,1,0:T(8,128)(2,1)S(1)}, bf16[3,32,512]{2,1,0:T(8,128)(2,1...) custom-call(s32[4]{0:T(128)S(1)} %pad_add_fusion.place.refs_0_, ...), custom_call_target="tpu_custom_call" | custom-call | flops 3200000000 | bytes 12000000 | tf_op jit(solution)/shard_map/grads/pallas_call | solution.py:187
  22.8 4.8 %collective-permute-start.4 = (bf16[64,64,128]{2,1,0:T(8,128)(2,1)S(1)}, bf16[64,64,128]{2,1,0:T(8,128)(2,1)S(1)}, u32[]{:S(2)}, u32[]{:S(2)}) collective-permute-start(bf16[64,64,128]{2,1,0:T(8,128)(2,1)S(1)} %get-tuple-element.69), channel_id=1, source_target_pairs={{0,1},{1,0},{2,3},{3,2},{4,5},{5,4},{6,7},{7,6},{8,9},{9,8},{10,11... | collective-permute-start | bytes 3145736 | tf_op jit(solution)/shard_map/ppermute | solution.py:377
  27.6 2.8 %tap_rows.1 = (bf16[32,8,128]{2,1,0:T(8,128)(2,1)S(1)}, bf16[32,8,128]{2,1,0:T(8,128)(2,1)S(1)}) custom-call(s32[4]{0:T(128)S(1)} %pad_add_fusion.place.refs_0_, f32[4,14,40,128]{3,2,1,0:T(8,128)S(1)} %get-tuple-element.71.pad, bf16[8,32,512]{2,1,0:T(8,128)(2,1)S(1)} %get-tuple-element.99.d_conv, f32[16,512]{1,0:T(8,128)S(1)} %get-tuple-element.72.rows), custom_call_target="tpu_custom_call" | custom-call | flops 30000000 | bytes 2000000 | tf_op jit(solution)/shard_map/tap_rows/pallas_call | solution.py:237
  30.5 0.9 %collective-permute-done.5.in_two = bf16[64,64,128]{2,1,0:T(8,128)(2,1)S(1)} collective-permute-done((bf16[64,64,128]{2,1,0:T(8,128)(2,1)S(1)}, bf16[64,64,128]{2,1,0:T(8,128)(2,1)S(1)}, u32[]{:S(2)}, u32[]{:S(2)}) %collective-permute-start.5) | collective-permute-done | bytes 1048608 | tf_op jit(solution)/shard_map/ppermute | solution.py:377
  31.4 0.9 %split_pair.1 = (bf16[32,128,128]{2,1,0:T(8,128)(2,1)S(1)}, bf16[32,128,128]{2,1,0:T(8,128)(2,1)S(1)}) custom-call(s32[4]{0:T(128)S(1)} %pad_add_fusion.place.refs_0_, bf16[64,64,128]{2,1,0:T(8,128)(2,1)S(1)} %get-tuple-element.68.out_one, bf16[64,64,128]{2,1,0:T(8,128)(2,1)S(1)} %collective-permute-done.4.out_two, ...), custom_call_target="tpu_custom_call" | custom-call | flops 1000000 | bytes 6000000 | tf_op jit(solution)/shard_map/split_pair/pallas_call | solution.py:258
  32.3 2.5 %collective-permute-start.6 = (bf16[32,128,128]{2,1,0:T(8,128)(2,1)S(1)}, bf16[32,128,128]{2,1,0:T(8,128)(2,1)S(1)}, u32[]{:S(2)}, u32[]{:S(2)}) collective-permute-start(bf16[32,128,128]{2,1,0:T(8,128)(2,1)S(1)} %get-tuple-element.79), channel_id=1, source_target_pairs={{0,4},{1,13},{4,0},{5,9},{8,12},{9,5},{12,8},{13,1},{2,6},{3,15},{... | collective-permute-start | bytes 3145736 | tf_op jit(solution)/shard_map/ppermute | solution.py:384
  34.8 1.1 %collective-permute-start.7 = (bf16[32,8,128]{2,1,0:T(8,128)(2,1)S(1)}, bf16[32,8,128]{2,1,0:T(8,128)(2,1)S(1)}, u32[]{:S(2)}, u32[]{:S(2)}) collective-permute-start(bf16[32,8,128]{2,1,0:T(8,128)(2,1)S(1)} %get-tuple-element.88.small_one), channel_id=1, source_target_pairs={{0,1},{1,0},{2,3},{3,2},{4,5},{5,4},{6,7},{7,6},{8,9},{9,8},{10,11... | collective-permute-start | bytes 196616 | tf_op jit(solution)/shard_map/ppermute | solution.py:377
  35.9 1.1 %collective-permute-start.9 = (bf16[32,8,128]{2,1,0:T(8,128)(2,1)S(1)}, bf16[32,8,128]{2,1,0:T(8,128)(2,1)S(1)}, u32[]{:S(2)}, u32[]{:S(2)}) collective-permute-start(bf16[32,8,128]{2,1,0:T(8,128)(2,1)S(1)} %get-tuple-element.85), channel_id=1, source_target_pairs={{0,13},{1,4},{4,9},{5,0},{8,5},{9,12},{12,1},{13,8},{2,15},{3,6},{... | collective-permute-start | bytes 196616 | tf_op jit(solution)/shard_map/ppermute | solution.py:391
  37.0 0.6 collective-permute-start.8
  37.6 1.3 %collective-permute-start.10 = (bf16[3,32,512]{2,1,0:T(8,128)(2,1)S(1)}, bf16[3,32,512]{2,1,0:T(8,128)(2,1)S(1)}, u32[]{:S(2)}, u32[]{:S(2)}) collective-permute-start(bf16[3,32,512]{2,1,0:T(8,128)(2,1)S(1)} %get-tuple-element.86), channel_id=1, source_target_pairs={{0,16},{16,0},{32,48},{48,32},{64,80},{80,64},{96,112},{112,96},{1... | collective-permute-start | bytes 294920 | tf_op jit(solution)/shard_map/ppermute | solution.py:364
  38.9 0.7 collective-permute-start.11
  39.6 0.8 collective-permute-done.9.small_four
  40.4 8.6 %collective-permute-done.8.small_three = bf16[32,8,128]{2,1,0:T(8,128)(2,1)S(1)} collective-permute-done((bf16[32,8,128]{2,1,0:T(8,128)(2,1)S(1)}, bf16[32,8,128]{2,1,0:T(8,128)(2,1)S(1)}, u32[]{:S(2)}, u32[]{:S(2)}) %collective-permute-start.8) | collective-permute-done | bytes 65568 | tf_op jit(solution)/shard_map/ppermute | solution.py:384
  49.0 0.8 %add_pair.1 = (bf16[16,136,128]{2,1,0:T(8,128)(2,1)S(1)}, bf16[16,136,128]{2,1,0:T(8,128)(2,1)S(1)}) custom-call(s32[4]{0:T(128)S(1)} %pad_add_fusion.place.refs_0_, bf16[32,128,128]{2,1,0:T(8,128)(2,1)S(1)} %get-tuple-element.78.one, bf16[32,128,128]{2,1,0:T(8,128)(2,1)S(1)} %collective-permute-done.6.two, ...), custom_call_target="tpu_custom_call" | custom-call | flops 1000000 | bytes 3000000 | tf_op jit(solution)/shard_map/add_pair/pallas_call | solution.py:283
  49.8 2.0 %collective-permute-start.12 = (bf16[16,136,128]{2,1,0:T(8,128)(2,1)S(1)}, bf16[16,136,128]{2,1,0:T(8,128)(2,1)S(1)}, u32[]{:S(2)}, u32[]{:S(2)}) collective-permute-start(bf16[16,136,128]{2,1,0:T(8,128)(2,1)S(1)} %get-tuple-element.93), channel_id=1, source_target_pairs={{0,32},{1,97},{32,0},{33,65},{64,96},{65,33},{96,64},{97,1},{2,34}... | collective-permute-start | bytes 1671176 | tf_op jit(solution)/shard_map/ppermute | solution.py:384
  52.0 0.7 collective-permute-start.14
  52.7 3.5 %collective-permute-start.13 = (bf16[14,3,512]{2,1,0:T(4,128)(2,1)S(1)}, bf16[14,3,512]{2,1,0:T(4,128)(2,1)S(1)}, u32[]{:S(2)}, u32[]{:S(2)}) collective-permute-start(bf16[14,3,512]{2,1,0:T(4,128)(2,1)S(1)} %get-tuple-element.117), channel_id=1, source_target_pairs={{0,1},{1,0},{2,3},{3,2},{4,5},{5,4},{6,7},{7,6},{8,9},{9,8},{10,11... | collective-permute-start | bytes 129032 | tf_op jit(solution)/shard_map/ppermute | solution.py:364
  56.2 0.9 %collective-permute-done.13.col_one = bf16[14,3,512]{2,1,0:T(4,128)(2,1)S(1)} collective-permute-done((bf16[14,3,512]{2,1,0:T(4,128)(2,1)S(1)}, bf16[14,3,512]{2,1,0:T(4,128)(2,1)S(1)}, u32[]{:S(2)}, u32[]{:S(2)}) %collective-permute-start.13) | collective-permute-done | bytes 43040 | tf_op jit(solution)/shard_map/ppermute | solution.py:364
  57.1 2.3 %collective-permute-done.12.two = bf16[16,136,128]{2,1,0:T(8,128)(2,1)S(1)} collective-permute-done((bf16[16,136,128]{2,1,0:T(8,128)(2,1)S(1)}, bf16[16,136,128]{2,1,0:T(8,128)(2,1)S(1)}, u32[]{:S(2)}, u32[]{:S(2)}) %collective-permute-start.12) | collective-permute-done | bytes 557088 | tf_op jit(solution)/shard_map/ppermute | solution.py:384
  59.5 0.9 %add_last.1 = bf16[16,136,128]{2,1,0:T(8,128)(2,1)} custom-call(bf16[16,136,128]{2,1,0:T(8,128)(2,1)S(1)} %get-tuple-element.92.one, bf16[16,136,128]{2,1,0:T(8,128)(2,1)S(1)} %collective-permute-done.12.two), custom_call_target="tpu_custom_call" | custom-call | flops 1000000 | bytes 1000000 | tf_op jit(solution)/shard_map/add_last/pallas_call | solution.py:298
  60.4 9.4 %all-to-all-start = ((bf16[16,136,128]{2,1,0:T(8,128)(2,1)}), bf16[16,136,128]{2,1,0:T(8,128)(2,1)S(1)}, u32[]{:S(2)}, u32[]{:S(2)}) async-start(bf16[16,136,128]{2,1,0:T(8,128)(2,1)} %add_last.1), calls=%async_computation | async-start | bytes 1114112 | tf_op jit(solution)/shard_map/all_to_all | solution.py:431
  69.8 3.6 %features_part.1 = bf16[8,32,512]{2,1,0:T(8,128)(2,1)} custom-call(s32[4]{0:T(128)S(1)} %pad_add_fusion.place.refs_0_, bf16[8,32,512]{2,1,0:T(8,128)(2,1)S(1)} %get-tuple-element.99.d_conv, bf16[3,32,512]{2,1,0:T(8,128)(2,1)S(1)} %collective-permute-done.10.row_one, bf16[3,32,512]{2,1,0:T(8,128)(2,1)S(1)} %collective-permute-done.11.row_two, ...), custom_call_target="tpu_custom_call" | custom-call | flops 30000000 | bytes 2000000 | tf_op jit(solution)/shard_map/features_part/pallas_call | solution.py:346
  73.4 9.7 %all-to-all-done.refs_1_ = bf16[16,136,128]{2,1,0:T(8,128)(2,1)S(1)} async-done(((bf16[16,136,128]{2,1,0:T(8,128)(2,1)}), bf16[16,136,128]{2,1,0:T(8,128)(2,1)S(1)}, u32[]{:S(2)}, u32[]{:S(2)}) %all-to-all-start) | async-done | bytes 557088 | tf_op jit(solution)/shard_map/all_to_all | solution.py:431
  83.2 1.3 %sum_chips.1 = (f32[4,2048]{1,0:T(4,128)}, f32[16,512]{1,0:T(8,128)}, f32[4,54]{1,0:T(4,128)}, f32[1,16]{1,0:T(1,128)}) custom-call(s32[4]{0:T(128)S(1)} %pad_add_fusion.place.refs_0_, bf16[16,136,128]{2,1,0:T(8,128)(2,1)S(1)} %all-to-all-done.refs_1_), custom_call_target="tpu_custom_call" | custom-call | flops 1000000 | bytes 1000000 | tf_op jit(solution)/shard_map/sum_chips/pallas_call | solution.py:326
  (20 shorter events, 0.5 us)
Async XLA Ops:
  1.6 11.8 %collective-permute-start.1 = (bf16[3,32,512]{2,1,0:T(8,128)(2,1)S(1)}, bf16[3,32,512]{2,1,0:T(8,128)(2,1)S(1)}, u32[]{:S(2)}, u32[]{:S(2)}) collective-permute-start(bf16[3,32,512]{2,1,0:T(8,128)(2,1)S(1)} %get-tuple-element.110), channel_id=1, source_target_pairs={{16,32},{32,16},{48,64},{64,48},{80,96},{96,80},{17,33},{33,17},{4... | collective-permute-start | bytes 294920 | tf_op jit(solution)/shard_map/ppermute | solution.py:364
  2.3 11.1 %collective-permute-start = (bf16[3,32,512]{2,1,0:T(8,128)(2,1)S(1)}, bf16[3,32,512]{2,1,0:T(8,128)(2,1)S(1)}, u32[]{:S(2)}, u32[]{:S(2)}) collective-permute-start(bf16[3,32,512]{2,1,0:T(8,128)(2,1)S(1)} %get-tuple-element.111), channel_id=1, source_target_pairs={{0,16},{16,0},{32,48},{48,32},{64,80},{80,64},{96,112},{112,96},{1... | collective-permute-start | bytes 294920 | tf_op jit(solution)/shard_map/ppermute | solution.py:364
  13.6 1.3 %collective-permute-start.2 = (bf16[14,3,512]{2,1,0:T(4,128)(2,1)S(1)}, bf16[14,3,512]{2,1,0:T(4,128)(2,1)S(1)}, u32[]{:S(2)}, u32[]{:S(2)}) collective-permute-start(bf16[14,3,512]{2,1,0:T(4,128)(2,1)S(1)} %get-tuple-element.58), channel_id=1, source_target_pairs={{0,1},{1,0},{2,3},{3,2},{4,5},{5,4},{6,7},{7,6},{8,9},{9,8},{10,11... | collective-permute-start | bytes 129032 | tf_op jit(solution)/shard_map/ppermute | solution.py:364
  13.7 1.2 %collective-permute-start.3 = (bf16[14,3,512]{2,1,0:T(4,128)(2,1)S(1)}, bf16[14,3,512]{2,1,0:T(4,128)(2,1)S(1)}, u32[]{:S(2)}, u32[]{:S(2)}) collective-permute-start(bf16[14,3,512]{2,1,0:T(4,128)(2,1)S(1)} %get-tuple-element.59), channel_id=1, source_target_pairs={{1,2},{2,1},{3,4},{4,3},{5,6},{6,5},{7,8},{8,7},{9,10},{10,9},{11,... | collective-permute-start | bytes 129032 | tf_op jit(solution)/shard_map/ppermute | solution.py:364
  22.8 7.6 %collective-permute-start.4 = (bf16[64,64,128]{2,1,0:T(8,128)(2,1)S(1)}, bf16[64,64,128]{2,1,0:T(8,128)(2,1)S(1)}, u32[]{:S(2)}, u32[]{:S(2)}) collective-permute-start(bf16[64,64,128]{2,1,0:T(8,128)(2,1)S(1)} %get-tuple-element.69), channel_id=1, source_target_pairs={{0,1},{1,0},{2,3},{3,2},{4,5},{5,4},{6,7},{7,6},{8,9},{9,8},{10,11... | collective-permute-start | bytes 3145736 | tf_op jit(solution)/shard_map/ppermute | solution.py:377
  27.6 3.8 %collective-permute-start.5 = (bf16[64,64,128]{2,1,0:T(8,128)(2,1)S(1)}, bf16[64,64,128]{2,1,0:T(8,128)(2,1)S(1)}, u32[]{:S(2)}, u32[]{:S(2)}) collective-permute-start(bf16[64,64,128]{2,1,0:T(8,128)(2,1)S(1)} %get-tuple-element.70), channel_id=1, source_target_pairs={{0,1},{1,0},{2,3},{3,2},{4,5},{5,4},{6,7},{7,6},{8,9},{9,8},{10,11... | collective-permute-start | bytes 3145736 | tf_op jit(solution)/shard_map/ppermute | solution.py:377
  32.3 16.6 %collective-permute-start.6 = (bf16[32,128,128]{2,1,0:T(8,128)(2,1)S(1)}, bf16[32,128,128]{2,1,0:T(8,128)(2,1)S(1)}, u32[]{:S(2)}, u32[]{:S(2)}) collective-permute-start(bf16[32,128,128]{2,1,0:T(8,128)(2,1)S(1)} %get-tuple-element.79), channel_id=1, source_target_pairs={{0,4},{1,13},{4,0},{5,9},{8,12},{9,5},{12,8},{13,1},{2,6},{3,15},{... | collective-permute-start | bytes 3145736 | tf_op jit(solution)/shard_map/ppermute | solution.py:384
  34.8 4.1 %collective-permute-start.7 = (bf16[32,8,128]{2,1,0:T(8,128)(2,1)S(1)}, bf16[32,8,128]{2,1,0:T(8,128)(2,1)S(1)}, u32[]{:S(2)}, u32[]{:S(2)}) collective-permute-start(bf16[32,8,128]{2,1,0:T(8,128)(2,1)S(1)} %get-tuple-element.88.small_one), channel_id=1, source_target_pairs={{0,1},{1,0},{2,3},{3,2},{4,5},{5,4},{6,7},{7,6},{8,9},{9,8},{10,11... | collective-permute-start | bytes 196616 | tf_op jit(solution)/shard_map/ppermute | solution.py:377
  35.9 4.5 %collective-permute-start.9 = (bf16[32,8,128]{2,1,0:T(8,128)(2,1)S(1)}, bf16[32,8,128]{2,1,0:T(8,128)(2,1)S(1)}, u32[]{:S(2)}, u32[]{:S(2)}) collective-permute-start(bf16[32,8,128]{2,1,0:T(8,128)(2,1)S(1)} %get-tuple-element.85), channel_id=1, source_target_pairs={{0,13},{1,4},{4,9},{5,0},{8,5},{9,12},{12,1},{13,8},{2,15},{3,6},{... | collective-permute-start | bytes 196616 | tf_op jit(solution)/shard_map/ppermute | solution.py:391
  37.0 12.0 %collective-permute-start.8 = (bf16[32,8,128]{2,1,0:T(8,128)(2,1)S(1)}, bf16[32,8,128]{2,1,0:T(8,128)(2,1)S(1)}, u32[]{:S(2)}, u32[]{:S(2)}) collective-permute-start(bf16[32,8,128]{2,1,0:T(8,128)(2,1)S(1)} %get-tuple-element.85), channel_id=1, source_target_pairs={{0,4},{1,13},{4,0},{5,9},{8,12},{9,5},{12,8},{13,1},{2,6},{3,15},{... | collective-permute-start | bytes 196616 | tf_op jit(solution)/shard_map/ppermute | solution.py:384
  37.6 11.4 %collective-permute-start.10 = (bf16[3,32,512]{2,1,0:T(8,128)(2,1)S(1)}, bf16[3,32,512]{2,1,0:T(8,128)(2,1)S(1)}, u32[]{:S(2)}, u32[]{:S(2)}) collective-permute-start(bf16[3,32,512]{2,1,0:T(8,128)(2,1)S(1)} %get-tuple-element.86), channel_id=1, source_target_pairs={{0,16},{16,0},{32,48},{48,32},{64,80},{80,64},{96,112},{112,96},{1... | collective-permute-start | bytes 294920 | tf_op jit(solution)/shard_map/ppermute | solution.py:364
  38.9 10.1 %collective-permute-start.11 = (bf16[3,32,512]{2,1,0:T(8,128)(2,1)S(1)}, bf16[3,32,512]{2,1,0:T(8,128)(2,1)S(1)}, u32[]{:S(2)}, u32[]{:S(2)}) collective-permute-start(bf16[3,32,512]{2,1,0:T(8,128)(2,1)S(1)} %get-tuple-element.87), channel_id=1, source_target_pairs={{16,32},{32,16},{48,64},{64,48},{80,96},{96,80},{17,33},{33,17},{4... | collective-permute-start | bytes 294920 | tf_op jit(solution)/shard_map/ppermute | solution.py:364
  49.8 9.6 %collective-permute-start.12 = (bf16[16,136,128]{2,1,0:T(8,128)(2,1)S(1)}, bf16[16,136,128]{2,1,0:T(8,128)(2,1)S(1)}, u32[]{:S(2)}, u32[]{:S(2)}) collective-permute-start(bf16[16,136,128]{2,1,0:T(8,128)(2,1)S(1)} %get-tuple-element.93), channel_id=1, source_target_pairs={{0,32},{1,97},{32,0},{33,65},{64,96},{65,33},{96,64},{97,1},{2,34}... | collective-permute-start | bytes 1671176 | tf_op jit(solution)/shard_map/ppermute | solution.py:384
  52.0 4.2 %collective-permute-start.14 = (bf16[14,3,512]{2,1,0:T(4,128)(2,1)S(1)}, bf16[14,3,512]{2,1,0:T(4,128)(2,1)S(1)}, u32[]{:S(2)}, u32[]{:S(2)}) collective-permute-start(bf16[14,3,512]{2,1,0:T(4,128)(2,1)S(1)} %get-tuple-element.116), channel_id=1, source_target_pairs={{1,2},{2,1},{3,4},{4,3},{5,6},{6,5},{7,8},{8,7},{9,10},{10,9},{11,... | collective-permute-start | bytes 129032 | tf_op jit(solution)/shard_map/ppermute | solution.py:364
  52.7 4.4 %collective-permute-start.13 = (bf16[14,3,512]{2,1,0:T(4,128)(2,1)S(1)}, bf16[14,3,512]{2,1,0:T(4,128)(2,1)S(1)}, u32[]{:S(2)}, u32[]{:S(2)}) collective-permute-start(bf16[14,3,512]{2,1,0:T(4,128)(2,1)S(1)} %get-tuple-element.117), channel_id=1, source_target_pairs={{0,1},{1,0},{2,3},{3,2},{4,5},{5,4},{6,7},{7,6},{8,9},{9,8},{10,11... | collective-permute-start | bytes 129032 | tf_op jit(solution)/shard_map/ppermute | solution.py:364
  60.4 22.8 %all-to-all-start = ((bf16[16,136,128]{2,1,0:T(8,128)(2,1)}), bf16[16,136,128]{2,1,0:T(8,128)(2,1)S(1)}, u32[]{:S(2)}, u32[]{:S(2)}) async-start(bf16[16,136,128]{2,1,0:T(8,128)(2,1)} %add_last.1), calls=%async_computation | async-start | bytes 1114112 | tf_op jit(solution)/shard_map/all_to_all | solution.py:431

commit v8 on v6

--- a/solution.py
+++ b/solution.py
@@ -1,3 +1,4 @@
+import itertools
 import math
 
 import jax
@@ -8,10 +9,10 @@
 from jax.sharding import Mesh
 from jax.sharding import PartitionSpec as P
 
-EVERY = ("z", "yh", "xh", "xl", "yl", "c")
-ROW = ("z", "yh")
+EVERY = ("zh", "zl", "yh", "xh", "xl", "yl", "c")
+ROW = ("zh", "zl", "yh")
 COL = ("xh", "xl", "yl", "c")
-GROUP = ("z", "yh", "xh", "yl")
+THIRDS = ((0, 48), (48, 96), (96, 136))
 ROWS, COLS, CH, HID, CHUNK = 8, 32, 512, 2048, 512
 COUNT = ROWS * COLS
 STEPS = HID // CHUNK
@@ -206,7 +207,7 @@
     )(place, *(near(value) for value in operands))
 
 
-def taps_kernel(place, pad, d_conv, rows, keep, give, d_tile, table):
+def taps_kernel(pad, d_conv, rows, small, d_tile, table):
     for k in range(BLOCKS):
         d_tile[k] = d_conv[:, :, 128 * k : 128 * k + 128].astype(F32)
     table[48:128, :] = jnp.zeros((80, CH), F32)
@@ -227,49 +228,59 @@
     lax.fori_loop(0, BLOCKS, block, 0)
     table[49:54, :] = rows[0:5, :]
     table[54:58, :] = rows[8:12, :]
-    turned = table[...].T.reshape(16, 2, 2, 8, 128)
-    even = place[2] == 0
-    keep[...] = jnp.where(even, turned[:, 0], turned[:, 1]).reshape(32, 8, 128).astype(BF16)
-    give[...] = jnp.where(even, turned[:, 1], turned[:, 0]).reshape(32, 8, 128).astype(BF16)
-
-
-def tap_rows(place, *operands):
+    small[...] = table[...].T.reshape(64, 8, 128)
+
+
+def tap_rows(*operands):
     return pl.pallas_call(
         taps_kernel,
-        in_specs=[SCALARS] + [WHOLE] * len(operands),
-        out_shape=[pltpu.VMEM((32, 8, 128), BF16)] * 2,
+        in_specs=[WHOLE] * len(operands),
+        out_shape=pltpu.VMEM((64, 8, 128), F32),
         scratch_shapes=[pltpu.VMEM(TILE, F32), pltpu.VMEM((128, CH), F32)],
         compiler_params=params(),
         cost_estimate=cost(30_000_000, 2_000_000),
         name="tap_rows",
-    )(place, *(near(value) for value in operands))
-
-
-def split_kernel(place, out_one, out_two, in_one, in_two, keep, give):
+    )(*(near(value) for value in operands))
+
+
+def split_kernel(place, out_one, out_two, in_one, in_two, small_one, small_two, keep, *gives):
     even = place[2] == 0
-    for at, one, two in ((0, out_one, out_two), (64, in_one, in_two)):
-        for k in range(16):
-            total = [(one[4 * k + 2 * p : 4 * k + 2 * p + 2] + two[4 * k + 2 * p : 4 * k + 2 * p + 2]) for p in range(2)]
-            keep[2 * k : 2 * k + 2, at : at + 64, :] = jnp.where(even, total[0], total[1])
-            give[2 * k : 2 * k + 2, at : at + 64, :] = jnp.where(even, total[1], total[0])
+
+    for k in range(32):
+        kept, given = [], []
+        for part in range(2):
+            q = 2 * k + part
+            rows = [out_one[q] + out_two[q], in_one[q] + in_two[q], (small_one[q] + small_two[q]).astype(BF16)]
+            kept.append(rows)
+        if (k ^ (k >> 3)) & 1:
+            kept.reverse()
+        at = 0
+        for low, high in zip(*kept):
+            size = low.shape[0]
+            mine, theirs = jnp.where(even, low, high), jnp.where(even, high, low)
+            keep[k, at : at + size, :] = mine
+            for give, (start, end) in zip(gives, THIRDS):
+                first, last = max(start, at), min(end, at + size)
+                if first < last:
+                    give[k, first - start : last - start, :] = theirs[first - at : last - at]
+            at += size
 
 
 def split_pair(place, *operands):
     return pl.pallas_call(
         split_kernel,
         in_specs=[SCALARS] + [WHOLE] * len(operands),
-        out_shape=[pltpu.VMEM((32, 128, 128), BF16)] * 2,
+        out_shape=[pltpu.VMEM((32, 136, 128), BF16)]
+        + [pltpu.VMEM((32, end - start, 128), BF16) for start, end in THIRDS],
         compiler_params=params(),
         cost_estimate=cost(1_000_000, 6_000_000),
         name="split_pair",
     )(place, *(near(value) for value in operands))
 
 
-def add_kernel(one, two, small_one, small_two, small_three, small_four, total):
-    total[:, 0:128, :] = one[...] + two[...]
-    small = small_one[...].astype(F32) + small_two[...].astype(F32)
-    small = small + small_three[...].astype(F32) + small_four[...].astype(F32)
-    total[:, 128:136, :] = small.astype(BF16)
+def add_kernel(keep, one, two, three, total):
+    for given, (start, end) in zip((one, two, three), THIRDS):
+        total[:, start:end, :] = keep[:, start:end, :] + given[...]
 
 
 def add_pair(*operands):
@@ -355,18 +366,26 @@
     return lax.ppermute(value, "c", [(0, 1), (1, 0)])
 
 
-def swap_chips(value):
+def places():
+    for zh, zl, yh, xh, xl, yl, core in itertools.product(range(2), repeat=7):
+        yield 2 * zh + zl, 2 * yh + yl, 2 * xh + xl, core
+
+
+def swap_chips(value, axis):
+    known = list(places())
     pairs = []
-    for x in range(4):
-        pairs += [(2 * x, 2 * (x ^ 1)), (2 * x + 1, 2 * (3 - x) + 1)]
-    return lax.ppermute(value, ("xh", "xl", "c"), pairs)
-
-
-def swap_across(value):
-    pairs = []
-    for x in range(4):
-        pairs += [(2 * x, 2 * (3 - x) + 1), (2 * x + 1, 2 * (x ^ 1))]
-    return lax.ppermute(value, ("xh", "xl", "c"), pairs)
+    for at, place in enumerate(known):
+        met = list(place)
+        met[axis] = 3 - met[axis] if place[3] else met[axis] ^ 1
+        pairs.append((at, known.index(tuple(met))))
+    return lax.ppermute(value, EVERY, pairs)
+
+
+def spread_chips(value):
+    groups = {}
+    for at, (z, y, x, core) in enumerate(places()):
+        groups.setdefault(((z + y + x) % 2, core), []).append(at)
+    return lax.all_to_all(value, EVERY, 0, 0, axis_index_groups=list(groups.values()), tiled=True)
 
 
 def shards(
@@ -374,8 +393,8 @@
     pw_in_weight, pw_in_bias, pw_out_weight, pw_out_bias, layer_scale,
 ):
     factor = 1.0 / math.sqrt(COUNT * lax.axis_size(EVERY))
-    core, y_hi, x_lo = (lax.axis_index(name).astype(jnp.int32) for name in ("c", "yh", "xl"))
-    place = jnp.stack([core, y_hi, x_lo])
+    core, y_hi, y_lo, x_lo, z_lo = (lax.axis_index(name).astype(jnp.int32) for name in ("c", "yh", "yl", "xl", "zl"))
+    place = jnp.stack([core, y_hi, (x_lo + y_lo + z_lo) % 2])
     even_row, even_col = y_hi == 0, core == 0
     vectors = jnp.stack([dw_bias, norm_gain_vector, norm_bias, layer_scale, pw_out_bias])
     ends = features[:3], features[ROWS - 3 :]
@@ -391,17 +410,15 @@
         place, tile, *rows_met, *cols_met, cot, taps, vectors, w_in, b_in, w_out
     )
     met_out, met_in = swap_cores(theirs_out), swap_cores(theirs_in)
-    small_keep, small_give = tap_rows(place, pad, d_conv, rows)
-    met_out, met_in, small_keep, small_give = lax.optimization_barrier((met_out, met_in, small_keep, small_give))
-    keep, give = split_pair(place, mine_out, met_out, mine_in, met_in)
-    given = swap_chips(give)
-    small_keep, small_give, give, d_one, d_two = lax.optimization_barrier((small_keep, small_give, give, d_one, d_two))
-    smalls = small_keep, swap_cores(small_keep), swap_chips(small_give), swap_across(small_give)
+    small = tap_rows(pad, d_conv, rows)
+    keep, *gives = split_pair(place, mine_out, met_out, mine_in, met_in, small, swap_cores(small))
+    given = [swap_chips(give, axis) for axis, give in enumerate(gives)]
+    gives, d_one, d_two = lax.optimization_barrier((gives, d_one, d_two))
     d_rows = exchange(d_one, d_two, ROW)
     d_cols = exchange(*halo_sides(*d_rows, d_conv, even_row, even_col), COL)
-    smalls, d_cols = lax.optimization_barrier((smalls, d_cols))
-    message = add_pair(keep, given, *smalls)
-    spread = lax.all_to_all(message, GROUP, 0, 0, tiled=True)
+    given, d_cols = lax.optimization_barrier((given, d_cols))
+    message = add_pair(keep, *given)
+    spread = spread_chips(message)
     d_conv, message = lax.optimization_barrier((d_conv, message))
     grad_features = features_part(place, d_conv, *d_rows, *d_cols, cot, taps)
     grad_in, grad_out, grad_channel, grad_bias = sum_chips(place, spread, factor)
@@ -416,7 +433,7 @@
 
 
 def solution(mesh):
-    fine = Mesh(mesh.devices.reshape(4, 2, 2, 2, 2, 2), EVERY)
+    fine = Mesh(mesh.devices.reshape(2, 2, 2, 2, 2, 2, 2), EVERY)
     return jax.shard_map(
         shards,
         mesh=fine,

time: 81.3 us -> 82.1 us (level)
  waiting for transfers between devices: 18.5 us -> 19.6 us
    ppermute x8, waiting for transfers between devices: 3.63 us -> 1.38 us  [exchange(): met.append(lax.ppermute(value, axis, pairs))]
    ppermute x3, starting transfers between devices: 3.45 us -> 5.67 us  [swap_chips(): return lax.ppermute(value, EVERY, pairs)]
    ppermute x3, starting transfers between devices: 6.96 us -> 5.33 us  [swap_cores(): return lax.ppermute(value, 'c', [(0, 1), (1, 0)])]
    ppermute x3, waiting for transfers between devices: 0.01 us -> 1.54 us  [swap_chips(): return lax.ppermute(value, EVERY, pairs)]
    all_to_all x1, waiting for transfers between devices: 13.9 us -> 15.4 us  [spread_chips(): lax.all_to_all(value, EVERY, 0, 0, axis_index_groups=list(groups.values()...]
    all_to_all x1, starting transfers between devices: 9.4 us -> 8.03 us  [spread_chips(): lax.all_to_all(value, EVERY, 0, 0, axis_index_groups=list(groups.values()...]
    ppermute x8, starting transfers between devices: 17.6 us -> 18.5 us  [exchange(): met.append(lax.ppermute(value, axis, pairs))]
  transfers between devices with their start and end apart: 15 -> 15, of which waited for: 5 -> 5; matrix products, arithmetic and copies ran while one was open for 3% -> 3% of each run, Pallas kernels for 11% -> 10%
where the time goes in v8:
time: 82.1 us; the launch traced here: 81.7 us
  starting transfers between devices  37.5 us (46%)
  Pallas kernels  20.1 us (24%)
  waiting for transfers between devices  19.6 us (24%)
  local copies, waits for them, and re-layouts  2.36 us (3%)
  other arithmetic  1.27 us (2%)
    ppermute x8, starting transfers between devices, exchange(): met.append(lax.ppermute(value, axis, pairs))  18.5 us
    all_to_all x1, waiting for transfers between devices, spread_chips(): lax.all_to_all(value, EVERY, 0, 0, axis_index_groups=list(groups.values()...  15.4 us
    all_to_all x1, starting transfers between devices, spread_chips(): lax.all_to_all(value, EVERY, 0, 0, axis_index_groups=list(groups.values()...  8.03 us
    pallas_call x1, Pallas kernels, grads(): pl.pallas_call(grads_kernel, in_specs=[SCALARS] + [WHOLE] * len(operands)...  7.95 us
    ppermute x3, starting transfers between devices, swap_chips(): return lax.ppermute(value, EVERY, pairs)  5.67 us
    ppermute x3, starting transfers between devices, swap_cores(): return lax.ppermute(value, 'c', [(0, 1), (1, 0)])  5.33 us
    pallas_call x1, Pallas kernels, features_part(): pl.pallas_call(features_kernel, in_specs=[SCALARS] + [WHOLE] * len(operan...  3.65 us
    pallas_call x1, Pallas kernels, fetch(): pl.pallas_call(lambda *refs: fetch_kernel(count, *refs), in_specs=[pl.Blo...  2.53 us
  transfers between devices with their start and end apart: 15, of which 5 were waited for; matrix products, arithmetic and copies ran while one was open for 3% of the time, Pallas kernels for 10%

profile of v8, /device:TPU:0, one launch (start us, length us, event | category | flops | bytes accessed | tf_op | source)
XLA Modules:
  0.0 81.7 jit_solution(3652189490483482864)
XLA Ops:
  0.6 1.0 %broadcast_select_fusion.4 = (bf16[3,32,512]{2,1,0:T(8,128)(2,1)S(1)}, bf16[3,32,512]{2,1,0:T(8,128)(2,1)S(1)}) fusion(pred[]{:T(512)S(6)} %eq.8, bf16[8,32,512]{2,1,0:T(8,128)(2,1)} %refs_0_.1), kind=kLoop, calls=%fused_computation.4 | loop fusion | flops 98304 | bytes 393217 | tf_op jit(solution)/shard_map/jit(_where)/select_n | solution.py:401
  1.6 0.7 collective-permute-start.1
  2.3 6.3 %collective-permute-start = (bf16[3,32,512]{2,1,0:T(8,128)(2,1)S(1)}, bf16[3,32,512]{2,1,0:T(8,128)(2,1)S(1)}, u32[]{:S(2)}, u32[]{:S(2)}) collective-permute-start(bf16[3,32,512]{2,1,0:T(8,128)(2,1)S(1)} %get-tuple-element.83), channel_id=1, source_target_pairs={{0,16},{16,0},{32,48},{48,32},{64,80},{80,64},{96,112},{112,96},{1... | collective-permute-start | bytes 294920 | tf_op jit(solution)/shard_map/ppermute | solution.py:353
  8.6 0.9 %fusion.1 = (bf16[8,3,512]{2,1,0:T(4,128)(2,1)S(1)}, bf16[8,3,512]{2,1,0:T(4,128)(2,1)S(1)}) fusion(bf16[8,32,512]{2,1,0:T(8,128)(2,1)} %refs_0_.1), kind=kLoop, calls=%fused_computation.16 | loop fusion | bytes 98304 | tf_op jit(solution)/shard_map/slice | solution.py:360
  9.5 1.4 %stack.39.refs_3_ = f32[5,512]{1,0:T(8,128)} concatenate(f32[1,512]{1,0:T(1,128)} %bitcast.15, f32[1,512]{1,0:T(1,128)} %bitcast.16, f32[1,512]{1,0:T(1,128)} %bitcast.17, f32[1,512]{1,0:T(1,128)} %bitcast.18, f32[1,512]{1,0:T(1,128)} %bitcast.19), dimensions={0} | concatenate | bytes 20480 | tf_op jit(solution)/shard_map/stack | solution.py:399
  10.9 2.5 %fetch.1 = (bf16[8,32,512]{2,1,0:T(8,128)(2,1)S(1)}, bf16[256,512]{1,0:T(8,128)(2,1)S(1)}, f32[49,512]{1,0:T(8,128)S(1)}, f32[5,512]{1,0:T(8,128)S(1)}, bf16[512...) custom-call(bf16[8,32,512]{2,1,0:T(8,128)(2,1)} %refs_0_.1, ...), custom_call_target="tpu_custom_call" | custom-call | bytes 5000000 | tf_op jit(solution)/shard_map/fetch/pallas_call | solution.py:65
  13.5 0.1 broadcast_select_fusion.8
  13.6 0.1 collective-permute-start.2
  13.7 0.7 collective-permute-start.3
  14.3 0.1 pad_add_fusion.place.refs_0_
  14.4 0.5 collective-permute-done.2.col_one
  14.9 8.0 %grads.1 = (f32[4,14,40,128]{3,2,1,0:T(8,128)S(1)}, bf16[256,512]{1,0:T(8,128)(2,1)}, bf16[8,32,512]{2,1,0:T(8,128)(2,1)S(1)}, bf16[3,32,512]{2,1,0:T(8,128)(2,1...) custom-call(s32[3]{0:T(128)S(1)} %pad_add_fusion.place.refs_0_, ...), custom_call_target="tpu_custom_call" | custom-call | flops 3200000000 | bytes 12000000 | tf_op jit(solution)/shard_map/grads/pallas_call | solution.py:188
  22.9 4.7 %collective-permute-start.4 = (bf16[64,64,128]{2,1,0:T(8,128)(2,1)S(1)}, bf16[64,64,128]{2,1,0:T(8,128)(2,1)S(1)}, u32[]{:S(2)}, u32[]{:S(2)}) collective-permute-start(bf16[64,64,128]{2,1,0:T(8,128)(2,1)S(1)} %get-tuple-element.55), channel_id=1, source_target_pairs={{0,1},{1,0},{2,3},{3,2},{4,5},{5,4},{6,7},{7,6},{8,9},{9,8},{10,11... | collective-permute-start | bytes 3145736 | tf_op jit(solution)/shard_map/ppermute | solution.py:366
  27.6 2.3 %tap_rows.1.small_one = f32[64,8,128]{2,1,0:T(8,128)S(1)} custom-call(f32[4,14,40,128]{3,2,1,0:T(8,128)S(1)} %get-tuple-element.58.pad, bf16[8,32,512]{2,1,0:T(8,128)(2,1)S(1)} %get-tuple-element.71.d_conv, f32[16,512]{1,0:T(8,128)S(1)} %get-tuple-element.59.rows), custom_call_target="tpu_custom_call" | custom-call | flops 30000000 | bytes 2000000 | tf_op jit(solution)/shard_map/tap_rows/pallas_call | solution.py:235
  29.9 0.6 collective-permute-start.6
  30.5 1.2 %collective-permute-done.6.small_two = f32[64,8,128]{2,1,0:T(8,128)S(1)} collective-permute-done((f32[64,8,128]{2,1,0:T(8,128)S(1)}, f32[64,8,128]{2,1,0:T(8,128)S(1)}, u32[]{:S(2)}, u32[]{:S(2)}) %collective-permute-start.6) | collective-permute-done | bytes 262176 | tf_op jit(solution)/shard_map/ppermute | solution.py:366
  31.8 1.0 %split_pair.1 = (bf16[32,136,128]{2,1,0:T(8,128)(2,1)S(1)}, bf16[32,48,128]{2,1,0:T(8,128)(2,1)S(1)}, bf16[32,48,128]{2,1,0:T(8,128)(2,1)S(1)}, bf16[32,40,128]{2,1,0:T(8,128)(2,1)S(1)}) custom-call(s32[3]{0:T(128)S(1)} %pad_add_fusion.place.refs_0_, bf16[64,64,128]{2,1,0:T(8,128)(2,1)S(1)} %get-tuple-element.54.out_one, ...), custom_call_target="tpu_custom_call" | custom-call | flops 1000000 | bytes 6000000 | tf_op jit(solution)/shard_map/split_pair/pallas_call | solution.py:270
  32.8 0.7 collective-permute-start.10
  33.5 6.2 %collective-permute-start.11 = (bf16[3,32,512]{2,1,0:T(8,128)(2,1)S(1)}, bf16[3,32,512]{2,1,0:T(8,128)(2,1)S(1)}, u32[]{:S(2)}, u32[]{:S(2)}) collective-permute-start(bf16[3,32,512]{2,1,0:T(8,128)(2,1)S(1)} %get-tuple-element.67), channel_id=1, source_target_pairs={{0,16},{16,0},{32,48},{48,32},{64,80},{80,64},{96,112},{112,96},{1... | collective-permute-start | bytes 294920 | tf_op jit(solution)/shard_map/ppermute | solution.py:353
  39.7 2.4 %collective-permute-start.9 = (bf16[32,40,128]{2,1,0:T(8,128)(2,1)S(1)}, bf16[32,40,128]{2,1,0:T(8,128)(2,1)S(1)}, u32[]{:S(2)}, u32[]{:S(2)}) collective-permute-start(bf16[32,40,128]{2,1,0:T(8,128)(2,1)S(1)} %get-tuple-element.63), channel_id=1, source_target_pairs={{0,4},{1,13},{2,6},{3,15},{4,0},{5,9},{6,2},{7,11},{8,12},{9,5},{1... | collective-permute-start | bytes 983048 | tf_op jit(solution)/shard_map/ppermute | solution.py:381
  42.2 1.6 %collective-permute-start.7 = (bf16[32,48,128]{2,1,0:T(8,128)(2,1)S(1)}, bf16[32,48,128]{2,1,0:T(8,128)(2,1)S(1)}, u32[]{:S(2)}, u32[]{:S(2)}) collective-permute-start(bf16[32,48,128]{2,1,0:T(8,128)(2,1)S(1)} %get-tuple-element.61), channel_id=1, source_target_pairs={{0,32},{1,97},{2,34},{3,99},{4,36},{5,101},{6,38},{7,103},{8,40},{... | collective-permute-start | bytes 1179656 | tf_op jit(solution)/shard_map/ppermute | solution.py:381
  43.8 1.6 %collective-permute-start.8 = (bf16[32,48,128]{2,1,0:T(8,128)(2,1)S(1)}, bf16[32,48,128]{2,1,0:T(8,128)(2,1)S(1)}, u32[]{:S(2)}, u32[]{:S(2)}) collective-permute-start(bf16[32,48,128]{2,1,0:T(8,128)(2,1)S(1)} %get-tuple-element.62), channel_id=1, source_target_pairs={{0,2},{1,19},{2,0},{3,17},{4,6},{5,23},{6,4},{7,21},{8,10},{9,27},... | collective-permute-start | bytes 1179656 | tf_op jit(solution)/shard_map/ppermute | solution.py:381
  45.5 0.1 broadcast_select_fusion.6
  45.6 0.7 collective-permute-start.13
  46.2 3.2 %collective-permute-start.12 = (bf16[14,3,512]{2,1,0:T(4,128)(2,1)S(1)}, bf16[14,3,512]{2,1,0:T(4,128)(2,1)S(1)}, u32[]{:S(2)}, u32[]{:S(2)}) collective-permute-start(bf16[14,3,512]{2,1,0:T(4,128)(2,1)S(1)} %get-tuple-element.89), channel_id=1, source_target_pairs={{0,1},{1,0},{2,3},{3,2},{4,5},{5,4},{6,7},{7,6},{8,9},{9,8},{10,11... | collective-permute-start | bytes 129032 | tf_op jit(solution)/shard_map/ppermute | solution.py:353
  49.5 0.9 %collective-permute-done.12.col_one = bf16[14,3,512]{2,1,0:T(4,128)(2,1)S(1)} collective-permute-done((bf16[14,3,512]{2,1,0:T(4,128)(2,1)S(1)}, bf16[14,3,512]{2,1,0:T(4,128)(2,1)S(1)}, u32[]{:S(2)}, u32[]{:S(2)}) %collective-permute-start.12) | collective-permute-done | bytes 43040 | tf_op jit(solution)/shard_map/ppermute | solution.py:353
  50.4 1.5 %collective-permute-done.8.two = bf16[32,48,128]{2,1,0:T(8,128)(2,1)S(1)} collective-permute-done((bf16[32,48,128]{2,1,0:T(8,128)(2,1)S(1)}, bf16[32,48,128]{2,1,0:T(8,128)(2,1)S(1)}, u32[]{:S(2)}, u32[]{:S(2)}) %collective-permute-start.8) | collective-permute-done | bytes 393248 | tf_op jit(solution)/shard_map/ppermute | solution.py:381
  51.9 1.3 %add_pair.1 = bf16[32,136,128]{2,1,0:T(8,128)(2,1)} custom-call(bf16[32,136,128]{2,1,0:T(8,128)(2,1)S(1)} %get-tuple-element.60.keep, bf16[32,48,128]{2,1,0:T(8,128)(2,1)S(1)} %collective-permute-done.7.one, bf16[32,48,128]{2,1,0:T(8,128)(2,1)S(1)} %collective-permute-done.8.two, bf16[32,40,128]{2,1,0:T(8,128)(2,1)S(1)} %collective-permute-done.9.three), custom_call_target="tpu_custom_call" | custom-call | flops 1000000 | bytes 3000000 | tf_op jit(solution)/shard_map/add_pair/pallas_call | solution.py:287
  53.2 8.0 %all-to-all-start = ((bf16[32,136,128]{2,1,0:T(8,128)(2,1)}), bf16[32,136,128]{2,1,0:T(8,128)(2,1)S(1)}, u32[]{:S(2)}, u32[]{:S(2)}) async-start(bf16[32,136,128]{2,1,0:T(8,128)(2,1)} %add_pair.1), calls=%async_computation | async-start | bytes 2228224 | tf_op jit(solution)/shard_map/all_to_all | solution.py:388
  61.3 3.6 %features_part.1 = bf16[8,32,512]{2,1,0:T(8,128)(2,1)} custom-call(s32[3]{0:T(128)S(1)} %pad_add_fusion.place.refs_0_, bf16[8,32,512]{2,1,0:T(8,128)(2,1)S(1)} %get-tuple-element.71.d_conv, bf16[3,32,512]{2,1,0:T(8,128)(2,1)S(1)} %collective-permute-done.11.row_one, bf16[3,32,512]{2,1,0:T(8,128)(2,1)S(1)} %collective-permute-done.10.row_two, ...), custom_call_target="tpu_custom_call" | custom-call | flops 30000000 | bytes 2000000 | tf_op jit(solution)/shard_map/features_part/pallas_call | solution.py:335
  64.9 15.4 %all-to-all-done.refs_1_ = bf16[32,136,128]{2,1,0:T(8,128)(2,1)S(1)} async-done(((bf16[32,136,128]{2,1,0:T(8,128)(2,1)}), bf16[32,136,128]{2,1,0:T(8,128)(2,1)S(1)}, u32[]{:S(2)}, u32[]{:S(2)}) %all-to-all-start) | async-done | bytes 1114144 | tf_op jit(solution)/shard_map/all_to_all | solution.py:388
  80.3 1.4 %sum_chips.1 = (f32[4,2048]{1,0:T(4,128)}, f32[16,512]{1,0:T(8,128)}, f32[4,54]{1,0:T(4,128)}, f32[1,16]{1,0:T(1,128)}) custom-call(s32[3]{0:T(128)S(1)} %pad_add_fusion.place.refs_0_, bf16[32,136,128]{2,1,0:T(8,128)(2,1)S(1)} %all-to-all-done.refs_1_), custom_call_target="tpu_custom_call" | custom-call | flops 1000000 | bytes 1000000 | tf_op jit(solution)/shard_map/sum_chips/pallas_call | solution.py:315
  (17 shorter events, 0.2 us)
Async XLA Ops:
  1.6 11.8 %collective-permute-start.1 = (bf16[3,32,512]{2,1,0:T(8,128)(2,1)S(1)}, bf16[3,32,512]{2,1,0:T(8,128)(2,1)S(1)}, u32[]{:S(2)}, u32[]{:S(2)}) collective-permute-start(bf16[3,32,512]{2,1,0:T(8,128)(2,1)S(1)} %get-tuple-element.82), channel_id=1, source_target_pairs={{16,32},{32,16},{48,64},{64,48},{80,96},{96,80},{17,33},{33,17},{4... | collective-permute-start | bytes 294920 | tf_op jit(solution)/shard_map/ppermute | solution.py:353
  2.3 11.1 %collective-permute-start = (bf16[3,32,512]{2,1,0:T(8,128)(2,1)S(1)}, bf16[3,32,512]{2,1,0:T(8,128)(2,1)S(1)}, u32[]{:S(2)}, u32[]{:S(2)}) collective-permute-start(bf16[3,32,512]{2,1,0:T(8,128)(2,1)S(1)} %get-tuple-element.83), channel_id=1, source_target_pairs={{0,16},{16,0},{32,48},{48,32},{64,80},{80,64},{96,112},{112,96},{1... | collective-permute-start | bytes 294920 | tf_op jit(solution)/shard_map/ppermute | solution.py:353
  13.6 1.3 %collective-permute-start.2 = (bf16[14,3,512]{2,1,0:T(4,128)(2,1)S(1)}, bf16[14,3,512]{2,1,0:T(4,128)(2,1)S(1)}, u32[]{:S(2)}, u32[]{:S(2)}) collective-permute-start(bf16[14,3,512]{2,1,0:T(4,128)(2,1)S(1)} %get-tuple-element.44), channel_id=1, source_target_pairs={{0,1},{1,0},{2,3},{3,2},{4,5},{5,4},{6,7},{7,6},{8,9},{9,8},{10,11... | collective-permute-start | bytes 129032 | tf_op jit(solution)/shard_map/ppermute | solution.py:353
  13.7 1.2 %collective-permute-start.3 = (bf16[14,3,512]{2,1,0:T(4,128)(2,1)S(1)}, bf16[14,3,512]{2,1,0:T(4,128)(2,1)S(1)}, u32[]{:S(2)}, u32[]{:S(2)}) collective-permute-start(bf16[14,3,512]{2,1,0:T(4,128)(2,1)S(1)} %get-tuple-element.45), channel_id=1, source_target_pairs={{1,2},{2,1},{3,4},{4,3},{5,6},{6,5},{7,8},{8,7},{9,10},{10,9},{11,... | collective-permute-start | bytes 129032 | tf_op jit(solution)/shard_map/ppermute | solution.py:353
  22.9 8.9 %collective-permute-start.4 = (bf16[64,64,128]{2,1,0:T(8,128)(2,1)S(1)}, bf16[64,64,128]{2,1,0:T(8,128)(2,1)S(1)}, u32[]{:S(2)}, u32[]{:S(2)}) collective-permute-start(bf16[64,64,128]{2,1,0:T(8,128)(2,1)S(1)} %get-tuple-element.55), channel_id=1, source_target_pairs={{0,1},{1,0},{2,3},{3,2},{4,5},{5,4},{6,7},{7,6},{8,9},{9,8},{10,11... | collective-permute-start | bytes 3145736 | tf_op jit(solution)/shard_map/ppermute | solution.py:366
  27.6 4.2 %collective-permute-start.5 = (bf16[64,64,128]{2,1,0:T(8,128)(2,1)S(1)}, bf16[64,64,128]{2,1,0:T(8,128)(2,1)S(1)}, u32[]{:S(2)}, u32[]{:S(2)}) collective-permute-start(bf16[64,64,128]{2,1,0:T(8,128)(2,1)S(1)} %get-tuple-element.57), channel_id=1, source_target_pairs={{0,1},{1,0},{2,3},{3,2},{4,5},{5,4},{6,7},{7,6},{8,9},{9,8},{10,11... | collective-permute-start | bytes 3145736 | tf_op jit(solution)/shard_map/ppermute | solution.py:366
  29.9 1.8 %collective-permute-start.6 = (f32[64,8,128]{2,1,0:T(8,128)S(1)}, f32[64,8,128]{2,1,0:T(8,128)S(1)}, u32[]{:S(2)}, u32[]{:S(2)}) collective-permute-start(f32[64,8,128]{2,1,0:T(8,128)S(1)} %tap_rows.1.small_one), channel_id=1, source_target_pairs={{0,1},{1,0},{2,3},{3,2},{4,5},{5,4},{6,7},{7,6},{8,9},{9,8},{10,11... | collective-permute-start | bytes 786440 | tf_op jit(solution)/shard_map/ppermute | solution.py:366
  32.8 12.6 %collective-permute-start.10 = (bf16[3,32,512]{2,1,0:T(8,128)(2,1)S(1)}, bf16[3,32,512]{2,1,0:T(8,128)(2,1)S(1)}, u32[]{:S(2)}, u32[]{:S(2)}) collective-permute-start(bf16[3,32,512]{2,1,0:T(8,128)(2,1)S(1)} %get-tuple-element.66), channel_id=1, source_target_pairs={{16,32},{32,16},{48,64},{64,48},{80,96},{96,80},{17,33},{33,17},{4... | collective-permute-start | bytes 294920 | tf_op jit(solution)/shard_map/ppermute | solution.py:353
  33.5 11.9 %collective-permute-start.11 = (bf16[3,32,512]{2,1,0:T(8,128)(2,1)S(1)}, bf16[3,32,512]{2,1,0:T(8,128)(2,1)S(1)}, u32[]{:S(2)}, u32[]{:S(2)}) collective-permute-start(bf16[3,32,512]{2,1,0:T(8,128)(2,1)S(1)} %get-tuple-element.67), channel_id=1, source_target_pairs={{0,16},{16,0},{32,48},{48,32},{64,80},{80,64},{96,112},{112,96},{1... | collective-permute-start | bytes 294920 | tf_op jit(solution)/shard_map/ppermute | solution.py:353
  39.7 10.7 %collective-permute-start.9 = (bf16[32,40,128]{2,1,0:T(8,128)(2,1)S(1)}, bf16[32,40,128]{2,1,0:T(8,128)(2,1)S(1)}, u32[]{:S(2)}, u32[]{:S(2)}) collective-permute-start(bf16[32,40,128]{2,1,0:T(8,128)(2,1)S(1)} %get-tuple-element.63), channel_id=1, source_target_pairs={{0,4},{1,13},{2,6},{3,15},{4,0},{5,9},{6,2},{7,11},{8,12},{9,5},{1... | collective-permute-start | bytes 983048 | tf_op jit(solution)/shard_map/ppermute | solution.py:381
  42.2 8.2 %collective-permute-start.7 = (bf16[32,48,128]{2,1,0:T(8,128)(2,1)S(1)}, bf16[32,48,128]{2,1,0:T(8,128)(2,1)S(1)}, u32[]{:S(2)}, u32[]{:S(2)}) collective-permute-start(bf16[32,48,128]{2,1,0:T(8,128)(2,1)S(1)} %get-tuple-element.61), channel_id=1, source_target_pairs={{0,32},{1,97},{2,34},{3,99},{4,36},{5,101},{6,38},{7,103},{8,40},{... | collective-permute-start | bytes 1179656 | tf_op jit(solution)/shard_map/ppermute | solution.py:381
  43.8 8.1 %collective-permute-start.8 = (bf16[32,48,128]{2,1,0:T(8,128)(2,1)S(1)}, bf16[32,48,128]{2,1,0:T(8,128)(2,1)S(1)}, u32[]{:S(2)}, u32[]{:S(2)}) collective-permute-start(bf16[32,48,128]{2,1,0:T(8,128)(2,1)S(1)} %get-tuple-element.62), channel_id=1, source_target_pairs={{0,2},{1,19},{2,0},{3,17},{4,6},{5,23},{6,4},{7,21},{8,10},{9,27},... | collective-permute-start | bytes 1179656 | tf_op jit(solution)/shard_map/ppermute | solution.py:381
  45.6 3.9 %collective-permute-start.13 = (bf16[14,3,512]{2,1,0:T(4,128)(2,1)S(1)}, bf16[14,3,512]{2,1,0:T(4,128)(2,1)S(1)}, u32[]{:S(2)}, u32[]{:S(2)}) collective-permute-start(bf16[14,3,512]{2,1,0:T(4,128)(2,1)S(1)} %get-tuple-element.88), channel_id=1, source_target_pairs={{1,2},{2,1},{3,4},{4,3},{5,6},{6,5},{7,8},{8,7},{9,10},{10,9},{11,... | collective-permute-start | bytes 129032 | tf_op jit(solution)/shard_map/ppermute | solution.py:353
  46.2 4.1 %collective-permute-start.12 = (bf16[14,3,512]{2,1,0:T(4,128)(2,1)S(1)}, bf16[14,3,512]{2,1,0:T(4,128)(2,1)S(1)}, u32[]{:S(2)}, u32[]{:S(2)}) collective-permute-start(bf16[14,3,512]{2,1,0:T(4,128)(2,1)S(1)} %get-tuple-element.89), channel_id=1, source_target_pairs={{0,1},{1,0},{2,3},{3,2},{4,5},{5,4},{6,7},{7,6},{8,9},{9,8},{10,11... | collective-permute-start | bytes 129032 | tf_op jit(solution)/shard_map/ppermute | solution.py:353
  53.2 27.1 %all-to-all-start = ((bf16[32,136,128]{2,1,0:T(8,128)(2,1)}), bf16[32,136,128]{2,1,0:T(8,128)(2,1)S(1)}, u32[]{:S(2)}, u32[]{:S(2)}) async-start(bf16[32,136,128]{2,1,0:T(8,128)(2,1)} %add_pair.1), calls=%async_computation | async-start | bytes 2228224 | tf_op jit(solution)/shard_map/all_to_all | solution.py:388

commit v9 on v8

--- a/solution.py
+++ b/solution.py
@@ -399,13 +399,13 @@
     vectors = jnp.stack([dw_bias, norm_gain_vector, norm_bias, layer_scale, pw_out_bias])
     ends = features[:3], features[ROWS - 3 :]
     rows_met = exchange(jnp.where(even_row, ends[1], ends[0]), jnp.where(even_row, ends[0], ends[1]), ROW)
+    sides = halo_sides(*rows_met, features, even_row, even_col)
+    sides, pw_in_weight = lax.optimization_barrier((sides, pw_in_weight))
+    cols_met = exchange(*sides, COL)
     tile, cot, taps, vectors, w_in, b_in, w_out = fetch(
         features, cotangent.reshape(COUNT, CH), dw_kernel, vectors, pw_in_weight,
         pw_in_bias.reshape(1, HID), pw_out_weight,
     )
-    sides = halo_sides(*rows_met, features, even_row, even_col)
-    sides, w_in = lax.optimization_barrier((sides, w_in))
-    cols_met = exchange(*sides, COL)
     pad, block_rows, d_conv, d_one, d_two, rows, mine_out, theirs_out, mine_in, theirs_in = grads(
         place, tile, *rows_met, *cols_met, cot, taps, vectors, w_in, b_in, w_out
     )
@@ -415,10 +415,11 @@
     given = [swap_chips(give, axis) for axis, give in enumerate(gives)]
     gives, d_one, d_two = lax.optimization_barrier((gives, d_one, d_two))
     d_rows = exchange(d_one, d_two, ROW)
+    given, d_rows = lax.optimization_barrier((given, d_rows))
+    message = add_pair(keep, *given)
+    message, d_rows = lax.optimization_barrier((message, d_rows))
+    spread = spread_chips(message)
     d_cols = exchange(*halo_sides(*d_rows, d_conv, even_row, even_col), COL)
-    given, d_cols = lax.optimization_barrier((given, d_cols))
-    message = add_pair(keep, *given)
-    spread = spread_chips(message)
     d_conv, message = lax.optimization_barrier((d_conv, message))
     grad_features = features_part(place, d_conv, *d_rows, *d_cols, cot, taps)
     grad_in, grad_out, grad_channel, grad_bias = sum_chips(place, spread, factor)

time: 82.1 us -> 77.9 us (0.949)
  starting transfers between devices: 37.5 us -> 32.6 us
    ppermute x8, waiting for transfers between devices: 1.38 us -> 9.72 us  [exchange(): met.append(lax.ppermute(value, axis, pairs))]
    all_to_all x1, waiting for transfers between devices: 15.4 us -> 9.35 us  [spread_chips(): lax.all_to_all(value, EVERY, 0, 0, axis_index_groups=list(groups.values()...]
    ppermute x8, starting transfers between devices: 18.5 us -> 13.1 us  [exchange(): met.append(lax.ppermute(value, axis, pairs))]
    all_to_all x1, starting transfers between devices: 8.03 us -> 11.1 us  [spread_chips(): lax.all_to_all(value, EVERY, 0, 0, axis_index_groups=list(groups.values()...]
    ppermute x3, starting transfers between devices: 5.33 us -> 3.52 us  [swap_cores(): return lax.ppermute(value, 'c', [(0, 1), (1, 0)])]
    ppermute x3, waiting for transfers between devices: 1.54 us -> 0.01 us  [swap_chips(): return lax.ppermute(value, EVERY, pairs)]
  transfers between devices with their start and end apart: 15 -> 15, of which waited for: 5 -> 5; matrix products, arithmetic and copies ran while one was open for 3% -> 3% of each run, Pallas kernels for 10% -> 11%
where the time goes in v9:
time: 77.9 us; the launch traced here: 77.5 us
  starting transfers between devices  32.6 us (42%)
  waiting for transfers between devices  20.3 us (26%)
  Pallas kernels  20.1 us (26%)
  local copies, waits for them, and re-layouts  2.35 us (3%)
  other arithmetic  1.27 us (2%)
  between operations  0.83 us (1%)
    ppermute x8, starting transfers between devices, exchange(): met.append(lax.ppermute(value, axis, pairs))  13.1 us
    all_to_all x1, starting transfers between devices, spread_chips(): lax.all_to_all(value, EVERY, 0, 0, axis_index_groups=list(groups.values()...  11.1 us
    ppermute x8, waiting for transfers between devices, exchange(): met.append(lax.ppermute(value, axis, pairs))  9.72 us
    all_to_all x1, waiting for transfers between devices, spread_chips(): lax.all_to_all(value, EVERY, 0, 0, axis_index_groups=list(groups.values()...  9.35 us
    pallas_call x1, Pallas kernels, grads(): pl.pallas_call(grads_kernel, in_specs=[SCALARS] + [WHOLE] * len(operands)...  7.96 us
    ppermute x3, starting transfers between devices, swap_chips(): return lax.ppermute(value, EVERY, pairs)  4.95 us
    pallas_call x1, Pallas kernels, features_part(): pl.pallas_call(features_kernel, in_specs=[SCALARS] + [WHOLE] * len(operan...  3.64 us
    ppermute x3, starting transfers between devices, swap_cores(): return lax.ppermute(value, 'c', [(0, 1), (1, 0)])  3.52 us
  transfers between devices with their start and end apart: 15, of which 5 were waited for; matrix products, arithmetic and copies ran while one was open for 3% of the time, Pallas kernels for 11%

profile of v9, /device:TPU:0, one launch (start us, length us, event | category | flops | bytes accessed | tf_op | source)
XLA Modules:
  0.0 77.5 jit_solution(6723435874100397016)
XLA Ops:
  0.6 1.0 %broadcast_select_fusion.5 = (bf16[3,32,512]{2,1,0:T(8,128)(2,1)S(1)}, bf16[3,32,512]{2,1,0:T(8,128)(2,1)S(1)}) fusion(pred[]{:T(512)S(6)} %eq.9, bf16[8,32,512]{2,1,0:T(8,128)(2,1)} %refs_0_.1), kind=kLoop, calls=%fused_computation.5 | loop fusion | flops 98304 | bytes 393217 | tf_op jit(solution)/shard_map/jit(_where)/select_n | solution.py:401
  1.6 0.7 collective-permute-start
  2.3 6.3 %collective-permute-start.1 = (bf16[3,32,512]{2,1,0:T(8,128)(2,1)S(1)}, bf16[3,32,512]{2,1,0:T(8,128)(2,1)S(1)}, u32[]{:S(2)}, u32[]{:S(2)}) collective-permute-start(bf16[3,32,512]{2,1,0:T(8,128)(2,1)S(1)} %get-tuple-element.89), channel_id=1, source_target_pairs={{0,16},{16,0},{32,48},{48,32},{64,80},{80,64},{96,112},{112,96},{1... | collective-permute-start | bytes 294920 | tf_op jit(solution)/shard_map/ppermute | solution.py:353
  8.6 0.9 %fusion.1 = (bf16[8,3,512]{2,1,0:T(4,128)(2,1)S(1)}, bf16[8,3,512]{2,1,0:T(4,128)(2,1)S(1)}) fusion(bf16[8,32,512]{2,1,0:T(8,128)(2,1)} %refs_0_.1), kind=kLoop, calls=%fused_computation.16 | loop fusion | bytes 98304 | tf_op jit(solution)/shard_map/slice | solution.py:360
  9.5 3.6 %collective-permute-done.1.row_one = bf16[3,32,512]{2,1,0:T(8,128)(2,1)S(1)} collective-permute-done((bf16[3,32,512]{2,1,0:T(8,128)(2,1)S(1)}, bf16[3,32,512]{2,1,0:T(8,128)(2,1)S(1)}, u32[]{:S(2)}, u32[]{:S(2)}) %collective-permute-start.1) | collective-permute-done | bytes 98336 | tf_op jit(solution)/shard_map/ppermute | solution.py:353
  13.1 0.1 broadcast_select_fusion.8
  13.2 0.1 collective-permute-start.2
  13.3 0.7 collective-permute-start.3
  14.0 0.1 pad_add_fusion.place.refs_0_
  14.1 1.4 %stack.39.refs_3_ = f32[5,512]{1,0:T(8,128)} concatenate(f32[1,512]{1,0:T(1,128)} %bitcast.15, f32[1,512]{1,0:T(1,128)} %bitcast.16, f32[1,512]{1,0:T(1,128)} %bitcast.17, f32[1,512]{1,0:T(1,128)} %bitcast.18, f32[1,512]{1,0:T(1,128)} %bitcast.19), dimensions={0} | concatenate | bytes 20480 | tf_op jit(solution)/shard_map/stack | solution.py:399
  15.5 2.5 %fetch.1 = (bf16[8,32,512]{2,1,0:T(8,128)(2,1)S(1)}, bf16[256,512]{1,0:T(8,128)(2,1)S(1)}, f32[49,512]{1,0:T(8,128)S(1)}, f32[5,512]{1,0:T(8,128)S(1)}, bf16[512...) custom-call(bf16[8,32,512]{2,1,0:T(8,128)(2,1)} %refs_0_.1, ...), custom_call_target="tpu_custom_call" | custom-call | bytes 5000000 | tf_op jit(solution)/shard_map/fetch/pallas_call | solution.py:65
  18.0 8.0 %grads.1 = (f32[4,14,40,128]{3,2,1,0:T(8,128)S(1)}, bf16[256,512]{1,0:T(8,128)(2,1)}, bf16[8,32,512]{2,1,0:T(8,128)(2,1)S(1)}, bf16[3,32,512]{2,1,0:T(8,128)(2,1...) custom-call(s32[3]{0:T(128)S(1)} %pad_add_fusion.place.refs_0_, ...), custom_call_target="tpu_custom_call" | custom-call | flops 3200000000 | bytes 12000000 | tf_op jit(solution)/shard_map/grads/pallas_call | solution.py:188
  26.0 2.9 %collective-permute-start.4 = (bf16[64,64,128]{2,1,0:T(8,128)(2,1)S(1)}, bf16[64,64,128]{2,1,0:T(8,128)(2,1)S(1)}, u32[]{:S(2)}, u32[]{:S(2)}) collective-permute-start(bf16[64,64,128]{2,1,0:T(8,128)(2,1)S(1)} %get-tuple-element.58), channel_id=1, source_target_pairs={{0,1},{1,0},{2,3},{3,2},{4,5},{5,4},{6,7},{7,6},{8,9},{9,8},{10,11... | collective-permute-start | bytes 3145736 | tf_op jit(solution)/shard_map/ppermute | solution.py:366
  28.9 2.3 %tap_rows.1.small_one = f32[64,8,128]{2,1,0:T(8,128)S(1)} custom-call(f32[4,14,40,128]{3,2,1,0:T(8,128)S(1)} %get-tuple-element.61.pad, bf16[8,32,512]{2,1,0:T(8,128)(2,1)S(1)} %get-tuple-element.77.d_conv, f32[16,512]{1,0:T(8,128)S(1)} %get-tuple-element.62.rows), custom_call_target="tpu_custom_call" | custom-call | flops 30000000 | bytes 2000000 | tf_op jit(solution)/shard_map/tap_rows/pallas_call | solution.py:235
  31.2 0.6 collective-permute-start.6
  31.8 1.2 %collective-permute-done.6.small_two = f32[64,8,128]{2,1,0:T(8,128)S(1)} collective-permute-done((f32[64,8,128]{2,1,0:T(8,128)S(1)}, f32[64,8,128]{2,1,0:T(8,128)S(1)}, u32[]{:S(2)}, u32[]{:S(2)}) %collective-permute-start.6) | collective-permute-done | bytes 262176 | tf_op jit(solution)/shard_map/ppermute | solution.py:366
  33.1 1.0 %split_pair.1 = (bf16[32,136,128]{2,1,0:T(8,128)(2,1)S(1)}, bf16[32,48,128]{2,1,0:T(8,128)(2,1)S(1)}, bf16[32,48,128]{2,1,0:T(8,128)(2,1)S(1)}, bf16[32,40,128]{2,1,0:T(8,128)(2,1)S(1)}) custom-call(s32[3]{0:T(128)S(1)} %pad_add_fusion.place.refs_0_, bf16[64,64,128]{2,1,0:T(8,128)(2,1)S(1)} %get-tuple-element.57.out_one, ...), custom_call_target="tpu_custom_call" | custom-call | flops 1000000 | bytes 6000000 | tf_op jit(solution)/shard_map/split_pair/pallas_call | solution.py:270
  34.1 2.0 %collective-permute-start.7 = (bf16[32,48,128]{2,1,0:T(8,128)(2,1)S(1)}, bf16[32,48,128]{2,1,0:T(8,128)(2,1)S(1)}, u32[]{:S(2)}, u32[]{:S(2)}) collective-permute-start(bf16[32,48,128]{2,1,0:T(8,128)(2,1)S(1)} %get-tuple-element.64), channel_id=1, source_target_pairs={{0,32},{1,97},{2,34},{3,99},{4,36},{5,101},{6,38},{7,103},{8,40},{... | collective-permute-start | bytes 1179656 | tf_op jit(solution)/shard_map/ppermute | solution.py:381
  36.1 1.5 %collective-permute-start.8 = (bf16[32,48,128]{2,1,0:T(8,128)(2,1)S(1)}, bf16[32,48,128]{2,1,0:T(8,128)(2,1)S(1)}, u32[]{:S(2)}, u32[]{:S(2)}) collective-permute-start(bf16[32,48,128]{2,1,0:T(8,128)(2,1)S(1)} %get-tuple-element.65), channel_id=1, source_target_pairs={{0,2},{1,19},{2,0},{3,17},{4,6},{5,23},{6,4},{7,21},{8,10},{9,27},... | collective-permute-start | bytes 1179656 | tf_op jit(solution)/shard_map/ppermute | solution.py:381
  37.6 1.5 %collective-permute-start.9 = (bf16[32,40,128]{2,1,0:T(8,128)(2,1)S(1)}, bf16[32,40,128]{2,1,0:T(8,128)(2,1)S(1)}, u32[]{:S(2)}, u32[]{:S(2)}) collective-permute-start(bf16[32,40,128]{2,1,0:T(8,128)(2,1)S(1)} %get-tuple-element.66), channel_id=1, source_target_pairs={{0,4},{1,13},{2,6},{3,15},{4,0},{5,9},{6,2},{7,11},{8,12},{9,5},{1... | collective-permute-start | bytes 983048 | tf_op jit(solution)/shard_map/ppermute | solution.py:381
  39.1 1.6 %collective-permute-start.10 = (bf16[3,32,512]{2,1,0:T(8,128)(2,1)S(1)}, bf16[3,32,512]{2,1,0:T(8,128)(2,1)S(1)}, u32[]{:S(2)}, u32[]{:S(2)}) collective-permute-start(bf16[3,32,512]{2,1,0:T(8,128)(2,1)S(1)} %get-tuple-element.69), channel_id=1, source_target_pairs={{0,16},{16,0},{32,48},{48,32},{64,80},{80,64},{96,112},{112,96},{1... | collective-permute-start | bytes 294920 | tf_op jit(solution)/shard_map/ppermute | solution.py:353
  40.6 0.7 collective-permute-start.11
  41.3 5.2 %collective-permute-done.10.row_one = bf16[3,32,512]{2,1,0:T(8,128)(2,1)S(1)} collective-permute-done((bf16[3,32,512]{2,1,0:T(8,128)(2,1)S(1)}, bf16[3,32,512]{2,1,0:T(8,128)(2,1)S(1)}, u32[]{:S(2)}, u32[]{:S(2)}) %collective-permute-start.10) | collective-permute-done | bytes 98336 | tf_op jit(solution)/shard_map/ppermute | solution.py:353
  46.6 1.3 %add_pair.1 = bf16[32,136,128]{2,1,0:T(8,128)(2,1)} custom-call(bf16[32,136,128]{2,1,0:T(8,128)(2,1)S(1)} %get-tuple-element.63.keep, bf16[32,48,128]{2,1,0:T(8,128)(2,1)S(1)} %collective-permute-done.7.one, bf16[32,48,128]{2,1,0:T(8,128)(2,1)S(1)} %collective-permute-done.8.two, bf16[32,40,128]{2,1,0:T(8,128)(2,1)S(1)} %collective-permute-done.9.three), custom_call_target="tpu_custom_call" | custom-call | flops 1000000 | bytes 3000000 | tf_op jit(solution)/shard_map/add_pair/pallas_call | solution.py:287
  47.9 11.1 %all-to-all-start = ((bf16[32,136,128]{2,1,0:T(8,128)(2,1)}), bf16[32,136,128]{2,1,0:T(8,128)(2,1)S(1)}, u32[]{:S(2)}, u32[]{:S(2)}) async-start(bf16[32,136,128]{2,1,0:T(8,128)(2,1)} %add_pair.1), calls=%async_computation | async-start | bytes 2228224 | tf_op jit(solution)/shard_map/all_to_all | solution.py:388
  59.0 0.1 broadcast_select_fusion.6
  59.1 0.7 collective-permute-start.13
  59.8 2.5 %collective-permute-start.12 = (bf16[14,3,512]{2,1,0:T(4,128)(2,1)S(1)}, bf16[14,3,512]{2,1,0:T(4,128)(2,1)S(1)}, u32[]{:S(2)}, u32[]{:S(2)}) collective-permute-start(bf16[14,3,512]{2,1,0:T(4,128)(2,1)S(1)} %get-tuple-element.95), channel_id=1, source_target_pairs={{0,1},{1,0},{2,3},{3,2},{4,5},{5,4},{6,7},{7,6},{8,9},{9,8},{10,11... | collective-permute-start | bytes 129032 | tf_op jit(solution)/shard_map/ppermute | solution.py:353
  62.3 0.9 %collective-permute-done.12.col_one = bf16[14,3,512]{2,1,0:T(4,128)(2,1)S(1)} collective-permute-done((bf16[14,3,512]{2,1,0:T(4,128)(2,1)S(1)}, bf16[14,3,512]{2,1,0:T(4,128)(2,1)S(1)}, u32[]{:S(2)}, u32[]{:S(2)}) %collective-permute-start.12) | collective-permute-done | bytes 43040 | tf_op jit(solution)/shard_map/ppermute | solution.py:353
  63.2 3.6 %features_part.1 = bf16[8,32,512]{2,1,0:T(8,128)(2,1)} custom-call(s32[3]{0:T(128)S(1)} %pad_add_fusion.place.refs_0_, bf16[8,32,512]{2,1,0:T(8,128)(2,1)S(1)} %get-tuple-element.77.d_conv, bf16[3,32,512]{2,1,0:T(8,128)(2,1)S(1)} %collective-permute-done.10.row_one, bf16[3,32,512]{2,1,0:T(8,128)(2,1)S(1)} %collective-permute-done.11.row_two, ...), custom_call_target="tpu_custom_call" | custom-call | flops 30000000 | bytes 2000000 | tf_op jit(solution)/shard_map/features_part/pallas_call | solution.py:335
  66.8 9.3 %all-to-all-done.refs_1_ = bf16[32,136,128]{2,1,0:T(8,128)(2,1)S(1)} async-done(((bf16[32,136,128]{2,1,0:T(8,128)(2,1)}), bf16[32,136,128]{2,1,0:T(8,128)(2,1)S(1)}, u32[]{:S(2)}, u32[]{:S(2)}) %all-to-all-start) | async-done | bytes 1114144 | tf_op jit(solution)/shard_map/all_to_all | solution.py:388
  76.2 1.4 %sum_chips.1 = (f32[4,2048]{1,0:T(4,128)}, f32[16,512]{1,0:T(8,128)}, f32[4,54]{1,0:T(4,128)}, f32[1,16]{1,0:T(1,128)}) custom-call(s32[3]{0:T(128)S(1)} %pad_add_fusion.place.refs_0_, bf16[32,136,128]{2,1,0:T(8,128)(2,1)S(1)} %all-to-all-done.refs_1_), custom_call_target="tpu_custom_call" | custom-call | flops 1000000 | bytes 1000000 | tf_op jit(solution)/shard_map/sum_chips/pallas_call | solution.py:315
  (17 shorter events, 0.2 us)
Async XLA Ops:
  1.6 7.9 %collective-permute-start = (bf16[3,32,512]{2,1,0:T(8,128)(2,1)S(1)}, bf16[3,32,512]{2,1,0:T(8,128)(2,1)S(1)}, u32[]{:S(2)}, u32[]{:S(2)}) collective-permute-start(bf16[3,32,512]{2,1,0:T(8,128)(2,1)S(1)} %get-tuple-element.88), channel_id=1, source_target_pairs={{16,32},{32,16},{48,64},{64,48},{80,96},{96,80},{17,33},{33,17},{4... | collective-permute-start | bytes 294920 | tf_op jit(solution)/shard_map/ppermute | solution.py:353
  2.3 10.8 %collective-permute-start.1 = (bf16[3,32,512]{2,1,0:T(8,128)(2,1)S(1)}, bf16[3,32,512]{2,1,0:T(8,128)(2,1)S(1)}, u32[]{:S(2)}, u32[]{:S(2)}) collective-permute-start(bf16[3,32,512]{2,1,0:T(8,128)(2,1)S(1)} %get-tuple-element.89), channel_id=1, source_target_pairs={{0,16},{16,0},{32,48},{48,32},{64,80},{80,64},{96,112},{112,96},{1... | collective-permute-start | bytes 294920 | tf_op jit(solution)/shard_map/ppermute | solution.py:353
  13.2 4.8 %collective-permute-start.2 = (bf16[14,3,512]{2,1,0:T(4,128)(2,1)S(1)}, bf16[14,3,512]{2,1,0:T(4,128)(2,1)S(1)}, u32[]{:S(2)}, u32[]{:S(2)}) collective-permute-start(bf16[14,3,512]{2,1,0:T(4,128)(2,1)S(1)} %get-tuple-element.47), channel_id=1, source_target_pairs={{0,1},{1,0},{2,3},{3,2},{4,5},{5,4},{6,7},{7,6},{8,9},{9,8},{10,11... | collective-permute-start | bytes 129032 | tf_op jit(solution)/shard_map/ppermute | solution.py:353
  13.3 4.7 %collective-permute-start.3 = (bf16[14,3,512]{2,1,0:T(4,128)(2,1)S(1)}, bf16[14,3,512]{2,1,0:T(4,128)(2,1)S(1)}, u32[]{:S(2)}, u32[]{:S(2)}) collective-permute-start(bf16[14,3,512]{2,1,0:T(4,128)(2,1)S(1)} %get-tuple-element.48), channel_id=1, source_target_pairs={{1,2},{2,1},{3,4},{4,3},{5,6},{6,5},{7,8},{8,7},{9,10},{10,9},{11,... | collective-permute-start | bytes 129032 | tf_op jit(solution)/shard_map/ppermute | solution.py:353
  26.0 7.1 %collective-permute-start.4 = (bf16[64,64,128]{2,1,0:T(8,128)(2,1)S(1)}, bf16[64,64,128]{2,1,0:T(8,128)(2,1)S(1)}, u32[]{:S(2)}, u32[]{:S(2)}) collective-permute-start(bf16[64,64,128]{2,1,0:T(8,128)(2,1)S(1)} %get-tuple-element.58), channel_id=1, source_target_pairs={{0,1},{1,0},{2,3},{3,2},{4,5},{5,4},{6,7},{7,6},{8,9},{9,8},{10,11... | collective-permute-start | bytes 3145736 | tf_op jit(solution)/shard_map/ppermute | solution.py:366
  28.9 4.2 %collective-permute-start.5 = (bf16[64,64,128]{2,1,0:T(8,128)(2,1)S(1)}, bf16[64,64,128]{2,1,0:T(8,128)(2,1)S(1)}, u32[]{:S(2)}, u32[]{:S(2)}) collective-permute-start(bf16[64,64,128]{2,1,0:T(8,128)(2,1)S(1)} %get-tuple-element.60), channel_id=1, source_target_pairs={{0,1},{1,0},{2,3},{3,2},{4,5},{5,4},{6,7},{7,6},{8,9},{9,8},{10,11... | collective-permute-start | bytes 3145736 | tf_op jit(solution)/shard_map/ppermute | solution.py:366
  31.2 1.8 %collective-permute-start.6 = (f32[64,8,128]{2,1,0:T(8,128)S(1)}, f32[64,8,128]{2,1,0:T(8,128)S(1)}, u32[]{:S(2)}, u32[]{:S(2)}) collective-permute-start(f32[64,8,128]{2,1,0:T(8,128)S(1)} %tap_rows.1.small_one), channel_id=1, source_target_pairs={{0,1},{1,0},{2,3},{3,2},{4,5},{5,4},{6,7},{7,6},{8,9},{9,8},{10,11... | collective-permute-start | bytes 786440 | tf_op jit(solution)/shard_map/ppermute | solution.py:366
  34.1 12.4 %collective-permute-start.7 = (bf16[32,48,128]{2,1,0:T(8,128)(2,1)S(1)}, bf16[32,48,128]{2,1,0:T(8,128)(2,1)S(1)}, u32[]{:S(2)}, u32[]{:S(2)}) collective-permute-start(bf16[32,48,128]{2,1,0:T(8,128)(2,1)S(1)} %get-tuple-element.64), channel_id=1, source_target_pairs={{0,32},{1,97},{2,34},{3,99},{4,36},{5,101},{6,38},{7,103},{8,40},{... | collective-permute-start | bytes 1179656 | tf_op jit(solution)/shard_map/ppermute | solution.py:381
  36.1 10.4 %collective-permute-start.8 = (bf16[32,48,128]{2,1,0:T(8,128)(2,1)S(1)}, bf16[32,48,128]{2,1,0:T(8,128)(2,1)S(1)}, u32[]{:S(2)}, u32[]{:S(2)}) collective-permute-start(bf16[32,48,128]{2,1,0:T(8,128)(2,1)S(1)} %get-tuple-element.65), channel_id=1, source_target_pairs={{0,2},{1,19},{2,0},{3,17},{4,6},{5,23},{6,4},{7,21},{8,10},{9,27},... | collective-permute-start | bytes 1179656 | tf_op jit(solution)/shard_map/ppermute | solution.py:381
  37.6 9.0 %collective-permute-start.9 = (bf16[32,40,128]{2,1,0:T(8,128)(2,1)S(1)}, bf16[32,40,128]{2,1,0:T(8,128)(2,1)S(1)}, u32[]{:S(2)}, u32[]{:S(2)}) collective-permute-start(bf16[32,40,128]{2,1,0:T(8,128)(2,1)S(1)} %get-tuple-element.66), channel_id=1, source_target_pairs={{0,4},{1,13},{2,6},{3,15},{4,0},{5,9},{6,2},{7,11},{8,12},{9,5},{1... | collective-permute-start | bytes 983048 | tf_op jit(solution)/shard_map/ppermute | solution.py:381
  39.1 7.5 %collective-permute-start.10 = (bf16[3,32,512]{2,1,0:T(8,128)(2,1)S(1)}, bf16[3,32,512]{2,1,0:T(8,128)(2,1)S(1)}, u32[]{:S(2)}, u32[]{:S(2)}) collective-permute-start(bf16[3,32,512]{2,1,0:T(8,128)(2,1)S(1)} %get-tuple-element.69), channel_id=1, source_target_pairs={{0,16},{16,0},{32,48},{48,32},{64,80},{80,64},{96,112},{112,96},{1... | collective-permute-start | bytes 294920 | tf_op jit(solution)/shard_map/ppermute | solution.py:353
  40.6 5.9 %collective-permute-start.11 = (bf16[3,32,512]{2,1,0:T(8,128)(2,1)S(1)}, bf16[3,32,512]{2,1,0:T(8,128)(2,1)S(1)}, u32[]{:S(2)}, u32[]{:S(2)}) collective-permute-start(bf16[3,32,512]{2,1,0:T(8,128)(2,1)S(1)} %get-tuple-element.70), channel_id=1, source_target_pairs={{16,32},{32,16},{48,64},{64,48},{80,96},{96,80},{17,33},{33,17},{4... | collective-permute-start | bytes 294920 | tf_op jit(solution)/shard_map/ppermute | solution.py:353
  47.9 28.3 %all-to-all-start = ((bf16[32,136,128]{2,1,0:T(8,128)(2,1)}), bf16[32,136,128]{2,1,0:T(8,128)(2,1)S(1)}, u32[]{:S(2)}, u32[]{:S(2)}) async-start(bf16[32,136,128]{2,1,0:T(8,128)(2,1)} %add_pair.1), calls=%async_computation | async-start | bytes 2228224 | tf_op jit(solution)/shard_map/all_to_all | solution.py:388
  59.1 3.1 %collective-permute-start.13 = (bf16[14,3,512]{2,1,0:T(4,128)(2,1)S(1)}, bf16[14,3,512]{2,1,0:T(4,128)(2,1)S(1)}, u32[]{:S(2)}, u32[]{:S(2)}) collective-permute-start(bf16[14,3,512]{2,1,0:T(4,128)(2,1)S(1)} %get-tuple-element.94), channel_id=1, source_target_pairs={{1,2},{2,1},{3,4},{4,3},{5,6},{6,5},{7,8},{8,7},{9,10},{10,9},{11,... | collective-permute-start | bytes 129032 | tf_op jit(solution)/shard_map/ppermute | solution.py:353
  59.8 3.4 %collective-permute-start.12 = (bf16[14,3,512]{2,1,0:T(4,128)(2,1)S(1)}, bf16[14,3,512]{2,1,0:T(4,128)(2,1)S(1)}, u32[]{:S(2)}, u32[]{:S(2)}) collective-permute-start(bf16[14,3,512]{2,1,0:T(4,128)(2,1)S(1)} %get-tuple-element.95), channel_id=1, source_target_pairs={{0,1},{1,0},{2,3},{3,2},{4,5},{5,4},{6,7},{7,6},{8,9},{9,8},{10,11... | collective-permute-start | bytes 129032 | tf_op jit(solution)/shard_map/ppermute | solution.py:353

commit v10 on v8

--- a/solution.py
+++ b/solution.py
@@ -322,24 +322,73 @@
     )(place, spread)
 
 
-def features_kernel(place, d_conv, row_one, row_two, col_one, col_two, cot, taps, out, pad, total):
-    assemble(pad, d_conv, row_one, row_two, col_one, col_two, place[1] == 0, place[0] == 0)
+def main_kernel(place, d_conv, row_one, row_two, cot, taps, total, pad):
+    even_row = place[1] == 0
+    cot_wide = cot[...].astype(F32).reshape(ROWS, COLS, CH)
+    for k in range(BLOCKS):
+        lanes = slice(128 * k, 128 * k + 128)
+        rows = row_one[:, :, lanes].astype(F32), row_two[:, :, lanes].astype(F32)
+        pad[k, :, 0:3, :] = jnp.zeros((ROWS + 6, 3, 128), F32)
+        pad[k, :, 3 + COLS : 6 + COLS, :] = jnp.zeros((ROWS + 6, 3, 128), F32)
+        pad[k, 0:3, 3 : 3 + COLS, :] = jnp.where(even_row, rows[1], rows[0])
+        pad[k, 3 : 3 + ROWS, 3 : 3 + COLS, :] = d_conv[:, :, lanes].astype(F32)
+        pad[k, 3 + ROWS : 6 + ROWS, 3 : 3 + COLS, :] = jnp.where(even_row, rows[0], rows[1])
     depthwise(pad, taps, total, True)
-    cot_wide = cot[...].astype(F32).reshape(ROWS, COLS, CH)
+    for k in range(BLOCKS):
+        total[k] = total[k] + cot_wide[:, :, 128 * k : 128 * k + 128]
+
+
+def features_main(place, *operands):
+    return pl.pallas_call(
+        main_kernel,
+        in_specs=[SCALARS] + [WHOLE] * len(operands),
+        out_shape=pltpu.VMEM(TILE, F32),
+        scratch_shapes=[pltpu.VMEM(PAD, F32)],
+        compiler_params=params(),
+        cost_estimate=cost(30_000_000, 2_000_000),
+        name="features_main",
+    )(place, *(near(value) for value in operands))
+
+
+def edge_kernel(place, total, col_one, col_two, taps, out, left, right, edges):
+    even_col = place[0] == 0
+    left[...] = jnp.zeros(left.shape, F32)
+    right[...] = jnp.zeros(right.shape, F32)
     for k in range(BLOCKS):
         lanes = slice(128 * k, 128 * k + 128)
-        out[:, :, lanes] = (cot_wide[:, :, lanes] + total[k]).astype(BF16)
-
-
-def features_part(place, *operands):
-    return pl.pallas_call(
-        features_kernel,
+        cols = col_one[:, :, lanes].astype(F32), col_two[:, :, lanes].astype(F32)
+        left[k, :, 0:3, :] = jnp.where(even_col, cols[1], cols[0])
+        right[k, :, 7:10, :] = jnp.where(even_col, cols[0], cols[1])
+
+    def block(cb, carry):
+        lanes = lanes_of(cb)
+        for at, halo, start in ((0, left, 0), (8, right, 4)):
+            column = 0 if at == 0 else COLS - 8
+            value = total[cb, :, column : column + 8, :]
+            for s in range(3):
+                band = halo[cb, :, s : s + 8, :]
+                for r in range(7):
+                    tap = 7 * (6 - r) + 6 - s - start
+                    value = value + band[r : r + ROWS] * taps[tap : tap + 1, lanes].reshape(1, 1, 128)
+            edges[cb, :, at : at + 8, :] = value
+        return carry
+
+    lax.fori_loop(0, BLOCKS, block, 0)
+    for k in range(BLOCKS):
+        parts = [edges[k, :, 0:8, :], total[k, :, 8 : COLS - 8, :], edges[k, :, 8:16, :]]
+        out[:, :, 128 * k : 128 * k + 128] = jnp.concatenate(parts, axis=1).astype(BF16)
+
+
+def features_edge(place, *operands):
+    side = (BLOCKS, ROWS + 6, 16, 128)
+    return pl.pallas_call(
+        edge_kernel,
         in_specs=[SCALARS] + [WHOLE] * len(operands),
         out_shape=jax.ShapeDtypeStruct((ROWS, COLS, CH), BF16),
-        scratch_shapes=[pltpu.VMEM(PAD, F32), pltpu.VMEM(TILE, F32)],
-        compiler_params=params(),
-        cost_estimate=cost(30_000_000, 2_000_000),
-        name="features_part",
+        scratch_shapes=[pltpu.VMEM(side, F32), pltpu.VMEM(side, F32), pltpu.VMEM((BLOCKS, ROWS, 16, 128), F32)],
+        compiler_params=params(),
+        cost_estimate=cost(6_000_000, 1_000_000),
+        name="features_edge",
     )(place, *(near(value) for value in operands))
 
 
@@ -415,12 +464,12 @@
     given = [swap_chips(give, axis) for axis, give in enumerate(gives)]
     gives, d_one, d_two = lax.optimization_barrier((gives, d_one, d_two))
     d_rows = exchange(d_one, d_two, ROW)
+    message = add_pair(keep, *given)
+    message, d_rows = lax.optimization_barrier((message, d_rows))
+    spread = spread_chips(message)
     d_cols = exchange(*halo_sides(*d_rows, d_conv, even_row, even_col), COL)
-    given, d_cols = lax.optimization_barrier((given, d_cols))
-    message = add_pair(keep, *given)
-    spread = spread_chips(message)
-    d_conv, message = lax.optimization_barrier((d_conv, message))
-    grad_features = features_part(place, d_conv, *d_rows, *d_cols, cot, taps)
+    total = features_main(place, d_conv, *d_rows, cot, taps)
+    grad_features = features_edge(place, total, *d_cols, taps)
     grad_in, grad_out, grad_channel, grad_bias = sum_chips(place, spread, factor)
     return (
         block_rows.reshape(ROWS, COLS, CH),

time: 82.1 us -> 77.1 us (0.939)
  waiting for transfers between devices: 19.6 us -> 16.5 us
  starting transfers between devices: 37.5 us -> 34.5 us
  Pallas kernels: 20.1 us -> 21.3 us
    ppermute x8, starting transfers between devices: 18.5 us -> 12.8 us  [exchange(): met.append(lax.ppermute(value, axis, pairs))]
    all_to_all x1, waiting for transfers between devices: 15.4 us -> 10.4 us  [spread_chips(): lax.all_to_all(value, EVERY, 0, 0, axis_index_groups=list(groups.values()...]
    all_to_all x1, starting transfers between devices: 8.03 us -> 10.5 us  [spread_chips(): lax.all_to_all(value, EVERY, 0, 0, axis_index_groups=list(groups.values()...]
    ppermute x3, waiting for transfers between devices: 1.54 us -> 3.05 us  [swap_chips(): return lax.ppermute(value, EVERY, pairs)]
    pallas_call x1 -> x2, Pallas kernels: 3.65 us -> 4.76 us  [the longest x1 2.95 us: features_main(): pl.pallas_call(main_kernel, in_specs=[SCALARS] + [WHOLE] * len(operands),...]
  transfers between devices with their start and end apart: 15 -> 15, of which waited for: 5 -> 5; matrix products, arithmetic and copies ran while one was open for 3% -> 3% of each run, Pallas kernels for 10% -> 14%
where the time goes in v10:
time: 77.1 us; the launch traced here: 76.8 us
  starting transfers between devices  34.5 us (45%)
  Pallas kernels  21.3 us (28%)
  waiting for transfers between devices  16.5 us (21%)
  local copies, waits for them, and re-layouts  2.36 us (3%)
  other arithmetic  1.27 us (2%)
  between operations  0.83 us (1%)
    ppermute x8, starting transfers between devices, exchange(): met.append(lax.ppermute(value, axis, pairs))  12.8 us
    all_to_all x1, starting transfers between devices, spread_chips(): lax.all_to_all(value, EVERY, 0, 0, axis_index_groups=list(groups.values()...  10.5 us
    all_to_all x1, waiting for transfers between devices, spread_chips(): lax.all_to_all(value, EVERY, 0, 0, axis_index_groups=list(groups.values()...  10.4 us
    pallas_call x1, Pallas kernels, grads(): pl.pallas_call(grads_kernel, in_specs=[SCALARS] + [WHOLE] * len(operands)...  7.95 us
    ppermute x3, starting transfers between devices, swap_chips(): return lax.ppermute(value, EVERY, pairs)  5.96 us
    ppermute x3, starting transfers between devices, swap_cores(): return lax.ppermute(value, 'c', [(0, 1), (1, 0)])  5.33 us
    ppermute x3, waiting for transfers between devices, swap_chips(): return lax.ppermute(value, EVERY, pairs)  3.05 us
    pallas_call x1, Pallas kernels, features_main(): pl.pallas_call(main_kernel, in_specs=[SCALARS] + [WHOLE] * len(operands),...  2.95 us
  transfers between devices with their start and end apart: 15, of which 5 were waited for; matrix products, arithmetic and copies ran while one was open for 3% of the time, Pallas kernels for 14%

profile of v10, /device:TPU:0, one launch (start us, length us, event | category | flops | bytes accessed | tf_op | source)
XLA Modules:
  0.0 76.8 jit_solution(6011128029050086428)
XLA Ops:
  0.6 1.0 %broadcast_select_fusion.4 = (bf16[3,32,512]{2,1,0:T(8,128)(2,1)S(1)}, bf16[3,32,512]{2,1,0:T(8,128)(2,1)S(1)}) fusion(pred[]{:T(512)S(6)} %eq.8, bf16[8,32,512]{2,1,0:T(8,128)(2,1)} %refs_0_.1), kind=kLoop, calls=%fused_computation.4 | loop fusion | flops 98304 | bytes 393217 | tf_op jit(solution)/shard_map/jit(_where)/select_n | solution.py:450
  1.6 0.7 collective-permute-start.1
  2.3 6.3 %collective-permute-start = (bf16[3,32,512]{2,1,0:T(8,128)(2,1)S(1)}, bf16[3,32,512]{2,1,0:T(8,128)(2,1)S(1)}, u32[]{:S(2)}, u32[]{:S(2)}) collective-permute-start(bf16[3,32,512]{2,1,0:T(8,128)(2,1)S(1)} %get-tuple-element.77), channel_id=1, source_target_pairs={{0,16},{16,0},{32,48},{48,32},{64,80},{80,64},{96,112},{112,96},{1... | collective-permute-start | bytes 294920 | tf_op jit(solution)/shard_map/ppermute | solution.py:402
  8.6 0.9 %fusion.1 = (bf16[8,3,512]{2,1,0:T(4,128)(2,1)S(1)}, bf16[8,3,512]{2,1,0:T(4,128)(2,1)S(1)}) fusion(bf16[8,32,512]{2,1,0:T(8,128)(2,1)} %refs_0_.1), kind=kLoop, calls=%fused_computation.16 | loop fusion | bytes 98304 | tf_op jit(solution)/shard_map/slice | solution.py:409
  9.5 1.4 %stack.39.refs_3_ = f32[5,512]{1,0:T(8,128)} concatenate(f32[1,512]{1,0:T(1,128)} %bitcast.15, f32[1,512]{1,0:T(1,128)} %bitcast.16, f32[1,512]{1,0:T(1,128)} %bitcast.17, f32[1,512]{1,0:T(1,128)} %bitcast.18, f32[1,512]{1,0:T(1,128)} %bitcast.19), dimensions={0} | concatenate | bytes 20480 | tf_op jit(solution)/shard_map/stack | solution.py:448
  10.9 2.5 %fetch.1 = (bf16[8,32,512]{2,1,0:T(8,128)(2,1)S(1)}, bf16[256,512]{1,0:T(8,128)(2,1)S(1)}, f32[49,512]{1,0:T(8,128)S(1)}, f32[5,512]{1,0:T(8,128)S(1)}, bf16[512...) custom-call(bf16[8,32,512]{2,1,0:T(8,128)(2,1)} %refs_0_.1, ...), custom_call_target="tpu_custom_call" | custom-call | bytes 5000000 | tf_op jit(solution)/shard_map/fetch/pallas_call | solution.py:65
  13.5 0.1 broadcast_select_fusion.8
  13.6 0.1 collective-permute-start.2
  13.7 0.7 collective-permute-start.3
  14.4 0.5 collective-permute-done.2.col_one
  14.9 7.9 %grads.1 = (f32[4,14,40,128]{3,2,1,0:T(8,128)S(1)}, bf16[256,512]{1,0:T(8,128)(2,1)}, bf16[8,32,512]{2,1,0:T(8,128)(2,1)S(1)}, bf16[3,32,512]{2,1,0:T(8,128)(2,1...) custom-call(s32[3]{0:T(128)S(1)} %pad_add_fusion.place.refs_0_, ...), custom_call_target="tpu_custom_call" | custom-call | flops 3200000000 | bytes 12000000 | tf_op jit(solution)/shard_map/grads/pallas_call | solution.py:188
  22.9 4.7 %collective-permute-start.4 = (bf16[64,64,128]{2,1,0:T(8,128)(2,1)S(1)}, bf16[64,64,128]{2,1,0:T(8,128)(2,1)S(1)}, u32[]{:S(2)}, u32[]{:S(2)}) collective-permute-start(bf16[64,64,128]{2,1,0:T(8,128)(2,1)S(1)} %get-tuple-element.52), channel_id=1, source_target_pairs={{0,1},{1,0},{2,3},{3,2},{4,5},{5,4},{6,7},{7,6},{8,9},{9,8},{10,11... | collective-permute-start | bytes 3145736 | tf_op jit(solution)/shard_map/ppermute | solution.py:415
  27.6 2.3 %tap_rows.1.small_one = f32[64,8,128]{2,1,0:T(8,128)S(1)} custom-call(f32[4,14,40,128]{3,2,1,0:T(8,128)S(1)} %get-tuple-element.55.pad, bf16[8,32,512]{2,1,0:T(8,128)(2,1)S(1)} %get-tuple-element.50.d_conv, f32[16,512]{1,0:T(8,128)S(1)} %get-tuple-element.56.rows), custom_call_target="tpu_custom_call" | custom-call | flops 30000000 | bytes 2000000 | tf_op jit(solution)/shard_map/tap_rows/pallas_call | solution.py:235
  29.9 0.6 collective-permute-start.6
  30.5 1.2 %collective-permute-done.6.small_two = f32[64,8,128]{2,1,0:T(8,128)S(1)} collective-permute-done((f32[64,8,128]{2,1,0:T(8,128)S(1)}, f32[64,8,128]{2,1,0:T(8,128)S(1)}, u32[]{:S(2)}, u32[]{:S(2)}) %collective-permute-start.6) | collective-permute-done | bytes 262176 | tf_op jit(solution)/shard_map/ppermute | solution.py:415
  31.8 1.0 %split_pair.1 = (bf16[32,136,128]{2,1,0:T(8,128)(2,1)S(1)}, bf16[32,48,128]{2,1,0:T(8,128)(2,1)S(1)}, bf16[32,48,128]{2,1,0:T(8,128)(2,1)S(1)}, bf16[32,40,128]{2,1,0:T(8,128)(2,1)S(1)}) custom-call(s32[3]{0:T(128)S(1)} %pad_add_fusion.place.refs_0_, bf16[64,64,128]{2,1,0:T(8,128)(2,1)S(1)} %get-tuple-element.51.out_one, ...), custom_call_target="tpu_custom_call" | custom-call | flops 1000000 | bytes 6000000 | tf_op jit(solution)/shard_map/split_pair/pallas_call | solution.py:270
  32.8 2.0 %collective-permute-start.7 = (bf16[32,48,128]{2,1,0:T(8,128)(2,1)S(1)}, bf16[32,48,128]{2,1,0:T(8,128)(2,1)S(1)}, u32[]{:S(2)}, u32[]{:S(2)}) collective-permute-start(bf16[32,48,128]{2,1,0:T(8,128)(2,1)S(1)} %get-tuple-element.58), channel_id=1, source_target_pairs={{0,32},{1,97},{2,34},{3,99},{4,36},{5,101},{6,38},{7,103},{8,40},{... | collective-permute-start | bytes 1179656 | tf_op jit(solution)/shard_map/ppermute | solution.py:430
  34.8 2.5 %collective-permute-start.8 = (bf16[32,48,128]{2,1,0:T(8,128)(2,1)S(1)}, bf16[32,48,128]{2,1,0:T(8,128)(2,1)S(1)}, u32[]{:S(2)}, u32[]{:S(2)}) collective-permute-start(bf16[32,48,128]{2,1,0:T(8,128)(2,1)S(1)} %get-tuple-element.59), channel_id=1, source_target_pairs={{0,2},{1,19},{2,0},{3,17},{4,6},{5,23},{6,4},{7,21},{8,10},{9,27},... | collective-permute-start | bytes 1179656 | tf_op jit(solution)/shard_map/ppermute | solution.py:430
  37.3 1.5 %collective-permute-start.9 = (bf16[32,40,128]{2,1,0:T(8,128)(2,1)S(1)}, bf16[32,40,128]{2,1,0:T(8,128)(2,1)S(1)}, u32[]{:S(2)}, u32[]{:S(2)}) collective-permute-start(bf16[32,40,128]{2,1,0:T(8,128)(2,1)S(1)} %get-tuple-element.60), channel_id=1, source_target_pairs={{0,4},{1,13},{2,6},{3,15},{4,0},{5,9},{6,2},{7,11},{8,12},{9,5},{1... | collective-permute-start | bytes 983048 | tf_op jit(solution)/shard_map/ppermute | solution.py:430
  38.8 1.9 %collective-permute-start.10 = (bf16[3,32,512]{2,1,0:T(8,128)(2,1)S(1)}, bf16[3,32,512]{2,1,0:T(8,128)(2,1)S(1)}, u32[]{:S(2)}, u32[]{:S(2)}) collective-permute-start(bf16[3,32,512]{2,1,0:T(8,128)(2,1)S(1)} %get-tuple-element.63), channel_id=1, source_target_pairs={{0,16},{16,0},{32,48},{48,32},{64,80},{80,64},{96,112},{112,96},{1... | collective-permute-start | bytes 294920 | tf_op jit(solution)/shard_map/ppermute | solution.py:402
  40.6 0.7 collective-permute-start.11
  41.3 3.0 %collective-permute-done.9.three = bf16[32,40,128]{2,1,0:T(8,128)(2,1)S(1)} collective-permute-done((bf16[32,40,128]{2,1,0:T(8,128)(2,1)S(1)}, bf16[32,40,128]{2,1,0:T(8,128)(2,1)S(1)}, u32[]{:S(2)}, u32[]{:S(2)}) %collective-permute-start.9) | collective-permute-done | bytes 327712 | tf_op jit(solution)/shard_map/ppermute | solution.py:430
  44.4 1.3 %add_pair.1 = bf16[32,136,128]{2,1,0:T(8,128)(2,1)} custom-call(bf16[32,136,128]{2,1,0:T(8,128)(2,1)S(1)} %get-tuple-element.57.keep, bf16[32,48,128]{2,1,0:T(8,128)(2,1)S(1)} %collective-permute-done.7.one, bf16[32,48,128]{2,1,0:T(8,128)(2,1)S(1)} %collective-permute-done.8.two, bf16[32,40,128]{2,1,0:T(8,128)(2,1)S(1)} %collective-permute-done.9.three), custom_call_target="tpu_custom_call" | custom-call | flops 1000000 | bytes 3000000 | tf_op jit(solution)/shard_map/add_pair/pallas_call | solution.py:287
  45.7 1.4 %collective-permute-done.10.row_one = bf16[3,32,512]{2,1,0:T(8,128)(2,1)S(1)} collective-permute-done((bf16[3,32,512]{2,1,0:T(8,128)(2,1)S(1)}, bf16[3,32,512]{2,1,0:T(8,128)(2,1)S(1)}, u32[]{:S(2)}, u32[]{:S(2)}) %collective-permute-start.10) | collective-permute-done | bytes 98336 | tf_op jit(solution)/shard_map/ppermute | solution.py:402
  47.0 10.5 %all-to-all-start = ((bf16[32,136,128]{2,1,0:T(8,128)(2,1)}), bf16[32,136,128]{2,1,0:T(8,128)(2,1)S(1)}, u32[]{:S(2)}, u32[]{:S(2)}) async-start(bf16[32,136,128]{2,1,0:T(8,128)(2,1)} %add_pair.1), calls=%async_computation | async-start | bytes 2228224 | tf_op jit(solution)/shard_map/all_to_all | solution.py:437
  57.6 0.1 broadcast_select_fusion.6
  57.7 0.7 collective-permute-start.13
  58.4 1.9 %collective-permute-start.12 = (bf16[14,3,512]{2,1,0:T(4,128)(2,1)S(1)}, bf16[14,3,512]{2,1,0:T(4,128)(2,1)S(1)}, u32[]{:S(2)}, u32[]{:S(2)}) collective-permute-start(bf16[14,3,512]{2,1,0:T(4,128)(2,1)S(1)} %get-tuple-element.83), channel_id=1, source_target_pairs={{0,1},{1,0},{2,3},{3,2},{4,5},{5,4},{6,7},{7,6},{8,9},{9,8},{10,11... | collective-permute-start | bytes 129032 | tf_op jit(solution)/shard_map/ppermute | solution.py:402
  60.2 2.9 %features_main.1.total = f32[4,8,32,128]{3,2,1,0:T(8,128)S(1)} custom-call(s32[3]{0:T(128)S(1)} %pad_add_fusion.place.refs_0_, bf16[8,32,512]{2,1,0:T(8,128)(2,1)S(1)} %get-tuple-element.50.d_conv, bf16[3,32,512]{2,1,0:T(8,128)(2,1)S(1)} %collective-permute-done.10.row_one, bf16[3,32,512]{2,1,0:T(8,128)(2,1)S(1)} %collective-permute-done.11.row_two, ...), custom_call_target="tpu_custom_call" | custom-call | flops 30000000 | bytes 2000000 | tf_op jit(solution)/shard_map/features_main/pallas_call | solution.py:342
  63.2 1.8 %features_edge.1 = bf16[8,32,512]{2,1,0:T(8,128)(2,1)} custom-call(s32[3]{0:T(128)S(1)} %pad_add_fusion.place.refs_0_, f32[4,8,32,128]{3,2,1,0:T(8,128)S(1)} %features_main.1.total, bf16[14,3,512]{2,1,0:T(4,128)(2,1)S(1)} %collective-permute-done.12.col_one, bf16[14,3,512]{2,1,0:T(4,128)(2,1)S(1)} %collective-permute-done.13.col_two, ...), custom_call_target="tpu_custom_call" | custom-call | flops 6000000 | bytes 1000000 | tf_op jit(solution)/shard_map/features_edge/pallas_call | solution.py:384
  65.0 10.4 %all-to-all-done.refs_1_ = bf16[32,136,128]{2,1,0:T(8,128)(2,1)S(1)} async-done(((bf16[32,136,128]{2,1,0:T(8,128)(2,1)}), bf16[32,136,128]{2,1,0:T(8,128)(2,1)S(1)}, u32[]{:S(2)}, u32[]{:S(2)}) %all-to-all-start) | async-done | bytes 1114144 | tf_op jit(solution)/shard_map/all_to_all | solution.py:437
  75.4 1.4 %sum_chips.1 = (f32[4,2048]{1,0:T(4,128)}, f32[16,512]{1,0:T(8,128)}, f32[4,54]{1,0:T(4,128)}, f32[1,16]{1,0:T(1,128)}) custom-call(s32[3]{0:T(128)S(1)} %pad_add_fusion.place.refs_0_, bf16[32,136,128]{2,1,0:T(8,128)(2,1)S(1)} %all-to-all-done.refs_1_), custom_call_target="tpu_custom_call" | custom-call | flops 1000000 | bytes 1000000 | tf_op jit(solution)/shard_map/sum_chips/pallas_call | solution.py:315
  (18 shorter events, 0.2 us)
Async XLA Ops:
  1.6 11.8 %collective-permute-start.1 = (bf16[3,32,512]{2,1,0:T(8,128)(2,1)S(1)}, bf16[3,32,512]{2,1,0:T(8,128)(2,1)S(1)}, u32[]{:S(2)}, u32[]{:S(2)}) collective-permute-start(bf16[3,32,512]{2,1,0:T(8,128)(2,1)S(1)} %get-tuple-element.76), channel_id=1, source_target_pairs={{16,32},{32,16},{48,64},{64,48},{80,96},{96,80},{17,33},{33,17},{4... | collective-permute-start | bytes 294920 | tf_op jit(solution)/shard_map/ppermute | solution.py:402
  2.3 11.1 %collective-permute-start = (bf16[3,32,512]{2,1,0:T(8,128)(2,1)S(1)}, bf16[3,32,512]{2,1,0:T(8,128)(2,1)S(1)}, u32[]{:S(2)}, u32[]{:S(2)}) collective-permute-start(bf16[3,32,512]{2,1,0:T(8,128)(2,1)S(1)} %get-tuple-element.77), channel_id=1, source_target_pairs={{0,16},{16,0},{32,48},{48,32},{64,80},{80,64},{96,112},{112,96},{1... | collective-permute-start | bytes 294920 | tf_op jit(solution)/shard_map/ppermute | solution.py:402
  13.6 1.3 %collective-permute-start.2 = (bf16[14,3,512]{2,1,0:T(4,128)(2,1)S(1)}, bf16[14,3,512]{2,1,0:T(4,128)(2,1)S(1)}, u32[]{:S(2)}, u32[]{:S(2)}) collective-permute-start(bf16[14,3,512]{2,1,0:T(4,128)(2,1)S(1)} %get-tuple-element.41), channel_id=1, source_target_pairs={{0,1},{1,0},{2,3},{3,2},{4,5},{5,4},{6,7},{7,6},{8,9},{9,8},{10,11... | collective-permute-start | bytes 129032 | tf_op jit(solution)/shard_map/ppermute | solution.py:402
  13.7 1.2 %collective-permute-start.3 = (bf16[14,3,512]{2,1,0:T(4,128)(2,1)S(1)}, bf16[14,3,512]{2,1,0:T(4,128)(2,1)S(1)}, u32[]{:S(2)}, u32[]{:S(2)}) collective-permute-start(bf16[14,3,512]{2,1,0:T(4,128)(2,1)S(1)} %get-tuple-element.42), channel_id=1, source_target_pairs={{1,2},{2,1},{3,4},{4,3},{5,6},{6,5},{7,8},{8,7},{9,10},{10,9},{11,... | collective-permute-start | bytes 129032 | tf_op jit(solution)/shard_map/ppermute | solution.py:402
  22.9 8.9 %collective-permute-start.4 = (bf16[64,64,128]{2,1,0:T(8,128)(2,1)S(1)}, bf16[64,64,128]{2,1,0:T(8,128)(2,1)S(1)}, u32[]{:S(2)}, u32[]{:S(2)}) collective-permute-start(bf16[64,64,128]{2,1,0:T(8,128)(2,1)S(1)} %get-tuple-element.52), channel_id=1, source_target_pairs={{0,1},{1,0},{2,3},{3,2},{4,5},{5,4},{6,7},{7,6},{8,9},{9,8},{10,11... | collective-permute-start | bytes 3145736 | tf_op jit(solution)/shard_map/ppermute | solution.py:415
  27.6 4.2 %collective-permute-start.5 = (bf16[64,64,128]{2,1,0:T(8,128)(2,1)S(1)}, bf16[64,64,128]{2,1,0:T(8,128)(2,1)S(1)}, u32[]{:S(2)}, u32[]{:S(2)}) collective-permute-start(bf16[64,64,128]{2,1,0:T(8,128)(2,1)S(1)} %get-tuple-element.54), channel_id=1, source_target_pairs={{0,1},{1,0},{2,3},{3,2},{4,5},{5,4},{6,7},{7,6},{8,9},{9,8},{10,11... | collective-permute-start | bytes 3145736 | tf_op jit(solution)/shard_map/ppermute | solution.py:415
  29.9 1.8 %collective-permute-start.6 = (f32[64,8,128]{2,1,0:T(8,128)S(1)}, f32[64,8,128]{2,1,0:T(8,128)S(1)}, u32[]{:S(2)}, u32[]{:S(2)}) collective-permute-start(f32[64,8,128]{2,1,0:T(8,128)S(1)} %tap_rows.1.small_one), channel_id=1, source_target_pairs={{0,1},{1,0},{2,3},{3,2},{4,5},{5,4},{6,7},{7,6},{8,9},{9,8},{10,11... | collective-permute-start | bytes 786440 | tf_op jit(solution)/shard_map/ppermute | solution.py:415
  32.8 11.6 %collective-permute-start.7 = (bf16[32,48,128]{2,1,0:T(8,128)(2,1)S(1)}, bf16[32,48,128]{2,1,0:T(8,128)(2,1)S(1)}, u32[]{:S(2)}, u32[]{:S(2)}) collective-permute-start(bf16[32,48,128]{2,1,0:T(8,128)(2,1)S(1)} %get-tuple-element.58), channel_id=1, source_target_pairs={{0,32},{1,97},{2,34},{3,99},{4,36},{5,101},{6,38},{7,103},{8,40},{... | collective-permute-start | bytes 1179656 | tf_op jit(solution)/shard_map/ppermute | solution.py:430
  34.8 9.6 %collective-permute-start.8 = (bf16[32,48,128]{2,1,0:T(8,128)(2,1)S(1)}, bf16[32,48,128]{2,1,0:T(8,128)(2,1)S(1)}, u32[]{:S(2)}, u32[]{:S(2)}) collective-permute-start(bf16[32,48,128]{2,1,0:T(8,128)(2,1)S(1)} %get-tuple-element.59), channel_id=1, source_target_pairs={{0,2},{1,19},{2,0},{3,17},{4,6},{5,23},{6,4},{7,21},{8,10},{9,27},... | collective-permute-start | bytes 1179656 | tf_op jit(solution)/shard_map/ppermute | solution.py:430
  37.3 7.1 %collective-permute-start.9 = (bf16[32,40,128]{2,1,0:T(8,128)(2,1)S(1)}, bf16[32,40,128]{2,1,0:T(8,128)(2,1)S(1)}, u32[]{:S(2)}, u32[]{:S(2)}) collective-permute-start(bf16[32,40,128]{2,1,0:T(8,128)(2,1)S(1)} %get-tuple-element.60), channel_id=1, source_target_pairs={{0,4},{1,13},{2,6},{3,15},{4,0},{5,9},{6,2},{7,11},{8,12},{9,5},{1... | collective-permute-start | bytes 983048 | tf_op jit(solution)/shard_map/ppermute | solution.py:430
  38.8 8.2 %collective-permute-start.10 = (bf16[3,32,512]{2,1,0:T(8,128)(2,1)S(1)}, bf16[3,32,512]{2,1,0:T(8,128)(2,1)S(1)}, u32[]{:S(2)}, u32[]{:S(2)}) collective-permute-start(bf16[3,32,512]{2,1,0:T(8,128)(2,1)S(1)} %get-tuple-element.63), channel_id=1, source_target_pairs={{0,16},{16,0},{32,48},{48,32},{64,80},{80,64},{96,112},{112,96},{1... | collective-permute-start | bytes 294920 | tf_op jit(solution)/shard_map/ppermute | solution.py:402
  40.6 6.4 %collective-permute-start.11 = (bf16[3,32,512]{2,1,0:T(8,128)(2,1)S(1)}, bf16[3,32,512]{2,1,0:T(8,128)(2,1)S(1)}, u32[]{:S(2)}, u32[]{:S(2)}) collective-permute-start(bf16[3,32,512]{2,1,0:T(8,128)(2,1)S(1)} %get-tuple-element.64), channel_id=1, source_target_pairs={{16,32},{32,16},{48,64},{64,48},{80,96},{96,80},{17,33},{33,17},{4... | collective-permute-start | bytes 294920 | tf_op jit(solution)/shard_map/ppermute | solution.py:402
  47.0 28.4 %all-to-all-start = ((bf16[32,136,128]{2,1,0:T(8,128)(2,1)}), bf16[32,136,128]{2,1,0:T(8,128)(2,1)S(1)}, u32[]{:S(2)}, u32[]{:S(2)}) async-start(bf16[32,136,128]{2,1,0:T(8,128)(2,1)} %add_pair.1), calls=%async_computation | async-start | bytes 2228224 | tf_op jit(solution)/shard_map/all_to_all | solution.py:437
  57.7 5.5 %collective-permute-start.13 = (bf16[14,3,512]{2,1,0:T(4,128)(2,1)S(1)}, bf16[14,3,512]{2,1,0:T(4,128)(2,1)S(1)}, u32[]{:S(2)}, u32[]{:S(2)}) collective-permute-start(bf16[14,3,512]{2,1,0:T(4,128)(2,1)S(1)} %get-tuple-element.82), channel_id=1, source_target_pairs={{1,2},{2,1},{3,4},{4,3},{5,6},{6,5},{7,8},{8,7},{9,10},{10,9},{11,... | collective-permute-start | bytes 129032 | tf_op jit(solution)/shard_map/ppermute | solution.py:402
  58.4 4.9 %collective-permute-start.12 = (bf16[14,3,512]{2,1,0:T(4,128)(2,1)S(1)}, bf16[14,3,512]{2,1,0:T(4,128)(2,1)S(1)}, u32[]{:S(2)}, u32[]{:S(2)}) collective-permute-start(bf16[14,3,512]{2,1,0:T(4,128)(2,1)S(1)} %get-tuple-element.83), channel_id=1, source_target_pairs={{0,1},{1,0},{2,3},{3,2},{4,5},{5,4},{6,7},{7,6},{8,9},{9,8},{10,11... | collective-permute-start | bytes 129032 | tf_op jit(solution)/shard_map/ppermute | solution.py:402

commit v11 on v10

--- a/solution.py
+++ b/solution.py
@@ -460,14 +460,17 @@
     )
     met_out, met_in = swap_cores(theirs_out), swap_cores(theirs_in)
     small = tap_rows(pad, d_conv, rows)
-    keep, *gives = split_pair(place, mine_out, met_out, mine_in, met_in, small, swap_cores(small))
+    d_rows = exchange(d_one, d_two, ROW)
+    met_small = swap_cores(small)
+    met_out, met_in, met_small, d_rows = lax.optimization_barrier((met_out, met_in, met_small, d_rows))
+    keep, *gives = split_pair(place, mine_out, met_out, mine_in, met_in, small, met_small)
     given = [swap_chips(give, axis) for axis, give in enumerate(gives)]
-    gives, d_one, d_two = lax.optimization_barrier((gives, d_one, d_two))
-    d_rows = exchange(d_one, d_two, ROW)
+    gives, sides = lax.optimization_barrier((gives, halo_sides(*d_rows, d_conv, even_row, even_col)))
+    d_cols = exchange(*sides, COL)
+    given, d_cols = lax.optimization_barrier((given, d_cols))
     message = add_pair(keep, *given)
-    message, d_rows = lax.optimization_barrier((message, d_rows))
     spread = spread_chips(message)
-    d_cols = exchange(*halo_sides(*d_rows, d_conv, even_row, even_col), COL)
+    d_conv, message = lax.optimization_barrier((d_conv, message))
     total = features_main(place, d_conv, *d_rows, cot, taps)
     grad_features = features_edge(place, total, *d_cols, taps)
     grad_in, grad_out, grad_channel, grad_bias = sum_chips(place, spread, factor)

time: 77.1 us -> 84.5 us (1.096)
  waiting for transfers between devices: 16.5 us -> 22.9 us
  starting transfers between devices: 34.5 us -> 35.5 us
    all_to_all x1, waiting for transfers between devices: 10.4 us -> 14.4 us  [spread_chips(): lax.all_to_all(value, EVERY, 0, 0, axis_index_groups=list(groups.values()...]
    ppermute x3, starting transfers between devices: 5.96 us -> 9.9 us  [swap_chips(): return lax.ppermute(value, EVERY, pairs)]
    ppermute x8, waiting for transfers between devices: 1.85 us -> 4.97 us  [exchange(): met.append(lax.ppermute(value, axis, pairs))]
    all_to_all x1, starting transfers between devices: 10.5 us -> 8.87 us  [spread_chips(): lax.all_to_all(value, EVERY, 0, 0, axis_index_groups=list(groups.values()...]
    ppermute x8, starting transfers between devices: 12.8 us -> 11.4 us  [exchange(): met.append(lax.ppermute(value, axis, pairs))]
    ppermute x3, waiting for transfers between devices: 1.24 us -> 0.01 us  [swap_cores(): return lax.ppermute(value, 'c', [(0, 1), (1, 0)])]
  transfers between devices with their start and end apart: 15 -> 15, of which waited for: 5 -> 5; matrix products, arithmetic and copies ran while one was open for 3% -> 3% of each run, Pallas kernels for 14% -> 11%
where the time goes in v11:
time: 84.5 us; the launch traced here: 84.1 us
  starting transfers between devices  35.5 us (42%)
  waiting for transfers between devices  22.9 us (27%)
  Pallas kernels  21.3 us (25%)
  local copies, waits for them, and re-layouts  2.35 us (3%)
  other arithmetic  1.27 us (2%)
    all_to_all x1, waiting for transfers between devices, spread_chips(): lax.all_to_all(value, EVERY, 0, 0, axis_index_groups=list(groups.values()...  14.4 us
    ppermute x8, starting transfers between devices, exchange(): met.append(lax.ppermute(value, axis, pairs))  11.4 us
    ppermute x3, starting transfers between devices, swap_chips(): return lax.ppermute(value, EVERY, pairs)  9.9 us
    all_to_all x1, starting transfers between devices, spread_chips(): lax.all_to_all(value, EVERY, 0, 0, axis_index_groups=list(groups.values()...  8.87 us
    pallas_call x1, Pallas kernels, grads(): pl.pallas_call(grads_kernel, in_specs=[SCALARS] + [WHOLE] * len(operands)...  7.95 us
    ppermute x3, starting transfers between devices, swap_cores(): return lax.ppermute(value, 'c', [(0, 1), (1, 0)])  5.33 us
    ppermute x8, waiting for transfers between devices, exchange(): met.append(lax.ppermute(value, axis, pairs))  4.97 us
    ppermute x3, waiting for transfers between devices, swap_chips(): return lax.ppermute(value, EVERY, pairs)  3.56 us
  transfers between devices with their start and end apart: 15, of which 5 were waited for; matrix products, arithmetic and copies ran while one was open for 3% of the time, Pallas kernels for 11%

profile of v11, /device:TPU:0, one launch (start us, length us, event | category | flops | bytes accessed | tf_op | source)
XLA Modules:
  0.0 84.1 jit_solution(10529895862301477971)
XLA Ops:
  0.6 1.0 %broadcast_select_fusion.4 = (bf16[3,32,512]{2,1,0:T(8,128)(2,1)S(1)}, bf16[3,32,512]{2,1,0:T(8,128)(2,1)S(1)}) fusion(pred[]{:T(512)S(6)} %eq.8, bf16[8,32,512]{2,1,0:T(8,128)(2,1)} %refs_0_.1), kind=kLoop, calls=%fused_computation.4 | loop fusion | flops 98304 | bytes 393217 | tf_op jit(solution)/shard_map/jit(_where)/select_n | solution.py:450
  1.6 0.7 collective-permute-start.1
  2.3 6.3 %collective-permute-start = (bf16[3,32,512]{2,1,0:T(8,128)(2,1)S(1)}, bf16[3,32,512]{2,1,0:T(8,128)(2,1)S(1)}, u32[]{:S(2)}, u32[]{:S(2)}) collective-permute-start(bf16[3,32,512]{2,1,0:T(8,128)(2,1)S(1)} %get-tuple-element.93), channel_id=1, source_target_pairs={{0,16},{16,0},{32,48},{48,32},{64,80},{80,64},{96,112},{112,96},{1... | collective-permute-start | bytes 294920 | tf_op jit(solution)/shard_map/ppermute | solution.py:402
  8.6 0.9 %fusion.1 = (bf16[8,3,512]{2,1,0:T(4,128)(2,1)S(1)}, bf16[8,3,512]{2,1,0:T(4,128)(2,1)S(1)}) fusion(bf16[8,32,512]{2,1,0:T(8,128)(2,1)} %refs_0_.1), kind=kLoop, calls=%fused_computation.16 | loop fusion | bytes 98304 | tf_op jit(solution)/shard_map/slice | solution.py:409
  9.5 1.4 %stack.39.refs_3_ = f32[5,512]{1,0:T(8,128)} concatenate(f32[1,512]{1,0:T(1,128)} %bitcast.15, f32[1,512]{1,0:T(1,128)} %bitcast.16, f32[1,512]{1,0:T(1,128)} %bitcast.17, f32[1,512]{1,0:T(1,128)} %bitcast.18, f32[1,512]{1,0:T(1,128)} %bitcast.19), dimensions={0} | concatenate | bytes 20480 | tf_op jit(solution)/shard_map/stack | solution.py:448
  10.9 2.5 %fetch.1 = (bf16[8,32,512]{2,1,0:T(8,128)(2,1)S(1)}, bf16[256,512]{1,0:T(8,128)(2,1)S(1)}, f32[49,512]{1,0:T(8,128)S(1)}, f32[5,512]{1,0:T(8,128)S(1)}, bf16[512...) custom-call(bf16[8,32,512]{2,1,0:T(8,128)(2,1)} %refs_0_.1, ...), custom_call_target="tpu_custom_call" | custom-call | bytes 5000000 | tf_op jit(solution)/shard_map/fetch/pallas_call | solution.py:65
  13.5 0.1 broadcast_select_fusion.8
  13.6 0.1 collective-permute-start.2
  13.7 0.7 collective-permute-start.3
  14.4 0.5 collective-permute-done.2.col_one
  14.9 7.9 %grads.1 = (f32[4,14,40,128]{3,2,1,0:T(8,128)S(1)}, bf16[256,512]{1,0:T(8,128)(2,1)}, bf16[8,32,512]{2,1,0:T(8,128)(2,1)S(1)}, bf16[3,32,512]{2,1,0:T(8,128)(2,1...) custom-call(s32[3]{0:T(128)S(1)} %pad_add_fusion.place.refs_0_, ...), custom_call_target="tpu_custom_call" | custom-call | flops 3200000000 | bytes 12000000 | tf_op jit(solution)/shard_map/grads/pallas_call | solution.py:188
  22.9 4.7 %collective-permute-start.4 = (bf16[64,64,128]{2,1,0:T(8,128)(2,1)S(1)}, bf16[64,64,128]{2,1,0:T(8,128)(2,1)S(1)}, u32[]{:S(2)}, u32[]{:S(2)}) collective-permute-start(bf16[64,64,128]{2,1,0:T(8,128)(2,1)S(1)} %get-tuple-element.60), channel_id=1, source_target_pairs={{0,1},{1,0},{2,3},{3,2},{4,5},{5,4},{6,7},{7,6},{8,9},{9,8},{10,11... | collective-permute-start | bytes 3145736 | tf_op jit(solution)/shard_map/ppermute | solution.py:415
  27.6 2.3 %tap_rows.1.small_one = f32[64,8,128]{2,1,0:T(8,128)S(1)} custom-call(f32[4,14,40,128]{3,2,1,0:T(8,128)S(1)} %get-tuple-element.62.pad, bf16[8,32,512]{2,1,0:T(8,128)(2,1)S(1)} %get-tuple-element.81.d_conv, f32[16,512]{1,0:T(8,128)S(1)} %get-tuple-element.63.rows), custom_call_target="tpu_custom_call" | custom-call | flops 30000000 | bytes 2000000 | tf_op jit(solution)/shard_map/tap_rows/pallas_call | solution.py:235
  29.9 0.6 collective-permute-start.6
  30.5 1.3 %collective-permute-start.7 = (bf16[3,32,512]{2,1,0:T(8,128)(2,1)S(1)}, bf16[3,32,512]{2,1,0:T(8,128)(2,1)S(1)}, u32[]{:S(2)}, u32[]{:S(2)}) collective-permute-start(bf16[3,32,512]{2,1,0:T(8,128)(2,1)S(1)} %get-tuple-element.64), channel_id=1, source_target_pairs={{0,16},{16,0},{32,48},{48,32},{64,80},{80,64},{96,112},{112,96},{1... | collective-permute-start | bytes 294920 | tf_op jit(solution)/shard_map/ppermute | solution.py:402
  31.9 0.7 collective-permute-start.8
  32.6 4.3 %collective-permute-done.7.row_one = bf16[3,32,512]{2,1,0:T(8,128)(2,1)S(1)} collective-permute-done((bf16[3,32,512]{2,1,0:T(8,128)(2,1)S(1)}, bf16[3,32,512]{2,1,0:T(8,128)(2,1)S(1)}, u32[]{:S(2)}, u32[]{:S(2)}) %collective-permute-start.7) | collective-permute-done | bytes 98336 | tf_op jit(solution)/shard_map/ppermute | solution.py:402
  36.8 1.0 %split_pair.1 = (bf16[32,136,128]{2,1,0:T(8,128)(2,1)S(1)}, bf16[32,48,128]{2,1,0:T(8,128)(2,1)S(1)}, bf16[32,48,128]{2,1,0:T(8,128)(2,1)S(1)}, bf16[32,40,128]{2,1,0:T(8,128)(2,1)S(1)}) custom-call(s32[3]{0:T(128)S(1)} %pad_add_fusion.place.refs_0_, bf16[64,64,128]{2,1,0:T(8,128)(2,1)S(1)} %get-tuple-element.59.out_one, ...), custom_call_target="tpu_custom_call" | custom-call | flops 1000000 | bytes 6000000 | tf_op jit(solution)/shard_map/split_pair/pallas_call | solution.py:270
  37.9 6.0 %collective-permute-start.9 = (bf16[32,48,128]{2,1,0:T(8,128)(2,1)S(1)}, bf16[32,48,128]{2,1,0:T(8,128)(2,1)S(1)}, u32[]{:S(2)}, u32[]{:S(2)}) collective-permute-start(bf16[32,48,128]{2,1,0:T(8,128)(2,1)S(1)} %get-tuple-element.71), channel_id=1, source_target_pairs={{0,32},{1,97},{2,34},{3,99},{4,36},{5,101},{6,38},{7,103},{8,40},{... | collective-permute-start | bytes 1179656 | tf_op jit(solution)/shard_map/ppermute | solution.py:430
  43.9 2.4 %collective-permute-start.10 = (bf16[32,48,128]{2,1,0:T(8,128)(2,1)S(1)}, bf16[32,48,128]{2,1,0:T(8,128)(2,1)S(1)}, u32[]{:S(2)}, u32[]{:S(2)}) collective-permute-start(bf16[32,48,128]{2,1,0:T(8,128)(2,1)S(1)} %get-tuple-element.72), channel_id=1, source_target_pairs={{0,2},{1,19},{2,0},{3,17},{4,6},{5,23},{6,4},{7,21},{8,10},{9,27},... | collective-permute-start | bytes 1179656 | tf_op jit(solution)/shard_map/ppermute | solution.py:430
  46.3 1.6 %collective-permute-start.11 = (bf16[32,40,128]{2,1,0:T(8,128)(2,1)S(1)}, bf16[32,40,128]{2,1,0:T(8,128)(2,1)S(1)}, u32[]{:S(2)}, u32[]{:S(2)}) collective-permute-start(bf16[32,40,128]{2,1,0:T(8,128)(2,1)S(1)} %get-tuple-element.73), channel_id=1, source_target_pairs={{0,4},{1,13},{2,6},{3,15},{4,0},{5,9},{6,2},{7,11},{8,12},{9,5},{1... | collective-permute-start | bytes 983048 | tf_op jit(solution)/shard_map/ppermute | solution.py:430
  47.8 0.1 broadcast_select_fusion.6
  47.9 1.0 %collective-permute-start.12 = (bf16[14,3,512]{2,1,0:T(4,128)(2,1)S(1)}, bf16[14,3,512]{2,1,0:T(4,128)(2,1)S(1)}, u32[]{:S(2)}, u32[]{:S(2)}) collective-permute-start(bf16[14,3,512]{2,1,0:T(4,128)(2,1)S(1)} %get-tuple-element.76), channel_id=1, source_target_pairs={{0,1},{1,0},{2,3},{3,2},{4,5},{5,4},{6,7},{7,6},{8,9},{9,8},{10,11... | collective-permute-start | bytes 129032 | tf_op jit(solution)/shard_map/ppermute | solution.py:402
  49.0 0.7 collective-permute-start.13
  49.6 0.2 collective-permute-done.12.col_one
  49.9 3.5 %collective-permute-done.11.three = bf16[32,40,128]{2,1,0:T(8,128)(2,1)S(1)} collective-permute-done((bf16[32,40,128]{2,1,0:T(8,128)(2,1)S(1)}, bf16[32,40,128]{2,1,0:T(8,128)(2,1)S(1)}, u32[]{:S(2)}, u32[]{:S(2)}) %collective-permute-start.11) | collective-permute-done | bytes 327712 | tf_op jit(solution)/shard_map/ppermute | solution.py:430
  53.4 1.3 %add_pair.1 = bf16[32,136,128]{2,1,0:T(8,128)(2,1)} custom-call(bf16[32,136,128]{2,1,0:T(8,128)(2,1)S(1)} %get-tuple-element.70.keep, bf16[32,48,128]{2,1,0:T(8,128)(2,1)S(1)} %collective-permute-done.9.one, bf16[32,48,128]{2,1,0:T(8,128)(2,1)S(1)} %collective-permute-done.10.two, bf16[32,40,128]{2,1,0:T(8,128)(2,1)S(1)} %collective-permute-done.11.three), custom_call_target="tpu_custom_call" | custom-call | flops 1000000 | bytes 3000000 | tf_op jit(solution)/shard_map/add_pair/pallas_call | solution.py:287
  54.7 8.9 %all-to-all-start = ((bf16[32,136,128]{2,1,0:T(8,128)(2,1)}), bf16[32,136,128]{2,1,0:T(8,128)(2,1)S(1)}, u32[]{:S(2)}, u32[]{:S(2)}) async-start(bf16[32,136,128]{2,1,0:T(8,128)(2,1)} %add_pair.1), calls=%async_computation | async-start | bytes 2228224 | tf_op jit(solution)/shard_map/all_to_all | solution.py:437
  63.6 3.0 %features_main.1.total = f32[4,8,32,128]{3,2,1,0:T(8,128)S(1)} custom-call(s32[3]{0:T(128)S(1)} %pad_add_fusion.place.refs_0_, bf16[8,32,512]{2,1,0:T(8,128)(2,1)S(1)} %get-tuple-element.81.d_conv, bf16[3,32,512]{2,1,0:T(8,128)(2,1)S(1)} %collective-permute-done.7.row_one, bf16[3,32,512]{2,1,0:T(8,128)(2,1)S(1)} %collective-permute-done.8.row_two, ...), custom_call_target="tpu_custom_call" | custom-call | flops 30000000 | bytes 2000000 | tf_op jit(solution)/shard_map/features_main/pallas_call | solution.py:342
  66.6 1.8 %features_edge.1 = bf16[8,32,512]{2,1,0:T(8,128)(2,1)} custom-call(s32[3]{0:T(128)S(1)} %pad_add_fusion.place.refs_0_, f32[4,8,32,128]{3,2,1,0:T(8,128)S(1)} %features_main.1.total, bf16[14,3,512]{2,1,0:T(4,128)(2,1)S(1)} %collective-permute-done.12.col_one, bf16[14,3,512]{2,1,0:T(4,128)(2,1)S(1)} %collective-permute-done.13.col_two, ...), custom_call_target="tpu_custom_call" | custom-call | flops 6000000 | bytes 1000000 | tf_op jit(solution)/shard_map/features_edge/pallas_call | solution.py:384
  68.4 14.4 %all-to-all-done.refs_1_ = bf16[32,136,128]{2,1,0:T(8,128)(2,1)S(1)} async-done(((bf16[32,136,128]{2,1,0:T(8,128)(2,1)}), bf16[32,136,128]{2,1,0:T(8,128)(2,1)S(1)}, u32[]{:S(2)}, u32[]{:S(2)}) %all-to-all-start) | async-done | bytes 1114144 | tf_op jit(solution)/shard_map/all_to_all | solution.py:437
  82.8 1.4 %sum_chips.1 = (f32[4,2048]{1,0:T(4,128)}, f32[16,512]{1,0:T(8,128)}, f32[4,54]{1,0:T(4,128)}, f32[1,16]{1,0:T(1,128)}) custom-call(s32[3]{0:T(128)S(1)} %pad_add_fusion.place.refs_0_, bf16[32,136,128]{2,1,0:T(8,128)(2,1)S(1)} %all-to-all-done.refs_1_), custom_call_target="tpu_custom_call" | custom-call | flops 1000000 | bytes 1000000 | tf_op jit(solution)/shard_map/sum_chips/pallas_call | solution.py:315
  (18 shorter events, 0.2 us)
Async XLA Ops:
  1.6 11.8 %collective-permute-start.1 = (bf16[3,32,512]{2,1,0:T(8,128)(2,1)S(1)}, bf16[3,32,512]{2,1,0:T(8,128)(2,1)S(1)}, u32[]{:S(2)}, u32[]{:S(2)}) collective-permute-start(bf16[3,32,512]{2,1,0:T(8,128)(2,1)S(1)} %get-tuple-element.92), channel_id=1, source_target_pairs={{16,32},{32,16},{48,64},{64,48},{80,96},{96,80},{17,33},{33,17},{4... | collective-permute-start | bytes 294920 | tf_op jit(solution)/shard_map/ppermute | solution.py:402
  2.3 11.1 %collective-permute-start = (bf16[3,32,512]{2,1,0:T(8,128)(2,1)S(1)}, bf16[3,32,512]{2,1,0:T(8,128)(2,1)S(1)}, u32[]{:S(2)}, u32[]{:S(2)}) collective-permute-start(bf16[3,32,512]{2,1,0:T(8,128)(2,1)S(1)} %get-tuple-element.93), channel_id=1, source_target_pairs={{0,16},{16,0},{32,48},{48,32},{64,80},{80,64},{96,112},{112,96},{1... | collective-permute-start | bytes 294920 | tf_op jit(solution)/shard_map/ppermute | solution.py:402
  13.6 1.3 %collective-permute-start.2 = (bf16[14,3,512]{2,1,0:T(4,128)(2,1)S(1)}, bf16[14,3,512]{2,1,0:T(4,128)(2,1)S(1)}, u32[]{:S(2)}, u32[]{:S(2)}) collective-permute-start(bf16[14,3,512]{2,1,0:T(4,128)(2,1)S(1)} %get-tuple-element.49), channel_id=1, source_target_pairs={{0,1},{1,0},{2,3},{3,2},{4,5},{5,4},{6,7},{7,6},{8,9},{9,8},{10,11... | collective-permute-start | bytes 129032 | tf_op jit(solution)/shard_map/ppermute | solution.py:402
  13.7 1.2 %collective-permute-start.3 = (bf16[14,3,512]{2,1,0:T(4,128)(2,1)S(1)}, bf16[14,3,512]{2,1,0:T(4,128)(2,1)S(1)}, u32[]{:S(2)}, u32[]{:S(2)}) collective-permute-start(bf16[14,3,512]{2,1,0:T(4,128)(2,1)S(1)} %get-tuple-element.50), channel_id=1, source_target_pairs={{1,2},{2,1},{3,4},{4,3},{5,6},{6,5},{7,8},{8,7},{9,10},{10,9},{11,... | collective-permute-start | bytes 129032 | tf_op jit(solution)/shard_map/ppermute | solution.py:402
  22.9 14.0 %collective-permute-start.4 = (bf16[64,64,128]{2,1,0:T(8,128)(2,1)S(1)}, bf16[64,64,128]{2,1,0:T(8,128)(2,1)S(1)}, u32[]{:S(2)}, u32[]{:S(2)}) collective-permute-start(bf16[64,64,128]{2,1,0:T(8,128)(2,1)S(1)} %get-tuple-element.60), channel_id=1, source_target_pairs={{0,1},{1,0},{2,3},{3,2},{4,5},{5,4},{6,7},{7,6},{8,9},{9,8},{10,11... | collective-permute-start | bytes 3145736 | tf_op jit(solution)/shard_map/ppermute | solution.py:415
  27.6 9.2 %collective-permute-start.5 = (bf16[64,64,128]{2,1,0:T(8,128)(2,1)S(1)}, bf16[64,64,128]{2,1,0:T(8,128)(2,1)S(1)}, u32[]{:S(2)}, u32[]{:S(2)}) collective-permute-start(bf16[64,64,128]{2,1,0:T(8,128)(2,1)S(1)} %get-tuple-element.61), channel_id=1, source_target_pairs={{0,1},{1,0},{2,3},{3,2},{4,5},{5,4},{6,7},{7,6},{8,9},{9,8},{10,11... | collective-permute-start | bytes 3145736 | tf_op jit(solution)/shard_map/ppermute | solution.py:415
  29.9 6.9 %collective-permute-start.6 = (f32[64,8,128]{2,1,0:T(8,128)S(1)}, f32[64,8,128]{2,1,0:T(8,128)S(1)}, u32[]{:S(2)}, u32[]{:S(2)}) collective-permute-start(f32[64,8,128]{2,1,0:T(8,128)S(1)} %tap_rows.1.small_one), channel_id=1, source_target_pairs={{0,1},{1,0},{2,3},{3,2},{4,5},{5,4},{6,7},{7,6},{8,9},{9,8},{10,11... | collective-permute-start | bytes 786440 | tf_op jit(solution)/shard_map/ppermute | solution.py:415
  30.5 6.3 %collective-permute-start.7 = (bf16[3,32,512]{2,1,0:T(8,128)(2,1)S(1)}, bf16[3,32,512]{2,1,0:T(8,128)(2,1)S(1)}, u32[]{:S(2)}, u32[]{:S(2)}) collective-permute-start(bf16[3,32,512]{2,1,0:T(8,128)(2,1)S(1)} %get-tuple-element.64), channel_id=1, source_target_pairs={{0,16},{16,0},{32,48},{48,32},{64,80},{80,64},{96,112},{112,96},{1... | collective-permute-start | bytes 294920 | tf_op jit(solution)/shard_map/ppermute | solution.py:402
  31.9 5.0 %collective-permute-start.8 = (bf16[3,32,512]{2,1,0:T(8,128)(2,1)S(1)}, bf16[3,32,512]{2,1,0:T(8,128)(2,1)S(1)}, u32[]{:S(2)}, u32[]{:S(2)}) collective-permute-start(bf16[3,32,512]{2,1,0:T(8,128)(2,1)S(1)} %get-tuple-element.65), channel_id=1, source_target_pairs={{16,32},{32,16},{48,64},{64,48},{80,96},{96,80},{17,33},{33,17},{4... | collective-permute-start | bytes 294920 | tf_op jit(solution)/shard_map/ppermute | solution.py:402
  37.9 15.5 %collective-permute-start.9 = (bf16[32,48,128]{2,1,0:T(8,128)(2,1)S(1)}, bf16[32,48,128]{2,1,0:T(8,128)(2,1)S(1)}, u32[]{:S(2)}, u32[]{:S(2)}) collective-permute-start(bf16[32,48,128]{2,1,0:T(8,128)(2,1)S(1)} %get-tuple-element.71), channel_id=1, source_target_pairs={{0,32},{1,97},{2,34},{3,99},{4,36},{5,101},{6,38},{7,103},{8,40},{... | collective-permute-start | bytes 1179656 | tf_op jit(solution)/shard_map/ppermute | solution.py:430
  43.9 9.6 %collective-permute-start.10 = (bf16[32,48,128]{2,1,0:T(8,128)(2,1)S(1)}, bf16[32,48,128]{2,1,0:T(8,128)(2,1)S(1)}, u32[]{:S(2)}, u32[]{:S(2)}) collective-permute-start(bf16[32,48,128]{2,1,0:T(8,128)(2,1)S(1)} %get-tuple-element.72), channel_id=1, source_target_pairs={{0,2},{1,19},{2,0},{3,17},{4,6},{5,23},{6,4},{7,21},{8,10},{9,27},... | collective-permute-start | bytes 1179656 | tf_op jit(solution)/shard_map/ppermute | solution.py:430
  46.3 7.2 %collective-permute-start.11 = (bf16[32,40,128]{2,1,0:T(8,128)(2,1)S(1)}, bf16[32,40,128]{2,1,0:T(8,128)(2,1)S(1)}, u32[]{:S(2)}, u32[]{:S(2)}) collective-permute-start(bf16[32,40,128]{2,1,0:T(8,128)(2,1)S(1)} %get-tuple-element.73), channel_id=1, source_target_pairs={{0,4},{1,13},{2,6},{3,15},{4,0},{5,9},{6,2},{7,11},{8,12},{9,5},{1... | collective-permute-start | bytes 983048 | tf_op jit(solution)/shard_map/ppermute | solution.py:430
  47.9 1.9 %collective-permute-start.12 = (bf16[14,3,512]{2,1,0:T(4,128)(2,1)S(1)}, bf16[14,3,512]{2,1,0:T(4,128)(2,1)S(1)}, u32[]{:S(2)}, u32[]{:S(2)}) collective-permute-start(bf16[14,3,512]{2,1,0:T(4,128)(2,1)S(1)} %get-tuple-element.76), channel_id=1, source_target_pairs={{0,1},{1,0},{2,3},{3,2},{4,5},{5,4},{6,7},{7,6},{8,9},{9,8},{10,11... | collective-permute-start | bytes 129032 | tf_op jit(solution)/shard_map/ppermute | solution.py:402
  49.0 0.9 %collective-permute-start.13 = (bf16[14,3,512]{2,1,0:T(4,128)(2,1)S(1)}, bf16[14,3,512]{2,1,0:T(4,128)(2,1)S(1)}, u32[]{:S(2)}, u32[]{:S(2)}) collective-permute-start(bf16[14,3,512]{2,1,0:T(4,128)(2,1)S(1)} %get-tuple-element.77), channel_id=1, source_target_pairs={{1,2},{2,1},{3,4},{4,3},{5,6},{6,5},{7,8},{8,7},{9,10},{10,9},{11,... | collective-permute-start | bytes 129032 | tf_op jit(solution)/shard_map/ppermute | solution.py:402
  54.7 28.1 %all-to-all-start = ((bf16[32,136,128]{2,1,0:T(8,128)(2,1)}), bf16[32,136,128]{2,1,0:T(8,128)(2,1)S(1)}, u32[]{:S(2)}, u32[]{:S(2)}) async-start(bf16[32,136,128]{2,1,0:T(8,128)(2,1)} %add_pair.1), calls=%async_computation | async-start | bytes 2228224 | tf_op jit(solution)/shard_map/all_to_all | solution.py:437
